TPU v7x, 32 devices: a whole 2x2x4 slice. The times are simulated.
32 devices in a mesh: px: 8 (over z, x), py: 4 (over y, core).
Axes of the slice: x: 2, y: 2, z: 4, core: 2. Of those that a mesh axis runs over, the one named last changes fastest.
Arguments:
- coords: float32 [3, 65536], P(None, ('px', 'py')), may hold values from -6 to 6
- displacement: float32 [3, 65536], P(None, ('px', 'py')), may hold values from -3 to 3
- velocity: float32 [3, 65536], P(None, ('px', 'py')), may hold values from -6 to 6
- inv_mass: float32 [65536], P(('px', 'py')), may hold values from 0.5 to 2
- ext_force: float32 [3, 65536], P(None, ('px', 'py')), may hold values from -6 to 6
- thickness: float32 [65536], P(('px', 'py')), may hold values from 0.5 to 2
- stiffness: float32 [12, 12], replicated, may hold values from -12 to 12
- elem_nodes: int32 [4, 65536], P(None, ('px', 'py')), may hold values from 0 to 4095
- block_class: int32 [512], P(('px', 'py')), may hold values from 0 to 1
- halo_lists: int32 [4, 16384], P(None, ('px', 'py')), may hold values from 0 to 2047
- contact_nodes: int32 [65536], P(('px', 'py')), may hold values from 0 to 2047
- contact_bucket: int32 [65536, 1], P(('px', 'py')), may hold values from 0 to 31; in each aligned block of 2048 rows (0 to 2047, 2048 to 4095, ...) at most 128 rows name the same one
- tile_pairs: int32 [2, 512], P(None, ('px', 'py')), may hold values from 0 to 31
Outputs:
- disp_out: float32 [3, 65536], P(None, ('px', 'py'))
- vel_out: float32 [3, 65536], P(None, ('px', 'py'))
Inputs may be any that keep to these rules, and one draw needn't show every extreme that they name: `elem_nodes`: indices into the device's extended list: 2048 own nodes, then four blocks of 512 received nodes. `halo_lists`: row 0 is sent to the neighbour one lower along px, row 1 one higher along px, row 2 one lower along py, row 3 one higher along py; entries are own node indices. `block_class`: class of each block of 128 consecutive elements. `contact_nodes`: own node indices of the device. `contact_bucket`: among the 2048 rows of one device no bucket is named more than 128 times, and in every draw some device names some bucket exactly 128 times. `tile_pairs`: tile numbers within the device's own bucket.
All inputs are finite; a program needn't handle non-finite values.
Results may differ from a plain program's by a relative error of at most 0.0003.
Values sent between devices are 32-bit elements; how exact they have to be, the bound alone decides.
No kernel may reach another device: no remote copies, remote signals or barrier semaphores. Data moves between devices by JAX's collectives and lax.ppermute only.
A program may use at most 64 MiB of HBM per device.

v0:
```python
import jax
import jax.numpy as jnp
from jax import lax
from jax.sharding import PartitionSpec as P

TILE = 128
EBLK = 128
STEPS = 2
SUBS = 2


FAR = 10000.0
DT = 0.05
PENALTY = 0.5
REACH = 4.0


def padded_2(cells, sides, width):
    for axis, dim in sides:
        count = lax.axis_size(axis)
        ends = count - 1
        head = lax.slice_in_dim(cells, 0, width, axis=dim)
        tail = lax.slice_in_dim(cells, cells.shape[dim] - width, cells.shape[dim], axis=dim)
        cells = jnp.concatenate(
            [
                lax.ppermute(tail, axis, [(i, (i + 1) % count) for i in range(ends)]),
                cells,
                lax.ppermute(head, axis, [((i + 1) % count, i) for i in range(ends)]),
            ],
            axis=dim,
        )
    return cells


def arrange(blocks):
    return jnp.stack([jnp.stack([blocks[0], blocks[3]]), jnp.stack([blocks[2], blocks[1]])])


def extend_edges(values, lists):
    picked = values[:, lists]
    square = arrange([picked[:, 0], picked[:, 1], picked[:, 2], picked[:, 3]])
    padded = padded_2(square, (("px", 0), ("py", 1)), 1)
    return jnp.concatenate([values, padded[0, 2], padded[3, 1], padded[1, 0], padded[2, 3]], axis=1)


def return_edges(force_ext, lists, owned_count):
    halo_width = lists.shape[1]
    blocks = [
        force_ext[:, owned_count + number * halo_width : owned_count + (number + 1) * halo_width]
        for number in range(4)
    ]
    padded = padded_2(arrange(blocks), (("px", 0), ("py", 1)), 1)
    returned = jnp.stack([padded[0, 2], padded[3, 1], padded[1, 0], padded[2, 3]], axis=1).reshape(
        3, -1
    )
    added = jnp.zeros((3, owned_count), jnp.float32).at[:, lists.reshape(-1)].add(returned)
    return force_ext[:, :owned_count] + added


def element_forces(ext_values, elem_nodes, thickness, stiffness):
    corners = ext_values[:, elem_nodes]
    local = corners.reshape(12, elem_nodes.shape[1])
    return thickness[None, :] * jnp.dot(stiffness, local, precision=lax.Precision.HIGHEST)


def assemble(forces, elem_nodes, extended):
    return (
        jnp.zeros((3, extended), jnp.float32)
        .at[:, elem_nodes.reshape(-1)]
        .add(forces.reshape(3, -1))
    )


def contact_slots(bucket, devices, capacity):
    onehot = (bucket[:, None] == jnp.arange(devices, dtype=jnp.int32)[None, :]).astype(jnp.int32)
    before = jnp.cumsum(onehot, axis=0) - onehot
    ranks = jnp.sum(before * onehot, axis=1)
    return bucket * capacity + ranks


def tile_forces(arrived, tile_pairs):
    tiles = arrived.reshape(3, -1, TILE)
    tile_count = tiles.shape[1]
    pair_count = tile_pairs.shape[1]
    group = min(pair_count, 64)
    grouped = tile_pairs.reshape(2, pair_count // group, group).transpose(1, 0, 2)
    numbers = jnp.arange(tile_count, dtype=jnp.int32)

    def one_group(total, pair_group):
        firsts = pair_group[0]
        pos_a = tiles[:, firsts]
        pos_b = tiles[:, pair_group[1]]
        gap = pos_a[:, :, :, None] - pos_b[:, :, None, :]
        dist = jnp.sum(gap * gap, axis=0)
        weight = PENALTY * jnp.exp(-dist / REACH)
        push = jnp.sum(weight[None] * gap, axis=3)
        onehot = (numbers[:, None] == firsts[None, :]).astype(jnp.float32)
        flat = jnp.transpose(push, (1, 0, 2)).reshape(group, 3 * TILE)
        return (total + jnp.dot(onehot, flat, precision=lax.Precision.HIGHEST), None)

    start = jnp.zeros((tile_count, 3 * TILE), jnp.float32)
    total, unused = lax.scan(one_group, start, grouped)
    return jnp.transpose(total.reshape(tile_count, 3, TILE), (1, 0, 2)).reshape(3, -1)


def contact_forces(positions, contact_nodes, slot_ids, tile_pairs, devices, capacity):
    width = devices * capacity
    outgoing = (
        jnp.full((3, width), FAR, jnp.float32).at[:, slot_ids].set(positions[:, contact_nodes])
    )
    arrived = lax.all_to_all(
        outgoing.reshape(3, devices, capacity),
        ("px", "py"),
        split_axis=1,
        concat_axis=1,
        tiled=True,
    ).reshape(3, width)
    pushes = tile_forces(arrived, tile_pairs)
    returned = lax.all_to_all(
        pushes.reshape(3, devices, capacity), ("px", "py"), split_axis=1, concat_axis=1, tiled=True
    ).reshape(3, width)
    return (
        jnp.zeros((3, positions.shape[1]), jnp.float32)
        .at[:, contact_nodes]
        .add(returned[:, slot_ids])
    )


def body(
    coords,
    displacement,
    velocity,
    inv_mass,
    ext_force,
    thickness,
    stiffness,
    elem_nodes,
    block_class,
    halo_lists,
    contact_nodes,
    contact_bucket,
    tile_pairs,
):
    owned_count = coords.shape[1]
    extended = owned_count + 4 * halo_lists.shape[1]
    devices = lax.axis_size("px") * lax.axis_size("py")
    capacity = 2 * contact_nodes.shape[0] // devices
    slot_ids = contact_slots(contact_bucket[:, 0], devices, capacity)
    slow_elems = jnp.repeat(block_class, EBLK) == 1
    for step_no in range(STEPS):
        contact = contact_forces(
            coords + displacement, contact_nodes, slot_ids, tile_pairs, devices, capacity
        )
        held_forces = None
        for sub_no in range(SUBS):
            ext_disp = extend_edges(displacement, halo_lists)
            forces = element_forces(ext_disp, elem_nodes, thickness, stiffness)
            if sub_no == 0:
                held_forces = forces
            else:
                forces = jnp.where(slow_elems[None, :], held_forces, forces)
            internal = return_edges(assemble(forces, elem_nodes, extended), halo_lists, owned_count)
            accel = inv_mass[None, :] * (ext_force - internal + contact)
            velocity = velocity + DT * accel
            displacement = displacement + DT * velocity
    return (displacement, velocity)


def solution(mesh):
    placed = (
        P(None, ("px", "py")),
        P(None, ("px", "py")),
        P(None, ("px", "py")),
        P(("px", "py")),
        P(None, ("px", "py")),
        P(("px", "py")),
        P(),
        P(None, ("px", "py")),
        P(("px", "py")),
        P(None, ("px", "py")),
        P(("px", "py")),
        P(("px", "py"), None),
        P(None, ("px", "py")),
    )
    return jax.shard_map(
        body,
        mesh=mesh,
        in_specs=placed,
        out_specs=(P(None, ("px", "py")), P(None, ("px", "py"))),
        check_vma=False,
    )
```

profile of v0, /device:TPU:0, one launch (start us, length us, event | category | flops | bytes accessed | tf_op | source)
XLA Modules:
  0.0 633.0 jit_solution(17033886220025861290)
XLA Ops:
  16.0 9.1 %reduce-window.6 = s32[32,16,128]{2,1,0:T(8,128)S(1)} reduce-window(s32[32,16,128]{2,1,0:T(8,128)S(1)} %fusion.37, s32[]{:T(128)} %constant.21.clone.1), window={size=1x1x128 pad=0_0x0_0x127_0}, to_apply=%region_2.3 | reduce-window | flops 8323072 | bytes 524292 | tf_op jit(solution)/shard_map/reduce-window
  26.3 13.1 %scatter_custom_fusion.2 = f32[3,4096]{0,1:T(8,128)S(1)} fusion(s32[2048]{0:T(1024)S(1)} %bitcast.407, f32[3,2048]{0,1:T(8,128)S(1)} %copy.328, s32[2048]{0:T(1024)S(1)} %get-tuple-element.99, f32[]{:T(128)} %constant.24.clone.1), kind=kCustom, calls=%fused_computation.62 | custom fusion | bytes 49156 | tf_op jit(solution)/shard_map/scatter | solution.py:109
  40.7 7.0 %all-to-all-start = ((f32[3,32,128]{2,0,1:T(4,128)}), f32[3,32,128]{2,0,1:T(4,128)S(1)}, u32[]{:S(2)}, u32[]{:S(2)}) async-start(f32[3,32,128]{2,0,1:T(4,128)} %copy.329), calls=%async_computation | async-start | bytes 131072 | tf_op jit(solution)/shard_map/all_to_all | solution.py:111
  58.6 27.8 %gather_fusion.1 = f32[8192,3]{1,0:T(8,128)} fusion(f32[3,4096]{0,1:T(8,128)S(1)} %copy.313, s32[8192]{0:T(1024)S(1)} %broadcast_clamp_fusion), kind=kCustom, calls=%fused_computation.1 | custom fusion | bytes 229376 | tf_op jit(solution)/shard_map/gather | solution.py:61
  92.3 40.9 %scatter_custom_fusion = f32[3,4096]{0,1:T(8,128)S(1)} fusion(s32[8192]{0:T(1024)S(1)} %bitcast.411, f32[3,8192]{0,1:T(8,128)} %copy.315, f32[]{:T(128)} %constant.20.clone.1), kind=kCustom, calls=%fused_computation.38 | custom fusion | flops 24576 | bytes 147460 | tf_op jit(solution)/shard_map/scatter-add | solution.py:70
  154.0 8.1 %all-to-all-start.1 = ((f32[3,32,128]{2,0,1:T(4,128)}), f32[3,32,128]{2,0,1:T(4,128)S(1)}, u32[]{:S(2)}, u32[]{:S(2)}) async-start(f32[3,32,128]{2,0,1:T(4,128)} %copy.334), calls=%async_computation.1 | async-start | bytes 131072 | tf_op jit(solution)/shard_map/all_to_all | solution.py:119
  162.5 11.9 %scatter_fusion = f32[3,2048]{0,1:T(8,128)S(1)} fusion(f32[3,2048]{0,1:T(8,128)S(1)} %slice-done.1, s32[2048]{0:T(1024)S(1)} %bitcast.375, f32[2048,3]{1,0:T(8,128)S(1)} %bitcast.363), kind=kCustom, calls=%fused_computation.17 | custom fusion | flops 6144 | bytes 81920 | tf_op jit(solution)/shard_map/scatter-add | solution.py:56
  175.4 17.8 %scatter_custom_fusion.3 = f32[3,2048]{0,1:T(8,128)S(1)} fusion(s32[2048]{0:T(1024)} %get-tuple-element.100, f32[3,4096]{0,1:T(8,128)S(1)} %bitcast.361, s32[2048]{0:T(1024)} %broadcast_clamp_fusion.1, f32[]{:T(128)} %constant.20.clone.1), kind=kCustom, calls=%fused_computation.60 | custom fusion | flops 6144 | bytes 25088 | tf_op jit(solution)/shard_map/scatter-add | solution.py:125
  194.0 5.5 gather_fusion.4
  214.4 27.8 %gather_fusion.5 = f32[8192,3]{1,0:T(8,128)} fusion(f32[3,4096]{0,1:T(8,128)S(1)} %copy.347, s32[8192]{0:T(1024)S(1)} %broadcast_clamp_fusion), kind=kCustom, calls=%fused_computation.7 | custom fusion | bytes 229376 | tf_op jit(solution)/shard_map/gather | solution.py:61
  248.0 40.8 %scatter_custom_fusion.4 = f32[3,4096]{0,1:T(8,128)S(1)} fusion(s32[8192]{0:T(1024)} %bitcast.412, f32[3,8192]{0,1:T(8,128)} %copy.349, f32[]{:T(128)} %constant.20.clone.1), kind=kCustom, calls=%fused_computation.36 | custom fusion | flops 24576 | bytes 4243968 | tf_op jit(solution)/shard_map/scatter-add | solution.py:70
  307.1 11.9 %scatter_fusion.1 = f32[3,2048]{0,1:T(8,128)S(1)} fusion(f32[3,2048]{0,1:T(8,128)S(1)} %slice.424, s32[2048]{0:T(1024)S(1)} %bitcast.376, f32[2048,3]{1,0:T(8,128)S(1)} %bitcast.364), kind=kCustom, calls=%fused_computation.21 | custom fusion | flops 6144 | bytes 81920 | tf_op jit(solution)/shard_map/scatter-add | solution.py:56
  319.8 5.5 gather_fusion.6
  343.0 27.8 %gather_fusion.7 = f32[8192,3]{1,0:T(8,128)} fusion(f32[3,4096]{0,1:T(8,128)S(1)} %copy.371, s32[8192]{0:T(1024)S(1)} %broadcast_clamp_fusion), kind=kCustom, calls=%fused_computation.9 | custom fusion | bytes 229376 | tf_op jit(solution)/shard_map/gather | solution.py:61
  376.6 40.8 %scatter_custom_fusion.6 = f32[3,4096]{0,1:T(8,128)S(1)} fusion(s32[8192]{0:T(1024)} %bitcast.413, f32[3,8192]{0,1:T(8,128)} %copy.373, f32[]{:T(128)} %constant.20.clone.1), kind=kCustom, calls=%fused_computation.34 | custom fusion | flops 24576 | bytes 4243968 | tf_op jit(solution)/shard_map/scatter-add | solution.py:70
  426.9 14.2 %scatter_custom_fusion.8 = f32[3,4096]{0,1:T(8,128)} fusion(s32[2048]{0:T(1024)S(1)} %bitcast.409, f32[3,2048]{0,1:T(8,128)S(1)} %copy.384, s32[2048]{0:T(1024)} %copy-done.19, f32[]{:T(128)} %constant.24.clone.1), kind=kCustom, calls=%fused_computation.58 | custom fusion | bytes 49664 | tf_op jit(solution)/shard_map/scatter | solution.py:109
  443.9 8.8 %all-to-all-start.2 = ((f32[3,32,128]{2,0,1:T(4,128)}), f32[3,32,128]{2,0,1:T(4,128)S(1)}, u32[]{:S(2)}, u32[]{:S(2)}) async-start(f32[3,32,128]{2,0,1:T(4,128)} %copy.385), calls=%async_computation.2 | async-start | bytes 131072 | tf_op jit(solution)/shard_map/all_to_all | solution.py:111
  467.1 7.4 %all-to-all-start.3 = ((f32[3,32,128]{2,0,1:T(4,128)}), f32[3,32,128]{2,0,1:T(4,128)S(1)}, u32[]{:S(2)}, u32[]{:S(2)}) async-start(f32[3,32,128]{2,0,1:T(4,128)} %copy.390), calls=%async_computation.3 | async-start | bytes 131072 | tf_op jit(solution)/shard_map/all_to_all | solution.py:119
  474.9 12.1 %scatter_fusion.2 = f32[3,2048]{0,1:T(8,128)S(1)} fusion(f32[3,2048]{0,1:T(8,128)S(1)} %slice-done, s32[2048]{0:T(1024)S(1)} %bitcast.377, f32[2048,3]{1,0:T(8,128)S(1)} %bitcast.365), kind=kCustom, calls=%fused_computation.23 | custom fusion | flops 6144 | bytes 81920 | tf_op jit(solution)/shard_map/scatter-add | solution.py:56
  488.0 17.8 %scatter_custom_fusion.9 = f32[3,2048]{0,1:T(8,128)S(1)} fusion(s32[2048]{0:T(1024)} %get-tuple-element.100, f32[3,4096]{0,1:T(8,128)S(1)} %bitcast.360, s32[2048]{0:T(1024)} %broadcast_clamp_fusion.1, f32[]{:T(128)} %constant.20.clone.1), kind=kCustom, calls=%fused_computation.56 | custom fusion | flops 6144 | bytes 25088 | tf_op jit(solution)/shard_map/scatter-add | solution.py:125
  506.6 5.5 gather_fusion.10
  526.9 27.8 %gather_fusion.11 = f32[8192,3]{1,0:T(8,128)} fusion(f32[3,4096]{0,1:T(8,128)S(1)} %copy.403, s32[8192]{0:T(1024)S(1)} %broadcast_clamp_fusion), kind=kCustom, calls=%fused_computation.15 | custom fusion | bytes 229376 | tf_op jit(solution)/shard_map/gather | solution.py:61
  560.6 40.8 %scatter_custom_fusion.10 = f32[3,4096]{0,1:T(8,128)S(1)} fusion(s32[8192]{0:T(1024)} %bitcast.414, f32[3,8192]{0,1:T(8,128)} %copy.405, f32[]{:T(128)} %constant.20.clone.1), kind=kCustom, calls=%fused_computation.32 | custom fusion | flops 24576 | bytes 4243968 | tf_op jit(solution)/shard_map/scatter-add | solution.py:70
  619.7 11.9 %scatter_fusion.3 = f32[3,2048]{0,1:T(8,128)S(1)} fusion(f32[3,2048]{0,1:T(8,128)S(1)} %slice.466, s32[2048]{0:T(1024)S(1)} %bitcast.378, f32[2048,3]{1,0:T(8,128)S(1)} %bitcast.362), kind=kCustom, calls=%fused_computation.27 | custom fusion | flops 6144 | bytes 81920 | tf_op jit(solution)/shard_map/scatter-add | solution.py:56
  (368 shorter events, 187.9 us)
Async XLA Ops:
  9.7 40.6 %collective-permute-start = (f32[1,2,3,512]{3,1,2,0:T(2,128)S(1)}, f32[1,2,3,512]{3,1,2,0:T(2,128)S(1)}, u32[]{:S(2)}, u32[]{:S(2)}) collective-permute-start(f32[1,2,3,512]{3,1,2,0:T(2,128)S(1)} %maximum_bitcast_fusion), channel_id=1, source_target_pairs={{0,4},{4,8},{8,12},{12,16},{16,20},{20,24},{24,28},{1,5},{5,9},{9,... | collective-permute-start | bytes 36872 | tf_op jit(solution)/shard_map/ppermute | solution.py:26
  14.6 35.7 %collective-permute-start.1 = (f32[1,2,3,512]{3,1,2,0:T(2,128)S(1)}, f32[1,2,3,512]{3,1,2,0:T(2,128)S(1)}, u32[]{:S(2)}, u32[]{:S(2)}) collective-permute-start(f32[1,2,3,512]{3,1,2,0:T(2,128)S(1)} %maximum_bitcast_fusion.1), channel_id=1, source_target_pairs={{4,0},{8,4},{12,8},{16,12},{20,16},{24,20},{28,24},{5,1},{9,5},{13... | collective-permute-start | bytes 36872 | tf_op jit(solution)/shard_map/ppermute | solution.py:28
  40.7 108.0 %all-to-all-start = ((f32[3,32,128]{2,0,1:T(4,128)}), f32[3,32,128]{2,0,1:T(4,128)S(1)}, u32[]{:S(2)}, u32[]{:S(2)}) async-start(f32[3,32,128]{2,0,1:T(4,128)} %copy.329), calls=%async_computation | async-start | bytes 131072 | tf_op jit(solution)/shard_map/all_to_all | solution.py:111
  137.2 5.6 collective-permute-start.5
  142.9 5.5 collective-permute-start.7
  154.0 20.7 %all-to-all-start.1 = ((f32[3,32,128]{2,0,1:T(4,128)}), f32[3,32,128]{2,0,1:T(4,128)S(1)}, u32[]{:S(2)}, u32[]{:S(2)}) async-start(f32[3,32,128]{2,0,1:T(4,128)} %copy.334), calls=%async_computation.1 | async-start | bytes 131072 | tf_op jit(solution)/shard_map/all_to_all | solution.py:119
  199.9 6.0 collective-permute-start.9
  201.2 6.0 collective-permute-start.8
  289.2 6.0 collective-permute-start.12
  293.8 6.8 %collective-permute-start.13 = (f32[1,2,3,512]{3,1,2,0:T(2,128)S(1)}, f32[1,2,3,512]{3,1,2,0:T(2,128)S(1)}, u32[]{:S(2)}, u32[]{:S(2)}) collective-permute-start(f32[1,2,3,512]{3,1,2,0:T(2,128)S(1)} %maximum_bitcast_fusion.5), channel_id=1, source_target_pairs={{4,0},{8,4},{12,8},{16,12},{20,16},{24,20},{28,24},{5,1},{9,5},{13... | collective-permute-start | bytes 36872 | tf_op jit(solution)/shard_map/ppermute | solution.py:28
  300.6 5.3 collective-permute-start.15
  325.6 6.6 %collective-permute-start.17 = (f32[1,2,3,512]{3,2,1,0:T(4,128)S(1)}, f32[1,2,3,512]{3,2,1,0:T(4,128)S(1)}, u32[]{:S(2)}, u32[]{:S(2)}) collective-permute-start(f32[1,2,3,512]{3,2,1,0:T(4,128)S(1)} %bitcast.394), channel_id=1, source_target_pairs={{4,0},{8,4},{12,8},{16,12},{20,16},{24,20},{28,24},{5,1},{9,5},{13... | collective-permute-start | bytes 36872 | tf_op jit(solution)/shard_map/ppermute | solution.py:28
  327.0 6.6 %collective-permute-start.16 = (f32[1,2,3,512]{3,2,1,0:T(4,128)S(1)}, f32[1,2,3,512]{3,2,1,0:T(4,128)S(1)}, u32[]{:S(2)}, u32[]{:S(2)}) collective-permute-start(f32[1,2,3,512]{3,2,1,0:T(4,128)S(1)} %bitcast.400), channel_id=1, source_target_pairs={{0,4},{4,8},{8,12},{12,16},{16,20},{20,24},{24,28},{1,5},{5,9},{9,... | collective-permute-start | bytes 36872 | tf_op jit(solution)/shard_map/ppermute | solution.py:26
  336.5 5.8 collective-permute-start.19
  418.7 35.4 %collective-permute-start.20 = (f32[1,2,3,512]{3,1,2,0:T(2,128)}, f32[1,2,3,512]{3,1,2,0:T(2,128)}, u32[]{:S(2)}, u32[]{:S(2)}) collective-permute-start(f32[1,2,3,512]{3,1,2,0:T(2,128)} %maximum_bitcast_fusion.6), channel_id=1, source_target_pairs={{0,4},{4,8},{8,12},{12,16},{16,20},{20,24},{24,28},{1,5},{5,9},{9,... | collective-permute-start | bytes 36872 | tf_op jit(solution)/shard_map/ppermute | solution.py:26
  425.0 29.9 %collective-permute-start.21 = (f32[1,2,3,512]{3,1,2,0:T(2,128)}, f32[1,2,3,512]{3,1,2,0:T(2,128)}, u32[]{:S(2)}, u32[]{:S(2)}) collective-permute-start(f32[1,2,3,512]{3,1,2,0:T(2,128)} %maximum_bitcast_fusion.7), channel_id=1, source_target_pairs={{4,0},{8,4},{12,8},{16,12},{20,16},{24,20},{28,24},{5,1},{9,5},{13... | collective-permute-start | bytes 36872 | tf_op jit(solution)/shard_map/ppermute | solution.py:28
  443.9 17.6 %all-to-all-start.2 = ((f32[3,32,128]{2,0,1:T(4,128)}), f32[3,32,128]{2,0,1:T(4,128)S(1)}, u32[]{:S(2)}, u32[]{:S(2)}) async-start(f32[3,32,128]{2,0,1:T(4,128)} %copy.385), calls=%async_computation.2 | async-start | bytes 131072 | tf_op jit(solution)/shard_map/all_to_all | solution.py:111
  455.7 5.8 collective-permute-start.23
  467.1 20.3 %all-to-all-start.3 = ((f32[3,32,128]{2,0,1:T(4,128)}), f32[3,32,128]{2,0,1:T(4,128)S(1)}, u32[]{:S(2)}, u32[]{:S(2)}) async-start(f32[3,32,128]{2,0,1:T(4,128)} %copy.390), calls=%async_computation.3 | async-start | bytes 131072 | tf_op jit(solution)/shard_map/all_to_all | solution.py:119
  512.5 5.9 collective-permute-start.25
  513.8 6.0 collective-permute-start.24
  601.8 6.0 collective-permute-start.28
  606.3 6.8 %collective-permute-start.29 = (f32[1,2,3,512]{3,1,2,0:T(2,128)S(1)}, f32[1,2,3,512]{3,1,2,0:T(2,128)S(1)}, u32[]{:S(2)}, u32[]{:S(2)}) collective-permute-start(f32[1,2,3,512]{3,1,2,0:T(2,128)S(1)} %maximum_bitcast_fusion.9), channel_id=1, source_target_pairs={{4,0},{8,4},{12,8},{16,12},{20,16},{24,20},{28,24},{5,1},{9,5},{13... | collective-permute-start | bytes 36872 | tf_op jit(solution)/shard_map/ppermute | solution.py:28
  613.2 5.3 collective-permute-start.31
  (43 other events, 598.4 us)
where the time goes:
time: 645 us; the launch traced here: 633 us
  other arithmetic  270 us (42%)
  local copies, waits for them, and re-layouts  213 us (33%)
  starting transfers between devices  111 us (17%)
  waiting for transfers between devices  33.8 us (5%)
    scatter-add x4, other arithmetic, assemble(): return jnp.zeros((3, extended), jnp.float32).at[:, elem_nodes.reshape(-1)...  163 us
    gather x8, local copies, waits for them, and re-layouts, element_forces(): corners = ext_values[:, elem_nodes]  122 us
    ppermute x16, starting transfers between devices, padded_2(): lax.ppermute(tail, axis, [(i, (i + 1) % count) for i in range(ends)])  59.1 us
    scatter-add x4, other arithmetic, return_edges(): jnp.zeros((3, owned_count), jnp.float32).at[:, lists.reshape(-1)]  47.7 us
    scatter-add x2, other arithmetic, contact_forces(): return jnp.zeros((3, positions.shape[1]), jnp.float32).at[:, contact_node...  35.6 us
    ppermute x16, waiting for transfers between devices, padded_2(): lax.ppermute(head, axis, [((i + 1) % count, i) for i in range(ends)])  27.9 us
    scatter x2, local copies, waits for them, and re-layouts, contact_forces(): jnp.full((3, width), FAR, jnp.float32).at[:, slot_ids]  27.4 us
    gather x8, local copies, waits for them, and re-layouts, extend_edges(): picked = values[:, lists]  23.2 us
  transfers between devices with their start and end apart: 36, of which 13 were waited for; matrix products, arithmetic and copies ran while one was open for 24% of the time, Pallas kernels for 0%

commit v1 on v0

v1 whole, which is shorter than its diff:
```python
import functools

import jax
import jax.numpy as jnp
from jax import lax
from jax.experimental import pallas as pl
from jax.experimental.pallas import tpu as pltpu
from jax.sharding import PartitionSpec as P

LANES = 128
EBLK = 128
STEPS = 2
SUBS = 2

FAR = 10000.0
DT = 0.05
PENALTY = 0.5
REACH = 4.0

F32 = jnp.float32
BF16 = jnp.bfloat16
I32 = jnp.int32

VMEM_BYTES = 40 * 1024 * 1024


def lookup(table_row, rows, index):
    hi = index >> 7
    lo = index & (LANES - 1)
    found = [jnp.zeros(index.shape, F32) for _ in range(3)]
    for h in range(rows):
        here = hi == h
        for c in range(3):
            row = jnp.broadcast_to(table_row(c, h), index.shape)
            got = jnp.take_along_axis(row, lo, axis=1, mode="promise_in_bounds")
            found[c] = jnp.where(here, got, found[c])
    return found


def halves(values):
    top = values.astype(BF16).astype(F32)
    return [top, values - top]


def scatter_dot(hi_rows, lo_rows, value_rows, rows):
    row_no = lax.broadcasted_iota(I32, (rows, LANES), 0)
    lane_no = lax.broadcasted_iota(I32, (LANES, LANES), 0)
    total = None
    group = 2
    for start in range(0, len(hi_rows), group):
        lefts, rights = [], []
        for r in range(start, start + group):
            here = row_no == hi_rows[r]
            lefts.append(
                jnp.concatenate(
                    [
                        jnp.where(here, jnp.broadcast_to(vals[r], (rows, LANES)), 0.0)
                        for vals in value_rows
                    ],
                    axis=0,
                ).astype(BF16)
            )
            rights.append((lane_no == lo_rows[r]).astype(F32).astype(BF16))
        part = lax.dot_general(
            jnp.concatenate(lefts, axis=1),
            jnp.concatenate(rights, axis=1),
            (((1,), (1,)), ((), ())),
            preferred_element_type=F32,
        )
        total = part if total is None else total + part
    return total


def scatter_add(index_row, value_row, count, rows):
    hi_rows, lo_rows = [], []
    value_rows = [[] for _ in range(6)]
    for r in range(count):
        idx = index_row(r)
        hi_rows.append(idx >> 7)
        lo_rows.append(idx & (LANES - 1))
        for c in range(3):
            for part, vals in enumerate(halves(value_row(c, r))):
                value_rows[2 * c + part].append(vals)
    total = scatter_dot(hi_rows, lo_rows, value_rows, rows)
    return [
        total[2 * c * rows : (2 * c + 1) * rows] + total[(2 * c + 1) * rows : (2 * c + 2) * rows]
        for c in range(3)
    ]


def spread_rows(source, target, groups):
    rows = source.shape[1] // LANES
    for g in range(groups):
        for h in range(rows):
            target[g * rows + h : g * rows + h + 1, :] = source[
                g : g + 1, h * LANES : (h + 1) * LANES
            ]


def gather_halo(disp, rows, lists, sends):
    found = lookup(lambda c, h: disp[c * rows + h : c * rows + h + 1, :], rows, lists[...])
    quarter = lists.shape[0] // 4
    for b in range(4):
        for c in range(3):
            sends[b][c * quarter : (c + 1) * quarter, :] = found[c][b * quarter : (b + 1) * quarter]


def gather_slots(coords, disp, rows, inverse, outgoing):
    slot_node = inverse[...]
    used = slot_node >= 0
    found = lookup(
        lambda c, h: coords[c * rows + h : c * rows + h + 1, :]
        + disp[c * rows + h : c * rows + h + 1, :],
        rows,
        jnp.maximum(slot_node, 0),
    )
    for c in range(3):
        outgoing[:, c, :] = jnp.where(used, found[c], FAR)


def setup_kernel(
    devices,
    capacity,
    coords_in,
    disp_in,
    vel_in,
    ext_in,
    nodes_in,
    lists_in,
    bucket,
    contact_nodes,
    coords,
    disp,
    vel,
    ext,
    nodes,
    lists,
    inverse,
    outgoing,
    send0,
    send1,
    send2,
    send3,
):
    rows = coords_in.shape[1] // LANES
    spread_rows(disp_in, disp, 3)
    spread_rows(lists_in, lists, 4)
    gather_halo(disp, rows, lists, (send0, send1, send2, send3))
    spread_rows(coords_in, coords, 3)
    count = bucket.shape[0]
    slot_rows = inverse.shape[0]
    dev_no = lax.broadcasted_iota(I32, (devices, LANES), 0)
    first = lax.broadcasted_iota(I32, (LANES, 2 * LANES), 0)
    second = lax.broadcasted_iota(I32, (LANES, 2 * LANES), 1)
    before = ((first < second) | (second >= LANES)).astype(F32).astype(BF16)
    base = jnp.zeros((devices, LANES), F32)
    hi_rows, lo_rows, digits = [], [], [[], []]
    for r in range(count):
        b = bucket[r : r + 1, :]
        onehot = (dev_no == b).astype(F32)
        counts = jnp.dot(onehot.astype(BF16), before, preferred_element_type=F32)
        rank = jnp.sum(onehot * (counts[:, :LANES] + base), axis=0, keepdims=True)
        base = base + counts[:, LANES:]
        slot = b * capacity + rank.astype(I32)
        hi_rows.append(slot >> 7)
        lo_rows.append(slot & (LANES - 1))
        value = contact_nodes[r : r + 1, :] + 1
        digits[0].append((value >> 6).astype(F32))
        digits[1].append((value & 63).astype(F32))
    total = scatter_dot(hi_rows, lo_rows, digits, slot_rows)
    inverse[...] = (total[:slot_rows] * 64.0 + total[slot_rows:]).astype(I32) - 1
    gather_slots(coords, disp, rows, inverse, outgoing)
    spread_rows(nodes_in, nodes, 4)
    spread_rows(vel_in, vel, 3)
    spread_rows(ext_in, ext, 3)


def element_kernel(later, *refs):
    if later:
        (disp, recv0, recv1, recv2, recv3, nodes, thick, stiff, held, slow) = refs[:10]
        (own, out0, out1, out2, out3) = refs[10:]
    else:
        (disp, recv0, recv1, recv2, recv3, nodes, thick, stiff) = refs[:8]
        (own, out0, out1, out2, out3, held) = refs[8:]
    rows = disp.shape[0] // 3
    quarter = recv0.shape[0] // 3
    recvs = (recv0, recv1, recv2, recv3)
    outs = (out0, out1, out2, out3)
    elem_rows = thick.shape[0]

    def table_row(c, h):
        if h < rows:
            return disp[c * rows + h : c * rows + h + 1, :]
        b, q = divmod(h - rows, quarter)
        return recvs[b][c * quarter + q : c * quarter + q + 1, :]

    extended = rows + 4 * quarter
    corners = []
    for k in range(4):
        corners.append(
            lookup(table_row, extended, nodes[k * elem_rows : (k + 1) * elem_rows, :])
        )
    factor = thick[...]
    forces = []
    for i in range(12):
        total = None
        for j in range(12):
            term = stiff[i, j] * corners[j % 4][j // 4]
            total = term if total is None else total + term
        total = factor * total
        span = slice(i * elem_rows, (i + 1) * elem_rows)
        if later:
            total = jnp.where(slow[...] == 1, held[span, :], total)
        else:
            held[span, :] = total
        forces.append(total)

    def value_row(c, r):
        k, h = divmod(r, elem_rows)
        return forces[c * 4 + k][h : h + 1, :]

    sums = scatter_add(lambda r: nodes[r : r + 1, :], value_row, 4 * elem_rows, extended)
    for c in range(3):
        own[c * rows : (c + 1) * rows, :] = sums[c][:rows]
        for b in range(4):
            start = rows + b * quarter
            outs[b][c * quarter : (c + 1) * quarter, :] = sums[c][start : start + quarter]


def contact_kernel(pairs, arrived, pushes, turned):
    tiles = arrived.shape[0]
    pushes[...] = jnp.zeros(pushes.shape, F32)
    for t in range(tiles):
        block = jnp.concatenate([arrived[t], jnp.zeros((5, LANES), F32)], axis=0)
        turned[t] = jnp.transpose(block)
    for p in range(pairs.shape[1]):
        a = pairs[0, p]
        b = pairs[1, p]
        pos_a = arrived[a]
        pos_b = turned[b]
        gaps = [
            jnp.broadcast_to(pos_a[c : c + 1, :], (LANES, LANES))
            - jnp.broadcast_to(pos_b[:, c : c + 1], (LANES, LANES))
            for c in range(3)
        ]
        dist = gaps[0] * gaps[0] + gaps[1] * gaps[1] + gaps[2] * gaps[2]
        weight = PENALTY * jnp.exp(dist * (-1.0 / REACH))
        push = jnp.concatenate(
            [jnp.sum(weight * gaps[c], axis=0, keepdims=True) for c in range(3)], axis=0
        )
        pushes[a] = pushes[a] + push


def update_kernel(first, last, final, *refs):
    refs = list(refs)
    own, back0, back1, back2, back3, lists, ext, inv_mass, vel, disp = refs[:10]
    refs = refs[10:]
    if first:
        returned, inverse = refs[:2]
        refs = refs[2:]
    else:
        contact_in = refs.pop(0)
    if last and not final:
        coords, inverse = refs[:2]
        refs = refs[2:]
    backs = (back0, back1, back2, back3)
    rows = disp.shape[0] // 3
    quarter = back0.shape[0] // 3
    new_vel, new_disp = refs[:2]
    refs = refs[2:]

    def back_row(c, r):
        b, q = divmod(r, quarter)
        return backs[b][c * quarter + q : c * quarter + q + 1, :]

    halo = scatter_add(lambda r: lists[r : r + 1, :], back_row, 4 * quarter, rows)
    if first:
        contact_out = refs.pop(0)
        contact = scatter_add(
            lambda r: inverse[r : r + 1, :],
            lambda c, r: returned[r, c : c + 1, :],
            inverse.shape[0],
            rows,
        )
        for c in range(3):
            contact_out[c * rows : (c + 1) * rows, :] = contact[c]
    else:
        contact = [contact_in[c * rows : (c + 1) * rows, :] for c in range(3)]
    for c in range(3):
        span = slice(c * rows, (c + 1) * rows)
        internal = own[span, :] + halo[c]
        accel = inv_mass[...] * (ext[span, :] - internal + contact[c])
        vel_c = vel[span, :] + DT * accel
        disp_c = disp[span, :] + DT * vel_c
        if final:
            for h in range(rows):
                new_vel[c : c + 1, h * LANES : (h + 1) * LANES] = vel_c[h : h + 1, :]
                new_disp[c : c + 1, h * LANES : (h + 1) * LANES] = disp_c[h : h + 1, :]
        else:
            new_vel[span, :] = vel_c
            new_disp[span, :] = disp_c
    if not final:
        gather_halo(new_disp, rows, lists, refs[:4])
        if last:
            gather_slots(coords, new_disp, rows, inverse, refs[4])


def vmem(count):
    return [pl.BlockSpec(memory_space=pltpu.VMEM)] * count


def shape(*dims):
    return jax.ShapeDtypeStruct(dims, F32)


def call(kernel, inputs, outputs, name, smem=(), scratch=()):
    specs = [
        pl.BlockSpec(memory_space=pltpu.SMEM if i in smem else pltpu.VMEM)
        for i in range(len(inputs))
    ]
    return pl.pallas_call(
        kernel,
        out_shape=tuple(outputs),
        in_specs=specs,
        out_specs=tuple(vmem(len(outputs))),
        scratch_shapes=list(scratch),
        compiler_params=pltpu.CompilerParams(vmem_limit_bytes=VMEM_BYTES),
        name=name,
    )(*inputs)


def shift(block, axis, step):
    count = lax.axis_size(axis)
    pairs = [(i, i + step) for i in range(count) if 0 <= i + step < count]
    return lax.ppermute(block, axis, pairs)


def exchange(to_low_x, to_high_x, to_low_y, to_high_y):
    return (
        shift(to_high_x, "px", 1),
        shift(to_low_x, "px", -1),
        shift(to_high_y, "py", 1),
        shift(to_low_y, "py", -1),
    )


def swap(slots, devices, capacity):
    axes = ("px", "py")
    if capacity == LANES:
        return lax.all_to_all(slots, axes, 0, 0, tiled=True)
    ratio = LANES // capacity
    parts = jnp.transpose(slots.reshape(-1, 3, ratio, capacity), (0, 2, 1, 3)).reshape(
        devices, 3, capacity
    )
    moved = lax.all_to_all(parts, axes, 0, 0, tiled=True)
    return jnp.transpose(moved.reshape(-1, ratio, 3, capacity), (0, 2, 1, 3)).reshape(
        -1, 3, LANES
    )


def body(
    coords,
    displacement,
    velocity,
    inv_mass,
    ext_force,
    thickness,
    stiffness,
    elem_nodes,
    block_class,
    halo_lists,
    contact_nodes,
    contact_bucket,
    tile_pairs,
):
    rows = coords.shape[1] // LANES
    quarter = halo_lists.shape[1] // LANES
    elem_rows = elem_nodes.shape[1] // LANES
    devices = lax.axis_size("px") * lax.axis_size("py")
    capacity = 2 * contact_nodes.shape[0] // devices
    slot_rows = devices * capacity // LANES
    inv_mass = inv_mass.reshape(rows, LANES)
    thickness = thickness.reshape(elem_rows, LANES)
    slow = jnp.broadcast_to(block_class[:, None], (elem_rows, LANES))
    nodal = shape(3 * rows, LANES)
    sent = [shape(3 * quarter, LANES)] * 4
    slots = shape(slot_rows, 3, LANES)

    coords, disp, vel, ext, nodes, lists, inverse, outgoing, *sends = call(
        functools.partial(setup_kernel, devices, capacity),
        [
            coords,
            displacement,
            velocity,
            ext_force,
            elem_nodes,
            halo_lists,
            contact_bucket.reshape(-1, LANES),
            contact_nodes.reshape(-1, LANES),
        ],
        [nodal] * 4
        + [
            jax.ShapeDtypeStruct((4 * elem_rows, LANES), I32),
            jax.ShapeDtypeStruct((4 * quarter, LANES), I32),
            jax.ShapeDtypeStruct((slot_rows, LANES), I32),
            slots,
        ]
        + sent,
        "setup",
    )
    for step_no in range(STEPS):
        for sub_no in range(SUBS):
            first = sub_no == 0
            last = sub_no == SUBS - 1
            final = last and step_no == STEPS - 1
            recvs = exchange(*sends)
            if first:
                arrived = swap(outgoing, devices, capacity)
                own, *rest = call(
                    functools.partial(element_kernel, False),
                    [disp, *recvs, nodes, thickness, stiffness],
                    [nodal] + sent + [shape(12 * elem_rows, LANES)],
                    "elements",
                    smem=(7,),
                )
                held = rest[4]
                backs = exchange(*rest[:4])
                (pushes,) = call(
                    contact_kernel,
                    [tile_pairs, arrived],
                    [slots],
                    "contact",
                    smem=(0,),
                    scratch=[pltpu.VMEM((slot_rows, LANES, 8), F32)],
                )
                returned = swap(pushes, devices, capacity)
            else:
                own, *rest = call(
                    functools.partial(element_kernel, True),
                    [disp, *recvs, nodes, thickness, stiffness, held, slow],
                    [nodal] + sent,
                    "elements_later",
                    smem=(7,),
                )
                backs = exchange(*rest[:4])
            inputs = [own, *backs]
            inputs += [lists, ext, inv_mass, vel, disp]
            inputs += [returned, inverse] if first else [contact]
            outputs = [shape(3, rows * LANES)] * 2 if final else [nodal] * 2
            if first:
                outputs.append(nodal)
            if last and not final:
                inputs += [coords, inverse]
            if not final:
                outputs += sent
                if last:
                    outputs.append(slots)
            vel, disp, *rest = call(
                functools.partial(update_kernel, first, last, final), inputs, outputs, "update"
            )
            if first:
                contact = rest.pop(0)
            if not final:
                sends = rest[:4]
                if last:
                    outgoing = rest[4]
    return (disp, vel)


def solution(mesh):
    placed = (
        P(None, ("px", "py")),
        P(None, ("px", "py")),
        P(None, ("px", "py")),
        P(("px", "py")),
        P(None, ("px", "py")),
        P(("px", "py")),
        P(),
        P(None, ("px", "py")),
        P(("px", "py")),
        P(None, ("px", "py")),
        P(("px", "py")),
        P(("px", "py"), None),
        P(None, ("px", "py")),
    )
    return jax.shard_map(
        body,
        mesh=mesh,
        in_specs=placed,
        out_specs=(P(None, ("px", "py")), P(None, ("px", "py"))),
        check_vma=False,
    )
```

time: 645 us -> 174 us (0.27)
  the two profiles are of different devices: /device:TPU:0 before, /device:TPU:9 now
where the time goes in v1:
time: 174 us; the launch traced here: 173 us
  starting transfers between devices  98.8 us (57%)
  Pallas kernels  22.4 us (13%)
  waiting for transfers between devices  22.2 us (13%)
  blocking collectives  21.5 us (12%)
  local copies, waits for them, and re-layouts  6.62 us (4%)
    ppermute x32, starting transfers between devices, shift(): return lax.ppermute(block, axis, pairs)  90 us
    pallas_call x11, Pallas kernels, call(): pl.pallas_call(kernel, out_shape=tuple(outputs), in_specs=specs, out_spec...  22.4 us
    ppermute x32, waiting for transfers between devices, shift(): return lax.ppermute(block, axis, pairs)  22.2 us
    all_to_all x2, blocking collectives, swap(): return lax.all_to_all(slots, axes, 0, 0, tiled=True)  21.5 us
    all_to_all x2, starting transfers between devices, swap(): return lax.all_to_all(slots, axes, 0, 0, tiled=True)  8.71 us
    unnamed x26, local copies, waits for them, and re-layouts  6.55 us
  transfers between devices with their start and end apart: 34, of which 8 were waited for; matrix products, arithmetic and copies ran while one was open for 0% of the time, Pallas kernels for 4%

profile of v1, /device:TPU:9, one launch (start us, length us, event | category | flops | bytes accessed | tf_op | source)
XLA Modules:
  0.0 172.5 jit_solution(12719688758288265550)
XLA Ops:
  7.4 11.8 %all_to_all.20.arrived = f32[32,3,128]{2,1,0:T(4,128)S(1)} all-to-all(f32[32,3,128]{2,1,0:T(4,128)S(1)} %get-tuple-element.73), channel_id=1, replica_groups=mesh['px'=8,'py'=4] {'px','py'}, dimensions={0} | all-to-all | bytes 98304 | tf_op jit(solution)/shard_map/all_to_all | solution.py:350
  22.1 4.4 %all-to-all-start.1 = ((f32[32,3,128]{2,1,0:T(4,128)}), f32[32,3,128]{2,1,0:T(4,128)S(1)}, u32[]{:S(2)}, u32[]{:S(2)}) async-start(f32[32,3,128]{2,1,0:T(4,128)} %contact.2), calls=%async_computation.1 | async-start | bytes 131072 | tf_op jit(solution)/shard_map/all_to_all | solution.py:350
  26.5 3.1 %collective-permute-start = (f32[12,128]{1,0:T(8,128)S(1)}, f32[12,128]{1,0:T(8,128)S(1)}, u32[]{:S(2)}, u32[]{:S(2)}) collective-permute-start(f32[12,128]{1,0:T(8,128)S(1)} %get-tuple-element.60), channel_id=1, source_target_pairs={{0,4},{4,8},{8,12},{12,16},{16,20},{20,24},{24,28},{1,5},{5,9},{9,... | collective-permute-start | bytes 18440 | tf_op jit(solution)/shard_map/ppermute | solution.py:335
  29.6 3.1 %collective-permute-start.1 = (f32[12,128]{1,0:T(8,128)S(1)}, f32[12,128]{1,0:T(8,128)S(1)}, u32[]{:S(2)}, u32[]{:S(2)}) collective-permute-start(f32[12,128]{1,0:T(8,128)S(1)} %get-tuple-element.61), channel_id=1, source_target_pairs={{4,0},{8,4},{12,8},{16,12},{20,16},{24,20},{28,24},{5,1},{9,5},{13... | collective-permute-start | bytes 18440 | tf_op jit(solution)/shard_map/ppermute | solution.py:335
  32.7 3.9 %collective-permute-start.2 = (f32[12,128]{1,0:T(8,128)S(1)}, f32[12,128]{1,0:T(8,128)S(1)}, u32[]{:S(2)}, u32[]{:S(2)}) collective-permute-start(f32[12,128]{1,0:T(8,128)S(1)} %get-tuple-element.62), channel_id=1, source_target_pairs={{0,1},{1,2},{2,3},{4,5},{5,6},{6,7},{8,9},{9,10},{10,11},{12,13},{... | collective-permute-start | bytes 18440 | tf_op jit(solution)/shard_map/ppermute | solution.py:335
  38.6 3.0 %collective-permute-done.3.refs_4_ = f32[12,128]{1,0:T(8,128)S(1)} collective-permute-done((f32[12,128]{1,0:T(8,128)S(1)}, f32[12,128]{1,0:T(8,128)S(1)}, u32[]{:S(2)}, u32[]{:S(2)}) %collective-permute-start.3) | collective-permute-done | bytes 6176 | tf_op jit(solution)/shard_map/ppermute | solution.py:335
  41.6 3.0 %elements.2 = (f32[48,128]{1,0:T(8,128)S(1)}, f32[12,128]{1,0:T(8,128)S(1)}, f32[12,128]{1,0:T(8,128)S(1)}, f32[12,128]{1,0:T(8,128)S(1)}, f32[12,128]{1,0:T(8,128)S(1)}, /*index=5*/f32[192,128]{1,0:T(8,128)S(1)}) custom-call(f32[48,128]{1,0:T(8,128)S(1)} %get-tuple-element.59.refs_0_.refs_9_, f32[12,128]{1,0:T(8,128)S(1)} %collective-permute-done.refs_1_, ...), custom_call_target="tpu_custom_call" | custom-call | tf_op jit(solution)/shard_map/elements/pallas_call | solution.py:321
  46.9 4.0 %collective-permute-start.5 = (f32[12,128]{1,0:T(8,128)S(1)}, f32[12,128]{1,0:T(8,128)S(1)}, u32[]{:S(2)}, u32[]{:S(2)}) collective-permute-start(f32[12,128]{1,0:T(8,128)S(1)} %get-tuple-element.67), channel_id=1, source_target_pairs={{4,0},{8,4},{12,8},{16,12},{20,16},{24,20},{28,24},{5,1},{9,5},{13... | collective-permute-start | bytes 18440 | tf_op jit(solution)/shard_map/ppermute | solution.py:335
  55.4 3.0 %collective-permute-done.7.refs_4_ = f32[12,128]{1,0:T(8,128)S(1)} collective-permute-done((f32[12,128]{1,0:T(8,128)S(1)}, f32[12,128]{1,0:T(8,128)S(1)}, u32[]{:S(2)}, u32[]{:S(2)}) %collective-permute-start.7) | collective-permute-done | bytes 6176 | tf_op jit(solution)/shard_map/ppermute | solution.py:335
  65.4 4.3 %collective-permute-start.9 = (f32[12,128]{1,0:T(8,128)S(1)}, f32[12,128]{1,0:T(8,128)S(1)}, u32[]{:S(2)}, u32[]{:S(2)}) collective-permute-start(f32[12,128]{1,0:T(8,128)S(1)} %get-tuple-element.77), channel_id=1, source_target_pairs={{4,0},{8,4},{12,8},{16,12},{20,16},{24,20},{28,24},{5,1},{9,5},{13... | collective-permute-start | bytes 18440 | tf_op jit(solution)/shard_map/ppermute | solution.py:335
  71.6 3.0 %elements_later.2 = (f32[48,128]{1,0:T(8,128)S(1)}, f32[12,128]{1,0:T(8,128)S(1)}, f32[12,128]{1,0:T(8,128)S(1)}, f32[12,128]{1,0:T(8,128)S(1)}, f32[12,128]{1,0:T(8,128)S(1)}) custom-call(f32[48,128]{1,0:T(8,128)S(1)} %get-tuple-element.75.refs_0_.refs_9_, f32[12,128]{1,0:T(8,128)S(1)} %collective-permute-done.8.refs_1_, ...), custom_call_target="tpu_custom_call" | custom-call | tf_op jit(solution)/shard_map/elements_later/pallas_call | solution.py:321
  74.7 4.1 %collective-permute-start.12 = (f32[12,128]{1,0:T(8,128)S(1)}, f32[12,128]{1,0:T(8,128)S(1)}, u32[]{:S(2)}, u32[]{:S(2)}) collective-permute-start(f32[12,128]{1,0:T(8,128)S(1)} %get-tuple-element.82), channel_id=1, source_target_pairs={{0,4},{4,8},{8,12},{12,16},{16,20},{20,24},{24,28},{1,5},{5,9},{9,... | collective-permute-start | bytes 18440 | tf_op jit(solution)/shard_map/ppermute | solution.py:335
  80.9 4.8 %collective-permute-start.14 = (f32[12,128]{1,0:T(8,128)S(1)}, f32[12,128]{1,0:T(8,128)S(1)}, u32[]{:S(2)}, u32[]{:S(2)}) collective-permute-start(f32[12,128]{1,0:T(8,128)S(1)} %get-tuple-element.84), channel_id=1, source_target_pairs={{0,1},{1,2},{2,3},{4,5},{5,6},{6,7},{8,9},{9,10},{10,11},{12,13},{... | collective-permute-start | bytes 18440 | tf_op jit(solution)/shard_map/ppermute | solution.py:335
  87.6 3.0 %collective-permute-done.15.refs_4_ = f32[12,128]{1,0:T(8,128)S(1)} collective-permute-done((f32[12,128]{1,0:T(8,128)S(1)}, f32[12,128]{1,0:T(8,128)S(1)}, u32[]{:S(2)}, u32[]{:S(2)}) %collective-permute-start.15) | collective-permute-done | bytes 6176 | tf_op jit(solution)/shard_map/ppermute | solution.py:335
  91.6 9.7 %all_to_all.21.arrived = f32[32,3,128]{2,1,0:T(4,128)S(1)} all-to-all(f32[32,3,128]{2,1,0:T(4,128)S(1)} %get-tuple-element.100), channel_id=1, replica_groups=mesh['px'=8,'py'=4] {'px','py'}, dimensions={0} | all-to-all | bytes 98304 | tf_op jit(solution)/shard_map/all_to_all | solution.py:350
  104.3 4.3 %all-to-all-start.3 = ((f32[32,3,128]{2,1,0:T(4,128)}), f32[32,3,128]{2,1,0:T(4,128)S(1)}, u32[]{:S(2)}, u32[]{:S(2)}) async-start(f32[32,3,128]{2,1,0:T(4,128)} %contact.3), calls=%async_computation.3 | async-start | bytes 131072 | tf_op jit(solution)/shard_map/all_to_all | solution.py:350
  108.6 3.1 %collective-permute-start.16 = (f32[12,128]{1,0:T(8,128)S(1)}, f32[12,128]{1,0:T(8,128)S(1)}, u32[]{:S(2)}, u32[]{:S(2)}) collective-permute-start(f32[12,128]{1,0:T(8,128)S(1)} %get-tuple-element.90), channel_id=1, source_target_pairs={{0,4},{4,8},{8,12},{12,16},{16,20},{20,24},{24,28},{1,5},{5,9},{9,... | collective-permute-start | bytes 18440 | tf_op jit(solution)/shard_map/ppermute | solution.py:335
  111.7 3.1 %collective-permute-start.17 = (f32[12,128]{1,0:T(8,128)S(1)}, f32[12,128]{1,0:T(8,128)S(1)}, u32[]{:S(2)}, u32[]{:S(2)}) collective-permute-start(f32[12,128]{1,0:T(8,128)S(1)} %get-tuple-element.91), channel_id=1, source_target_pairs={{4,0},{8,4},{12,8},{16,12},{20,16},{24,20},{28,24},{5,1},{9,5},{13... | collective-permute-start | bytes 18440 | tf_op jit(solution)/shard_map/ppermute | solution.py:335
  114.8 3.9 %collective-permute-start.18 = (f32[12,128]{1,0:T(8,128)S(1)}, f32[12,128]{1,0:T(8,128)S(1)}, u32[]{:S(2)}, u32[]{:S(2)}) collective-permute-start(f32[12,128]{1,0:T(8,128)S(1)} %get-tuple-element.92), channel_id=1, source_target_pairs={{0,1},{1,2},{2,3},{4,5},{5,6},{6,7},{8,9},{9,10},{10,11},{12,13},{... | collective-permute-start | bytes 18440 | tf_op jit(solution)/shard_map/ppermute | solution.py:335
  123.7 3.0 %elements.3 = (f32[48,128]{1,0:T(8,128)S(1)}, f32[12,128]{1,0:T(8,128)S(1)}, f32[12,128]{1,0:T(8,128)S(1)}, f32[12,128]{1,0:T(8,128)S(1)}, f32[12,128]{1,0:T(8,128)S(1)}, /*index=5*/f32[192,128]{1,0:T(8,128)S(1)}) custom-call(f32[48,128]{1,0:T(8,128)S(1)} %get-tuple-element.89.refs_0_.refs_9_, f32[12,128]{1,0:T(8,128)S(1)} %collective-permute-done.16.refs_1_, ...), custom_call_target="tpu_custom_call" | custom-call | tf_op jit(solution)/shard_map/elements/pallas_call | solution.py:321
  128.9 4.0 %collective-permute-start.21 = (f32[12,128]{1,0:T(8,128)S(1)}, f32[12,128]{1,0:T(8,128)S(1)}, u32[]{:S(2)}, u32[]{:S(2)}) collective-permute-start(f32[12,128]{1,0:T(8,128)S(1)} %get-tuple-element.96), channel_id=1, source_target_pairs={{4,0},{8,4},{12,8},{16,12},{20,16},{24,20},{28,24},{5,1},{9,5},{13... | collective-permute-start | bytes 18440 | tf_op jit(solution)/shard_map/ppermute | solution.py:335
  143.1 4.3 %collective-permute-start.25 = (f32[12,128]{1,0:T(8,128)S(1)}, f32[12,128]{1,0:T(8,128)S(1)}, u32[]{:S(2)}, u32[]{:S(2)}) collective-permute-start(f32[12,128]{1,0:T(8,128)S(1)} %get-tuple-element.103), channel_id=1, source_target_pairs={{4,0},{8,4},{12,8},{16,12},{20,16},{24,20},{28,24},{5,1},{9,5},{13... | collective-permute-start | bytes 18440 | tf_op jit(solution)/shard_map/ppermute | solution.py:335
  154.8 3.0 %elements_later.3 = (f32[48,128]{1,0:T(8,128)S(1)}, f32[12,128]{1,0:T(8,128)S(1)}, f32[12,128]{1,0:T(8,128)S(1)}, f32[12,128]{1,0:T(8,128)S(1)}, f32[12,128]{1,0:T(8,128)S(1)}) custom-call(f32[48,128]{1,0:T(8,128)S(1)} %get-tuple-element.101.refs_0_.refs_9_, f32[12,128]{1,0:T(8,128)S(1)} %collective-permute-done.24.refs_1_, ...), custom_call_target="tpu_custom_call" | custom-call | tf_op jit(solution)/shard_map/elements_later/pallas_call | solution.py:321
  159.8 4.3 %collective-permute-start.29 = (f32[12,128]{1,0:T(8,128)S(1)}, f32[12,128]{1,0:T(8,128)S(1)}, u32[]{:S(2)}, u32[]{:S(2)}) collective-permute-start(f32[12,128]{1,0:T(8,128)S(1)} %get-tuple-element.109), channel_id=1, source_target_pairs={{4,0},{8,4},{12,8},{16,12},{20,16},{24,20},{28,24},{5,1},{9,5},{13... | collective-permute-start | bytes 18440 | tf_op jit(solution)/shard_map/ppermute | solution.py:335
  (84 shorter events, 70.1 us)
Async XLA Ops:
  22.1 36.3 %all-to-all-start.1 = ((f32[32,3,128]{2,1,0:T(4,128)}), f32[32,3,128]{2,1,0:T(4,128)S(1)}, u32[]{:S(2)}, u32[]{:S(2)}) async-start(f32[32,3,128]{2,1,0:T(4,128)} %contact.2), calls=%async_computation.1 | async-start | bytes 131072 | tf_op jit(solution)/shard_map/all_to_all | solution.py:350
  26.5 12.1 %collective-permute-start = (f32[12,128]{1,0:T(8,128)S(1)}, f32[12,128]{1,0:T(8,128)S(1)}, u32[]{:S(2)}, u32[]{:S(2)}) collective-permute-start(f32[12,128]{1,0:T(8,128)S(1)} %get-tuple-element.60), channel_id=1, source_target_pairs={{0,4},{4,8},{8,12},{12,16},{16,20},{20,24},{24,28},{1,5},{5,9},{9,... | collective-permute-start | bytes 18440 | tf_op jit(solution)/shard_map/ppermute | solution.py:335
  29.6 9.0 %collective-permute-start.1 = (f32[12,128]{1,0:T(8,128)S(1)}, f32[12,128]{1,0:T(8,128)S(1)}, u32[]{:S(2)}, u32[]{:S(2)}) collective-permute-start(f32[12,128]{1,0:T(8,128)S(1)} %get-tuple-element.61), channel_id=1, source_target_pairs={{4,0},{8,4},{12,8},{16,12},{20,16},{24,20},{28,24},{5,1},{9,5},{13... | collective-permute-start | bytes 18440 | tf_op jit(solution)/shard_map/ppermute | solution.py:335
  32.7 5.9 %collective-permute-start.2 = (f32[12,128]{1,0:T(8,128)S(1)}, f32[12,128]{1,0:T(8,128)S(1)}, u32[]{:S(2)}, u32[]{:S(2)}) collective-permute-start(f32[12,128]{1,0:T(8,128)S(1)} %get-tuple-element.62), channel_id=1, source_target_pairs={{0,1},{1,2},{2,3},{4,5},{5,6},{6,7},{8,9},{9,10},{10,11},{12,13},{... | collective-permute-start | bytes 18440 | tf_op jit(solution)/shard_map/ppermute | solution.py:335
  36.7 5.0 %collective-permute-start.3 = (f32[12,128]{1,0:T(8,128)S(1)}, f32[12,128]{1,0:T(8,128)S(1)}, u32[]{:S(2)}, u32[]{:S(2)}) collective-permute-start(f32[12,128]{1,0:T(8,128)S(1)} %get-tuple-element.63), channel_id=1, source_target_pairs={{1,0},{2,1},{3,2},{5,4},{6,5},{7,6},{9,8},{10,9},{11,10},{13,12},{... | collective-permute-start | bytes 18440 | tf_op jit(solution)/shard_map/ppermute | solution.py:335
  44.7 10.7 %collective-permute-start.4 = (f32[12,128]{1,0:T(8,128)S(1)}, f32[12,128]{1,0:T(8,128)S(1)}, u32[]{:S(2)}, u32[]{:S(2)}) collective-permute-start(f32[12,128]{1,0:T(8,128)S(1)} %get-tuple-element.66), channel_id=1, source_target_pairs={{0,4},{4,8},{8,12},{12,16},{16,20},{20,24},{24,28},{1,5},{5,9},{9,... | collective-permute-start | bytes 18440 | tf_op jit(solution)/shard_map/ppermute | solution.py:335
  46.9 8.4 %collective-permute-start.5 = (f32[12,128]{1,0:T(8,128)S(1)}, f32[12,128]{1,0:T(8,128)S(1)}, u32[]{:S(2)}, u32[]{:S(2)}) collective-permute-start(f32[12,128]{1,0:T(8,128)S(1)} %get-tuple-element.67), channel_id=1, source_target_pairs={{4,0},{8,4},{12,8},{16,12},{20,16},{24,20},{28,24},{5,1},{9,5},{13... | collective-permute-start | bytes 18440 | tf_op jit(solution)/shard_map/ppermute | solution.py:335
  59.1 10.5 %collective-permute-start.10 = (f32[12,128]{1,0:T(8,128)S(1)}, f32[12,128]{1,0:T(8,128)S(1)}, u32[]{:S(2)}, u32[]{:S(2)}) collective-permute-start(f32[12,128]{1,0:T(8,128)S(1)} %get-tuple-element.78), channel_id=1, source_target_pairs={{0,1},{1,2},{2,3},{4,5},{5,6},{6,7},{8,9},{9,10},{10,11},{12,13},{... | collective-permute-start | bytes 18440 | tf_op jit(solution)/shard_map/ppermute | solution.py:335
  61.1 8.6 %collective-permute-start.11 = (f32[12,128]{1,0:T(8,128)S(1)}, f32[12,128]{1,0:T(8,128)S(1)}, u32[]{:S(2)}, u32[]{:S(2)}) collective-permute-start(f32[12,128]{1,0:T(8,128)S(1)} %get-tuple-element.79), channel_id=1, source_target_pairs={{1,0},{2,1},{3,2},{5,4},{6,5},{7,6},{9,8},{10,9},{11,10},{13,12},{... | collective-permute-start | bytes 18440 | tf_op jit(solution)/shard_map/ppermute | solution.py:335
  63.5 6.2 %collective-permute-start.8 = (f32[12,128]{1,0:T(8,128)S(1)}, f32[12,128]{1,0:T(8,128)S(1)}, u32[]{:S(2)}, u32[]{:S(2)}) collective-permute-start(f32[12,128]{1,0:T(8,128)S(1)} %get-tuple-element.76), channel_id=1, source_target_pairs={{0,4},{4,8},{8,12},{12,16},{16,20},{20,24},{24,28},{1,5},{5,9},{9,... | collective-permute-start | bytes 18440 | tf_op jit(solution)/shard_map/ppermute | solution.py:335
  65.4 5.5 %collective-permute-start.9 = (f32[12,128]{1,0:T(8,128)S(1)}, f32[12,128]{1,0:T(8,128)S(1)}, u32[]{:S(2)}, u32[]{:S(2)}) collective-permute-start(f32[12,128]{1,0:T(8,128)S(1)} %get-tuple-element.77), channel_id=1, source_target_pairs={{4,0},{8,4},{12,8},{16,12},{20,16},{24,20},{28,24},{5,1},{9,5},{13... | collective-permute-start | bytes 18440 | tf_op jit(solution)/shard_map/ppermute | solution.py:335
  74.7 12.9 %collective-permute-start.12 = (f32[12,128]{1,0:T(8,128)S(1)}, f32[12,128]{1,0:T(8,128)S(1)}, u32[]{:S(2)}, u32[]{:S(2)}) collective-permute-start(f32[12,128]{1,0:T(8,128)S(1)} %get-tuple-element.82), channel_id=1, source_target_pairs={{0,4},{4,8},{8,12},{12,16},{16,20},{20,24},{24,28},{1,5},{5,9},{9,... | collective-permute-start | bytes 18440 | tf_op jit(solution)/shard_map/ppermute | solution.py:335
  78.8 8.8 %collective-permute-start.13 = (f32[12,128]{1,0:T(8,128)S(1)}, f32[12,128]{1,0:T(8,128)S(1)}, u32[]{:S(2)}, u32[]{:S(2)}) collective-permute-start(f32[12,128]{1,0:T(8,128)S(1)} %get-tuple-element.83), channel_id=1, source_target_pairs={{4,0},{8,4},{12,8},{16,12},{20,16},{24,20},{28,24},{5,1},{9,5},{13... | collective-permute-start | bytes 18440 | tf_op jit(solution)/shard_map/ppermute | solution.py:335
  80.9 6.7 %collective-permute-start.14 = (f32[12,128]{1,0:T(8,128)S(1)}, f32[12,128]{1,0:T(8,128)S(1)}, u32[]{:S(2)}, u32[]{:S(2)}) collective-permute-start(f32[12,128]{1,0:T(8,128)S(1)} %get-tuple-element.84), channel_id=1, source_target_pairs={{0,1},{1,2},{2,3},{4,5},{5,6},{6,7},{8,9},{9,10},{10,11},{12,13},{... | collective-permute-start | bytes 18440 | tf_op jit(solution)/shard_map/ppermute | solution.py:335
  104.3 36.1 %all-to-all-start.3 = ((f32[32,3,128]{2,1,0:T(4,128)}), f32[32,3,128]{2,1,0:T(4,128)S(1)}, u32[]{:S(2)}, u32[]{:S(2)}) async-start(f32[32,3,128]{2,1,0:T(4,128)} %contact.3), calls=%async_computation.3 | async-start | bytes 131072 | tf_op jit(solution)/shard_map/all_to_all | solution.py:350
  108.6 12.2 %collective-permute-start.16 = (f32[12,128]{1,0:T(8,128)S(1)}, f32[12,128]{1,0:T(8,128)S(1)}, u32[]{:S(2)}, u32[]{:S(2)}) collective-permute-start(f32[12,128]{1,0:T(8,128)S(1)} %get-tuple-element.90), channel_id=1, source_target_pairs={{0,4},{4,8},{8,12},{12,16},{16,20},{20,24},{24,28},{1,5},{5,9},{9,... | collective-permute-start | bytes 18440 | tf_op jit(solution)/shard_map/ppermute | solution.py:335
  111.7 9.1 %collective-permute-start.17 = (f32[12,128]{1,0:T(8,128)S(1)}, f32[12,128]{1,0:T(8,128)S(1)}, u32[]{:S(2)}, u32[]{:S(2)}) collective-permute-start(f32[12,128]{1,0:T(8,128)S(1)} %get-tuple-element.91), channel_id=1, source_target_pairs={{4,0},{8,4},{12,8},{16,12},{20,16},{24,20},{28,24},{5,1},{9,5},{13... | collective-permute-start | bytes 18440 | tf_op jit(solution)/shard_map/ppermute | solution.py:335
  114.8 6.1 %collective-permute-start.18 = (f32[12,128]{1,0:T(8,128)S(1)}, f32[12,128]{1,0:T(8,128)S(1)}, u32[]{:S(2)}, u32[]{:S(2)}) collective-permute-start(f32[12,128]{1,0:T(8,128)S(1)} %get-tuple-element.92), channel_id=1, source_target_pairs={{0,1},{1,2},{2,3},{4,5},{5,6},{6,7},{8,9},{9,10},{10,11},{12,13},{... | collective-permute-start | bytes 18440 | tf_op jit(solution)/shard_map/ppermute | solution.py:335
  126.7 10.6 %collective-permute-start.20 = (f32[12,128]{1,0:T(8,128)S(1)}, f32[12,128]{1,0:T(8,128)S(1)}, u32[]{:S(2)}, u32[]{:S(2)}) collective-permute-start(f32[12,128]{1,0:T(8,128)S(1)} %get-tuple-element.95), channel_id=1, source_target_pairs={{0,4},{4,8},{8,12},{12,16},{16,20},{20,24},{24,28},{1,5},{5,9},{9,... | collective-permute-start | bytes 18440 | tf_op jit(solution)/shard_map/ppermute | solution.py:335
  128.9 8.4 %collective-permute-start.21 = (f32[12,128]{1,0:T(8,128)S(1)}, f32[12,128]{1,0:T(8,128)S(1)}, u32[]{:S(2)}, u32[]{:S(2)}) collective-permute-start(f32[12,128]{1,0:T(8,128)S(1)} %get-tuple-element.96), channel_id=1, source_target_pairs={{4,0},{8,4},{12,8},{16,12},{20,16},{24,20},{28,24},{5,1},{9,5},{13... | collective-permute-start | bytes 18440 | tf_op jit(solution)/shard_map/ppermute | solution.py:335
  141.1 10.6 %collective-permute-start.24 = (f32[12,128]{1,0:T(8,128)S(1)}, f32[12,128]{1,0:T(8,128)S(1)}, u32[]{:S(2)}, u32[]{:S(2)}) collective-permute-start(f32[12,128]{1,0:T(8,128)S(1)} %get-tuple-element.102), channel_id=1, source_target_pairs={{0,4},{4,8},{8,12},{12,16},{16,20},{20,24},{24,28},{1,5},{5,9},{9,... | collective-permute-start | bytes 18440 | tf_op jit(solution)/shard_map/ppermute | solution.py:335
  143.1 8.7 %collective-permute-start.25 = (f32[12,128]{1,0:T(8,128)S(1)}, f32[12,128]{1,0:T(8,128)S(1)}, u32[]{:S(2)}, u32[]{:S(2)}) collective-permute-start(f32[12,128]{1,0:T(8,128)S(1)} %get-tuple-element.103), channel_id=1, source_target_pairs={{4,0},{8,4},{12,8},{16,12},{20,16},{24,20},{28,24},{5,1},{9,5},{13... | collective-permute-start | bytes 18440 | tf_op jit(solution)/shard_map/ppermute | solution.py:335
  157.9 10.6 %collective-permute-start.28 = (f32[12,128]{1,0:T(8,128)S(1)}, f32[12,128]{1,0:T(8,128)S(1)}, u32[]{:S(2)}, u32[]{:S(2)}) collective-permute-start(f32[12,128]{1,0:T(8,128)S(1)} %get-tuple-element.108), channel_id=1, source_target_pairs={{0,4},{4,8},{8,12},{12,16},{16,20},{20,24},{24,28},{1,5},{5,9},{9,... | collective-permute-start | bytes 18440 | tf_op jit(solution)/shard_map/ppermute | solution.py:335
  159.8 8.7 %collective-permute-start.29 = (f32[12,128]{1,0:T(8,128)S(1)}, f32[12,128]{1,0:T(8,128)S(1)}, u32[]{:S(2)}, u32[]{:S(2)}) collective-permute-start(f32[12,128]{1,0:T(8,128)S(1)} %get-tuple-element.109), channel_id=1, source_target_pairs={{4,0},{8,4},{12,8},{16,12},{20,16},{24,20},{28,24},{5,1},{9,5},{13... | collective-permute-start | bytes 18440 | tf_op jit(solution)/shard_map/ppermute | solution.py:335
  (23 other events, 112.1 us)

commit v2 on v1

--- a/solution.py
+++ b/solution.py
@@ -118,34 +118,57 @@
         outgoing[:, c, :] = jnp.where(used, found[c], FAR)
 
 
-def setup_kernel(
-    devices,
-    capacity,
-    coords_in,
-    disp_in,
-    vel_in,
-    ext_in,
-    nodes_in,
-    lists_in,
-    bucket,
-    contact_nodes,
-    coords,
-    disp,
-    vel,
-    ext,
-    nodes,
-    lists,
-    inverse,
-    outgoing,
-    send0,
-    send1,
-    send2,
-    send3,
-):
-    rows = coords_in.shape[1] // LANES
+def block_remap(index, own_count, width, px_no, py_no, px_count, py_count):
+    block = (index - own_count) >> (width.bit_length() - 1)
+    along_x = block < 2
+    place = jnp.where(along_x, px_no, py_no)
+    ends = jnp.where(along_x, px_count - 1, py_count - 1)
+    edge = jnp.where((block & 1) == 0, 0, ends)
+    moved = index ^ ((1 - (place & 1)) * width)
+    moved = jnp.where(place == edge, -1, moved)
+    return jnp.where(index < own_count, index, moved)
+
+
+def setup_kernel(devices, capacity, counts, *refs):
+    places = refs[0]
+    sources = refs[1:9]
+    (coords, disp, vel, ext, nodes, lists, inverse, outgoing) = refs[9:17]
+    sends = refs[17:21]
+    buffers = refs[21:29]
+    sems = refs[29]
+    (coords_in, disp_in, vel_in, ext_in, nodes_in, lists_in, bucket, contact_nodes) = buffers
+    copies = [
+        pltpu.make_async_copy(source, target, sems.at[n])
+        for n, (source, target) in enumerate(zip(sources, buffers))
+    ]
+    for copy in copies:
+        copy.start()
+    for copy in copies:
+        copy.wait()
+    px_no = places[0]
+    py_no = places[1]
+    own_count = coords_in.shape[1]
+    rows = own_count // LANES
     spread_rows(disp_in, disp, 3)
-    spread_rows(lists_in, lists, 4)
-    gather_halo(disp, rows, lists, (send0, send1, send2, send3))
+    width = lists_in.shape[1]
+    quarter = width // LANES
+    for b in range(4):
+        place = px_no if b < 2 else py_no
+        count = counts[b // 2]
+        to_high = (place & 1) ^ (1 - b % 2)
+        row = (b // 2) * 2
+        missing = (place == to_high * (count - 1)).astype(I32)
+        for q in range(quarter):
+            span = slice(q * LANES, (q + 1) * LANES)
+            chosen = jnp.where(
+                jnp.full((1, LANES), to_high) == 1,
+                lists_in[row + 1 : row + 2, span],
+                lists_in[row : row + 1, span],
+            )
+            lists[b * quarter + q : b * quarter + q + 1, :] = jnp.where(
+                jnp.full((1, LANES), missing) == 1, -1, chosen
+            )
+    gather_halo(disp, rows, lists, sends)
     spread_rows(coords_in, coords, 3)
     count = bucket.shape[0]
     slot_rows = inverse.shape[0]
@@ -158,9 +181,9 @@
     for r in range(count):
         b = bucket[r : r + 1, :]
         onehot = (dev_no == b).astype(F32)
-        counts = jnp.dot(onehot.astype(BF16), before, preferred_element_type=F32)
-        rank = jnp.sum(onehot * (counts[:, :LANES] + base), axis=0, keepdims=True)
-        base = base + counts[:, LANES:]
+        sums = jnp.dot(onehot.astype(BF16), before, preferred_element_type=F32)
+        rank = jnp.sum(onehot * (sums[:, :LANES] + base), axis=0, keepdims=True)
+        base = base + sums[:, LANES:]
         slot = b * capacity + rank.astype(I32)
         hi_rows.append(slot >> 7)
         lo_rows.append(slot & (LANES - 1))
@@ -171,6 +194,7 @@
     inverse[...] = (total[:slot_rows] * 64.0 + total[slot_rows:]).astype(I32) - 1
     gather_slots(coords, disp, rows, inverse, outgoing)
     spread_rows(nodes_in, nodes, 4)
+    nodes[...] = block_remap(nodes[...], own_count, width, px_no, py_no, *counts)
     spread_rows(vel_in, vel, 3)
     spread_rows(ext_in, ext, 3)
 
@@ -180,8 +204,9 @@
         (disp, recv0, recv1, recv2, recv3, nodes, thick, stiff, held, slow) = refs[:10]
         (own, out0, out1, out2, out3) = refs[10:]
     else:
-        (disp, recv0, recv1, recv2, recv3, nodes, thick, stiff) = refs[:8]
-        (own, out0, out1, out2, out3, held) = refs[8:]
+        (disp, recv0, recv1, recv2, recv3, nodes, thick, stiff, pairs, arrived) = refs[:10]
+        (own, out0, out1, out2, out3, held, pushes) = refs[10:]
+        contact_tiles(pairs, arrived, pushes)
     rows = disp.shape[0] // 3
     quarter = recv0.shape[0] // 3
     recvs = (recv0, recv1, recv2, recv3)
@@ -227,28 +252,32 @@
             outs[b][c * quarter : (c + 1) * quarter, :] = sums[c][start : start + quarter]
 
 
-def contact_kernel(pairs, arrived, pushes, turned):
-    tiles = arrived.shape[0]
+def contact_tiles(pairs, arrived, pushes):
     pushes[...] = jnp.zeros(pushes.shape, F32)
-    for t in range(tiles):
-        block = jnp.concatenate([arrived[t], jnp.zeros((5, LANES), F32)], axis=0)
-        turned[t] = jnp.transpose(block)
-    for p in range(pairs.shape[1]):
-        a = pairs[0, p]
-        b = pairs[1, p]
-        pos_a = arrived[a]
-        pos_b = turned[b]
-        gaps = [
-            jnp.broadcast_to(pos_a[c : c + 1, :], (LANES, LANES))
-            - jnp.broadcast_to(pos_b[:, c : c + 1], (LANES, LANES))
-            for c in range(3)
-        ]
-        dist = gaps[0] * gaps[0] + gaps[1] * gaps[1] + gaps[2] * gaps[2]
-        weight = PENALTY * jnp.exp(dist * (-1.0 / REACH))
-        push = jnp.concatenate(
-            [jnp.sum(weight * gaps[c], axis=0, keepdims=True) for c in range(3)], axis=0
-        )
-        pushes[a] = pushes[a] + push
+    empty = jnp.zeros((5, LANES), F32)
+    for start in range(0, pairs.shape[1], LANES // 8):
+        stop = min(start + LANES // 8, pairs.shape[1])
+        others = []
+        for p in range(start, stop):
+            others += [arrived[pairs[1, p]], empty]
+        if stop - start < LANES // 8:
+            others.append(jnp.zeros((LANES - 8 * (stop - start), LANES), F32))
+        turned = jnp.transpose(jnp.concatenate(others, axis=0))
+        for p in range(start, stop):
+            a = pairs[0, p]
+            pos_a = arrived[a]
+            column = 8 * (p - start)
+            gaps = [
+                jnp.broadcast_to(pos_a[c : c + 1, :], (LANES, LANES))
+                - jnp.broadcast_to(turned[:, column + c : column + c + 1], (LANES, LANES))
+                for c in range(3)
+            ]
+            dist = gaps[0] * gaps[0] + gaps[1] * gaps[1] + gaps[2] * gaps[2]
+            weight = jnp.exp(dist * (-1.0 / REACH))
+            push = jnp.concatenate(
+                [jnp.sum(weight * gaps[c], axis=0, keepdims=True) for c in range(3)], axis=0
+            )
+            pushes[a] = pushes[a] + PENALTY * push
 
 
 def update_kernel(first, last, final, *refs):
@@ -313,9 +342,11 @@
     return jax.ShapeDtypeStruct(dims, F32)
 
 
-def call(kernel, inputs, outputs, name, smem=(), scratch=()):
+def call(kernel, inputs, outputs, name, smem=(), far=(), scratch=()):
     specs = [
-        pl.BlockSpec(memory_space=pltpu.SMEM if i in smem else pltpu.VMEM)
+        pl.BlockSpec(
+            memory_space=pltpu.SMEM if i in smem else pltpu.HBM if i in far else pltpu.VMEM
+        )
         for i in range(len(inputs))
     ]
     return pl.pallas_call(
@@ -329,19 +360,24 @@
     )(*inputs)
 
 
-def shift(block, axis, step):
-    count = lax.axis_size(axis)
-    pairs = [(i, i + step) for i in range(count) if 0 <= i + step < count]
-    return lax.ppermute(block, axis, pairs)
-
-
-def exchange(to_low_x, to_high_x, to_low_y, to_high_y):
-    return (
-        shift(to_high_x, "px", 1),
-        shift(to_low_x, "px", -1),
-        shift(to_high_y, "py", 1),
-        shift(to_low_y, "py", -1),
-    )
+def partners():
+    px, py = lax.axis_size("px"), lax.axis_size("py")
+    number = lambda i, j: i * py + j
+    swaps = [[] for _ in range(4)]
+    for i in range(px):
+        for j in range(py):
+            me = number(i, j)
+            swaps[0].append((me, number(i ^ 1, j)))
+            other = i - 1 if i % 2 == 0 else i + 1
+            swaps[1].append((me, number(other, j) if 0 <= other < px else number(i, j ^ 1)))
+            swaps[2].append((me, number(i, j ^ 1)))
+            other = j - 1 if j % 2 == 0 else j + 1
+            swaps[3].append((me, number(i, other % py)))
+    return swaps
+
+
+def exchange(blocks):
+    return [lax.ppermute(block, ("px", "py"), pairs) for block, pairs in zip(blocks, partners())]
 
 
 def swap(slots, devices, capacity):
@@ -386,18 +422,22 @@
     sent = [shape(3 * quarter, LANES)] * 4
     slots = shape(slot_rows, 3, LANES)
 
+    places = jnp.stack([lax.axis_index("px"), lax.axis_index("py")]).astype(I32)
+    sources = [
+        coords,
+        displacement,
+        velocity,
+        ext_force,
+        elem_nodes,
+        halo_lists,
+        contact_bucket.reshape(-1, LANES),
+        contact_nodes.reshape(-1, LANES),
+    ]
     coords, disp, vel, ext, nodes, lists, inverse, outgoing, *sends = call(
-        functools.partial(setup_kernel, devices, capacity),
-        [
-            coords,
-            displacement,
-            velocity,
-            ext_force,
-            elem_nodes,
-            halo_lists,
-            contact_bucket.reshape(-1, LANES),
-            contact_nodes.reshape(-1, LANES),
-        ],
+        functools.partial(
+            setup_kernel, devices, capacity, (lax.axis_size("px"), lax.axis_size("py"))
+        ),
+        [places] + sources,
         [nodal] * 4
         + [
             jax.ShapeDtypeStruct((4 * elem_rows, LANES), I32),
@@ -407,32 +447,28 @@
         ]
         + sent,
         "setup",
+        smem=(0,),
+        far=range(1, 9),
+        scratch=[pltpu.VMEM(source.shape, source.dtype) for source in sources]
+        + [pltpu.SemaphoreType.DMA((len(sources),))],
     )
     for step_no in range(STEPS):
         for sub_no in range(SUBS):
             first = sub_no == 0
             last = sub_no == SUBS - 1
             final = last and step_no == STEPS - 1
-            recvs = exchange(*sends)
             if first:
                 arrived = swap(outgoing, devices, capacity)
+            recvs = exchange(sends)
+            if first:
                 own, *rest = call(
                     functools.partial(element_kernel, False),
-                    [disp, *recvs, nodes, thickness, stiffness],
-                    [nodal] + sent + [shape(12 * elem_rows, LANES)],
+                    [disp, *recvs, nodes, thickness, stiffness, tile_pairs, arrived],
+                    [nodal] + sent + [shape(12 * elem_rows, LANES), slots],
                     "elements",
-                    smem=(7,),
+                    smem=(7, 8),
                 )
-                held = rest[4]
-                backs = exchange(*rest[:4])
-                (pushes,) = call(
-                    contact_kernel,
-                    [tile_pairs, arrived],
-                    [slots],
-                    "contact",
-                    smem=(0,),
-                    scratch=[pltpu.VMEM((slot_rows, LANES, 8), F32)],
-                )
+                held, pushes = rest[4:]
                 returned = swap(pushes, devices, capacity)
             else:
                 own, *rest = call(
@@ -442,7 +478,7 @@
                     "elements_later",
                     smem=(7,),
                 )
-                backs = exchange(*rest[:4])
+            backs = exchange(rest[:4])
             inputs = [own, *backs]
             inputs += [lists, ext, inv_mass, vel, disp]
             inputs += [returned, inverse] if first else [contact]

time: 174 us -> 101 us (0.58)
  the two profiles are of different devices: /device:TPU:9 before, /device:TPU:0 now
where the time goes in v2:
time: 101 us; the launch traced here: 99.7 us
  starting transfers between devices  46.8 us (46%)
  waiting for transfers between devices  23.6 us (23%)
  Pallas kernels  21.9 us (22%)
  local copies, waits for them, and re-layouts  6.52 us (6%)
    ppermute x32, starting transfers between devices, exchange(): lax.ppermute(block, ('px', 'py'), pairs)  27.1 us
    pallas_call x9, Pallas kernels, call(): pl.pallas_call(kernel, out_shape=tuple(outputs), in_specs=specs, out_spec...  21.9 us
    all_to_all x4, starting transfers between devices, swap(): return lax.all_to_all(slots, axes, 0, 0, tiled=True)  19.6 us
    ppermute x32, waiting for transfers between devices, exchange(): lax.ppermute(block, ('px', 'py'), pairs)  15.7 us
    all_to_all x4, waiting for transfers between devices, swap(): return lax.all_to_all(slots, axes, 0, 0, tiled=True)  7.87 us
    unnamed x26, local copies, waits for them, and re-layouts  6.45 us
  transfers between devices with their start and end apart: 36, of which 18 were waited for; matrix products, arithmetic and copies ran while one was open for 0% of the time, Pallas kernels for 0%

profile of v2, /device:TPU:0, one launch (start us, length us, event | category | flops | bytes accessed | tf_op | source)
XLA Modules:
  0.0 99.7 jit_solution(15005151533395814268)
XLA Ops:
  5.8 2.5 %setup.1 = (f32[48,128]{1,0:T(8,128)S(1)}, f32[48,128]{1,0:T(8,128)S(1)}, f32[48,128]{1,0:T(8,128)S(1)}, f32[48,128]{1,0:T(8,128)S(1)}, s32[64,128]{1,0:T(8,128)...) custom-call(s32[2]{0:T(128)S(1)} %pad_add_fusion.refs_0_, ...), custom_call_target="tpu_custom_call" | custom-call | tf_op jit(solution)/shard_map/setup/pallas_call | solution.py:352
  8.3 7.3 %all-to-all-start = ((f32[32,3,128]{2,1,0:T(4,128)}), f32[32,3,128]{2,1,0:T(4,128)S(1)}, u32[]{:S(2)}, u32[]{:S(2)}) async-start(f32[32,3,128]{2,1,0:T(4,128)} %get-tuple-element.67), calls=%async_computation | async-start | bytes 131072 | tf_op jit(solution)/shard_map/all_to_all | solution.py:386
  15.6 1.8 %collective-permute-start = (f32[12,128]{1,0:T(8,128)S(1)}, f32[12,128]{1,0:T(8,128)S(1)}, u32[]{:S(2)}, u32[]{:S(2)}) collective-permute-start(f32[12,128]{1,0:T(8,128)S(1)} %get-tuple-element.62), channel_id=1, source_target_pairs={{0,4},{1,5},{2,6},{3,7},{4,0},{5,1},{6,2},{7,3},{8,12},{9,13},{10,... | collective-permute-start | bytes 18440 | tf_op jit(solution)/shard_map/ppermute | solution.py:380
  19.4 1.7 %collective-permute-done.3.refs_4_ = f32[12,128]{1,0:T(8,128)S(1)} collective-permute-done((f32[12,128]{1,0:T(8,128)S(1)}, f32[12,128]{1,0:T(8,128)S(1)}, u32[]{:S(2)}, u32[]{:S(2)}) %collective-permute-start.3) | collective-permute-done | bytes 6176 | tf_op jit(solution)/shard_map/ppermute | solution.py:380
  21.1 1.9 %all-to-all-done.refs_9_ = f32[32,3,128]{2,1,0:T(4,128)S(1)} async-done(((f32[32,3,128]{2,1,0:T(4,128)}), f32[32,3,128]{2,1,0:T(4,128)S(1)}, u32[]{:S(2)}, u32[]{:S(2)}) %all-to-all-start) | async-done | bytes 49184 | tf_op jit(solution)/shard_map/all_to_all | solution.py:386
  23.7 4.6 %elements.2 = (f32[48,128]{1,0:T(8,128)S(1)}, f32[12,128]{1,0:T(8,128)S(1)}, f32[12,128]{1,0:T(8,128)S(1)}, f32[12,128]{1,0:T(8,128)S(1)}, f32[12,128]{1,0:T(8,1...) custom-call(f32[48,128]{1,0:T(8,128)S(1)} %get-tuple-element.61.refs_0_.refs_9_, ...), custom_call_target="tpu_custom_call" | custom-call | tf_op jit(solution)/shard_map/elements/pallas_call | solution.py:352
  28.4 3.7 %all-to-all-start.1 = ((f32[32,3,128]{2,1,0:T(4,128)}), f32[32,3,128]{2,1,0:T(4,128)S(1)}, u32[]{:S(2)}, u32[]{:S(2)}) async-start(f32[32,3,128]{2,1,0:T(4,128)} %get-tuple-element.76), calls=%async_computation.1 | async-start | bytes 131072 | tf_op jit(solution)/shard_map/all_to_all | solution.py:386
  32.1 1.8 %collective-permute-start.4 = (f32[12,128]{1,0:T(8,128)S(1)}, f32[12,128]{1,0:T(8,128)S(1)}, u32[]{:S(2)}, u32[]{:S(2)}) collective-permute-start(f32[12,128]{1,0:T(8,128)S(1)} %get-tuple-element.69), channel_id=1, source_target_pairs={{0,4},{1,5},{2,6},{3,7},{4,0},{5,1},{6,2},{7,3},{8,12},{9,13},{10,... | collective-permute-start | bytes 18440 | tf_op jit(solution)/shard_map/ppermute | solution.py:380
  35.8 1.7 %collective-permute-done.7.refs_4_ = f32[12,128]{1,0:T(8,128)S(1)} collective-permute-done((f32[12,128]{1,0:T(8,128)S(1)}, f32[12,128]{1,0:T(8,128)S(1)}, u32[]{:S(2)}, u32[]{:S(2)}) %collective-permute-start.7) | collective-permute-done | bytes 6176 | tf_op jit(solution)/shard_map/ppermute | solution.py:380
  37.5 2.0 %all-to-all-done.1.refs_10_ = f32[32,3,128]{2,1,0:T(4,128)S(1)} async-done(((f32[32,3,128]{2,1,0:T(4,128)}), f32[32,3,128]{2,1,0:T(4,128)S(1)}, u32[]{:S(2)}, u32[]{:S(2)}) %all-to-all-start.1) | async-done | bytes 49184 | tf_op jit(solution)/shard_map/all_to_all | solution.py:386
  45.2 3.0 %elements_later.2 = (f32[48,128]{1,0:T(8,128)S(1)}, f32[12,128]{1,0:T(8,128)S(1)}, f32[12,128]{1,0:T(8,128)S(1)}, f32[12,128]{1,0:T(8,128)S(1)}, f32[12,128]{1,0:T(8,128)S(1)}) custom-call(f32[48,128]{1,0:T(8,128)S(1)} %get-tuple-element.78.refs_0_.refs_9_, f32[12,128]{1,0:T(8,128)S(1)} %collective-permute-done.8.refs_1_, ...), custom_call_target="tpu_custom_call" | custom-call | tf_op jit(solution)/shard_map/elements_later/pallas_call | solution.py:352
  48.3 3.0 %collective-permute-start.12 = (f32[12,128]{1,0:T(8,128)S(1)}, f32[12,128]{1,0:T(8,128)S(1)}, u32[]{:S(2)}, u32[]{:S(2)}) collective-permute-start(f32[12,128]{1,0:T(8,128)S(1)} %get-tuple-element.85), channel_id=1, source_target_pairs={{0,4},{1,5},{2,6},{3,7},{4,0},{5,1},{6,2},{7,3},{8,12},{9,13},{10,... | collective-permute-start | bytes 18440 | tf_op jit(solution)/shard_map/ppermute | solution.py:380
  53.0 1.9 %collective-permute-done.15.refs_4_ = f32[12,128]{1,0:T(8,128)S(1)} collective-permute-done((f32[12,128]{1,0:T(8,128)S(1)}, f32[12,128]{1,0:T(8,128)S(1)}, u32[]{:S(2)}, u32[]{:S(2)}) %collective-permute-start.15) | collective-permute-done | bytes 6176 | tf_op jit(solution)/shard_map/ppermute | solution.py:380
  56.5 4.9 %all-to-all-start.2 = ((f32[32,3,128]{2,1,0:T(4,128)}), f32[32,3,128]{2,1,0:T(4,128)S(1)}, u32[]{:S(2)}, u32[]{:S(2)}) async-start(f32[32,3,128]{2,1,0:T(4,128)} %get-tuple-element.97), calls=%async_computation.2 | async-start | bytes 131072 | tf_op jit(solution)/shard_map/all_to_all | solution.py:386
  61.4 1.8 %collective-permute-start.16 = (f32[12,128]{1,0:T(8,128)S(1)}, f32[12,128]{1,0:T(8,128)S(1)}, u32[]{:S(2)}, u32[]{:S(2)}) collective-permute-start(f32[12,128]{1,0:T(8,128)S(1)} %get-tuple-element.93), channel_id=1, source_target_pairs={{0,4},{1,5},{2,6},{3,7},{4,0},{5,1},{6,2},{7,3},{8,12},{9,13},{10,... | collective-permute-start | bytes 18440 | tf_op jit(solution)/shard_map/ppermute | solution.py:380
  65.1 1.7 %collective-permute-done.19.refs_4_ = f32[12,128]{1,0:T(8,128)S(1)} collective-permute-done((f32[12,128]{1,0:T(8,128)S(1)}, f32[12,128]{1,0:T(8,128)S(1)}, u32[]{:S(2)}, u32[]{:S(2)}) %collective-permute-start.19) | collective-permute-done | bytes 6176 | tf_op jit(solution)/shard_map/ppermute | solution.py:380
  66.8 2.0 %all-to-all-done.2.refs_9_ = f32[32,3,128]{2,1,0:T(4,128)S(1)} async-done(((f32[32,3,128]{2,1,0:T(4,128)}), f32[32,3,128]{2,1,0:T(4,128)S(1)}, u32[]{:S(2)}, u32[]{:S(2)}) %all-to-all-start.2) | async-done | bytes 49184 | tf_op jit(solution)/shard_map/all_to_all | solution.py:386
  68.8 4.7 %elements.3 = (f32[48,128]{1,0:T(8,128)S(1)}, f32[12,128]{1,0:T(8,128)S(1)}, f32[12,128]{1,0:T(8,128)S(1)}, f32[12,128]{1,0:T(8,128)S(1)}, f32[12,128]{1,0:T(8,1...) custom-call(f32[48,128]{1,0:T(8,128)S(1)} %get-tuple-element.92.refs_0_.refs_9_, ...), custom_call_target="tpu_custom_call" | custom-call | tf_op jit(solution)/shard_map/elements/pallas_call | solution.py:352
  73.5 3.7 %all-to-all-start.3 = ((f32[32,3,128]{2,1,0:T(4,128)}), f32[32,3,128]{2,1,0:T(4,128)S(1)}, u32[]{:S(2)}, u32[]{:S(2)}) async-start(f32[32,3,128]{2,1,0:T(4,128)} %get-tuple-element.104), calls=%async_computation.3 | async-start | bytes 131072 | tf_op jit(solution)/shard_map/all_to_all | solution.py:386
  77.2 1.8 %collective-permute-start.20 = (f32[12,128]{1,0:T(8,128)S(1)}, f32[12,128]{1,0:T(8,128)S(1)}, u32[]{:S(2)}, u32[]{:S(2)}) collective-permute-start(f32[12,128]{1,0:T(8,128)S(1)} %get-tuple-element.99), channel_id=1, source_target_pairs={{0,4},{1,5},{2,6},{3,7},{4,0},{5,1},{6,2},{7,3},{8,12},{9,13},{10,... | collective-permute-start | bytes 18440 | tf_op jit(solution)/shard_map/ppermute | solution.py:380
  82.6 2.0 %all-to-all-done.3.refs_10_ = f32[32,3,128]{2,1,0:T(4,128)S(1)} async-done(((f32[32,3,128]{2,1,0:T(4,128)}), f32[32,3,128]{2,1,0:T(4,128)S(1)}, u32[]{:S(2)}, u32[]{:S(2)}) %all-to-all-start.3) | async-done | bytes 49184 | tf_op jit(solution)/shard_map/all_to_all | solution.py:386
  89.6 3.0 %elements_later.3 = (f32[48,128]{1,0:T(8,128)S(1)}, f32[12,128]{1,0:T(8,128)S(1)}, f32[12,128]{1,0:T(8,128)S(1)}, f32[12,128]{1,0:T(8,128)S(1)}, f32[12,128]{1,0:T(8,128)S(1)}) custom-call(f32[48,128]{1,0:T(8,128)S(1)} %get-tuple-element.105.refs_0_.refs_9_, f32[12,128]{1,0:T(8,128)S(1)} %collective-permute-done.24.refs_1_, ...), custom_call_target="tpu_custom_call" | custom-call | tf_op jit(solution)/shard_map/elements_later/pallas_call | solution.py:352
  92.7 2.5 %collective-permute-start.28 = (f32[12,128]{1,0:T(8,128)S(1)}, f32[12,128]{1,0:T(8,128)S(1)}, u32[]{:S(2)}, u32[]{:S(2)}) collective-permute-start(f32[12,128]{1,0:T(8,128)S(1)} %get-tuple-element.112), channel_id=1, source_target_pairs={{0,4},{1,5},{2,6},{3,7},{4,0},{5,1},{6,2},{7,3},{8,12},{9,13},{10,... | collective-permute-start | bytes 18440 | tf_op jit(solution)/shard_map/ppermute | solution.py:380
  96.8 1.9 %collective-permute-done.31.refs_4_ = f32[12,128]{1,0:T(8,128)S(1)} collective-permute-done((f32[12,128]{1,0:T(8,128)S(1)}, f32[12,128]{1,0:T(8,128)S(1)}, u32[]{:S(2)}, u32[]{:S(2)}) %collective-permute-start.31) | collective-permute-done | bytes 6176 | tf_op jit(solution)/shard_map/ppermute | solution.py:380
  (85 shorter events, 31.9 us)
Async XLA Ops:
  8.3 14.7 %all-to-all-start = ((f32[32,3,128]{2,1,0:T(4,128)}), f32[32,3,128]{2,1,0:T(4,128)S(1)}, u32[]{:S(2)}, u32[]{:S(2)}) async-start(f32[32,3,128]{2,1,0:T(4,128)} %get-tuple-element.67), calls=%async_computation | async-start | bytes 131072 | tf_op jit(solution)/shard_map/all_to_all | solution.py:386
  15.6 3.7 %collective-permute-start = (f32[12,128]{1,0:T(8,128)S(1)}, f32[12,128]{1,0:T(8,128)S(1)}, u32[]{:S(2)}, u32[]{:S(2)}) collective-permute-start(f32[12,128]{1,0:T(8,128)S(1)} %get-tuple-element.62), channel_id=1, source_target_pairs={{0,4},{1,5},{2,6},{3,7},{4,0},{5,1},{6,2},{7,3},{8,12},{9,13},{10,... | collective-permute-start | bytes 18440 | tf_op jit(solution)/shard_map/ppermute | solution.py:380
  18.0 3.1 %collective-permute-start.3 = (f32[12,128]{1,0:T(8,128)S(1)}, f32[12,128]{1,0:T(8,128)S(1)}, u32[]{:S(2)}, u32[]{:S(2)}) collective-permute-start(f32[12,128]{1,0:T(8,128)S(1)} %get-tuple-element.65), channel_id=1, source_target_pairs={{0,3},{1,2},{2,1},{3,0},{4,7},{5,6},{6,5},{7,4},{8,11},{9,10},{10,... | collective-permute-start | bytes 18440 | tf_op jit(solution)/shard_map/ppermute | solution.py:380
  28.4 11.1 %all-to-all-start.1 = ((f32[32,3,128]{2,1,0:T(4,128)}), f32[32,3,128]{2,1,0:T(4,128)S(1)}, u32[]{:S(2)}, u32[]{:S(2)}) async-start(f32[32,3,128]{2,1,0:T(4,128)} %get-tuple-element.76), calls=%async_computation.1 | async-start | bytes 131072 | tf_op jit(solution)/shard_map/all_to_all | solution.py:386
  32.1 3.7 %collective-permute-start.4 = (f32[12,128]{1,0:T(8,128)S(1)}, f32[12,128]{1,0:T(8,128)S(1)}, u32[]{:S(2)}, u32[]{:S(2)}) collective-permute-start(f32[12,128]{1,0:T(8,128)S(1)} %get-tuple-element.69), channel_id=1, source_target_pairs={{0,4},{1,5},{2,6},{3,7},{4,0},{5,1},{6,2},{7,3},{8,12},{9,13},{10,... | collective-permute-start | bytes 18440 | tf_op jit(solution)/shard_map/ppermute | solution.py:380
  34.4 3.1 %collective-permute-start.7 = (f32[12,128]{1,0:T(8,128)S(1)}, f32[12,128]{1,0:T(8,128)S(1)}, u32[]{:S(2)}, u32[]{:S(2)}) collective-permute-start(f32[12,128]{1,0:T(8,128)S(1)} %get-tuple-element.72), channel_id=1, source_target_pairs={{0,3},{1,2},{2,1},{3,0},{4,7},{5,6},{6,5},{7,4},{8,11},{9,10},{10,... | collective-permute-start | bytes 18440 | tf_op jit(solution)/shard_map/ppermute | solution.py:380
  40.3 2.3 %collective-permute-start.10 = (f32[12,128]{1,0:T(8,128)S(1)}, f32[12,128]{1,0:T(8,128)S(1)}, u32[]{:S(2)}, u32[]{:S(2)}) collective-permute-start(f32[12,128]{1,0:T(8,128)S(1)} %get-tuple-element.81), channel_id=1, source_target_pairs={{0,1},{1,0},{2,3},{3,2},{4,5},{5,4},{6,7},{7,6},{8,9},{9,8},{10,11... | collective-permute-start | bytes 18440 | tf_op jit(solution)/shard_map/ppermute | solution.py:380
  40.4 3.1 %collective-permute-start.11 = (f32[12,128]{1,0:T(8,128)S(1)}, f32[12,128]{1,0:T(8,128)S(1)}, u32[]{:S(2)}, u32[]{:S(2)}) collective-permute-start(f32[12,128]{1,0:T(8,128)S(1)} %get-tuple-element.82), channel_id=1, source_target_pairs={{0,3},{1,2},{2,1},{3,0},{4,7},{5,6},{6,5},{7,4},{8,11},{9,10},{10,... | collective-permute-start | bytes 18440 | tf_op jit(solution)/shard_map/ppermute | solution.py:380
  40.9 3.7 %collective-permute-start.8 = (f32[12,128]{1,0:T(8,128)S(1)}, f32[12,128]{1,0:T(8,128)S(1)}, u32[]{:S(2)}, u32[]{:S(2)}) collective-permute-start(f32[12,128]{1,0:T(8,128)S(1)} %get-tuple-element.79), channel_id=1, source_target_pairs={{0,4},{1,5},{2,6},{3,7},{4,0},{5,1},{6,2},{7,3},{8,12},{9,13},{10,... | collective-permute-start | bytes 18440 | tf_op jit(solution)/shard_map/ppermute | solution.py:380
  42.4 2.1 %collective-permute-start.9 = (f32[12,128]{1,0:T(8,128)S(1)}, f32[12,128]{1,0:T(8,128)S(1)}, u32[]{:S(2)}, u32[]{:S(2)}) collective-permute-start(f32[12,128]{1,0:T(8,128)S(1)} %get-tuple-element.80), channel_id=1, source_target_pairs={{0,1},{1,0},{2,3},{3,2},{4,8},{5,9},{6,10},{7,11},{8,4},{9,5},{10,... | collective-permute-start | bytes 18440 | tf_op jit(solution)/shard_map/ppermute | solution.py:380
  48.3 4.7 %collective-permute-start.12 = (f32[12,128]{1,0:T(8,128)S(1)}, f32[12,128]{1,0:T(8,128)S(1)}, u32[]{:S(2)}, u32[]{:S(2)}) collective-permute-start(f32[12,128]{1,0:T(8,128)S(1)} %get-tuple-element.85), channel_id=1, source_target_pairs={{0,4},{1,5},{2,6},{3,7},{4,0},{5,1},{6,2},{7,3},{8,12},{9,13},{10,... | collective-permute-start | bytes 18440 | tf_op jit(solution)/shard_map/ppermute | solution.py:380
  51.8 3.1 %collective-permute-start.15 = (f32[12,128]{1,0:T(8,128)S(1)}, f32[12,128]{1,0:T(8,128)S(1)}, u32[]{:S(2)}, u32[]{:S(2)}) collective-permute-start(f32[12,128]{1,0:T(8,128)S(1)} %get-tuple-element.88), channel_id=1, source_target_pairs={{0,3},{1,2},{2,1},{3,0},{4,7},{5,6},{6,5},{7,4},{8,11},{9,10},{10,... | collective-permute-start | bytes 18440 | tf_op jit(solution)/shard_map/ppermute | solution.py:380
  56.5 12.3 %all-to-all-start.2 = ((f32[32,3,128]{2,1,0:T(4,128)}), f32[32,3,128]{2,1,0:T(4,128)S(1)}, u32[]{:S(2)}, u32[]{:S(2)}) async-start(f32[32,3,128]{2,1,0:T(4,128)} %get-tuple-element.97), calls=%async_computation.2 | async-start | bytes 131072 | tf_op jit(solution)/shard_map/all_to_all | solution.py:386
  61.4 3.7 %collective-permute-start.16 = (f32[12,128]{1,0:T(8,128)S(1)}, f32[12,128]{1,0:T(8,128)S(1)}, u32[]{:S(2)}, u32[]{:S(2)}) collective-permute-start(f32[12,128]{1,0:T(8,128)S(1)} %get-tuple-element.93), channel_id=1, source_target_pairs={{0,4},{1,5},{2,6},{3,7},{4,0},{5,1},{6,2},{7,3},{8,12},{9,13},{10,... | collective-permute-start | bytes 18440 | tf_op jit(solution)/shard_map/ppermute | solution.py:380
  63.8 3.1 %collective-permute-start.19 = (f32[12,128]{1,0:T(8,128)S(1)}, f32[12,128]{1,0:T(8,128)S(1)}, u32[]{:S(2)}, u32[]{:S(2)}) collective-permute-start(f32[12,128]{1,0:T(8,128)S(1)} %get-tuple-element.96), channel_id=1, source_target_pairs={{0,3},{1,2},{2,1},{3,0},{4,7},{5,6},{6,5},{7,4},{8,11},{9,10},{10,... | collective-permute-start | bytes 18440 | tf_op jit(solution)/shard_map/ppermute | solution.py:380
  73.5 11.1 %all-to-all-start.3 = ((f32[32,3,128]{2,1,0:T(4,128)}), f32[32,3,128]{2,1,0:T(4,128)S(1)}, u32[]{:S(2)}, u32[]{:S(2)}) async-start(f32[32,3,128]{2,1,0:T(4,128)} %get-tuple-element.104), calls=%async_computation.3 | async-start | bytes 131072 | tf_op jit(solution)/shard_map/all_to_all | solution.py:386
  77.2 3.7 %collective-permute-start.20 = (f32[12,128]{1,0:T(8,128)S(1)}, f32[12,128]{1,0:T(8,128)S(1)}, u32[]{:S(2)}, u32[]{:S(2)}) collective-permute-start(f32[12,128]{1,0:T(8,128)S(1)} %get-tuple-element.99), channel_id=1, source_target_pairs={{0,4},{1,5},{2,6},{3,7},{4,0},{5,1},{6,2},{7,3},{8,12},{9,13},{10,... | collective-permute-start | bytes 18440 | tf_op jit(solution)/shard_map/ppermute | solution.py:380
  79.5 3.1 %collective-permute-start.23 = (f32[12,128]{1,0:T(8,128)S(1)}, f32[12,128]{1,0:T(8,128)S(1)}, u32[]{:S(2)}, u32[]{:S(2)}) collective-permute-start(f32[12,128]{1,0:T(8,128)S(1)} %get-tuple-element.102), channel_id=1, source_target_pairs={{0,3},{1,2},{2,1},{3,0},{4,7},{5,6},{6,5},{7,4},{8,11},{9,10},{10,... | collective-permute-start | bytes 18440 | tf_op jit(solution)/shard_map/ppermute | solution.py:380
  85.3 3.7 %collective-permute-start.24 = (f32[12,128]{1,0:T(8,128)S(1)}, f32[12,128]{1,0:T(8,128)S(1)}, u32[]{:S(2)}, u32[]{:S(2)}) collective-permute-start(f32[12,128]{1,0:T(8,128)S(1)} %get-tuple-element.106), channel_id=1, source_target_pairs={{0,4},{1,5},{2,6},{3,7},{4,0},{5,1},{6,2},{7,3},{8,12},{9,13},{10,... | collective-permute-start | bytes 18440 | tf_op jit(solution)/shard_map/ppermute | solution.py:380
  86.0 3.0 %collective-permute-start.25 = (f32[12,128]{1,0:T(8,128)S(1)}, f32[12,128]{1,0:T(8,128)S(1)}, u32[]{:S(2)}, u32[]{:S(2)}) collective-permute-start(f32[12,128]{1,0:T(8,128)S(1)} %get-tuple-element.107), channel_id=1, source_target_pairs={{0,1},{1,0},{2,3},{3,2},{4,8},{5,9},{6,10},{7,11},{8,4},{9,5},{10,... | collective-permute-start | bytes 18440 | tf_op jit(solution)/shard_map/ppermute | solution.py:380
  86.1 3.0 %collective-permute-start.26 = (f32[12,128]{1,0:T(8,128)S(1)}, f32[12,128]{1,0:T(8,128)S(1)}, u32[]{:S(2)}, u32[]{:S(2)}) collective-permute-start(f32[12,128]{1,0:T(8,128)S(1)} %get-tuple-element.108), channel_id=1, source_target_pairs={{0,1},{1,0},{2,3},{3,2},{4,5},{5,4},{6,7},{7,6},{8,9},{9,8},{10,11... | collective-permute-start | bytes 18440 | tf_op jit(solution)/shard_map/ppermute | solution.py:380
  86.5 3.1 %collective-permute-start.27 = (f32[12,128]{1,0:T(8,128)S(1)}, f32[12,128]{1,0:T(8,128)S(1)}, u32[]{:S(2)}, u32[]{:S(2)}) collective-permute-start(f32[12,128]{1,0:T(8,128)S(1)} %get-tuple-element.109), channel_id=1, source_target_pairs={{0,3},{1,2},{2,1},{3,0},{4,7},{5,6},{6,5},{7,4},{8,11},{9,10},{10,... | collective-permute-start | bytes 18440 | tf_op jit(solution)/shard_map/ppermute | solution.py:380
  92.7 4.2 %collective-permute-start.28 = (f32[12,128]{1,0:T(8,128)S(1)}, f32[12,128]{1,0:T(8,128)S(1)}, u32[]{:S(2)}, u32[]{:S(2)}) collective-permute-start(f32[12,128]{1,0:T(8,128)S(1)} %get-tuple-element.112), channel_id=1, source_target_pairs={{0,4},{1,5},{2,6},{3,7},{4,0},{5,1},{6,2},{7,3},{8,12},{9,13},{10,... | collective-permute-start | bytes 18440 | tf_op jit(solution)/shard_map/ppermute | solution.py:380
  95.6 3.1 %collective-permute-start.31 = (f32[12,128]{1,0:T(8,128)S(1)}, f32[12,128]{1,0:T(8,128)S(1)}, u32[]{:S(2)}, u32[]{:S(2)}) collective-permute-start(f32[12,128]{1,0:T(8,128)S(1)} %get-tuple-element.115), channel_id=1, source_target_pairs={{0,3},{1,2},{2,1},{3,0},{4,7},{5,6},{6,5},{7,4},{8,11},{9,10},{10,... | collective-permute-start | bytes 18440 | tf_op jit(solution)/shard_map/ppermute | solution.py:380
  (25 other events, 56.8 us)

commit v3 on v2

--- a/solution.py
+++ b/solution.py
@@ -21,20 +21,25 @@
 BF16 = jnp.bfloat16
 I32 = jnp.int32
 
-VMEM_BYTES = 40 * 1024 * 1024
+VMEM_BYTES = 32 * 1024 * 1024
+WHOLE_VMEM = 64 * 1024 * 1024
 
 
 def lookup(table_row, rows, index):
-    hi = index >> 7
-    lo = index & (LANES - 1)
-    found = [jnp.zeros(index.shape, F32) for _ in range(3)]
-    for h in range(rows):
-        here = hi == h
-        for c in range(3):
-            row = jnp.broadcast_to(table_row(c, h), index.shape)
-            got = jnp.take_along_axis(row, lo, axis=1, mode="promise_in_bounds")
-            found[c] = jnp.where(here, got, found[c])
-    return found
+    parts = []
+    for start in range(0, index.shape[0], 8):
+        block = index[start : start + 8]
+        hi = block >> 7
+        lo = block & (LANES - 1)
+        found = [jnp.zeros(block.shape, F32) for _ in range(3)]
+        for h in range(rows):
+            here = hi == h
+            for c in range(3):
+                row = jnp.broadcast_to(table_row(c, h), block.shape)
+                got = jnp.take_along_axis(row, lo, axis=1, mode="promise_in_bounds")
+                found[c] = jnp.where(here, got, found[c])
+        parts.append(found)
+    return [jnp.concatenate([part[c] for part in parts], axis=0) for c in range(3)]
 
 
 def halves(values):
@@ -130,13 +135,13 @@
 
 
 def setup_kernel(devices, capacity, counts, *refs):
-    places = refs[0]
-    sources = refs[1:9]
-    (coords, disp, vel, ext, nodes, lists, inverse, outgoing) = refs[9:17]
-    sends = refs[17:21]
-    buffers = refs[21:29]
-    sems = refs[29]
-    (coords_in, disp_in, vel_in, ext_in, nodes_in, lists_in, bucket, contact_nodes) = buffers
+    sources = refs[:11]
+    (coords, disp, vel, ext, nodes, lists, inverse, outgoing, splat, slow, select) = refs[11:22]
+    sends = refs[22:26]
+    buffers = refs[26:37]
+    sems = refs[37]
+    (coords_in, disp_in, vel_in, ext_in, nodes_in, lists_in, bucket, contact_nodes) = buffers[:8]
+    (stiff, classes, pairs) = buffers[8:]
     copies = [
         pltpu.make_async_copy(source, target, sems.at[n])
         for n, (source, target) in enumerate(zip(sources, buffers))
@@ -145,8 +150,8 @@
         copy.start()
     for copy in copies:
         copy.wait()
-    px_no = places[0]
-    py_no = places[1]
+    px_no = lax.axis_index("px")
+    py_no = lax.axis_index("py")
     own_count = coords_in.shape[1]
     rows = own_count // LANES
     spread_rows(disp_in, disp, 3)
@@ -197,20 +202,28 @@
     nodes[...] = block_remap(nodes[...], own_count, width, px_no, py_no, *counts)
     spread_rows(vel_in, vel, 3)
     spread_rows(ext_in, ext, 3)
-
-
-def element_kernel(later, *refs):
-    if later:
-        (disp, recv0, recv1, recv2, recv3, nodes, thick, stiff, held, slow) = refs[:10]
-        (own, out0, out1, out2, out3) = refs[10:]
-    else:
-        (disp, recv0, recv1, recv2, recv3, nodes, thick, stiff, pairs, arrived) = refs[:10]
-        (own, out0, out1, out2, out3, held, pushes) = refs[10:]
-        contact_tiles(pairs, arrived, pushes)
+    size = stiff.shape[0]
+    for j in range(size):
+        splat[j * size : (j + 1) * size, :] = jnp.broadcast_to(stiff[:, j : j + 1], (size, LANES))
+    for h in range(slow.shape[0]):
+        slow[h : h + 1, :] = jnp.full((1, LANES), classes[h])
+    tile_no = lax.broadcasted_iota(I32, (slot_rows, LANES), 0)
+    short = LANES - pairs.shape[1]
+    onehots = []
+    for side in range(2):
+        row = pairs[side : side + 1, :]
+        if short:
+            row = jnp.concatenate([row, jnp.full((1, short), -1)], axis=1)
+        onehots.append((tile_no == row).astype(F32))
+    onehots.append(jnp.zeros((LANES - 2 * slot_rows, LANES), F32))
+    onehots = jnp.concatenate(onehots, axis=0)
+    select[0] = onehots
+    select[1] = jnp.transpose(onehots)
+
+
+def corner_forces(disp, recvs, nodes, thick, splat):
     rows = disp.shape[0] // 3
-    quarter = recv0.shape[0] // 3
-    recvs = (recv0, recv1, recv2, recv3)
-    outs = (out0, out1, out2, out3)
+    quarter = recvs[0].shape[0] // 3
     elem_rows = thick.shape[0]
 
     def table_row(c, h):
@@ -219,32 +232,27 @@
         b, q = divmod(h - rows, quarter)
         return recvs[b][c * quarter + q : c * quarter + q + 1, :]
 
-    extended = rows + 4 * quarter
-    corners = []
-    for k in range(4):
-        corners.append(
-            lookup(table_row, extended, nodes[k * elem_rows : (k + 1) * elem_rows, :])
-        )
+    corners = [
+        lookup(table_row, rows + 4 * quarter, nodes[k * elem_rows : (k + 1) * elem_rows, :])
+        for k in range(4)
+    ]
     factor = thick[...]
     forces = []
     for i in range(12):
         total = None
         for j in range(12):
-            term = stiff[i, j] * corners[j % 4][j // 4]
+            term = splat[j * 12 + i : j * 12 + i + 1, :] * corners[j % 4][j // 4]
             total = term if total is None else total + term
-        total = factor * total
-        span = slice(i * elem_rows, (i + 1) * elem_rows)
-        if later:
-            total = jnp.where(slow[...] == 1, held[span, :], total)
-        else:
-            held[span, :] = total
-        forces.append(total)
-
-    def value_row(c, r):
-        k, h = divmod(r, elem_rows)
-        return forces[c * 4 + k][h : h + 1, :]
-
-    sums = scatter_add(lambda r: nodes[r : r + 1, :], value_row, 4 * elem_rows, extended)
+        forces.append(factor * total)
+    return forces
+
+
+def assemble(force_row, nodes, own, outs):
+    rows = own.shape[0] // 3
+    quarter = outs[0].shape[0] // 3
+    sums = scatter_add(
+        lambda r: nodes[r : r + 1, :], force_row, nodes.shape[0], rows + 4 * quarter
+    )
     for c in range(3):
         own[c * rows : (c + 1) * rows, :] = sums[c][:rows]
         for b in range(4):
@@ -252,32 +260,97 @@
             outs[b][c * quarter : (c + 1) * quarter, :] = sums[c][start : start + quarter]
 
 
-def contact_tiles(pairs, arrived, pushes):
-    pushes[...] = jnp.zeros(pushes.shape, F32)
-    empty = jnp.zeros((5, LANES), F32)
-    for start in range(0, pairs.shape[1], LANES // 8):
-        stop = min(start + LANES // 8, pairs.shape[1])
-        others = []
+def force_kernel(disp, recv0, recv1, recv2, recv3, nodes, thick, splat, held):
+    elem_rows = thick.shape[0]
+    forces = corner_forces(disp, (recv0, recv1, recv2, recv3), nodes, thick, splat)
+    for i in range(12):
+        held[i * elem_rows : (i + 1) * elem_rows, :] = forces[i]
+
+
+def assemble_kernel(held, nodes, after, own, out0, out1, out2, out3):
+    count = nodes.shape[0]
+    assemble(
+        lambda c, r: held[c * count + r : c * count + r + 1, :], nodes, own, (out0, out1, out2, out3)
+    )
+
+
+def later_kernel(
+    disp,
+    recv0,
+    recv1,
+    recv2,
+    recv3,
+    nodes,
+    thick,
+    splat,
+    held,
+    slow,
+    own,
+    out0,
+    out1,
+    out2,
+    out3,
+):
+    elem_rows = thick.shape[0]
+    forces = corner_forces(disp, (recv0, recv1, recv2, recv3), nodes, thick, splat)
+    kept = slow[...] == 1
+    forces = [
+        jnp.where(kept, held[i * elem_rows : (i + 1) * elem_rows, :], forces[i])
+        for i in range(12)
+    ]
+
+    def force_row(c, r):
+        k, h = divmod(r, elem_rows)
+        return forces[c * 4 + k][h : h + 1, :]
+
+    assemble(force_row, nodes, own, (out0, out1, out2, out3))
+
+
+def contact_kernel(pair_count, select, arrived, after, pushes):
+    tiles = arrived.shape[0]
+    points = jnp.concatenate([arrived[:, c, :] for c in range(3)], axis=1)
+    picked = []
+    for side in range(2):
+        onehot = select[1, :pair_count, side * tiles : (side + 1) * tiles]
+        picked.append(
+            jnp.dot(onehot, points, preferred_element_type=F32, precision=lax.Precision.HIGHEST)
+        )
+    first, second = picked
+    group = LANES // 4
+    pushed = []
+    for start in range(0, pair_count, group):
+        stop = min(start + group, pair_count)
+        block = jnp.concatenate(
+            [second[start:stop, c * LANES : (c + 1) * LANES] for c in range(3)]
+            + [jnp.zeros((LANES - 3 * (stop - start), LANES), F32)],
+            axis=0,
+        )
+        turned = jnp.transpose(block)
         for p in range(start, stop):
-            others += [arrived[pairs[1, p]], empty]
-        if stop - start < LANES // 8:
-            others.append(jnp.zeros((LANES - 8 * (stop - start), LANES), F32))
-        turned = jnp.transpose(jnp.concatenate(others, axis=0))
-        for p in range(start, stop):
-            a = pairs[0, p]
-            pos_a = arrived[a]
-            column = 8 * (p - start)
-            gaps = [
-                jnp.broadcast_to(pos_a[c : c + 1, :], (LANES, LANES))
-                - jnp.broadcast_to(turned[:, column + c : column + c + 1], (LANES, LANES))
-                for c in range(3)
-            ]
+            gaps = []
+            for c in range(3):
+                column = c * (stop - start) + p - start
+                gaps.append(
+                    jnp.broadcast_to(
+                        first[p : p + 1, c * LANES : (c + 1) * LANES], (LANES, LANES)
+                    )
+                    - jnp.broadcast_to(turned[:, column : column + 1], (LANES, LANES))
+                )
             dist = gaps[0] * gaps[0] + gaps[1] * gaps[1] + gaps[2] * gaps[2]
             weight = jnp.exp(dist * (-1.0 / REACH))
-            push = jnp.concatenate(
-                [jnp.sum(weight * gaps[c], axis=0, keepdims=True) for c in range(3)], axis=0
+            pushed.append(
+                jnp.concatenate(
+                    [jnp.sum(weight * gaps[c], axis=0, keepdims=True) for c in range(3)], axis=1
+                )
             )
-            pushes[a] = pushes[a] + PENALTY * push
+    total = PENALTY * jnp.dot(
+        select[0, :tiles, :pair_count],
+        jnp.concatenate(pushed, axis=0),
+        preferred_element_type=F32,
+        precision=lax.Precision.HIGHEST,
+    )
+    for c in range(3):
+        pushes[:, c, :] = total[:, c * LANES : (c + 1) * LANES]
 
 
 def update_kernel(first, last, final, *refs):
@@ -342,10 +415,10 @@
     return jax.ShapeDtypeStruct(dims, F32)
 
 
-def call(kernel, inputs, outputs, name, smem=(), far=(), scratch=()):
+def call(kernel, inputs, outputs, name, smem=(), far=(), scratch=(), vmem_bytes=VMEM_BYTES):
     specs = [
         pl.BlockSpec(
-            memory_space=pltpu.SMEM if i in smem else pltpu.HBM if i in far else pltpu.VMEM
+            memory_space=pltpu.SMEM if i in smem else pl.ANY if i in far else pltpu.VMEM
         )
         for i in range(len(inputs))
     ]
@@ -355,7 +428,7 @@
         in_specs=specs,
         out_specs=tuple(vmem(len(outputs))),
         scratch_shapes=list(scratch),
-        compiler_params=pltpu.CompilerParams(vmem_limit_bytes=VMEM_BYTES),
+        compiler_params=pltpu.CompilerParams(vmem_limit_bytes=vmem_bytes),
         name=name,
     )(*inputs)
 
@@ -417,12 +490,10 @@
     slot_rows = devices * capacity // LANES
     inv_mass = inv_mass.reshape(rows, LANES)
     thickness = thickness.reshape(elem_rows, LANES)
-    slow = jnp.broadcast_to(block_class[:, None], (elem_rows, LANES))
     nodal = shape(3 * rows, LANES)
     sent = [shape(3 * quarter, LANES)] * 4
     slots = shape(slot_rows, 3, LANES)
 
-    places = jnp.stack([lax.axis_index("px"), lax.axis_index("py")]).astype(I32)
     sources = [
         coords,
         displacement,
@@ -432,25 +503,34 @@
         halo_lists,
         contact_bucket.reshape(-1, LANES),
         contact_nodes.reshape(-1, LANES),
+        stiffness,
+        block_class,
+        tile_pairs,
     ]
-    coords, disp, vel, ext, nodes, lists, inverse, outgoing, *sends = call(
+    memories = [pltpu.SMEM if source is block_class else pltpu.VMEM for source in sources]
+    coords, disp, vel, ext, nodes, lists, inverse, outgoing, splat, slow, select, *sends = call(
         functools.partial(
             setup_kernel, devices, capacity, (lax.axis_size("px"), lax.axis_size("py"))
         ),
-        [places] + sources,
+        sources,
         [nodal] * 4
         + [
             jax.ShapeDtypeStruct((4 * elem_rows, LANES), I32),
             jax.ShapeDtypeStruct((4 * quarter, LANES), I32),
             jax.ShapeDtypeStruct((slot_rows, LANES), I32),
             slots,
+            shape(144, LANES),
+            jax.ShapeDtypeStruct((elem_rows, LANES), I32),
+            shape(2, LANES, LANES),
         ]
         + sent,
         "setup",
-        smem=(0,),
-        far=range(1, 9),
-        scratch=[pltpu.VMEM(source.shape, source.dtype) for source in sources]
+        far=range(len(sources)),
+        scratch=[
+            memory(source.shape, source.dtype) for memory, source in zip(memories, sources)
+        ]
         + [pltpu.SemaphoreType.DMA((len(sources),))],
+        vmem_bytes=WHOLE_VMEM,
     )
     for step_no in range(STEPS):
         for sub_no in range(SUBS):
@@ -460,23 +540,25 @@
             if first:
                 arrived = swap(outgoing, devices, capacity)
             recvs = exchange(sends)
+            field = [disp, *recvs, nodes, thickness, splat]
             if first:
+                (held,) = call(
+                    force_kernel, field, [shape(12 * elem_rows, LANES)], "forces"
+                )
+                (pushes,) = call(
+                    functools.partial(contact_kernel, tile_pairs.shape[1]),
+                    [select, arrived, held],
+                    [slots],
+                    "contact",
+                    far=(2,),
+                )
+                returned = swap(pushes, devices, capacity)
                 own, *rest = call(
-                    functools.partial(element_kernel, False),
-                    [disp, *recvs, nodes, thickness, stiffness, tile_pairs, arrived],
-                    [nodal] + sent + [shape(12 * elem_rows, LANES), slots],
-                    "elements",
-                    smem=(7, 8),
+                    assemble_kernel, [held, nodes, pushes], [nodal] + sent, "assemble", far=(2,)
                 )
-                held, pushes = rest[4:]
-                returned = swap(pushes, devices, capacity)
             else:
                 own, *rest = call(
-                    functools.partial(element_kernel, True),
-                    [disp, *recvs, nodes, thickness, stiffness, held, slow],
-                    [nodal] + sent,
-                    "elements_later",
-                    smem=(7,),
+                    later_kernel, field + [held, slow], [nodal] + sent, "forces_assemble"
                 )
             backs = exchange(rest[:4])
             inputs = [own, *backs]

time: 101 us -> 90.4 us (0.90)
  local copies, waits for them, and re-layouts: 6.52 us -> 0.06 us
  waiting for transfers between devices: 23.6 us -> 19 us
  starting transfers between devices: 46.8 us -> 50.7 us
  Pallas kernels: 21.9 us -> 19.2 us
    unnamed x26, local copies, waits for them, and re-layouts: 6.45 us -> 0.06 us
    all_to_all x4, waiting for transfers between devices: 7.87 us -> 3.84 us  [swap(): return lax.all_to_all(slots, axes, 0, 0, tiled=True)]
    pallas_call x9 -> x13, Pallas kernels: 21.9 us -> 19.2 us  [call(): pl.pallas_call(kernel, out_shape=tuple(outputs), in_specs=specs, out_spec...]
    all_to_all x4, starting transfers between devices: 19.6 us -> 21.8 us  [swap(): return lax.all_to_all(slots, axes, 0, 0, tiled=True)]
    ppermute x32, starting transfers between devices: 27.1 us -> 28.8 us  [exchange(): lax.ppermute(block, ('px', 'py'), pairs)]
  transfers between devices with their start and end apart: 36 -> 36, of which waited for: 18 -> 18; matrix products, arithmetic and copies ran while one was open for 0% -> 0% of each run, Pallas kernels for 0% -> 4%
where the time goes in v3:
time: 90.4 us; the launch traced here: 89.8 us
  starting transfers between devices  50.7 us (56%)
  Pallas kernels  19.2 us (21%)
  waiting for transfers between devices  19 us (21%)
  between operations  0.91 us (1%)
    ppermute x32, starting transfers between devices, exchange(): lax.ppermute(block, ('px', 'py'), pairs)  28.8 us
    all_to_all x4, starting transfers between devices, swap(): return lax.all_to_all(slots, axes, 0, 0, tiled=True)  21.8 us
    pallas_call x13, Pallas kernels, call(): pl.pallas_call(kernel, out_shape=tuple(outputs), in_specs=specs, out_spec...  19.2 us
    ppermute x32, waiting for transfers between devices, exchange(): lax.ppermute(block, ('px', 'py'), pairs)  15.1 us
    all_to_all x4, waiting for transfers between devices, swap(): return lax.all_to_all(slots, axes, 0, 0, tiled=True)  3.84 us
  transfers between devices with their start and end apart: 36, of which 18 were waited for; matrix products, arithmetic and copies ran while one was open for 0% of the time, Pallas kernels for 4%

profile of v3, /device:TPU:0, one launch (start us, length us, event | category | flops | bytes accessed | tf_op | source)
XLA Modules:
  0.0 89.8 jit_solution(14227931185483939953)
XLA Ops:
  0.6 2.6 %setup.1 = (f32[48,128]{1,0:T(8,128)}, f32[48,128]{1,0:T(8,128)}, f32[48,128]{1,0:T(8,128)}, f32[48,128]{1,0:T(8,128)}, s32[64,128]{1,0:T(8,128)}, /*index=5*/s3...) custom-call(f32[3,2048]{1,0:T(4,128)} %refs_0_.1, ...), custom_call_target="tpu_custom_call" | custom-call | tf_op jit(solution)/shard_map/setup/pallas_call | solution.py:425
  3.2 7.3 %all-to-all-start = ((f32[32,3,128]{2,1,0:T(4,128)}), f32[32,3,128]{2,1,0:T(4,128)S(1)}, u32[]{:S(2)}, u32[]{:S(2)}) async-start(f32[32,3,128]{2,1,0:T(4,128)} %get-tuple-element.68), calls=%async_computation | async-start | bytes 131072 | tf_op jit(solution)/shard_map/all_to_all | solution.py:459
  10.6 1.8 %collective-permute-start = (f32[12,128]{1,0:T(8,128)}, f32[12,128]{1,0:T(8,128)S(1)}, u32[]{:S(2)}, u32[]{:S(2)}) collective-permute-start(f32[12,128]{1,0:T(8,128)} %get-tuple-element.61), channel_id=1, source_target_pairs={{0,4},{1,5},{2,6},{3,7},{4,0},{5,1},{6,2},{7,3},{8,12},{9,13},{10,... | collective-permute-start | bytes 18440 | tf_op jit(solution)/shard_map/ppermute | solution.py:453
  14.5 1.5 %collective-permute-done.3.recv3 = f32[12,128]{1,0:T(8,128)S(1)} collective-permute-done((f32[12,128]{1,0:T(8,128)S(1)}, f32[12,128]{1,0:T(8,128)S(1)}, u32[]{:S(2)}, u32[]{:S(2)}) %collective-permute-start.3) | collective-permute-done | bytes 6176 | tf_op jit(solution)/shard_map/ppermute | solution.py:453
  18.0 2.2 %contact.2.after = f32[32,3,128]{2,1,0:T(4,128)} custom-call(f32[2,128,128]{2,1,0:T(8,128)S(1)} %copy-done.2, f32[32,3,128]{2,1,0:T(4,128)S(1)} %all-to-all-done.arrived, f32[192,128]{1,0:T(8,128)S(1)} %forces.2.after.held), custom_call_target="tpu_custom_call" | custom-call | tf_op jit(solution)/shard_map/contact/pallas_call | solution.py:425
  20.2 4.9 %all-to-all-start.1 = ((f32[32,3,128]{2,1,0:T(4,128)}), f32[32,3,128]{2,1,0:T(4,128)S(1)}, u32[]{:S(2)}, u32[]{:S(2)}) async-start(f32[32,3,128]{2,1,0:T(4,128)} %contact.2.after), calls=%async_computation.1 | async-start | bytes 131072 | tf_op jit(solution)/shard_map/all_to_all | solution.py:459
  26.1 1.8 %collective-permute-start.4 = (f32[12,128]{1,0:T(8,128)S(1)}, f32[12,128]{1,0:T(8,128)S(1)}, u32[]{:S(2)}, u32[]{:S(2)}) collective-permute-start(f32[12,128]{1,0:T(8,128)S(1)} %get-tuple-element.70), channel_id=1, source_target_pairs={{0,4},{1,5},{2,6},{3,7},{4,0},{5,1},{6,2},{7,3},{8,12},{9,13},{10,... | collective-permute-start | bytes 18440 | tf_op jit(solution)/shard_map/ppermute | solution.py:453
  29.8 1.7 %collective-permute-done.7.refs_4_ = f32[12,128]{1,0:T(8,128)S(1)} collective-permute-done((f32[12,128]{1,0:T(8,128)S(1)}, f32[12,128]{1,0:T(8,128)S(1)}, u32[]{:S(2)}, u32[]{:S(2)}) %collective-permute-start.7) | collective-permute-done | bytes 6176 | tf_op jit(solution)/shard_map/ppermute | solution.py:453
  33.2 1.6 %collective-permute-start.8 = (f32[12,128]{1,0:T(8,128)S(1)}, f32[12,128]{1,0:T(8,128)S(1)}, u32[]{:S(2)}, u32[]{:S(2)}) collective-permute-start(f32[12,128]{1,0:T(8,128)S(1)} %get-tuple-element.79), channel_id=1, source_target_pairs={{0,4},{1,5},{2,6},{3,7},{4,0},{5,1},{6,2},{7,3},{8,12},{9,13},{10,... | collective-permute-start | bytes 18440 | tf_op jit(solution)/shard_map/ppermute | solution.py:453
  37.0 1.4 %collective-permute-done.11.recv3 = f32[12,128]{1,0:T(8,128)S(1)} collective-permute-done((f32[12,128]{1,0:T(8,128)S(1)}, f32[12,128]{1,0:T(8,128)S(1)}, u32[]{:S(2)}, u32[]{:S(2)}) %collective-permute-start.11) | collective-permute-done | bytes 6176 | tf_op jit(solution)/shard_map/ppermute | solution.py:453
  38.4 2.2 %forces_assemble.2 = (f32[48,128]{1,0:T(8,128)S(1)}, f32[12,128]{1,0:T(8,128)S(1)}, f32[12,128]{1,0:T(8,128)S(1)}, f32[12,128]{1,0:T(8,128)S(1)}, f32[12,128]{1,0:T(8,128)S(1)}) custom-call(f32[48,128]{1,0:T(8,128)S(1)} %get-tuple-element.78.disp.refs_9_, f32[12,128]{1,0:T(8,128)S(1)} %collective-permute-done.8.recv0, ...), custom_call_target="tpu_custom_call" | custom-call | tf_op jit(solution)/shard_map/forces_assemble/pallas_call | solution.py:425
  40.6 2.5 %collective-permute-start.12 = (f32[12,128]{1,0:T(8,128)S(1)}, f32[12,128]{1,0:T(8,128)S(1)}, u32[]{:S(2)}, u32[]{:S(2)}) collective-permute-start(f32[12,128]{1,0:T(8,128)S(1)} %get-tuple-element.85), channel_id=1, source_target_pairs={{0,4},{1,5},{2,6},{3,7},{4,0},{5,1},{6,2},{7,3},{8,12},{9,13},{10,... | collective-permute-start | bytes 18440 | tf_op jit(solution)/shard_map/ppermute | solution.py:453
  45.0 1.7 %collective-permute-done.15.refs_4_ = f32[12,128]{1,0:T(8,128)S(1)} collective-permute-done((f32[12,128]{1,0:T(8,128)S(1)}, f32[12,128]{1,0:T(8,128)S(1)}, u32[]{:S(2)}, u32[]{:S(2)}) %collective-permute-start.15) | collective-permute-done | bytes 6176 | tf_op jit(solution)/shard_map/ppermute | solution.py:453
  48.1 4.8 %all-to-all-start.2 = ((f32[32,3,128]{2,1,0:T(4,128)}), f32[32,3,128]{2,1,0:T(4,128)S(1)}, u32[]{:S(2)}, u32[]{:S(2)}) async-start(f32[32,3,128]{2,1,0:T(4,128)} %get-tuple-element.97), calls=%async_computation.2 | async-start | bytes 131072 | tf_op jit(solution)/shard_map/all_to_all | solution.py:459
  52.9 1.8 %collective-permute-start.16 = (f32[12,128]{1,0:T(8,128)S(1)}, f32[12,128]{1,0:T(8,128)S(1)}, u32[]{:S(2)}, u32[]{:S(2)}) collective-permute-start(f32[12,128]{1,0:T(8,128)S(1)} %get-tuple-element.93), channel_id=1, source_target_pairs={{0,4},{1,5},{2,6},{3,7},{4,0},{5,1},{6,2},{7,3},{8,12},{9,13},{10,... | collective-permute-start | bytes 18440 | tf_op jit(solution)/shard_map/ppermute | solution.py:453
  56.7 1.7 %collective-permute-done.19.recv3 = f32[12,128]{1,0:T(8,128)S(1)} collective-permute-done((f32[12,128]{1,0:T(8,128)S(1)}, f32[12,128]{1,0:T(8,128)S(1)}, u32[]{:S(2)}, u32[]{:S(2)}) %collective-permute-start.19) | collective-permute-done | bytes 6176 | tf_op jit(solution)/shard_map/ppermute | solution.py:453
  60.3 2.2 %contact.3.after = f32[32,3,128]{2,1,0:T(4,128)} custom-call(f32[2,128,128]{2,1,0:T(8,128)S(1)} %copy-done.2, f32[32,3,128]{2,1,0:T(4,128)S(1)} %all-to-all-done.2.arrived, f32[192,128]{1,0:T(8,128)S(1)} %forces.3.after.held), custom_call_target="tpu_custom_call" | custom-call | tf_op jit(solution)/shard_map/contact/pallas_call | solution.py:425
  62.5 4.9 %all-to-all-start.3 = ((f32[32,3,128]{2,1,0:T(4,128)}), f32[32,3,128]{2,1,0:T(4,128)S(1)}, u32[]{:S(2)}, u32[]{:S(2)}) async-start(f32[32,3,128]{2,1,0:T(4,128)} %contact.3.after), calls=%async_computation.3 | async-start | bytes 131072 | tf_op jit(solution)/shard_map/all_to_all | solution.py:459
  68.4 1.7 %collective-permute-start.20 = (f32[12,128]{1,0:T(8,128)S(1)}, f32[12,128]{1,0:T(8,128)S(1)}, u32[]{:S(2)}, u32[]{:S(2)}) collective-permute-start(f32[12,128]{1,0:T(8,128)S(1)} %get-tuple-element.99), channel_id=1, source_target_pairs={{0,4},{1,5},{2,6},{3,7},{4,0},{5,1},{6,2},{7,3},{8,12},{9,13},{10,... | collective-permute-start | bytes 18440 | tf_op jit(solution)/shard_map/ppermute | solution.py:453
  72.1 1.5 %collective-permute-done.23.refs_4_ = f32[12,128]{1,0:T(8,128)S(1)} collective-permute-done((f32[12,128]{1,0:T(8,128)S(1)}, f32[12,128]{1,0:T(8,128)S(1)}, u32[]{:S(2)}, u32[]{:S(2)}) %collective-permute-start.23) | collective-permute-done | bytes 6176 | tf_op jit(solution)/shard_map/ppermute | solution.py:453
  75.4 1.5 %collective-permute-start.24 = (f32[12,128]{1,0:T(8,128)S(1)}, f32[12,128]{1,0:T(8,128)S(1)}, u32[]{:S(2)}, u32[]{:S(2)}) collective-permute-start(f32[12,128]{1,0:T(8,128)S(1)} %get-tuple-element.105), channel_id=1, source_target_pairs={{0,4},{1,5},{2,6},{3,7},{4,0},{5,1},{6,2},{7,3},{8,12},{9,13},{10,... | collective-permute-start | bytes 18440 | tf_op jit(solution)/shard_map/ppermute | solution.py:453
  80.5 2.2 %forces_assemble.3 = (f32[48,128]{1,0:T(8,128)S(1)}, f32[12,128]{1,0:T(8,128)S(1)}, f32[12,128]{1,0:T(8,128)S(1)}, f32[12,128]{1,0:T(8,128)S(1)}, f32[12,128]{1,0:T(8,128)S(1)}) custom-call(f32[48,128]{1,0:T(8,128)S(1)} %get-tuple-element.104.disp.refs_9_, f32[12,128]{1,0:T(8,128)S(1)} %collective-permute-done.24.recv0, ...), custom_call_target="tpu_custom_call" | custom-call | tf_op jit(solution)/shard_map/forces_assemble/pallas_call | solution.py:425
  82.8 2.5 %collective-permute-start.28 = (f32[12,128]{1,0:T(8,128)S(1)}, f32[12,128]{1,0:T(8,128)S(1)}, u32[]{:S(2)}, u32[]{:S(2)}) collective-permute-start(f32[12,128]{1,0:T(8,128)S(1)} %get-tuple-element.110), channel_id=1, source_target_pairs={{0,4},{1,5},{2,6},{3,7},{4,0},{5,1},{6,2},{7,3},{8,12},{9,13},{10,... | collective-permute-start | bytes 18440 | tf_op jit(solution)/shard_map/ppermute | solution.py:453
  87.1 1.7 %collective-permute-done.31.refs_4_ = f32[12,128]{1,0:T(8,128)S(1)} collective-permute-done((f32[12,128]{1,0:T(8,128)S(1)}, f32[12,128]{1,0:T(8,128)S(1)}, u32[]{:S(2)}, u32[]{:S(2)}) %collective-permute-start.31) | collective-permute-done | bytes 6176 | tf_op jit(solution)/shard_map/ppermute | solution.py:453
  (87 shorter events, 29.0 us)
Async XLA Ops:
  3.2 14.7 %all-to-all-start = ((f32[32,3,128]{2,1,0:T(4,128)}), f32[32,3,128]{2,1,0:T(4,128)S(1)}, u32[]{:S(2)}, u32[]{:S(2)}) async-start(f32[32,3,128]{2,1,0:T(4,128)} %get-tuple-element.68), calls=%async_computation | async-start | bytes 131072 | tf_op jit(solution)/shard_map/all_to_all | solution.py:459
  10.6 3.9 %collective-permute-start = (f32[12,128]{1,0:T(8,128)}, f32[12,128]{1,0:T(8,128)S(1)}, u32[]{:S(2)}, u32[]{:S(2)}) collective-permute-start(f32[12,128]{1,0:T(8,128)} %get-tuple-element.61), channel_id=1, source_target_pairs={{0,4},{1,5},{2,6},{3,7},{4,0},{5,1},{6,2},{7,3},{8,12},{9,13},{10,... | collective-permute-start | bytes 18440 | tf_op jit(solution)/shard_map/ppermute | solution.py:453
  12.4 2.1 %collective-permute-start.1 = (f32[12,128]{1,0:T(8,128)}, f32[12,128]{1,0:T(8,128)S(1)}, u32[]{:S(2)}, u32[]{:S(2)}) collective-permute-start(f32[12,128]{1,0:T(8,128)} %get-tuple-element.62), channel_id=1, source_target_pairs={{0,1},{1,0},{2,3},{3,2},{4,8},{5,9},{6,10},{7,11},{8,4},{9,5},{10,... | collective-permute-start | bytes 18440 | tf_op jit(solution)/shard_map/ppermute | solution.py:453
  12.4 2.1 %collective-permute-start.2 = (f32[12,128]{1,0:T(8,128)}, f32[12,128]{1,0:T(8,128)S(1)}, u32[]{:S(2)}, u32[]{:S(2)}) collective-permute-start(f32[12,128]{1,0:T(8,128)} %get-tuple-element.63), channel_id=1, source_target_pairs={{0,1},{1,0},{2,3},{3,2},{4,5},{5,4},{6,7},{7,6},{8,9},{9,8},{10,11... | collective-permute-start | bytes 18440 | tf_op jit(solution)/shard_map/ppermute | solution.py:453
  12.9 3.1 %collective-permute-start.3 = (f32[12,128]{1,0:T(8,128)S(1)}, f32[12,128]{1,0:T(8,128)S(1)}, u32[]{:S(2)}, u32[]{:S(2)}) collective-permute-start(f32[12,128]{1,0:T(8,128)S(1)} %copy-done.12), channel_id=1, source_target_pairs={{0,3},{1,2},{2,1},{3,0},{4,7},{5,6},{6,5},{7,4},{8,11},{9,10},{10,... | collective-permute-start | bytes 18440 | tf_op jit(solution)/shard_map/ppermute | solution.py:453
  20.2 12.3 %all-to-all-start.1 = ((f32[32,3,128]{2,1,0:T(4,128)}), f32[32,3,128]{2,1,0:T(4,128)S(1)}, u32[]{:S(2)}, u32[]{:S(2)}) async-start(f32[32,3,128]{2,1,0:T(4,128)} %contact.2.after), calls=%async_computation.1 | async-start | bytes 131072 | tf_op jit(solution)/shard_map/all_to_all | solution.py:459
  26.1 3.7 %collective-permute-start.4 = (f32[12,128]{1,0:T(8,128)S(1)}, f32[12,128]{1,0:T(8,128)S(1)}, u32[]{:S(2)}, u32[]{:S(2)}) collective-permute-start(f32[12,128]{1,0:T(8,128)S(1)} %get-tuple-element.70), channel_id=1, source_target_pairs={{0,4},{1,5},{2,6},{3,7},{4,0},{5,1},{6,2},{7,3},{8,12},{9,13},{10,... | collective-permute-start | bytes 18440 | tf_op jit(solution)/shard_map/ppermute | solution.py:453
  28.4 3.1 %collective-permute-start.7 = (f32[12,128]{1,0:T(8,128)S(1)}, f32[12,128]{1,0:T(8,128)S(1)}, u32[]{:S(2)}, u32[]{:S(2)}) collective-permute-start(f32[12,128]{1,0:T(8,128)S(1)} %get-tuple-element.73), channel_id=1, source_target_pairs={{0,3},{1,2},{2,1},{3,0},{4,7},{5,6},{6,5},{7,4},{8,11},{9,10},{10,... | collective-permute-start | bytes 18440 | tf_op jit(solution)/shard_map/ppermute | solution.py:453
  33.2 3.7 %collective-permute-start.8 = (f32[12,128]{1,0:T(8,128)S(1)}, f32[12,128]{1,0:T(8,128)S(1)}, u32[]{:S(2)}, u32[]{:S(2)}) collective-permute-start(f32[12,128]{1,0:T(8,128)S(1)} %get-tuple-element.79), channel_id=1, source_target_pairs={{0,4},{1,5},{2,6},{3,7},{4,0},{5,1},{6,2},{7,3},{8,12},{9,13},{10,... | collective-permute-start | bytes 18440 | tf_op jit(solution)/shard_map/ppermute | solution.py:453
  34.8 2.1 %collective-permute-start.9 = (f32[12,128]{1,0:T(8,128)S(1)}, f32[12,128]{1,0:T(8,128)S(1)}, u32[]{:S(2)}, u32[]{:S(2)}) collective-permute-start(f32[12,128]{1,0:T(8,128)S(1)} %get-tuple-element.80), channel_id=1, source_target_pairs={{0,1},{1,0},{2,3},{3,2},{4,8},{5,9},{6,10},{7,11},{8,4},{9,5},{10,... | collective-permute-start | bytes 18440 | tf_op jit(solution)/shard_map/ppermute | solution.py:453
  35.3 3.1 %collective-permute-start.11 = (f32[12,128]{1,0:T(8,128)S(1)}, f32[12,128]{1,0:T(8,128)S(1)}, u32[]{:S(2)}, u32[]{:S(2)}) collective-permute-start(f32[12,128]{1,0:T(8,128)S(1)} %get-tuple-element.82), channel_id=1, source_target_pairs={{0,3},{1,2},{2,1},{3,0},{4,7},{5,6},{6,5},{7,4},{8,11},{9,10},{10,... | collective-permute-start | bytes 18440 | tf_op jit(solution)/shard_map/ppermute | solution.py:453
  40.6 4.3 %collective-permute-start.12 = (f32[12,128]{1,0:T(8,128)S(1)}, f32[12,128]{1,0:T(8,128)S(1)}, u32[]{:S(2)}, u32[]{:S(2)}) collective-permute-start(f32[12,128]{1,0:T(8,128)S(1)} %get-tuple-element.85), channel_id=1, source_target_pairs={{0,4},{1,5},{2,6},{3,7},{4,0},{5,1},{6,2},{7,3},{8,12},{9,13},{10,... | collective-permute-start | bytes 18440 | tf_op jit(solution)/shard_map/ppermute | solution.py:453
  43.6 3.1 %collective-permute-start.15 = (f32[12,128]{1,0:T(8,128)S(1)}, f32[12,128]{1,0:T(8,128)S(1)}, u32[]{:S(2)}, u32[]{:S(2)}) collective-permute-start(f32[12,128]{1,0:T(8,128)S(1)} %get-tuple-element.88), channel_id=1, source_target_pairs={{0,3},{1,2},{2,1},{3,0},{4,7},{5,6},{6,5},{7,4},{8,11},{9,10},{10,... | collective-permute-start | bytes 18440 | tf_op jit(solution)/shard_map/ppermute | solution.py:453
  48.1 12.2 %all-to-all-start.2 = ((f32[32,3,128]{2,1,0:T(4,128)}), f32[32,3,128]{2,1,0:T(4,128)S(1)}, u32[]{:S(2)}, u32[]{:S(2)}) async-start(f32[32,3,128]{2,1,0:T(4,128)} %get-tuple-element.97), calls=%async_computation.2 | async-start | bytes 131072 | tf_op jit(solution)/shard_map/all_to_all | solution.py:459
  52.9 3.7 %collective-permute-start.16 = (f32[12,128]{1,0:T(8,128)S(1)}, f32[12,128]{1,0:T(8,128)S(1)}, u32[]{:S(2)}, u32[]{:S(2)}) collective-permute-start(f32[12,128]{1,0:T(8,128)S(1)} %get-tuple-element.93), channel_id=1, source_target_pairs={{0,4},{1,5},{2,6},{3,7},{4,0},{5,1},{6,2},{7,3},{8,12},{9,13},{10,... | collective-permute-start | bytes 18440 | tf_op jit(solution)/shard_map/ppermute | solution.py:453
  55.3 3.1 %collective-permute-start.19 = (f32[12,128]{1,0:T(8,128)S(1)}, f32[12,128]{1,0:T(8,128)S(1)}, u32[]{:S(2)}, u32[]{:S(2)}) collective-permute-start(f32[12,128]{1,0:T(8,128)S(1)} %get-tuple-element.96), channel_id=1, source_target_pairs={{0,3},{1,2},{2,1},{3,0},{4,7},{5,6},{6,5},{7,4},{8,11},{9,10},{10,... | collective-permute-start | bytes 18440 | tf_op jit(solution)/shard_map/ppermute | solution.py:453
  62.5 12.1 %all-to-all-start.3 = ((f32[32,3,128]{2,1,0:T(4,128)}), f32[32,3,128]{2,1,0:T(4,128)S(1)}, u32[]{:S(2)}, u32[]{:S(2)}) async-start(f32[32,3,128]{2,1,0:T(4,128)} %contact.3.after), calls=%async_computation.3 | async-start | bytes 131072 | tf_op jit(solution)/shard_map/all_to_all | solution.py:459
  68.4 3.7 %collective-permute-start.20 = (f32[12,128]{1,0:T(8,128)S(1)}, f32[12,128]{1,0:T(8,128)S(1)}, u32[]{:S(2)}, u32[]{:S(2)}) collective-permute-start(f32[12,128]{1,0:T(8,128)S(1)} %get-tuple-element.99), channel_id=1, source_target_pairs={{0,4},{1,5},{2,6},{3,7},{4,0},{5,1},{6,2},{7,3},{8,12},{9,13},{10,... | collective-permute-start | bytes 18440 | tf_op jit(solution)/shard_map/ppermute | solution.py:453
  70.6 3.1 %collective-permute-start.23 = (f32[12,128]{1,0:T(8,128)S(1)}, f32[12,128]{1,0:T(8,128)S(1)}, u32[]{:S(2)}, u32[]{:S(2)}) collective-permute-start(f32[12,128]{1,0:T(8,128)S(1)} %get-tuple-element.102), channel_id=1, source_target_pairs={{0,3},{1,2},{2,1},{3,0},{4,7},{5,6},{6,5},{7,4},{8,11},{9,10},{10,... | collective-permute-start | bytes 18440 | tf_op jit(solution)/shard_map/ppermute | solution.py:453
  75.4 3.7 %collective-permute-start.24 = (f32[12,128]{1,0:T(8,128)S(1)}, f32[12,128]{1,0:T(8,128)S(1)}, u32[]{:S(2)}, u32[]{:S(2)}) collective-permute-start(f32[12,128]{1,0:T(8,128)S(1)} %get-tuple-element.105), channel_id=1, source_target_pairs={{0,4},{1,5},{2,6},{3,7},{4,0},{5,1},{6,2},{7,3},{8,12},{9,13},{10,... | collective-permute-start | bytes 18440 | tf_op jit(solution)/shard_map/ppermute | solution.py:453
  76.9 2.2 %collective-permute-start.25 = (f32[12,128]{1,0:T(8,128)S(1)}, f32[12,128]{1,0:T(8,128)S(1)}, u32[]{:S(2)}, u32[]{:S(2)}) collective-permute-start(f32[12,128]{1,0:T(8,128)S(1)} %get-tuple-element.106), channel_id=1, source_target_pairs={{0,1},{1,0},{2,3},{3,2},{4,8},{5,9},{6,10},{7,11},{8,4},{9,5},{10,... | collective-permute-start | bytes 18440 | tf_op jit(solution)/shard_map/ppermute | solution.py:453
  77.4 3.1 %collective-permute-start.27 = (f32[12,128]{1,0:T(8,128)S(1)}, f32[12,128]{1,0:T(8,128)S(1)}, u32[]{:S(2)}, u32[]{:S(2)}) collective-permute-start(f32[12,128]{1,0:T(8,128)S(1)} %get-tuple-element.108), channel_id=1, source_target_pairs={{0,3},{1,2},{2,1},{3,0},{4,7},{5,6},{6,5},{7,4},{8,11},{9,10},{10,... | collective-permute-start | bytes 18440 | tf_op jit(solution)/shard_map/ppermute | solution.py:453
  82.8 4.3 %collective-permute-start.28 = (f32[12,128]{1,0:T(8,128)S(1)}, f32[12,128]{1,0:T(8,128)S(1)}, u32[]{:S(2)}, u32[]{:S(2)}) collective-permute-start(f32[12,128]{1,0:T(8,128)S(1)} %get-tuple-element.110), channel_id=1, source_target_pairs={{0,4},{1,5},{2,6},{3,7},{4,0},{5,1},{6,2},{7,3},{8,12},{9,13},{10,... | collective-permute-start | bytes 18440 | tf_op jit(solution)/shard_map/ppermute | solution.py:453
  85.8 3.1 %collective-permute-start.31 = (f32[12,128]{1,0:T(8,128)S(1)}, f32[12,128]{1,0:T(8,128)S(1)}, u32[]{:S(2)}, u32[]{:S(2)}) collective-permute-start(f32[12,128]{1,0:T(8,128)S(1)} %get-tuple-element.113), channel_id=1, source_target_pairs={{0,3},{1,2},{2,1},{3,0},{4,7},{5,6},{6,5},{7,4},{8,11},{9,10},{10,... | collective-permute-start | bytes 18440 | tf_op jit(solution)/shard_map/ppermute | solution.py:453
  (25 other events, 127.5 us)

commit v4 on v3

--- a/solution.py
+++ b/solution.py
@@ -47,10 +47,9 @@
     return [top, values - top]
 
 
-def scatter_dot(hi_rows, lo_rows, value_rows, rows):
+def scatter_dot(hi_rows, lo_rows, value_rows, rows, total=None):
     row_no = lax.broadcasted_iota(I32, (rows, LANES), 0)
     lane_no = lax.broadcasted_iota(I32, (LANES, LANES), 0)
-    total = None
     group = 2
     for start in range(0, len(hi_rows), group):
         lefts, rights = [], []
@@ -76,21 +75,28 @@
     return total
 
 
-def scatter_add(index_row, value_row, count, rows):
+def scatter_some(index_row, value_row, numbers, rows, total=None):
     hi_rows, lo_rows = [], []
     value_rows = [[] for _ in range(6)]
-    for r in range(count):
+    for r in numbers:
         idx = index_row(r)
         hi_rows.append(idx >> 7)
         lo_rows.append(idx & (LANES - 1))
         for c in range(3):
             for part, vals in enumerate(halves(value_row(c, r))):
                 value_rows[2 * c + part].append(vals)
-    total = scatter_dot(hi_rows, lo_rows, value_rows, rows)
+    return scatter_dot(hi_rows, lo_rows, value_rows, rows, total)
+
+
+def add_halves(total, rows):
     return [
         total[2 * c * rows : (2 * c + 1) * rows] + total[(2 * c + 1) * rows : (2 * c + 2) * rows]
         for c in range(3)
     ]
+
+
+def scatter_add(index_row, value_row, count, rows):
+    return add_halves(scatter_some(index_row, value_row, range(count), rows), rows)
 
 
 def spread_rows(source, target, groups):
@@ -148,8 +154,8 @@
     ]
     for copy in copies:
         copy.start()
-    for copy in copies:
-        copy.wait()
+    copies[1].wait()
+    copies[5].wait()
     px_no = lax.axis_index("px")
     py_no = lax.axis_index("py")
     own_count = coords_in.shape[1]
@@ -174,6 +180,8 @@
                 jnp.full((1, LANES), missing) == 1, -1, chosen
             )
     gather_halo(disp, rows, lists, sends)
+    for n in (0, 6, 7):
+        copies[n].wait()
     spread_rows(coords_in, coords, 3)
     count = bucket.shape[0]
     slot_rows = inverse.shape[0]
@@ -198,6 +206,8 @@
     total = scatter_dot(hi_rows, lo_rows, digits, slot_rows)
     inverse[...] = (total[:slot_rows] * 64.0 + total[slot_rows:]).astype(I32) - 1
     gather_slots(coords, disp, rows, inverse, outgoing)
+    for n in (2, 3, 4, 8, 9, 10):
+        copies[n].wait()
     spread_rows(nodes_in, nodes, 4)
     nodes[...] = block_remap(nodes[...], own_count, width, px_no, py_no, *counts)
     spread_rows(vel_in, vel, 3)
@@ -207,24 +217,22 @@
         splat[j * size : (j + 1) * size, :] = jnp.broadcast_to(stiff[:, j : j + 1], (size, LANES))
     for h in range(slow.shape[0]):
         slow[h : h + 1, :] = jnp.full((1, LANES), classes[h])
-    tile_no = lax.broadcasted_iota(I32, (slot_rows, LANES), 0)
-    short = LANES - pairs.shape[1]
-    onehots = []
-    for side in range(2):
-        row = pairs[side : side + 1, :]
-        if short:
-            row = jnp.concatenate([row, jnp.full((1, short), -1)], axis=1)
-        onehots.append((tile_no == row).astype(F32))
-    onehots.append(jnp.zeros((LANES - 2 * slot_rows, LANES), F32))
-    onehots = jnp.concatenate(onehots, axis=0)
-    select[0] = onehots
-    select[1] = jnp.transpose(onehots)
-
-
-def corner_forces(disp, recvs, nodes, thick, splat):
+    ends = [pairs[0:1, :], pairs[1:2, :]]
+    short = LANES - 2 * pairs.shape[1]
+    if short:
+        ends.append(jnp.full((1, short), -1))
+    tile_no = lax.broadcasted_iota(I32, (LANES, LANES), 0)
+    onehot = (tile_no == jnp.concatenate(ends, axis=1)).astype(F32)
+    select[0] = onehot
+    select[1] = jnp.transpose(onehot)
+
+
+BLOCK = 8
+
+
+def corner_forces(disp, recvs, nodes, factor, splat, elem_rows, start):
     rows = disp.shape[0] // 3
     quarter = recvs[0].shape[0] // 3
-    elem_rows = thick.shape[0]
 
     def table_row(c, h):
         if h < rows:
@@ -232,11 +240,10 @@
         b, q = divmod(h - rows, quarter)
         return recvs[b][c * quarter + q : c * quarter + q + 1, :]
 
-    corners = [
-        lookup(table_row, rows + 4 * quarter, nodes[k * elem_rows : (k + 1) * elem_rows, :])
-        for k in range(4)
-    ]
-    factor = thick[...]
+    corners = []
+    for k in range(4):
+        first = k * elem_rows + start
+        corners.append(lookup(table_row, rows + 4 * quarter, nodes[first : first + BLOCK, :]))
     forces = []
     for i in range(12):
         total = None
@@ -247,12 +254,9 @@
     return forces
 
 
-def assemble(force_row, nodes, own, outs):
+def store_sums(sums, own, outs):
     rows = own.shape[0] // 3
     quarter = outs[0].shape[0] // 3
-    sums = scatter_add(
-        lambda r: nodes[r : r + 1, :], force_row, nodes.shape[0], rows + 4 * quarter
-    )
     for c in range(3):
         own[c * rows : (c + 1) * rows, :] = sums[c][:rows]
         for b in range(4):
@@ -262,16 +266,25 @@
 
 def force_kernel(disp, recv0, recv1, recv2, recv3, nodes, thick, splat, held):
     elem_rows = thick.shape[0]
-    forces = corner_forces(disp, (recv0, recv1, recv2, recv3), nodes, thick, splat)
-    for i in range(12):
-        held[i * elem_rows : (i + 1) * elem_rows, :] = forces[i]
+    recvs = (recv0, recv1, recv2, recv3)
+    for start in range(0, elem_rows, BLOCK):
+        factor = thick[start : start + BLOCK, :]
+        forces = corner_forces(disp, recvs, nodes, factor, splat, elem_rows, start)
+        for i in range(12):
+            first = i * elem_rows + start
+            held[first : first + BLOCK, :] = forces[i]
 
 
 def assemble_kernel(held, nodes, after, own, out0, out1, out2, out3):
     count = nodes.shape[0]
-    assemble(
-        lambda c, r: held[c * count + r : c * count + r + 1, :], nodes, own, (out0, out1, out2, out3)
+    outs = (out0, out1, out2, out3)
+    sums = scatter_add(
+        lambda r: nodes[r : r + 1, :],
+        lambda c, r: held[c * count + r : c * count + r + 1, :],
+        count,
+        (own.shape[0] + sum(out.shape[0] for out in outs)) // 3,
     )
+    store_sums(sums, own, outs)
 
 
 def later_kernel(
@@ -292,30 +305,49 @@
     out3,
 ):
     elem_rows = thick.shape[0]
-    forces = corner_forces(disp, (recv0, recv1, recv2, recv3), nodes, thick, splat)
-    kept = slow[...] == 1
-    forces = [
-        jnp.where(kept, held[i * elem_rows : (i + 1) * elem_rows, :], forces[i])
-        for i in range(12)
-    ]
-
-    def force_row(c, r):
-        k, h = divmod(r, elem_rows)
-        return forces[c * 4 + k][h : h + 1, :]
-
-    assemble(force_row, nodes, own, (out0, out1, out2, out3))
+    recvs = (recv0, recv1, recv2, recv3)
+    outs = (out0, out1, out2, out3)
+    extended = (own.shape[0] + sum(out.shape[0] for out in outs)) // 3
+    total = None
+    for start in range(0, elem_rows, BLOCK):
+        factor = thick[start : start + BLOCK, :]
+        forces = corner_forces(disp, recvs, nodes, factor, splat, elem_rows, start)
+        kept = slow[start : start + BLOCK, :] == 1
+        for i in range(12):
+            first = i * elem_rows + start
+            forces[i] = jnp.where(kept, held[first : first + BLOCK, :], forces[i])
+        total = scatter_some(
+            lambda r: nodes[r : r + 1, :],
+            lambda c, r: forces[c * 4 + r // elem_rows][
+                r % elem_rows - start : r % elem_rows - start + 1, :
+            ],
+            [k * elem_rows + h for k in range(4) for h in range(start, start + BLOCK)],
+            extended,
+            total,
+        )
+    store_sums(add_halves(total, extended), own, outs)
+
+
+def thirds(values):
+    parts = []
+    for _ in range(3):
+        top = values.astype(BF16)
+        parts.append(top)
+        values = values - top.astype(F32)
+    return jnp.concatenate(parts, axis=1)
+
+
+def dot_thirds(onehot, values):
+    width = values.shape[1]
+    sums = jnp.dot(onehot.astype(BF16), thirds(values), preferred_element_type=F32)
+    return sums[:, :width] + sums[:, width : 2 * width] + sums[:, 2 * width :]
 
 
 def contact_kernel(pair_count, select, arrived, after, pushes):
     tiles = arrived.shape[0]
     points = jnp.concatenate([arrived[:, c, :] for c in range(3)], axis=1)
-    picked = []
-    for side in range(2):
-        onehot = select[1, :pair_count, side * tiles : (side + 1) * tiles]
-        picked.append(
-            jnp.dot(onehot, points, preferred_element_type=F32, precision=lax.Precision.HIGHEST)
-        )
-    first, second = picked
+    picked = dot_thirds(select[1, : 2 * pair_count, :tiles], points)
+    first, second = picked[:pair_count], picked[pair_count:]
     group = LANES // 4
     pushed = []
     for start in range(0, pair_count, group):
@@ -343,12 +375,7 @@
                     [jnp.sum(weight * gaps[c], axis=0, keepdims=True) for c in range(3)], axis=1
                 )
             )
-    total = PENALTY * jnp.dot(
-        select[0, :tiles, :pair_count],
-        jnp.concatenate(pushed, axis=0),
-        preferred_element_type=F32,
-        precision=lax.Precision.HIGHEST,
-    )
+    total = PENALTY * dot_thirds(select[0, :tiles, :pair_count], jnp.concatenate(pushed, axis=0))
     for c in range(3):
         pushes[:, c, :] = total[:, c * LANES : (c + 1) * LANES]
 
@@ -450,7 +477,11 @@
 
 
 def exchange(blocks):
-    return [lax.ppermute(block, ("px", "py"), pairs) for block, pairs in zip(blocks, partners())]
+    swaps = partners()
+    arrived = [None] * 4
+    for n in (1, 3, 0, 2):
+        arrived[n] = lax.ppermute(blocks[n], ("px", "py"), swaps[n])
+    return arrived
 
 
 def swap(slots, devices, capacity):

time: 90.4 us -> 90.9 us (level)
  no operation moved by 1% of the time
where the time goes in v4:
time: 90.9 us; the launch traced here: 90.3 us
  starting transfers between devices  50.6 us (56%)
  Pallas kernels  19.7 us (22%)
  waiting for transfers between devices  19 us (21%)
  between operations  0.91 us (1%)
    ppermute x32, starting transfers between devices, exchange(): arrived[n] = lax.ppermute(blocks[n], ('px', 'py'), swaps[n])  28.8 us
    all_to_all x4, starting transfers between devices, swap(): return lax.all_to_all(slots, axes, 0, 0, tiled=True)  21.8 us
    pallas_call x13, Pallas kernels, call(): pl.pallas_call(kernel, out_shape=tuple(outputs), in_specs=specs, out_spec...  19.7 us
    ppermute x32, waiting for transfers between devices, exchange(): arrived[n] = lax.ppermute(blocks[n], ('px', 'py'), swaps[n])  15.1 us
    all_to_all x4, waiting for transfers between devices, swap(): return lax.all_to_all(slots, axes, 0, 0, tiled=True)  3.86 us
  transfers between devices with their start and end apart: 36, of which 18 were waited for; matrix products, arithmetic and copies ran while one was open for 0% of the time, Pallas kernels for 4%

profile of v4, /device:TPU:0, one launch (start us, length us, event | category | flops | bytes accessed | tf_op | source)
XLA Modules:
  0.0 90.3 jit_solution(14027314203123391059)
XLA Ops:
  0.6 2.8 %setup.1 = (f32[48,128]{1,0:T(8,128)}, f32[48,128]{1,0:T(8,128)}, f32[48,128]{1,0:T(8,128)}, f32[48,128]{1,0:T(8,128)}, s32[64,128]{1,0:T(8,128)}, /*index=5*/s3...) custom-call(f32[3,2048]{1,0:T(4,128)} %refs_0_.1, ...), custom_call_target="tpu_custom_call" | custom-call | tf_op jit(solution)/shard_map/setup/pallas_call | solution.py:452
  3.5 7.3 %all-to-all-start = ((f32[32,3,128]{2,1,0:T(4,128)}), f32[32,3,128]{2,1,0:T(4,128)S(1)}, u32[]{:S(2)}, u32[]{:S(2)}) async-start(f32[32,3,128]{2,1,0:T(4,128)} %get-tuple-element.68), calls=%async_computation | async-start | bytes 131072 | tf_op jit(solution)/shard_map/all_to_all | solution.py:490
  10.8 1.8 %collective-permute-start = (f32[12,128]{1,0:T(8,128)}, f32[12,128]{1,0:T(8,128)S(1)}, u32[]{:S(2)}, u32[]{:S(2)}) collective-permute-start(f32[12,128]{1,0:T(8,128)} %get-tuple-element.61), channel_id=1, source_target_pairs={{0,4},{1,5},{2,6},{3,7},{4,0},{5,1},{6,2},{7,3},{8,12},{9,13},{10,... | collective-permute-start | bytes 18440 | tf_op jit(solution)/shard_map/ppermute | solution.py:483
  14.7 1.5 %collective-permute-done.3.recv3 = f32[12,128]{1,0:T(8,128)S(1)} collective-permute-done((f32[12,128]{1,0:T(8,128)S(1)}, f32[12,128]{1,0:T(8,128)S(1)}, u32[]{:S(2)}, u32[]{:S(2)}) %collective-permute-start.3) | collective-permute-done | bytes 6176 | tf_op jit(solution)/shard_map/ppermute | solution.py:483
  18.2 2.1 %contact.2.after = f32[32,3,128]{2,1,0:T(4,128)} custom-call(f32[2,128,128]{2,1,0:T(8,128)S(1)} %copy-done.2, f32[32,3,128]{2,1,0:T(4,128)S(1)} %all-to-all-done.arrived, f32[192,128]{1,0:T(8,128)S(1)} %forces.2.after.held), custom_call_target="tpu_custom_call" | custom-call | tf_op jit(solution)/shard_map/contact/pallas_call | solution.py:452
  20.3 4.8 %all-to-all-start.1 = ((f32[32,3,128]{2,1,0:T(4,128)}), f32[32,3,128]{2,1,0:T(4,128)S(1)}, u32[]{:S(2)}, u32[]{:S(2)}) async-start(f32[32,3,128]{2,1,0:T(4,128)} %contact.2.after), calls=%async_computation.1 | async-start | bytes 131072 | tf_op jit(solution)/shard_map/all_to_all | solution.py:490
  26.2 1.8 %collective-permute-start.4 = (f32[12,128]{1,0:T(8,128)S(1)}, f32[12,128]{1,0:T(8,128)S(1)}, u32[]{:S(2)}, u32[]{:S(2)}) collective-permute-start(f32[12,128]{1,0:T(8,128)S(1)} %get-tuple-element.70), channel_id=1, source_target_pairs={{0,4},{1,5},{2,6},{3,7},{4,0},{5,1},{6,2},{7,3},{8,12},{9,13},{10,... | collective-permute-start | bytes 18440 | tf_op jit(solution)/shard_map/ppermute | solution.py:483
  30.0 1.7 %collective-permute-done.7.refs_4_ = f32[12,128]{1,0:T(8,128)S(1)} collective-permute-done((f32[12,128]{1,0:T(8,128)S(1)}, f32[12,128]{1,0:T(8,128)S(1)}, u32[]{:S(2)}, u32[]{:S(2)}) %collective-permute-start.7) | collective-permute-done | bytes 6176 | tf_op jit(solution)/shard_map/ppermute | solution.py:483
  33.4 1.6 %collective-permute-start.8 = (f32[12,128]{1,0:T(8,128)S(1)}, f32[12,128]{1,0:T(8,128)S(1)}, u32[]{:S(2)}, u32[]{:S(2)}) collective-permute-start(f32[12,128]{1,0:T(8,128)S(1)} %get-tuple-element.79), channel_id=1, source_target_pairs={{0,4},{1,5},{2,6},{3,7},{4,0},{5,1},{6,2},{7,3},{8,12},{9,13},{10,... | collective-permute-start | bytes 18440 | tf_op jit(solution)/shard_map/ppermute | solution.py:483
  37.1 1.4 %collective-permute-done.11.recv3 = f32[12,128]{1,0:T(8,128)S(1)} collective-permute-done((f32[12,128]{1,0:T(8,128)S(1)}, f32[12,128]{1,0:T(8,128)S(1)}, u32[]{:S(2)}, u32[]{:S(2)}) %collective-permute-start.11) | collective-permute-done | bytes 6176 | tf_op jit(solution)/shard_map/ppermute | solution.py:483
  38.6 2.4 %forces_assemble.2 = (f32[48,128]{1,0:T(8,128)S(1)}, f32[12,128]{1,0:T(8,128)S(1)}, f32[12,128]{1,0:T(8,128)S(1)}, f32[12,128]{1,0:T(8,128)S(1)}, f32[12,128]{1,0:T(8,128)S(1)}) custom-call(f32[48,128]{1,0:T(8,128)S(1)} %get-tuple-element.78.disp.refs_9_, f32[12,128]{1,0:T(8,128)S(1)} %collective-permute-done.8.recv0, ...), custom_call_target="tpu_custom_call" | custom-call | tf_op jit(solution)/shard_map/forces_assemble/pallas_call | solution.py:452
  41.0 2.5 %collective-permute-start.12 = (f32[12,128]{1,0:T(8,128)S(1)}, f32[12,128]{1,0:T(8,128)S(1)}, u32[]{:S(2)}, u32[]{:S(2)}) collective-permute-start(f32[12,128]{1,0:T(8,128)S(1)} %get-tuple-element.85), channel_id=1, source_target_pairs={{0,4},{1,5},{2,6},{3,7},{4,0},{5,1},{6,2},{7,3},{8,12},{9,13},{10,... | collective-permute-start | bytes 18440 | tf_op jit(solution)/shard_map/ppermute | solution.py:483
  45.3 1.7 %collective-permute-done.15.refs_4_ = f32[12,128]{1,0:T(8,128)S(1)} collective-permute-done((f32[12,128]{1,0:T(8,128)S(1)}, f32[12,128]{1,0:T(8,128)S(1)}, u32[]{:S(2)}, u32[]{:S(2)}) %collective-permute-start.15) | collective-permute-done | bytes 6176 | tf_op jit(solution)/shard_map/ppermute | solution.py:483
  48.5 4.8 %all-to-all-start.2 = ((f32[32,3,128]{2,1,0:T(4,128)}), f32[32,3,128]{2,1,0:T(4,128)S(1)}, u32[]{:S(2)}, u32[]{:S(2)}) async-start(f32[32,3,128]{2,1,0:T(4,128)} %get-tuple-element.97), calls=%async_computation.2 | async-start | bytes 131072 | tf_op jit(solution)/shard_map/all_to_all | solution.py:490
  53.3 1.8 %collective-permute-start.16 = (f32[12,128]{1,0:T(8,128)S(1)}, f32[12,128]{1,0:T(8,128)S(1)}, u32[]{:S(2)}, u32[]{:S(2)}) collective-permute-start(f32[12,128]{1,0:T(8,128)S(1)} %get-tuple-element.93), channel_id=1, source_target_pairs={{0,4},{1,5},{2,6},{3,7},{4,0},{5,1},{6,2},{7,3},{8,12},{9,13},{10,... | collective-permute-start | bytes 18440 | tf_op jit(solution)/shard_map/ppermute | solution.py:483
  57.0 1.7 %collective-permute-done.19.recv3 = f32[12,128]{1,0:T(8,128)S(1)} collective-permute-done((f32[12,128]{1,0:T(8,128)S(1)}, f32[12,128]{1,0:T(8,128)S(1)}, u32[]{:S(2)}, u32[]{:S(2)}) %collective-permute-start.19) | collective-permute-done | bytes 6176 | tf_op jit(solution)/shard_map/ppermute | solution.py:483
  60.7 2.1 %contact.3.after = f32[32,3,128]{2,1,0:T(4,128)} custom-call(f32[2,128,128]{2,1,0:T(8,128)S(1)} %copy-done.2, f32[32,3,128]{2,1,0:T(4,128)S(1)} %all-to-all-done.2.arrived, f32[192,128]{1,0:T(8,128)S(1)} %forces.3.after.held), custom_call_target="tpu_custom_call" | custom-call | tf_op jit(solution)/shard_map/contact/pallas_call | solution.py:452
  62.8 4.8 %all-to-all-start.3 = ((f32[32,3,128]{2,1,0:T(4,128)}), f32[32,3,128]{2,1,0:T(4,128)S(1)}, u32[]{:S(2)}, u32[]{:S(2)}) async-start(f32[32,3,128]{2,1,0:T(4,128)} %contact.3.after), calls=%async_computation.3 | async-start | bytes 131072 | tf_op jit(solution)/shard_map/all_to_all | solution.py:490
  68.7 1.7 %collective-permute-start.20 = (f32[12,128]{1,0:T(8,128)S(1)}, f32[12,128]{1,0:T(8,128)S(1)}, u32[]{:S(2)}, u32[]{:S(2)}) collective-permute-start(f32[12,128]{1,0:T(8,128)S(1)} %get-tuple-element.99), channel_id=1, source_target_pairs={{0,4},{1,5},{2,6},{3,7},{4,0},{5,1},{6,2},{7,3},{8,12},{9,13},{10,... | collective-permute-start | bytes 18440 | tf_op jit(solution)/shard_map/ppermute | solution.py:483
  72.4 1.5 %collective-permute-done.23.refs_4_ = f32[12,128]{1,0:T(8,128)S(1)} collective-permute-done((f32[12,128]{1,0:T(8,128)S(1)}, f32[12,128]{1,0:T(8,128)S(1)}, u32[]{:S(2)}, u32[]{:S(2)}) %collective-permute-start.23) | collective-permute-done | bytes 6176 | tf_op jit(solution)/shard_map/ppermute | solution.py:483
  75.7 1.5 %collective-permute-start.24 = (f32[12,128]{1,0:T(8,128)S(1)}, f32[12,128]{1,0:T(8,128)S(1)}, u32[]{:S(2)}, u32[]{:S(2)}) collective-permute-start(f32[12,128]{1,0:T(8,128)S(1)} %get-tuple-element.105), channel_id=1, source_target_pairs={{0,4},{1,5},{2,6},{3,7},{4,0},{5,1},{6,2},{7,3},{8,12},{9,13},{10,... | collective-permute-start | bytes 18440 | tf_op jit(solution)/shard_map/ppermute | solution.py:483
  80.8 2.4 %forces_assemble.3 = (f32[48,128]{1,0:T(8,128)S(1)}, f32[12,128]{1,0:T(8,128)S(1)}, f32[12,128]{1,0:T(8,128)S(1)}, f32[12,128]{1,0:T(8,128)S(1)}, f32[12,128]{1,0:T(8,128)S(1)}) custom-call(f32[48,128]{1,0:T(8,128)S(1)} %get-tuple-element.104.disp.refs_9_, f32[12,128]{1,0:T(8,128)S(1)} %collective-permute-done.24.recv0, ...), custom_call_target="tpu_custom_call" | custom-call | tf_op jit(solution)/shard_map/forces_assemble/pallas_call | solution.py:452
  83.2 2.5 %collective-permute-start.28 = (f32[12,128]{1,0:T(8,128)S(1)}, f32[12,128]{1,0:T(8,128)S(1)}, u32[]{:S(2)}, u32[]{:S(2)}) collective-permute-start(f32[12,128]{1,0:T(8,128)S(1)} %get-tuple-element.110), channel_id=1, source_target_pairs={{0,4},{1,5},{2,6},{3,7},{4,0},{5,1},{6,2},{7,3},{8,12},{9,13},{10,... | collective-permute-start | bytes 18440 | tf_op jit(solution)/shard_map/ppermute | solution.py:483
  87.6 1.7 %collective-permute-done.31.refs_4_ = f32[12,128]{1,0:T(8,128)S(1)} collective-permute-done((f32[12,128]{1,0:T(8,128)S(1)}, f32[12,128]{1,0:T(8,128)S(1)}, u32[]{:S(2)}, u32[]{:S(2)}) %collective-permute-start.31) | collective-permute-done | bytes 6176 | tf_op jit(solution)/shard_map/ppermute | solution.py:483
  (87 shorter events, 29.0 us)
Async XLA Ops:
  3.5 14.7 %all-to-all-start = ((f32[32,3,128]{2,1,0:T(4,128)}), f32[32,3,128]{2,1,0:T(4,128)S(1)}, u32[]{:S(2)}, u32[]{:S(2)}) async-start(f32[32,3,128]{2,1,0:T(4,128)} %get-tuple-element.68), calls=%async_computation | async-start | bytes 131072 | tf_op jit(solution)/shard_map/all_to_all | solution.py:490
  10.8 3.9 %collective-permute-start = (f32[12,128]{1,0:T(8,128)}, f32[12,128]{1,0:T(8,128)S(1)}, u32[]{:S(2)}, u32[]{:S(2)}) collective-permute-start(f32[12,128]{1,0:T(8,128)} %get-tuple-element.61), channel_id=1, source_target_pairs={{0,4},{1,5},{2,6},{3,7},{4,0},{5,1},{6,2},{7,3},{8,12},{9,13},{10,... | collective-permute-start | bytes 18440 | tf_op jit(solution)/shard_map/ppermute | solution.py:483
  12.6 2.1 %collective-permute-start.1 = (f32[12,128]{1,0:T(8,128)}, f32[12,128]{1,0:T(8,128)S(1)}, u32[]{:S(2)}, u32[]{:S(2)}) collective-permute-start(f32[12,128]{1,0:T(8,128)} %get-tuple-element.62), channel_id=1, source_target_pairs={{0,1},{1,0},{2,3},{3,2},{4,8},{5,9},{6,10},{7,11},{8,4},{9,5},{10,... | collective-permute-start | bytes 18440 | tf_op jit(solution)/shard_map/ppermute | solution.py:483
  12.6 2.1 %collective-permute-start.2 = (f32[12,128]{1,0:T(8,128)}, f32[12,128]{1,0:T(8,128)S(1)}, u32[]{:S(2)}, u32[]{:S(2)}) collective-permute-start(f32[12,128]{1,0:T(8,128)} %get-tuple-element.63), channel_id=1, source_target_pairs={{0,1},{1,0},{2,3},{3,2},{4,5},{5,4},{6,7},{7,6},{8,9},{9,8},{10,11... | collective-permute-start | bytes 18440 | tf_op jit(solution)/shard_map/ppermute | solution.py:483
  13.1 3.1 %collective-permute-start.3 = (f32[12,128]{1,0:T(8,128)S(1)}, f32[12,128]{1,0:T(8,128)S(1)}, u32[]{:S(2)}, u32[]{:S(2)}) collective-permute-start(f32[12,128]{1,0:T(8,128)S(1)} %copy-done.12), channel_id=1, source_target_pairs={{0,3},{1,2},{2,1},{3,0},{4,7},{5,6},{6,5},{7,4},{8,11},{9,10},{10,... | collective-permute-start | bytes 18440 | tf_op jit(solution)/shard_map/ppermute | solution.py:483
  20.3 12.3 %all-to-all-start.1 = ((f32[32,3,128]{2,1,0:T(4,128)}), f32[32,3,128]{2,1,0:T(4,128)S(1)}, u32[]{:S(2)}, u32[]{:S(2)}) async-start(f32[32,3,128]{2,1,0:T(4,128)} %contact.2.after), calls=%async_computation.1 | async-start | bytes 131072 | tf_op jit(solution)/shard_map/all_to_all | solution.py:490
  26.2 3.7 %collective-permute-start.4 = (f32[12,128]{1,0:T(8,128)S(1)}, f32[12,128]{1,0:T(8,128)S(1)}, u32[]{:S(2)}, u32[]{:S(2)}) collective-permute-start(f32[12,128]{1,0:T(8,128)S(1)} %get-tuple-element.70), channel_id=1, source_target_pairs={{0,4},{1,5},{2,6},{3,7},{4,0},{5,1},{6,2},{7,3},{8,12},{9,13},{10,... | collective-permute-start | bytes 18440 | tf_op jit(solution)/shard_map/ppermute | solution.py:483
  28.6 3.1 %collective-permute-start.7 = (f32[12,128]{1,0:T(8,128)S(1)}, f32[12,128]{1,0:T(8,128)S(1)}, u32[]{:S(2)}, u32[]{:S(2)}) collective-permute-start(f32[12,128]{1,0:T(8,128)S(1)} %get-tuple-element.73), channel_id=1, source_target_pairs={{0,3},{1,2},{2,1},{3,0},{4,7},{5,6},{6,5},{7,4},{8,11},{9,10},{10,... | collective-permute-start | bytes 18440 | tf_op jit(solution)/shard_map/ppermute | solution.py:483
  33.4 3.7 %collective-permute-start.8 = (f32[12,128]{1,0:T(8,128)S(1)}, f32[12,128]{1,0:T(8,128)S(1)}, u32[]{:S(2)}, u32[]{:S(2)}) collective-permute-start(f32[12,128]{1,0:T(8,128)S(1)} %get-tuple-element.79), channel_id=1, source_target_pairs={{0,4},{1,5},{2,6},{3,7},{4,0},{5,1},{6,2},{7,3},{8,12},{9,13},{10,... | collective-permute-start | bytes 18440 | tf_op jit(solution)/shard_map/ppermute | solution.py:483
  35.0 2.1 %collective-permute-start.9 = (f32[12,128]{1,0:T(8,128)S(1)}, f32[12,128]{1,0:T(8,128)S(1)}, u32[]{:S(2)}, u32[]{:S(2)}) collective-permute-start(f32[12,128]{1,0:T(8,128)S(1)} %get-tuple-element.80), channel_id=1, source_target_pairs={{0,1},{1,0},{2,3},{3,2},{4,8},{5,9},{6,10},{7,11},{8,4},{9,5},{10,... | collective-permute-start | bytes 18440 | tf_op jit(solution)/shard_map/ppermute | solution.py:483
  35.5 3.1 %collective-permute-start.11 = (f32[12,128]{1,0:T(8,128)S(1)}, f32[12,128]{1,0:T(8,128)S(1)}, u32[]{:S(2)}, u32[]{:S(2)}) collective-permute-start(f32[12,128]{1,0:T(8,128)S(1)} %get-tuple-element.82), channel_id=1, source_target_pairs={{0,3},{1,2},{2,1},{3,0},{4,7},{5,6},{6,5},{7,4},{8,11},{9,10},{10,... | collective-permute-start | bytes 18440 | tf_op jit(solution)/shard_map/ppermute | solution.py:483
  41.0 4.3 %collective-permute-start.12 = (f32[12,128]{1,0:T(8,128)S(1)}, f32[12,128]{1,0:T(8,128)S(1)}, u32[]{:S(2)}, u32[]{:S(2)}) collective-permute-start(f32[12,128]{1,0:T(8,128)S(1)} %get-tuple-element.85), channel_id=1, source_target_pairs={{0,4},{1,5},{2,6},{3,7},{4,0},{5,1},{6,2},{7,3},{8,12},{9,13},{10,... | collective-permute-start | bytes 18440 | tf_op jit(solution)/shard_map/ppermute | solution.py:483
  44.0 3.1 %collective-permute-start.15 = (f32[12,128]{1,0:T(8,128)S(1)}, f32[12,128]{1,0:T(8,128)S(1)}, u32[]{:S(2)}, u32[]{:S(2)}) collective-permute-start(f32[12,128]{1,0:T(8,128)S(1)} %get-tuple-element.88), channel_id=1, source_target_pairs={{0,3},{1,2},{2,1},{3,0},{4,7},{5,6},{6,5},{7,4},{8,11},{9,10},{10,... | collective-permute-start | bytes 18440 | tf_op jit(solution)/shard_map/ppermute | solution.py:483
  48.5 12.2 %all-to-all-start.2 = ((f32[32,3,128]{2,1,0:T(4,128)}), f32[32,3,128]{2,1,0:T(4,128)S(1)}, u32[]{:S(2)}, u32[]{:S(2)}) async-start(f32[32,3,128]{2,1,0:T(4,128)} %get-tuple-element.97), calls=%async_computation.2 | async-start | bytes 131072 | tf_op jit(solution)/shard_map/all_to_all | solution.py:490
  53.3 3.7 %collective-permute-start.16 = (f32[12,128]{1,0:T(8,128)S(1)}, f32[12,128]{1,0:T(8,128)S(1)}, u32[]{:S(2)}, u32[]{:S(2)}) collective-permute-start(f32[12,128]{1,0:T(8,128)S(1)} %get-tuple-element.93), channel_id=1, source_target_pairs={{0,4},{1,5},{2,6},{3,7},{4,0},{5,1},{6,2},{7,3},{8,12},{9,13},{10,... | collective-permute-start | bytes 18440 | tf_op jit(solution)/shard_map/ppermute | solution.py:483
  55.6 3.1 %collective-permute-start.19 = (f32[12,128]{1,0:T(8,128)S(1)}, f32[12,128]{1,0:T(8,128)S(1)}, u32[]{:S(2)}, u32[]{:S(2)}) collective-permute-start(f32[12,128]{1,0:T(8,128)S(1)} %get-tuple-element.96), channel_id=1, source_target_pairs={{0,3},{1,2},{2,1},{3,0},{4,7},{5,6},{6,5},{7,4},{8,11},{9,10},{10,... | collective-permute-start | bytes 18440 | tf_op jit(solution)/shard_map/ppermute | solution.py:483
  62.8 12.1 %all-to-all-start.3 = ((f32[32,3,128]{2,1,0:T(4,128)}), f32[32,3,128]{2,1,0:T(4,128)S(1)}, u32[]{:S(2)}, u32[]{:S(2)}) async-start(f32[32,3,128]{2,1,0:T(4,128)} %contact.3.after), calls=%async_computation.3 | async-start | bytes 131072 | tf_op jit(solution)/shard_map/all_to_all | solution.py:490
  68.7 3.7 %collective-permute-start.20 = (f32[12,128]{1,0:T(8,128)S(1)}, f32[12,128]{1,0:T(8,128)S(1)}, u32[]{:S(2)}, u32[]{:S(2)}) collective-permute-start(f32[12,128]{1,0:T(8,128)S(1)} %get-tuple-element.99), channel_id=1, source_target_pairs={{0,4},{1,5},{2,6},{3,7},{4,0},{5,1},{6,2},{7,3},{8,12},{9,13},{10,... | collective-permute-start | bytes 18440 | tf_op jit(solution)/shard_map/ppermute | solution.py:483
  70.9 3.1 %collective-permute-start.23 = (f32[12,128]{1,0:T(8,128)S(1)}, f32[12,128]{1,0:T(8,128)S(1)}, u32[]{:S(2)}, u32[]{:S(2)}) collective-permute-start(f32[12,128]{1,0:T(8,128)S(1)} %get-tuple-element.102), channel_id=1, source_target_pairs={{0,3},{1,2},{2,1},{3,0},{4,7},{5,6},{6,5},{7,4},{8,11},{9,10},{10,... | collective-permute-start | bytes 18440 | tf_op jit(solution)/shard_map/ppermute | solution.py:483
  75.7 3.7 %collective-permute-start.24 = (f32[12,128]{1,0:T(8,128)S(1)}, f32[12,128]{1,0:T(8,128)S(1)}, u32[]{:S(2)}, u32[]{:S(2)}) collective-permute-start(f32[12,128]{1,0:T(8,128)S(1)} %get-tuple-element.105), channel_id=1, source_target_pairs={{0,4},{1,5},{2,6},{3,7},{4,0},{5,1},{6,2},{7,3},{8,12},{9,13},{10,... | collective-permute-start | bytes 18440 | tf_op jit(solution)/shard_map/ppermute | solution.py:483
  77.2 2.2 %collective-permute-start.25 = (f32[12,128]{1,0:T(8,128)S(1)}, f32[12,128]{1,0:T(8,128)S(1)}, u32[]{:S(2)}, u32[]{:S(2)}) collective-permute-start(f32[12,128]{1,0:T(8,128)S(1)} %get-tuple-element.106), channel_id=1, source_target_pairs={{0,1},{1,0},{2,3},{3,2},{4,8},{5,9},{6,10},{7,11},{8,4},{9,5},{10,... | collective-permute-start | bytes 18440 | tf_op jit(solution)/shard_map/ppermute | solution.py:483
  77.7 3.1 %collective-permute-start.27 = (f32[12,128]{1,0:T(8,128)S(1)}, f32[12,128]{1,0:T(8,128)S(1)}, u32[]{:S(2)}, u32[]{:S(2)}) collective-permute-start(f32[12,128]{1,0:T(8,128)S(1)} %get-tuple-element.108), channel_id=1, source_target_pairs={{0,3},{1,2},{2,1},{3,0},{4,7},{5,6},{6,5},{7,4},{8,11},{9,10},{10,... | collective-permute-start | bytes 18440 | tf_op jit(solution)/shard_map/ppermute | solution.py:483
  83.2 4.3 %collective-permute-start.28 = (f32[12,128]{1,0:T(8,128)S(1)}, f32[12,128]{1,0:T(8,128)S(1)}, u32[]{:S(2)}, u32[]{:S(2)}) collective-permute-start(f32[12,128]{1,0:T(8,128)S(1)} %get-tuple-element.110), channel_id=1, source_target_pairs={{0,4},{1,5},{2,6},{3,7},{4,0},{5,1},{6,2},{7,3},{8,12},{9,13},{10,... | collective-permute-start | bytes 18440 | tf_op jit(solution)/shard_map/ppermute | solution.py:483
  86.2 3.1 %collective-permute-start.31 = (f32[12,128]{1,0:T(8,128)S(1)}, f32[12,128]{1,0:T(8,128)S(1)}, u32[]{:S(2)}, u32[]{:S(2)}) collective-permute-start(f32[12,128]{1,0:T(8,128)S(1)} %get-tuple-element.113), channel_id=1, source_target_pairs={{0,3},{1,2},{2,1},{3,0},{4,7},{5,6},{6,5},{7,4},{8,11},{9,10},{10,... | collective-permute-start | bytes 18440 | tf_op jit(solution)/shard_map/ppermute | solution.py:483
  (25 other events, 127.7 us)

commit v5 on v3

--- a/solution.py
+++ b/solution.py
@@ -47,10 +47,9 @@
     return [top, values - top]
 
 
-def scatter_dot(hi_rows, lo_rows, value_rows, rows):
+def scatter_dot(hi_rows, lo_rows, value_rows, rows, total=None):
     row_no = lax.broadcasted_iota(I32, (rows, LANES), 0)
     lane_no = lax.broadcasted_iota(I32, (LANES, LANES), 0)
-    total = None
     group = 2
     for start in range(0, len(hi_rows), group):
         lefts, rights = [], []
@@ -76,21 +75,28 @@
     return total
 
 
-def scatter_add(index_row, value_row, count, rows):
+def scatter_some(index_row, value_row, numbers, rows, total=None):
     hi_rows, lo_rows = [], []
     value_rows = [[] for _ in range(6)]
-    for r in range(count):
+    for r in numbers:
         idx = index_row(r)
         hi_rows.append(idx >> 7)
         lo_rows.append(idx & (LANES - 1))
         for c in range(3):
             for part, vals in enumerate(halves(value_row(c, r))):
                 value_rows[2 * c + part].append(vals)
-    total = scatter_dot(hi_rows, lo_rows, value_rows, rows)
+    return scatter_dot(hi_rows, lo_rows, value_rows, rows, total)
+
+
+def add_halves(total, rows):
     return [
         total[2 * c * rows : (2 * c + 1) * rows] + total[(2 * c + 1) * rows : (2 * c + 2) * rows]
         for c in range(3)
     ]
+
+
+def scatter_add(index_row, value_row, count, rows):
+    return add_halves(scatter_some(index_row, value_row, range(count), rows), rows)
 
 
 def spread_rows(source, target, groups):
@@ -148,8 +154,8 @@
     ]
     for copy in copies:
         copy.start()
-    for copy in copies:
-        copy.wait()
+    copies[1].wait()
+    copies[5].wait()
     px_no = lax.axis_index("px")
     py_no = lax.axis_index("py")
     own_count = coords_in.shape[1]
@@ -174,6 +180,8 @@
                 jnp.full((1, LANES), missing) == 1, -1, chosen
             )
     gather_halo(disp, rows, lists, sends)
+    for n in (0, 6, 7):
+        copies[n].wait()
     spread_rows(coords_in, coords, 3)
     count = bucket.shape[0]
     slot_rows = inverse.shape[0]
@@ -198,6 +206,8 @@
     total = scatter_dot(hi_rows, lo_rows, digits, slot_rows)
     inverse[...] = (total[:slot_rows] * 64.0 + total[slot_rows:]).astype(I32) - 1
     gather_slots(coords, disp, rows, inverse, outgoing)
+    for n in (2, 3, 4, 8, 9, 10):
+        copies[n].wait()
     spread_rows(nodes_in, nodes, 4)
     nodes[...] = block_remap(nodes[...], own_count, width, px_no, py_no, *counts)
     spread_rows(vel_in, vel, 3)
@@ -207,18 +217,14 @@
         splat[j * size : (j + 1) * size, :] = jnp.broadcast_to(stiff[:, j : j + 1], (size, LANES))
     for h in range(slow.shape[0]):
         slow[h : h + 1, :] = jnp.full((1, LANES), classes[h])
-    tile_no = lax.broadcasted_iota(I32, (slot_rows, LANES), 0)
-    short = LANES - pairs.shape[1]
-    onehots = []
-    for side in range(2):
-        row = pairs[side : side + 1, :]
-        if short:
-            row = jnp.concatenate([row, jnp.full((1, short), -1)], axis=1)
-        onehots.append((tile_no == row).astype(F32))
-    onehots.append(jnp.zeros((LANES - 2 * slot_rows, LANES), F32))
-    onehots = jnp.concatenate(onehots, axis=0)
-    select[0] = onehots
-    select[1] = jnp.transpose(onehots)
+    ends = [pairs[0:1, :], pairs[1:2, :]]
+    short = LANES - 2 * pairs.shape[1]
+    if short:
+        ends.append(jnp.full((1, short), -1))
+    tile_no = lax.broadcasted_iota(I32, (LANES, LANES), 0)
+    onehot = (tile_no == jnp.concatenate(ends, axis=1)).astype(F32)
+    select[0] = onehot
+    select[1] = jnp.transpose(onehot)
 
 
 def corner_forces(disp, recvs, nodes, thick, splat):
@@ -260,7 +266,7 @@
             outs[b][c * quarter : (c + 1) * quarter, :] = sums[c][start : start + quarter]
 
 
-def force_kernel(disp, recv0, recv1, recv2, recv3, nodes, thick, splat, held):
+def force_kernel(disp, recv1, recv3, recv0, recv2, nodes, thick, splat, held):
     elem_rows = thick.shape[0]
     forces = corner_forces(disp, (recv0, recv1, recv2, recv3), nodes, thick, splat)
     for i in range(12):
@@ -276,10 +282,10 @@
 
 def later_kernel(
     disp,
+    recv1,
+    recv3,
     recv0,
-    recv1,
     recv2,
-    recv3,
     nodes,
     thick,
     splat,
@@ -306,16 +312,26 @@
     assemble(force_row, nodes, own, (out0, out1, out2, out3))
 
 
+def thirds(values):
+    parts = []
+    for _ in range(3):
+        top = values.astype(BF16)
+        parts.append(top)
+        values = values - top.astype(F32)
+    return jnp.concatenate(parts, axis=1)
+
+
+def dot_thirds(onehot, values):
+    width = values.shape[1]
+    sums = jnp.dot(onehot.astype(BF16), thirds(values), preferred_element_type=F32)
+    return sums[:, :width] + sums[:, width : 2 * width] + sums[:, 2 * width :]
+
+
 def contact_kernel(pair_count, select, arrived, after, pushes):
     tiles = arrived.shape[0]
     points = jnp.concatenate([arrived[:, c, :] for c in range(3)], axis=1)
-    picked = []
-    for side in range(2):
-        onehot = select[1, :pair_count, side * tiles : (side + 1) * tiles]
-        picked.append(
-            jnp.dot(onehot, points, preferred_element_type=F32, precision=lax.Precision.HIGHEST)
-        )
-    first, second = picked
+    picked = dot_thirds(select[1, : 2 * pair_count, :tiles], points)
+    first, second = picked[:pair_count], picked[pair_count:]
     group = LANES // 4
     pushed = []
     for start in range(0, pair_count, group):
@@ -343,19 +359,14 @@
                     [jnp.sum(weight * gaps[c], axis=0, keepdims=True) for c in range(3)], axis=1
                 )
             )
-    total = PENALTY * jnp.dot(
-        select[0, :tiles, :pair_count],
-        jnp.concatenate(pushed, axis=0),
-        preferred_element_type=F32,
-        precision=lax.Precision.HIGHEST,
-    )
+    total = PENALTY * dot_thirds(select[0, :tiles, :pair_count], jnp.concatenate(pushed, axis=0))
     for c in range(3):
         pushes[:, c, :] = total[:, c * LANES : (c + 1) * LANES]
 
 
 def update_kernel(first, last, final, *refs):
     refs = list(refs)
-    own, back0, back1, back2, back3, lists, ext, inv_mass, vel, disp = refs[:10]
+    own, back1, back3, back0, back2, lists, ext, inv_mass, vel, disp = refs[:10]
     refs = refs[10:]
     if first:
         returned, inverse = refs[:2]
@@ -450,7 +461,8 @@
 
 
 def exchange(blocks):
-    return [lax.ppermute(block, ("px", "py"), pairs) for block, pairs in zip(blocks, partners())]
+    swaps = partners()
+    return [lax.ppermute(blocks[n], ("px", "py"), swaps[n]) for n in (1, 3, 0, 2)]
 
 
 def swap(slots, devices, capacity):

time: 90.4 us -> 86 us (0.951)
  waiting for transfers between devices: 19 us -> 12.4 us
  starting transfers between devices: 50.7 us -> 53 us
    ppermute x32, starting transfers between devices: 28.8 us -> 33.5 us  [exchange(): lax.ppermute(blocks[n], ('px', 'py'), swaps[n])]
    ppermute x32, waiting for transfers between devices: 15.1 us -> 10.7 us  [exchange(): lax.ppermute(blocks[n], ('px', 'py'), swaps[n])]
    all_to_all x4, starting transfers between devices: 21.8 us -> 19.6 us  [swap(): return lax.all_to_all(slots, axes, 0, 0, tiled=True)]
    all_to_all x4, waiting for transfers between devices: 3.84 us -> 1.67 us  [swap(): return lax.all_to_all(slots, axes, 0, 0, tiled=True)]
  transfers between devices with their start and end apart: 36 -> 36, of which waited for: 18 -> 12; matrix products, arithmetic and copies ran while one was open for 0% -> 0% of each run, Pallas kernels for 4% -> 5%
where the time goes in v5:
time: 86 us; the launch traced here: 85.7 us
  starting transfers between devices  53 us (62%)
  Pallas kernels  19.3 us (22%)
  waiting for transfers between devices  12.4 us (14%)
  between operations  0.91 us (1%)
    ppermute x32, starting transfers between devices, exchange(): lax.ppermute(blocks[n], ('px', 'py'), swaps[n])  33.5 us
    all_to_all x4, starting transfers between devices, swap(): return lax.all_to_all(slots, axes, 0, 0, tiled=True)  19.6 us
    pallas_call x13, Pallas kernels, call(): pl.pallas_call(kernel, out_shape=tuple(outputs), in_specs=specs, out_spec...  19.3 us
    ppermute x32, waiting for transfers between devices, exchange(): lax.ppermute(blocks[n], ('px', 'py'), swaps[n])  10.7 us
  transfers between devices with their start and end apart: 36, of which 12 were waited for; matrix products, arithmetic and copies ran while one was open for 0% of the time, Pallas kernels for 5%

profile of v5, /device:TPU:0, one launch (start us, length us, event | category | flops | bytes accessed | tf_op | source)
XLA Modules:
  0.0 85.7 jit_solution(17840476592464079060)
XLA Ops:
  0.6 2.8 %setup.1 = (f32[48,128]{1,0:T(8,128)}, f32[48,128]{1,0:T(8,128)}, f32[48,128]{1,0:T(8,128)}, f32[48,128]{1,0:T(8,128)}, s32[64,128]{1,0:T(8,128)}, /*index=5*/s3...) custom-call(f32[3,2048]{1,0:T(4,128)} %refs_0_.1, ...), custom_call_target="tpu_custom_call" | custom-call | tf_op jit(solution)/shard_map/setup/pallas_call | solution.py:436
  3.5 7.3 %all-to-all-start = ((f32[32,3,128]{2,1,0:T(4,128)}), f32[32,3,128]{2,1,0:T(4,128)S(1)}, u32[]{:S(2)}, u32[]{:S(2)}) async-start(f32[32,3,128]{2,1,0:T(4,128)} %get-tuple-element.68), calls=%async_computation | async-start | bytes 131072 | tf_op jit(solution)/shard_map/all_to_all | solution.py:471
  11.1 1.6 %collective-permute-start.1 = (f32[12,128]{1,0:T(8,128)}, f32[12,128]{1,0:T(8,128)S(1)}, u32[]{:S(2)}, u32[]{:S(2)}) collective-permute-start(f32[12,128]{1,0:T(8,128)} %get-tuple-element.62), channel_id=1, source_target_pairs={{0,3},{1,2},{2,1},{3,0},{4,7},{5,6},{6,5},{7,4},{8,11},{9,10},{10,... | collective-permute-start | bytes 18440 | tf_op jit(solution)/shard_map/ppermute | solution.py:465
  12.7 2.3 %collective-permute-start.2 = (f32[12,128]{1,0:T(8,128)}, f32[12,128]{1,0:T(8,128)S(1)}, u32[]{:S(2)}, u32[]{:S(2)}) collective-permute-start(f32[12,128]{1,0:T(8,128)} %get-tuple-element.63), channel_id=1, source_target_pairs={{0,4},{1,5},{2,6},{3,7},{4,0},{5,1},{6,2},{7,3},{8,12},{9,13},{10,... | collective-permute-start | bytes 18440 | tf_op jit(solution)/shard_map/ppermute | solution.py:465
  15.4 1.6 %collective-permute-done.2.recv0 = f32[12,128]{1,0:T(8,128)S(1)} collective-permute-done((f32[12,128]{1,0:T(8,128)}, f32[12,128]{1,0:T(8,128)S(1)}, u32[]{:S(2)}, u32[]{:S(2)}) %collective-permute-start.2) | collective-permute-done | bytes 6176 | tf_op jit(solution)/shard_map/ppermute | solution.py:465
  18.2 2.1 %contact.2.after = f32[32,3,128]{2,1,0:T(4,128)} custom-call(f32[2,128,128]{2,1,0:T(8,128)S(1)} %copy-done.2, f32[32,3,128]{2,1,0:T(4,128)S(1)} %all-to-all-done.arrived, f32[192,128]{1,0:T(8,128)S(1)} %forces.2.after.held), custom_call_target="tpu_custom_call" | custom-call | tf_op jit(solution)/shard_map/contact/pallas_call | solution.py:436
  20.3 4.1 %all-to-all-start.1 = ((f32[32,3,128]{2,1,0:T(4,128)}), f32[32,3,128]{2,1,0:T(4,128)S(1)}, u32[]{:S(2)}, u32[]{:S(2)}) async-start(f32[32,3,128]{2,1,0:T(4,128)} %contact.2.after), calls=%async_computation.1 | async-start | bytes 131072 | tf_op jit(solution)/shard_map/all_to_all | solution.py:471
  25.8 1.6 %collective-permute-start.5 = (f32[12,128]{1,0:T(8,128)S(1)}, f32[12,128]{1,0:T(8,128)S(1)}, u32[]{:S(2)}, u32[]{:S(2)}) collective-permute-start(f32[12,128]{1,0:T(8,128)S(1)} %get-tuple-element.71), channel_id=1, source_target_pairs={{0,3},{1,2},{2,1},{3,0},{4,7},{5,6},{6,5},{7,4},{8,11},{9,10},{10,... | collective-permute-start | bytes 18440 | tf_op jit(solution)/shard_map/ppermute | solution.py:465
  27.4 2.3 %collective-permute-start.6 = (f32[12,128]{1,0:T(8,128)S(1)}, f32[12,128]{1,0:T(8,128)S(1)}, u32[]{:S(2)}, u32[]{:S(2)}) collective-permute-start(f32[12,128]{1,0:T(8,128)S(1)} %get-tuple-element.72), channel_id=1, source_target_pairs={{0,4},{1,5},{2,6},{3,7},{4,0},{5,1},{6,2},{7,3},{8,12},{9,13},{10,... | collective-permute-start | bytes 18440 | tf_op jit(solution)/shard_map/ppermute | solution.py:465
  33.2 2.5 %collective-permute-start.10 = (f32[12,128]{1,0:T(8,128)S(1)}, f32[12,128]{1,0:T(8,128)S(1)}, u32[]{:S(2)}, u32[]{:S(2)}) collective-permute-start(f32[12,128]{1,0:T(8,128)S(1)} %get-tuple-element.81), channel_id=1, source_target_pairs={{0,4},{1,5},{2,6},{3,7},{4,0},{5,1},{6,2},{7,3},{8,12},{9,13},{10,... | collective-permute-start | bytes 18440 | tf_op jit(solution)/shard_map/ppermute | solution.py:465
  37.4 2.2 %forces_assemble.2 = (f32[48,128]{1,0:T(8,128)S(1)}, f32[12,128]{1,0:T(8,128)S(1)}, f32[12,128]{1,0:T(8,128)S(1)}, f32[12,128]{1,0:T(8,128)S(1)}, f32[12,128]{1,0:T(8,128)S(1)}) custom-call(f32[48,128]{1,0:T(8,128)S(1)} %get-tuple-element.78.disp.refs_9_, f32[12,128]{1,0:T(8,128)S(1)} %collective-permute-done.8.recv1, ...), custom_call_target="tpu_custom_call" | custom-call | tf_op jit(solution)/shard_map/forces_assemble/pallas_call | solution.py:436
  40.9 2.6 %collective-permute-start.14 = (f32[12,128]{1,0:T(8,128)S(1)}, f32[12,128]{1,0:T(8,128)S(1)}, u32[]{:S(2)}, u32[]{:S(2)}) collective-permute-start(f32[12,128]{1,0:T(8,128)S(1)} %get-tuple-element.87), channel_id=1, source_target_pairs={{0,4},{1,5},{2,6},{3,7},{4,0},{5,1},{6,2},{7,3},{8,12},{9,13},{10,... | collective-permute-start | bytes 18440 | tf_op jit(solution)/shard_map/ppermute | solution.py:465
  45.1 1.4 %update.5 = (f32[48,128]{1,0:T(8,128)S(1)}, f32[48,128]{1,0:T(8,128)S(1)}, f32[12,128]{1,0:T(8,128)S(1)}, f32[12,128]{1,0:T(8,128)S(1)}, f32[12,128]{1,0:T(8,128...) custom-call(f32[48,128]{1,0:T(8,128)S(1)} %get-tuple-element.84.refs_0_, ...), custom_call_target="tpu_custom_call" | custom-call | tf_op jit(solution)/shard_map/update/pallas_call | solution.py:436
  46.5 4.2 %all-to-all-start.2 = ((f32[32,3,128]{2,1,0:T(4,128)}), f32[32,3,128]{2,1,0:T(4,128)S(1)}, u32[]{:S(2)}, u32[]{:S(2)}) async-start(f32[32,3,128]{2,1,0:T(4,128)} %get-tuple-element.97), calls=%async_computation.2 | async-start | bytes 131072 | tf_op jit(solution)/shard_map/all_to_all | solution.py:471
  51.1 1.6 %collective-permute-start.17 = (f32[12,128]{1,0:T(8,128)S(1)}, f32[12,128]{1,0:T(8,128)S(1)}, u32[]{:S(2)}, u32[]{:S(2)}) collective-permute-start(f32[12,128]{1,0:T(8,128)S(1)} %get-tuple-element.94), channel_id=1, source_target_pairs={{0,3},{1,2},{2,1},{3,0},{4,7},{5,6},{6,5},{7,4},{8,11},{9,10},{10,... | collective-permute-start | bytes 18440 | tf_op jit(solution)/shard_map/ppermute | solution.py:465
  52.7 2.3 %collective-permute-start.18 = (f32[12,128]{1,0:T(8,128)S(1)}, f32[12,128]{1,0:T(8,128)S(1)}, u32[]{:S(2)}, u32[]{:S(2)}) collective-permute-start(f32[12,128]{1,0:T(8,128)S(1)} %get-tuple-element.95), channel_id=1, source_target_pairs={{0,4},{1,5},{2,6},{3,7},{4,0},{5,1},{6,2},{7,3},{8,12},{9,13},{10,... | collective-permute-start | bytes 18440 | tf_op jit(solution)/shard_map/ppermute | solution.py:465
  55.4 1.3 %collective-permute-done.18.recv0 = f32[12,128]{1,0:T(8,128)S(1)} collective-permute-done((f32[12,128]{1,0:T(8,128)S(1)}, f32[12,128]{1,0:T(8,128)S(1)}, u32[]{:S(2)}, u32[]{:S(2)}) %collective-permute-start.18) | collective-permute-done | bytes 6176 | tf_op jit(solution)/shard_map/ppermute | solution.py:465
  58.2 2.1 %contact.3.after = f32[32,3,128]{2,1,0:T(4,128)} custom-call(f32[2,128,128]{2,1,0:T(8,128)S(1)} %copy-done.2, f32[32,3,128]{2,1,0:T(4,128)S(1)} %all-to-all-done.2.arrived, f32[192,128]{1,0:T(8,128)S(1)} %forces.3.after.held), custom_call_target="tpu_custom_call" | custom-call | tf_op jit(solution)/shard_map/contact/pallas_call | solution.py:436
  60.3 4.0 %all-to-all-start.3 = ((f32[32,3,128]{2,1,0:T(4,128)}), f32[32,3,128]{2,1,0:T(4,128)S(1)}, u32[]{:S(2)}, u32[]{:S(2)}) async-start(f32[32,3,128]{2,1,0:T(4,128)} %contact.3.after), calls=%async_computation.3 | async-start | bytes 131072 | tf_op jit(solution)/shard_map/all_to_all | solution.py:471
  65.4 1.6 %collective-permute-start.21 = (f32[12,128]{1,0:T(8,128)S(1)}, f32[12,128]{1,0:T(8,128)S(1)}, u32[]{:S(2)}, u32[]{:S(2)}) collective-permute-start(f32[12,128]{1,0:T(8,128)S(1)} %get-tuple-element.100), channel_id=1, source_target_pairs={{0,3},{1,2},{2,1},{3,0},{4,7},{5,6},{6,5},{7,4},{8,11},{9,10},{10,... | collective-permute-start | bytes 18440 | tf_op jit(solution)/shard_map/ppermute | solution.py:465
  67.1 2.3 %collective-permute-start.22 = (f32[12,128]{1,0:T(8,128)S(1)}, f32[12,128]{1,0:T(8,128)S(1)}, u32[]{:S(2)}, u32[]{:S(2)}) collective-permute-start(f32[12,128]{1,0:T(8,128)S(1)} %get-tuple-element.101), channel_id=1, source_target_pairs={{0,4},{1,5},{2,6},{3,7},{4,0},{5,1},{6,2},{7,3},{8,12},{9,13},{10,... | collective-permute-start | bytes 18440 | tf_op jit(solution)/shard_map/ppermute | solution.py:465
  72.9 2.4 %collective-permute-start.26 = (f32[12,128]{1,0:T(8,128)S(1)}, f32[12,128]{1,0:T(8,128)S(1)}, u32[]{:S(2)}, u32[]{:S(2)}) collective-permute-start(f32[12,128]{1,0:T(8,128)S(1)} %get-tuple-element.107), channel_id=1, source_target_pairs={{0,4},{1,5},{2,6},{3,7},{4,0},{5,1},{6,2},{7,3},{8,12},{9,13},{10,... | collective-permute-start | bytes 18440 | tf_op jit(solution)/shard_map/ppermute | solution.py:465
  77.0 2.2 %forces_assemble.3 = (f32[48,128]{1,0:T(8,128)S(1)}, f32[12,128]{1,0:T(8,128)S(1)}, f32[12,128]{1,0:T(8,128)S(1)}, f32[12,128]{1,0:T(8,128)S(1)}, f32[12,128]{1,0:T(8,128)S(1)}) custom-call(f32[48,128]{1,0:T(8,128)S(1)} %get-tuple-element.104.disp.refs_9_, f32[12,128]{1,0:T(8,128)S(1)} %collective-permute-done.24.recv1, ...), custom_call_target="tpu_custom_call" | custom-call | tf_op jit(solution)/shard_map/forces_assemble/pallas_call | solution.py:436
  80.5 2.5 %collective-permute-start.30 = (f32[12,128]{1,0:T(8,128)S(1)}, f32[12,128]{1,0:T(8,128)S(1)}, u32[]{:S(2)}, u32[]{:S(2)}) collective-permute-start(f32[12,128]{1,0:T(8,128)S(1)} %get-tuple-element.112), channel_id=1, source_target_pairs={{0,4},{1,5},{2,6},{3,7},{4,0},{5,1},{6,2},{7,3},{8,12},{9,13},{10,... | collective-permute-start | bytes 18440 | tf_op jit(solution)/shard_map/ppermute | solution.py:465
  (87 shorter events, 23.8 us)
Async XLA Ops:
  3.5 14.7 %all-to-all-start = ((f32[32,3,128]{2,1,0:T(4,128)}), f32[32,3,128]{2,1,0:T(4,128)S(1)}, u32[]{:S(2)}, u32[]{:S(2)}) async-start(f32[32,3,128]{2,1,0:T(4,128)} %get-tuple-element.68), calls=%async_computation | async-start | bytes 131072 | tf_op jit(solution)/shard_map/all_to_all | solution.py:471
  10.8 4.6 %collective-permute-start = (f32[12,128]{1,0:T(8,128)}, f32[12,128]{1,0:T(8,128)S(1)}, u32[]{:S(2)}, u32[]{:S(2)}) collective-permute-start(f32[12,128]{1,0:T(8,128)} %get-tuple-element.61), channel_id=1, source_target_pairs={{0,1},{1,0},{2,3},{3,2},{4,8},{5,9},{6,10},{7,11},{8,4},{9,5},{10,... | collective-permute-start | bytes 18440 | tf_op jit(solution)/shard_map/ppermute | solution.py:465
  11.1 4.3 %collective-permute-start.1 = (f32[12,128]{1,0:T(8,128)}, f32[12,128]{1,0:T(8,128)S(1)}, u32[]{:S(2)}, u32[]{:S(2)}) collective-permute-start(f32[12,128]{1,0:T(8,128)} %get-tuple-element.62), channel_id=1, source_target_pairs={{0,3},{1,2},{2,1},{3,0},{4,7},{5,6},{6,5},{7,4},{8,11},{9,10},{10,... | collective-permute-start | bytes 18440 | tf_op jit(solution)/shard_map/ppermute | solution.py:465
  12.7 4.2 %collective-permute-start.2 = (f32[12,128]{1,0:T(8,128)}, f32[12,128]{1,0:T(8,128)S(1)}, u32[]{:S(2)}, u32[]{:S(2)}) collective-permute-start(f32[12,128]{1,0:T(8,128)} %get-tuple-element.63), channel_id=1, source_target_pairs={{0,4},{1,5},{2,6},{3,7},{4,0},{5,1},{6,2},{7,3},{8,12},{9,13},{10,... | collective-permute-start | bytes 18440 | tf_op jit(solution)/shard_map/ppermute | solution.py:465
  20.3 11.5 %all-to-all-start.1 = ((f32[32,3,128]{2,1,0:T(4,128)}), f32[32,3,128]{2,1,0:T(4,128)S(1)}, u32[]{:S(2)}, u32[]{:S(2)}) async-start(f32[32,3,128]{2,1,0:T(4,128)} %contact.2.after), calls=%async_computation.1 | async-start | bytes 131072 | tf_op jit(solution)/shard_map/all_to_all | solution.py:471
  25.4 4.6 %collective-permute-start.4 = (f32[12,128]{1,0:T(8,128)S(1)}, f32[12,128]{1,0:T(8,128)S(1)}, u32[]{:S(2)}, u32[]{:S(2)}) collective-permute-start(f32[12,128]{1,0:T(8,128)S(1)} %get-tuple-element.70), channel_id=1, source_target_pairs={{0,1},{1,0},{2,3},{3,2},{4,8},{5,9},{6,10},{7,11},{8,4},{9,5},{10,... | collective-permute-start | bytes 18440 | tf_op jit(solution)/shard_map/ppermute | solution.py:465
  25.8 4.3 %collective-permute-start.5 = (f32[12,128]{1,0:T(8,128)S(1)}, f32[12,128]{1,0:T(8,128)S(1)}, u32[]{:S(2)}, u32[]{:S(2)}) collective-permute-start(f32[12,128]{1,0:T(8,128)S(1)} %get-tuple-element.71), channel_id=1, source_target_pairs={{0,3},{1,2},{2,1},{3,0},{4,7},{5,6},{6,5},{7,4},{8,11},{9,10},{10,... | collective-permute-start | bytes 18440 | tf_op jit(solution)/shard_map/ppermute | solution.py:465
  27.4 4.0 %collective-permute-start.6 = (f32[12,128]{1,0:T(8,128)S(1)}, f32[12,128]{1,0:T(8,128)S(1)}, u32[]{:S(2)}, u32[]{:S(2)}) collective-permute-start(f32[12,128]{1,0:T(8,128)S(1)} %get-tuple-element.72), channel_id=1, source_target_pairs={{0,4},{1,5},{2,6},{3,7},{4,0},{5,1},{6,2},{7,3},{8,12},{9,13},{10,... | collective-permute-start | bytes 18440 | tf_op jit(solution)/shard_map/ppermute | solution.py:465
  33.2 4.2 %collective-permute-start.10 = (f32[12,128]{1,0:T(8,128)S(1)}, f32[12,128]{1,0:T(8,128)S(1)}, u32[]{:S(2)}, u32[]{:S(2)}) collective-permute-start(f32[12,128]{1,0:T(8,128)S(1)} %get-tuple-element.81), channel_id=1, source_target_pairs={{0,4},{1,5},{2,6},{3,7},{4,0},{5,1},{6,2},{7,3},{8,12},{9,13},{10,... | collective-permute-start | bytes 18440 | tf_op jit(solution)/shard_map/ppermute | solution.py:465
  39.7 4.2 %collective-permute-start.12 = (f32[12,128]{1,0:T(8,128)S(1)}, f32[12,128]{1,0:T(8,128)S(1)}, u32[]{:S(2)}, u32[]{:S(2)}) collective-permute-start(f32[12,128]{1,0:T(8,128)S(1)} %get-tuple-element.85), channel_id=1, source_target_pairs={{0,1},{1,0},{2,3},{3,2},{4,8},{5,9},{6,10},{7,11},{8,4},{9,5},{10,... | collective-permute-start | bytes 18440 | tf_op jit(solution)/shard_map/ppermute | solution.py:465
  39.8 4.0 %collective-permute-start.13 = (f32[12,128]{1,0:T(8,128)S(1)}, f32[12,128]{1,0:T(8,128)S(1)}, u32[]{:S(2)}, u32[]{:S(2)}) collective-permute-start(f32[12,128]{1,0:T(8,128)S(1)} %get-tuple-element.86), channel_id=1, source_target_pairs={{0,3},{1,2},{2,1},{3,0},{4,7},{5,6},{6,5},{7,4},{8,11},{9,10},{10,... | collective-permute-start | bytes 18440 | tf_op jit(solution)/shard_map/ppermute | solution.py:465
  40.9 4.2 %collective-permute-start.14 = (f32[12,128]{1,0:T(8,128)S(1)}, f32[12,128]{1,0:T(8,128)S(1)}, u32[]{:S(2)}, u32[]{:S(2)}) collective-permute-start(f32[12,128]{1,0:T(8,128)S(1)} %get-tuple-element.87), channel_id=1, source_target_pairs={{0,4},{1,5},{2,6},{3,7},{4,0},{5,1},{6,2},{7,3},{8,12},{9,13},{10,... | collective-permute-start | bytes 18440 | tf_op jit(solution)/shard_map/ppermute | solution.py:465
  46.5 11.7 %all-to-all-start.2 = ((f32[32,3,128]{2,1,0:T(4,128)}), f32[32,3,128]{2,1,0:T(4,128)S(1)}, u32[]{:S(2)}, u32[]{:S(2)}) async-start(f32[32,3,128]{2,1,0:T(4,128)} %get-tuple-element.97), calls=%async_computation.2 | async-start | bytes 131072 | tf_op jit(solution)/shard_map/all_to_all | solution.py:471
  50.8 4.6 %collective-permute-start.16 = (f32[12,128]{1,0:T(8,128)S(1)}, f32[12,128]{1,0:T(8,128)S(1)}, u32[]{:S(2)}, u32[]{:S(2)}) collective-permute-start(f32[12,128]{1,0:T(8,128)S(1)} %get-tuple-element.93), channel_id=1, source_target_pairs={{0,1},{1,0},{2,3},{3,2},{4,8},{5,9},{6,10},{7,11},{8,4},{9,5},{10,... | collective-permute-start | bytes 18440 | tf_op jit(solution)/shard_map/ppermute | solution.py:465
  51.1 4.3 %collective-permute-start.17 = (f32[12,128]{1,0:T(8,128)S(1)}, f32[12,128]{1,0:T(8,128)S(1)}, u32[]{:S(2)}, u32[]{:S(2)}) collective-permute-start(f32[12,128]{1,0:T(8,128)S(1)} %get-tuple-element.94), channel_id=1, source_target_pairs={{0,3},{1,2},{2,1},{3,0},{4,7},{5,6},{6,5},{7,4},{8,11},{9,10},{10,... | collective-permute-start | bytes 18440 | tf_op jit(solution)/shard_map/ppermute | solution.py:465
  52.7 4.0 %collective-permute-start.18 = (f32[12,128]{1,0:T(8,128)S(1)}, f32[12,128]{1,0:T(8,128)S(1)}, u32[]{:S(2)}, u32[]{:S(2)}) collective-permute-start(f32[12,128]{1,0:T(8,128)S(1)} %get-tuple-element.95), channel_id=1, source_target_pairs={{0,4},{1,5},{2,6},{3,7},{4,0},{5,1},{6,2},{7,3},{8,12},{9,13},{10,... | collective-permute-start | bytes 18440 | tf_op jit(solution)/shard_map/ppermute | solution.py:465
  60.3 11.2 %all-to-all-start.3 = ((f32[32,3,128]{2,1,0:T(4,128)}), f32[32,3,128]{2,1,0:T(4,128)S(1)}, u32[]{:S(2)}, u32[]{:S(2)}) async-start(f32[32,3,128]{2,1,0:T(4,128)} %contact.3.after), calls=%async_computation.3 | async-start | bytes 131072 | tf_op jit(solution)/shard_map/all_to_all | solution.py:471
  65.3 4.4 %collective-permute-start.20 = (f32[12,128]{1,0:T(8,128)S(1)}, f32[12,128]{1,0:T(8,128)S(1)}, u32[]{:S(2)}, u32[]{:S(2)}) collective-permute-start(f32[12,128]{1,0:T(8,128)S(1)} %get-tuple-element.99), channel_id=1, source_target_pairs={{0,1},{1,0},{2,3},{3,2},{4,8},{5,9},{6,10},{7,11},{8,4},{9,5},{10,... | collective-permute-start | bytes 18440 | tf_op jit(solution)/shard_map/ppermute | solution.py:465
  65.4 4.3 %collective-permute-start.21 = (f32[12,128]{1,0:T(8,128)S(1)}, f32[12,128]{1,0:T(8,128)S(1)}, u32[]{:S(2)}, u32[]{:S(2)}) collective-permute-start(f32[12,128]{1,0:T(8,128)S(1)} %get-tuple-element.100), channel_id=1, source_target_pairs={{0,3},{1,2},{2,1},{3,0},{4,7},{5,6},{6,5},{7,4},{8,11},{9,10},{10,... | collective-permute-start | bytes 18440 | tf_op jit(solution)/shard_map/ppermute | solution.py:465
  67.1 4.0 %collective-permute-start.22 = (f32[12,128]{1,0:T(8,128)S(1)}, f32[12,128]{1,0:T(8,128)S(1)}, u32[]{:S(2)}, u32[]{:S(2)}) collective-permute-start(f32[12,128]{1,0:T(8,128)S(1)} %get-tuple-element.101), channel_id=1, source_target_pairs={{0,4},{1,5},{2,6},{3,7},{4,0},{5,1},{6,2},{7,3},{8,12},{9,13},{10,... | collective-permute-start | bytes 18440 | tf_op jit(solution)/shard_map/ppermute | solution.py:465
  72.9 4.1 %collective-permute-start.26 = (f32[12,128]{1,0:T(8,128)S(1)}, f32[12,128]{1,0:T(8,128)S(1)}, u32[]{:S(2)}, u32[]{:S(2)}) collective-permute-start(f32[12,128]{1,0:T(8,128)S(1)} %get-tuple-element.107), channel_id=1, source_target_pairs={{0,4},{1,5},{2,6},{3,7},{4,0},{5,1},{6,2},{7,3},{8,12},{9,13},{10,... | collective-permute-start | bytes 18440 | tf_op jit(solution)/shard_map/ppermute | solution.py:465
  79.2 4.2 %collective-permute-start.28 = (f32[12,128]{1,0:T(8,128)S(1)}, f32[12,128]{1,0:T(8,128)S(1)}, u32[]{:S(2)}, u32[]{:S(2)}) collective-permute-start(f32[12,128]{1,0:T(8,128)S(1)} %get-tuple-element.110), channel_id=1, source_target_pairs={{0,1},{1,0},{2,3},{3,2},{4,8},{5,9},{6,10},{7,11},{8,4},{9,5},{10,... | collective-permute-start | bytes 18440 | tf_op jit(solution)/shard_map/ppermute | solution.py:465
  79.4 4.0 %collective-permute-start.29 = (f32[12,128]{1,0:T(8,128)S(1)}, f32[12,128]{1,0:T(8,128)S(1)}, u32[]{:S(2)}, u32[]{:S(2)}) collective-permute-start(f32[12,128]{1,0:T(8,128)S(1)} %get-tuple-element.111), channel_id=1, source_target_pairs={{0,3},{1,2},{2,1},{3,0},{4,7},{5,6},{6,5},{7,4},{8,11},{9,10},{10,... | collective-permute-start | bytes 18440 | tf_op jit(solution)/shard_map/ppermute | solution.py:465
  80.5 4.2 %collective-permute-start.30 = (f32[12,128]{1,0:T(8,128)S(1)}, f32[12,128]{1,0:T(8,128)S(1)}, u32[]{:S(2)}, u32[]{:S(2)}) collective-permute-start(f32[12,128]{1,0:T(8,128)S(1)} %get-tuple-element.112), channel_id=1, source_target_pairs={{0,4},{1,5},{2,6},{3,7},{4,0},{5,1},{6,2},{7,3},{8,12},{9,13},{10,... | collective-permute-start | bytes 18440 | tf_op jit(solution)/shard_map/ppermute | solution.py:465
  (25 other events, 135.2 us)

commit v6 on v5

--- a/solution.py
+++ b/solution.py
@@ -25,14 +25,17 @@
 WHOLE_VMEM = 64 * 1024 * 1024
 
 
-def lookup(table_row, rows, index):
+def lookup(table_row, rows, index, start=None):
     parts = []
-    for start in range(0, index.shape[0], 8):
-        block = index[start : start + 8]
+    for at in range(0, index.shape[0], 8):
+        block = index[at : at + 8]
         hi = block >> 7
         lo = block & (LANES - 1)
-        found = [jnp.zeros(block.shape, F32) for _ in range(3)]
-        for h in range(rows):
+        if start is None:
+            found = [jnp.zeros(block.shape, F32) for _ in range(3)]
+        else:
+            found = [start[c][at : at + 8] for c in range(3)]
+        for h in rows:
             here = hi == h
             for c in range(3):
                 row = jnp.broadcast_to(table_row(c, h), block.shape)
@@ -109,7 +112,7 @@
 
 
 def gather_halo(disp, rows, lists, sends):
-    found = lookup(lambda c, h: disp[c * rows + h : c * rows + h + 1, :], rows, lists[...])
+    found = lookup(lambda c, h: disp[c * rows + h : c * rows + h + 1, :], range(rows), lists[...])
     quarter = lists.shape[0] // 4
     for b in range(4):
         for c in range(3):
@@ -122,7 +125,7 @@
     found = lookup(
         lambda c, h: coords[c * rows + h : c * rows + h + 1, :]
         + disp[c * rows + h : c * rows + h + 1, :],
-        rows,
+        range(rows),
         jnp.maximum(slot_node, 0),
     )
     for c in range(3):
@@ -227,21 +230,32 @@
     select[1] = jnp.transpose(onehot)
 
 
-def corner_forces(disp, recvs, nodes, thick, splat):
+def own_kernel(disp, nodes, found):
     rows = disp.shape[0] // 3
+    count = nodes.shape[0]
+    values = lookup(
+        lambda c, h: disp[c * rows + h : c * rows + h + 1, :], range(rows), nodes[...]
+    )
+    for c in range(3):
+        found[c * count : (c + 1) * count, :] = values[c]
+
+
+def corner_forces(found, rows, recvs, nodes, thick, splat):
     quarter = recvs[0].shape[0] // 3
     elem_rows = thick.shape[0]
 
     def table_row(c, h):
-        if h < rows:
-            return disp[c * rows + h : c * rows + h + 1, :]
         b, q = divmod(h - rows, quarter)
         return recvs[b][c * quarter + q : c * quarter + q + 1, :]
 
-    corners = [
-        lookup(table_row, rows + 4 * quarter, nodes[k * elem_rows : (k + 1) * elem_rows, :])
-        for k in range(4)
-    ]
+    count = nodes.shape[0]
+    corners = []
+    for k in range(4):
+        span = slice(k * elem_rows, (k + 1) * elem_rows)
+        own = [found[c * count + span.start : c * count + span.stop, :] for c in range(3)]
+        corners.append(
+            lookup(table_row, range(rows, rows + 4 * quarter), nodes[span, :], own)
+        )
     factor = thick[...]
     forces = []
     for i in range(12):
@@ -266,9 +280,9 @@
             outs[b][c * quarter : (c + 1) * quarter, :] = sums[c][start : start + quarter]
 
 
-def force_kernel(disp, recv1, recv3, recv0, recv2, nodes, thick, splat, held):
+def force_kernel(rows, found, recv1, recv3, recv0, recv2, nodes, thick, splat, held):
     elem_rows = thick.shape[0]
-    forces = corner_forces(disp, (recv0, recv1, recv2, recv3), nodes, thick, splat)
+    forces = corner_forces(found, rows, (recv0, recv1, recv2, recv3), nodes, thick, splat)
     for i in range(12):
         held[i * elem_rows : (i + 1) * elem_rows, :] = forces[i]
 
@@ -281,7 +295,8 @@
 
 
 def later_kernel(
-    disp,
+    rows,
+    found,
     recv1,
     recv3,
     recv0,
@@ -298,7 +313,7 @@
     out3,
 ):
     elem_rows = thick.shape[0]
-    forces = corner_forces(disp, (recv0, recv1, recv2, recv3), nodes, thick, splat)
+    forces = corner_forces(found, rows, (recv0, recv1, recv2, recv3), nodes, thick, splat)
     kept = slow[...] == 1
     forces = [
         jnp.where(kept, held[i * elem_rows : (i + 1) * elem_rows, :], forces[i])
@@ -552,10 +567,14 @@
             if first:
                 arrived = swap(outgoing, devices, capacity)
             recvs = exchange(sends)
-            field = [disp, *recvs, nodes, thickness, splat]
+            (found,) = call(own_kernel, [disp, nodes], [shape(12 * elem_rows, LANES)], "own_corners")
+            field = [found, *recvs, nodes, thickness, splat]
             if first:
                 (held,) = call(
-                    force_kernel, field, [shape(12 * elem_rows, LANES)], "forces"
+                    functools.partial(force_kernel, rows),
+                    field,
+                    [shape(12 * elem_rows, LANES)],
+                    "forces",
                 )
                 (pushes,) = call(
                     functools.partial(contact_kernel, tile_pairs.shape[1]),
@@ -570,7 +589,10 @@
                 )
             else:
                 own, *rest = call(
-                    later_kernel, field + [held, slow], [nodal] + sent, "forces_assemble"
+                    functools.partial(later_kernel, rows),
+                    field + [held, slow],
+                    [nodal] + sent,
+                    "forces_assemble",
                 )
             backs = exchange(rest[:4])
             inputs = [own, *backs]

time: 86 us -> 84.6 us (0.984)
  waiting for transfers between devices: 12.4 us -> 11.2 us
    ppermute x32, waiting for transfers between devices: 10.7 us -> 8.42 us  [exchange(): lax.ppermute(blocks[n], ('px', 'py'), swaps[n])]
    all_to_all x4, waiting for transfers between devices: 1.67 us -> 2.74 us  [swap(): return lax.all_to_all(slots, axes, 0, 0, tiled=True)]
    pallas_call x13 -> x17, Pallas kernels: 19.3 us -> 19.6 us  [call(): pl.pallas_call(kernel, out_shape=tuple(outputs), in_specs=specs, out_spec...]
  transfers between devices with their start and end apart: 36 -> 36, of which waited for: 12 -> 12; matrix products, arithmetic and copies ran while one was open for 0% -> 0% of each run, Pallas kernels for 5% -> 6%
where the time goes in v6:
time: 84.6 us; the launch traced here: 84.2 us
  starting transfers between devices  52.3 us (62%)
  Pallas kernels  19.6 us (23%)
  waiting for transfers between devices  11.2 us (13%)
  between operations  1 us (1%)
    ppermute x32, starting transfers between devices, exchange(): lax.ppermute(blocks[n], ('px', 'py'), swaps[n])  33.5 us
    pallas_call x17, Pallas kernels, call(): pl.pallas_call(kernel, out_shape=tuple(outputs), in_specs=specs, out_spec...  19.6 us
    all_to_all x4, starting transfers between devices, swap(): return lax.all_to_all(slots, axes, 0, 0, tiled=True)  18.8 us
    ppermute x32, waiting for transfers between devices, exchange(): lax.ppermute(blocks[n], ('px', 'py'), swaps[n])  8.42 us
    all_to_all x4, waiting for transfers between devices, swap(): return lax.all_to_all(slots, axes, 0, 0, tiled=True)  2.74 us
  transfers between devices with their start and end apart: 36, of which 12 were waited for; matrix products, arithmetic and copies ran while one was open for 0% of the time, Pallas kernels for 6%

profile of v6, /device:TPU:0, one launch (start us, length us, event | category | flops | bytes accessed | tf_op | source)
XLA Modules:
  0.0 84.2 jit_solution(13852483227110144345)
XLA Ops:
  0.6 2.8 %setup.1 = (f32[48,128]{1,0:T(8,128)}, f32[48,128]{1,0:T(8,128)}, f32[48,128]{1,0:T(8,128)}, f32[48,128]{1,0:T(8,128)}, s32[64,128]{1,0:T(8,128)}, /*index=5*/s3...) custom-call(f32[3,2048]{1,0:T(4,128)} %refs_0_.1, ...), custom_call_target="tpu_custom_call" | custom-call | tf_op jit(solution)/shard_map/setup/pallas_call | solution.py:451
  3.5 7.3 %all-to-all-start = ((f32[32,3,128]{2,1,0:T(4,128)}), f32[32,3,128]{2,1,0:T(4,128)S(1)}, u32[]{:S(2)}, u32[]{:S(2)}) async-start(f32[32,3,128]{2,1,0:T(4,128)} %get-tuple-element.68), calls=%async_computation | async-start | bytes 131072 | tf_op jit(solution)/shard_map/all_to_all | solution.py:486
  11.1 1.6 %collective-permute-start.1 = (f32[12,128]{1,0:T(8,128)S(1)}, f32[12,128]{1,0:T(8,128)S(1)}, u32[]{:S(2)}, u32[]{:S(2)}) collective-permute-start(f32[12,128]{1,0:T(8,128)S(1)} %copy-done.14), channel_id=1, source_target_pairs={{0,3},{1,2},{2,1},{3,0},{4,7},{5,6},{6,5},{7,4},{8,11},{9,10},{10,... | collective-permute-start | bytes 18440 | tf_op jit(solution)/shard_map/ppermute | solution.py:480
  12.8 2.3 %collective-permute-start.2 = (f32[12,128]{1,0:T(8,128)S(1)}, f32[12,128]{1,0:T(8,128)S(1)}, u32[]{:S(2)}, u32[]{:S(2)}) collective-permute-start(f32[12,128]{1,0:T(8,128)S(1)} %copy-done.13), channel_id=1, source_target_pairs={{0,4},{1,5},{2,6},{3,7},{4,0},{5,1},{6,2},{7,3},{8,12},{9,13},{10,... | collective-permute-start | bytes 18440 | tf_op jit(solution)/shard_map/ppermute | solution.py:480
  18.2 2.1 %contact.2.after = f32[32,3,128]{2,1,0:T(4,128)} custom-call(f32[2,128,128]{2,1,0:T(8,128)S(1)} %copy-done.2, f32[32,3,128]{2,1,0:T(4,128)S(1)} %all-to-all-done.arrived, f32[192,128]{1,0:T(8,128)S(1)} %forces.2.after.held), custom_call_target="tpu_custom_call" | custom-call | tf_op jit(solution)/shard_map/contact/pallas_call | solution.py:451
  20.3 3.7 %all-to-all-start.1 = ((f32[32,3,128]{2,1,0:T(4,128)}), f32[32,3,128]{2,1,0:T(4,128)S(1)}, u32[]{:S(2)}, u32[]{:S(2)}) async-start(f32[32,3,128]{2,1,0:T(4,128)} %contact.2.after), calls=%async_computation.1 | async-start | bytes 131072 | tf_op jit(solution)/shard_map/all_to_all | solution.py:486
  25.5 1.6 %collective-permute-start.5 = (f32[12,128]{1,0:T(8,128)S(1)}, f32[12,128]{1,0:T(8,128)S(1)}, u32[]{:S(2)}, u32[]{:S(2)}) collective-permute-start(f32[12,128]{1,0:T(8,128)S(1)} %get-tuple-element.71), channel_id=1, source_target_pairs={{0,3},{1,2},{2,1},{3,0},{4,7},{5,6},{6,5},{7,4},{8,11},{9,10},{10,... | collective-permute-start | bytes 18440 | tf_op jit(solution)/shard_map/ppermute | solution.py:480
  27.1 2.3 %collective-permute-start.6 = (f32[12,128]{1,0:T(8,128)S(1)}, f32[12,128]{1,0:T(8,128)S(1)}, u32[]{:S(2)}, u32[]{:S(2)}) collective-permute-start(f32[12,128]{1,0:T(8,128)S(1)} %get-tuple-element.72), channel_id=1, source_target_pairs={{0,4},{1,5},{2,6},{3,7},{4,0},{5,1},{6,2},{7,3},{8,12},{9,13},{10,... | collective-permute-start | bytes 18440 | tf_op jit(solution)/shard_map/ppermute | solution.py:480
  29.8 1.3 %collective-permute-done.6.refs_3_ = f32[12,128]{1,0:T(8,128)S(1)} collective-permute-done((f32[12,128]{1,0:T(8,128)S(1)}, f32[12,128]{1,0:T(8,128)S(1)}, u32[]{:S(2)}, u32[]{:S(2)}) %collective-permute-start.6) | collective-permute-done | bytes 6176 | tf_op jit(solution)/shard_map/ppermute | solution.py:480
  33.0 2.4 %collective-permute-start.10 = (f32[12,128]{1,0:T(8,128)S(1)}, f32[12,128]{1,0:T(8,128)S(1)}, u32[]{:S(2)}, u32[]{:S(2)}) collective-permute-start(f32[12,128]{1,0:T(8,128)S(1)} %get-tuple-element.81), channel_id=1, source_target_pairs={{0,4},{1,5},{2,6},{3,7},{4,0},{5,1},{6,2},{7,3},{8,12},{9,13},{10,... | collective-permute-start | bytes 18440 | tf_op jit(solution)/shard_map/ppermute | solution.py:480
  37.1 1.8 %forces_assemble.2 = (f32[48,128]{1,0:T(8,128)S(1)}, f32[12,128]{1,0:T(8,128)S(1)}, f32[12,128]{1,0:T(8,128)S(1)}, f32[12,128]{1,0:T(8,128)S(1)}, f32[12,128]{1,0:T(8,128)S(1)}) custom-call(f32[192,128]{1,0:T(8,128)S(1)} %own_corners.5.found, f32[12,128]{1,0:T(8,128)S(1)} %collective-permute-done.8.recv1, f32[12,128]{1,0:T(8,128)S(1)} %collective-permute-done.9.recv3, ...), custom_call_target="tpu_custom_call" | custom-call | tf_op jit(solution)/shard_map/forces_assemble/pallas_call | solution.py:451
  40.2 2.5 %collective-permute-start.14 = (f32[12,128]{1,0:T(8,128)S(1)}, f32[12,128]{1,0:T(8,128)S(1)}, u32[]{:S(2)}, u32[]{:S(2)}) collective-permute-start(f32[12,128]{1,0:T(8,128)S(1)} %get-tuple-element.87), channel_id=1, source_target_pairs={{0,4},{1,5},{2,6},{3,7},{4,0},{5,1},{6,2},{7,3},{8,12},{9,13},{10,... | collective-permute-start | bytes 18440 | tf_op jit(solution)/shard_map/ppermute | solution.py:480
  43.1 1.3 %collective-permute-done.14.refs_3_ = f32[12,128]{1,0:T(8,128)S(1)} collective-permute-done((f32[12,128]{1,0:T(8,128)S(1)}, f32[12,128]{1,0:T(8,128)S(1)}, u32[]{:S(2)}, u32[]{:S(2)}) %collective-permute-start.14) | collective-permute-done | bytes 6176 | tf_op jit(solution)/shard_map/ppermute | solution.py:480
  44.4 1.4 %update.5 = (f32[48,128]{1,0:T(8,128)S(1)}, f32[48,128]{1,0:T(8,128)S(1)}, f32[12,128]{1,0:T(8,128)S(1)}, f32[12,128]{1,0:T(8,128)S(1)}, f32[12,128]{1,0:T(8,128...) custom-call(f32[48,128]{1,0:T(8,128)S(1)} %get-tuple-element.84.refs_0_, ...), custom_call_target="tpu_custom_call" | custom-call | tf_op jit(solution)/shard_map/update/pallas_call | solution.py:451
  45.8 4.2 %all-to-all-start.2 = ((f32[32,3,128]{2,1,0:T(4,128)}), f32[32,3,128]{2,1,0:T(4,128)S(1)}, u32[]{:S(2)}, u32[]{:S(2)}) async-start(f32[32,3,128]{2,1,0:T(4,128)} %get-tuple-element.97), calls=%async_computation.2 | async-start | bytes 131072 | tf_op jit(solution)/shard_map/all_to_all | solution.py:486
  50.4 1.6 %collective-permute-start.17 = (f32[12,128]{1,0:T(8,128)S(1)}, f32[12,128]{1,0:T(8,128)S(1)}, u32[]{:S(2)}, u32[]{:S(2)}) collective-permute-start(f32[12,128]{1,0:T(8,128)S(1)} %get-tuple-element.94), channel_id=1, source_target_pairs={{0,3},{1,2},{2,1},{3,0},{4,7},{5,6},{6,5},{7,4},{8,11},{9,10},{10,... | collective-permute-start | bytes 18440 | tf_op jit(solution)/shard_map/ppermute | solution.py:480
  52.0 2.3 %collective-permute-start.18 = (f32[12,128]{1,0:T(8,128)S(1)}, f32[12,128]{1,0:T(8,128)S(1)}, u32[]{:S(2)}, u32[]{:S(2)}) collective-permute-start(f32[12,128]{1,0:T(8,128)S(1)} %get-tuple-element.95), channel_id=1, source_target_pairs={{0,4},{1,5},{2,6},{3,7},{4,0},{5,1},{6,2},{7,3},{8,12},{9,13},{10,... | collective-permute-start | bytes 18440 | tf_op jit(solution)/shard_map/ppermute | solution.py:480
  57.5 2.1 %contact.3.after = f32[32,3,128]{2,1,0:T(4,128)} custom-call(f32[2,128,128]{2,1,0:T(8,128)S(1)} %copy-done.2, f32[32,3,128]{2,1,0:T(4,128)S(1)} %all-to-all-done.2.arrived, f32[192,128]{1,0:T(8,128)S(1)} %forces.3.after.held), custom_call_target="tpu_custom_call" | custom-call | tf_op jit(solution)/shard_map/contact/pallas_call | solution.py:451
  59.6 3.6 %all-to-all-start.3 = ((f32[32,3,128]{2,1,0:T(4,128)}), f32[32,3,128]{2,1,0:T(4,128)S(1)}, u32[]{:S(2)}, u32[]{:S(2)}) async-start(f32[32,3,128]{2,1,0:T(4,128)} %contact.3.after), calls=%async_computation.3 | async-start | bytes 131072 | tf_op jit(solution)/shard_map/all_to_all | solution.py:486
  64.3 1.6 %collective-permute-start.21 = (f32[12,128]{1,0:T(8,128)S(1)}, f32[12,128]{1,0:T(8,128)S(1)}, u32[]{:S(2)}, u32[]{:S(2)}) collective-permute-start(f32[12,128]{1,0:T(8,128)S(1)} %get-tuple-element.100), channel_id=1, source_target_pairs={{0,3},{1,2},{2,1},{3,0},{4,7},{5,6},{6,5},{7,4},{8,11},{9,10},{10,... | collective-permute-start | bytes 18440 | tf_op jit(solution)/shard_map/ppermute | solution.py:480
  66.0 2.3 %collective-permute-start.22 = (f32[12,128]{1,0:T(8,128)S(1)}, f32[12,128]{1,0:T(8,128)S(1)}, u32[]{:S(2)}, u32[]{:S(2)}) collective-permute-start(f32[12,128]{1,0:T(8,128)S(1)} %get-tuple-element.101), channel_id=1, source_target_pairs={{0,4},{1,5},{2,6},{3,7},{4,0},{5,1},{6,2},{7,3},{8,12},{9,13},{10,... | collective-permute-start | bytes 18440 | tf_op jit(solution)/shard_map/ppermute | solution.py:480
  71.8 2.4 %collective-permute-start.26 = (f32[12,128]{1,0:T(8,128)S(1)}, f32[12,128]{1,0:T(8,128)S(1)}, u32[]{:S(2)}, u32[]{:S(2)}) collective-permute-start(f32[12,128]{1,0:T(8,128)S(1)} %get-tuple-element.107), channel_id=1, source_target_pairs={{0,4},{1,5},{2,6},{3,7},{4,0},{5,1},{6,2},{7,3},{8,12},{9,13},{10,... | collective-permute-start | bytes 18440 | tf_op jit(solution)/shard_map/ppermute | solution.py:480
  75.9 1.8 %forces_assemble.3 = (f32[48,128]{1,0:T(8,128)S(1)}, f32[12,128]{1,0:T(8,128)S(1)}, f32[12,128]{1,0:T(8,128)S(1)}, f32[12,128]{1,0:T(8,128)S(1)}, f32[12,128]{1,0:T(8,128)S(1)}) custom-call(f32[192,128]{1,0:T(8,128)S(1)} %own_corners.7.found, f32[12,128]{1,0:T(8,128)S(1)} %collective-permute-done.24.recv1, f32[12,128]{1,0:T(8,128)S(1)} %collective-permute-done.25.recv3, ...), custom_call_target="tpu_custom_call" | custom-call | tf_op jit(solution)/shard_map/forces_assemble/pallas_call | solution.py:451
  79.0 2.5 %collective-permute-start.30 = (f32[12,128]{1,0:T(8,128)S(1)}, f32[12,128]{1,0:T(8,128)S(1)}, u32[]{:S(2)}, u32[]{:S(2)}) collective-permute-start(f32[12,128]{1,0:T(8,128)S(1)} %get-tuple-element.112), channel_id=1, source_target_pairs={{0,4},{1,5},{2,6},{3,7},{4,0},{5,1},{6,2},{7,3},{8,12},{9,13},{10,... | collective-permute-start | bytes 18440 | tf_op jit(solution)/shard_map/ppermute | solution.py:480
  (97 shorter events, 24.1 us)
Async XLA Ops:
  3.5 14.7 %all-to-all-start = ((f32[32,3,128]{2,1,0:T(4,128)}), f32[32,3,128]{2,1,0:T(4,128)S(1)}, u32[]{:S(2)}, u32[]{:S(2)}) async-start(f32[32,3,128]{2,1,0:T(4,128)} %get-tuple-element.68), calls=%async_computation | async-start | bytes 131072 | tf_op jit(solution)/shard_map/all_to_all | solution.py:486
  10.8 5.1 %collective-permute-start = (f32[12,128]{1,0:T(8,128)S(1)}, f32[12,128]{1,0:T(8,128)S(1)}, u32[]{:S(2)}, u32[]{:S(2)}) collective-permute-start(f32[12,128]{1,0:T(8,128)S(1)} %copy-done.15), channel_id=1, source_target_pairs={{0,1},{1,0},{2,3},{3,2},{4,8},{5,9},{6,10},{7,11},{8,4},{9,5},{10,... | collective-permute-start | bytes 18440 | tf_op jit(solution)/shard_map/ppermute | solution.py:480
  11.1 4.8 %collective-permute-start.1 = (f32[12,128]{1,0:T(8,128)S(1)}, f32[12,128]{1,0:T(8,128)S(1)}, u32[]{:S(2)}, u32[]{:S(2)}) collective-permute-start(f32[12,128]{1,0:T(8,128)S(1)} %copy-done.14), channel_id=1, source_target_pairs={{0,3},{1,2},{2,1},{3,0},{4,7},{5,6},{6,5},{7,4},{8,11},{9,10},{10,... | collective-permute-start | bytes 18440 | tf_op jit(solution)/shard_map/ppermute | solution.py:480
  12.8 4.0 %collective-permute-start.2 = (f32[12,128]{1,0:T(8,128)S(1)}, f32[12,128]{1,0:T(8,128)S(1)}, u32[]{:S(2)}, u32[]{:S(2)}) collective-permute-start(f32[12,128]{1,0:T(8,128)S(1)} %copy-done.13), channel_id=1, source_target_pairs={{0,4},{1,5},{2,6},{3,7},{4,0},{5,1},{6,2},{7,3},{8,12},{9,13},{10,... | collective-permute-start | bytes 18440 | tf_op jit(solution)/shard_map/ppermute | solution.py:480
  20.3 11.2 %all-to-all-start.1 = ((f32[32,3,128]{2,1,0:T(4,128)}), f32[32,3,128]{2,1,0:T(4,128)S(1)}, u32[]{:S(2)}, u32[]{:S(2)}) async-start(f32[32,3,128]{2,1,0:T(4,128)} %contact.2.after), calls=%async_computation.1 | async-start | bytes 131072 | tf_op jit(solution)/shard_map/all_to_all | solution.py:486
  25.2 4.6 %collective-permute-start.4 = (f32[12,128]{1,0:T(8,128)S(1)}, f32[12,128]{1,0:T(8,128)S(1)}, u32[]{:S(2)}, u32[]{:S(2)}) collective-permute-start(f32[12,128]{1,0:T(8,128)S(1)} %get-tuple-element.70), channel_id=1, source_target_pairs={{0,1},{1,0},{2,3},{3,2},{4,8},{5,9},{6,10},{7,11},{8,4},{9,5},{10,... | collective-permute-start | bytes 18440 | tf_op jit(solution)/shard_map/ppermute | solution.py:480
  25.5 4.3 %collective-permute-start.5 = (f32[12,128]{1,0:T(8,128)S(1)}, f32[12,128]{1,0:T(8,128)S(1)}, u32[]{:S(2)}, u32[]{:S(2)}) collective-permute-start(f32[12,128]{1,0:T(8,128)S(1)} %get-tuple-element.71), channel_id=1, source_target_pairs={{0,3},{1,2},{2,1},{3,0},{4,7},{5,6},{6,5},{7,4},{8,11},{9,10},{10,... | collective-permute-start | bytes 18440 | tf_op jit(solution)/shard_map/ppermute | solution.py:480
  27.1 4.0 %collective-permute-start.6 = (f32[12,128]{1,0:T(8,128)S(1)}, f32[12,128]{1,0:T(8,128)S(1)}, u32[]{:S(2)}, u32[]{:S(2)}) collective-permute-start(f32[12,128]{1,0:T(8,128)S(1)} %get-tuple-element.72), channel_id=1, source_target_pairs={{0,4},{1,5},{2,6},{3,7},{4,0},{5,1},{6,2},{7,3},{8,12},{9,13},{10,... | collective-permute-start | bytes 18440 | tf_op jit(solution)/shard_map/ppermute | solution.py:480
  32.3 4.0 %collective-permute-start.8 = (f32[12,128]{1,0:T(8,128)S(1)}, f32[12,128]{1,0:T(8,128)S(1)}, u32[]{:S(2)}, u32[]{:S(2)}) collective-permute-start(f32[12,128]{1,0:T(8,128)S(1)} %get-tuple-element.79), channel_id=1, source_target_pairs={{0,1},{1,0},{2,3},{3,2},{4,8},{5,9},{6,10},{7,11},{8,4},{9,5},{10,... | collective-permute-start | bytes 18440 | tf_op jit(solution)/shard_map/ppermute | solution.py:480
  33.0 4.2 %collective-permute-start.10 = (f32[12,128]{1,0:T(8,128)S(1)}, f32[12,128]{1,0:T(8,128)S(1)}, u32[]{:S(2)}, u32[]{:S(2)}) collective-permute-start(f32[12,128]{1,0:T(8,128)S(1)} %get-tuple-element.81), channel_id=1, source_target_pairs={{0,4},{1,5},{2,6},{3,7},{4,0},{5,1},{6,2},{7,3},{8,12},{9,13},{10,... | collective-permute-start | bytes 18440 | tf_op jit(solution)/shard_map/ppermute | solution.py:480
  38.9 4.2 %collective-permute-start.12 = (f32[12,128]{1,0:T(8,128)S(1)}, f32[12,128]{1,0:T(8,128)S(1)}, u32[]{:S(2)}, u32[]{:S(2)}) collective-permute-start(f32[12,128]{1,0:T(8,128)S(1)} %get-tuple-element.85), channel_id=1, source_target_pairs={{0,1},{1,0},{2,3},{3,2},{4,8},{5,9},{6,10},{7,11},{8,4},{9,5},{10,... | collective-permute-start | bytes 18440 | tf_op jit(solution)/shard_map/ppermute | solution.py:480
  39.1 4.0 %collective-permute-start.13 = (f32[12,128]{1,0:T(8,128)S(1)}, f32[12,128]{1,0:T(8,128)S(1)}, u32[]{:S(2)}, u32[]{:S(2)}) collective-permute-start(f32[12,128]{1,0:T(8,128)S(1)} %get-tuple-element.86), channel_id=1, source_target_pairs={{0,3},{1,2},{2,1},{3,0},{4,7},{5,6},{6,5},{7,4},{8,11},{9,10},{10,... | collective-permute-start | bytes 18440 | tf_op jit(solution)/shard_map/ppermute | solution.py:480
  40.2 4.2 %collective-permute-start.14 = (f32[12,128]{1,0:T(8,128)S(1)}, f32[12,128]{1,0:T(8,128)S(1)}, u32[]{:S(2)}, u32[]{:S(2)}) collective-permute-start(f32[12,128]{1,0:T(8,128)S(1)} %get-tuple-element.87), channel_id=1, source_target_pairs={{0,4},{1,5},{2,6},{3,7},{4,0},{5,1},{6,2},{7,3},{8,12},{9,13},{10,... | collective-permute-start | bytes 18440 | tf_op jit(solution)/shard_map/ppermute | solution.py:480
  45.8 11.7 %all-to-all-start.2 = ((f32[32,3,128]{2,1,0:T(4,128)}), f32[32,3,128]{2,1,0:T(4,128)S(1)}, u32[]{:S(2)}, u32[]{:S(2)}) async-start(f32[32,3,128]{2,1,0:T(4,128)} %get-tuple-element.97), calls=%async_computation.2 | async-start | bytes 131072 | tf_op jit(solution)/shard_map/all_to_all | solution.py:486
  50.1 5.1 %collective-permute-start.16 = (f32[12,128]{1,0:T(8,128)S(1)}, f32[12,128]{1,0:T(8,128)S(1)}, u32[]{:S(2)}, u32[]{:S(2)}) collective-permute-start(f32[12,128]{1,0:T(8,128)S(1)} %get-tuple-element.93), channel_id=1, source_target_pairs={{0,1},{1,0},{2,3},{3,2},{4,8},{5,9},{6,10},{7,11},{8,4},{9,5},{10,... | collective-permute-start | bytes 18440 | tf_op jit(solution)/shard_map/ppermute | solution.py:480
  50.4 4.8 %collective-permute-start.17 = (f32[12,128]{1,0:T(8,128)S(1)}, f32[12,128]{1,0:T(8,128)S(1)}, u32[]{:S(2)}, u32[]{:S(2)}) collective-permute-start(f32[12,128]{1,0:T(8,128)S(1)} %get-tuple-element.94), channel_id=1, source_target_pairs={{0,3},{1,2},{2,1},{3,0},{4,7},{5,6},{6,5},{7,4},{8,11},{9,10},{10,... | collective-permute-start | bytes 18440 | tf_op jit(solution)/shard_map/ppermute | solution.py:480
  52.0 4.0 %collective-permute-start.18 = (f32[12,128]{1,0:T(8,128)S(1)}, f32[12,128]{1,0:T(8,128)S(1)}, u32[]{:S(2)}, u32[]{:S(2)}) collective-permute-start(f32[12,128]{1,0:T(8,128)S(1)} %get-tuple-element.95), channel_id=1, source_target_pairs={{0,4},{1,5},{2,6},{3,7},{4,0},{5,1},{6,2},{7,3},{8,12},{9,13},{10,... | collective-permute-start | bytes 18440 | tf_op jit(solution)/shard_map/ppermute | solution.py:480
  59.6 10.8 %all-to-all-start.3 = ((f32[32,3,128]{2,1,0:T(4,128)}), f32[32,3,128]{2,1,0:T(4,128)S(1)}, u32[]{:S(2)}, u32[]{:S(2)}) async-start(f32[32,3,128]{2,1,0:T(4,128)} %contact.3.after), calls=%async_computation.3 | async-start | bytes 131072 | tf_op jit(solution)/shard_map/all_to_all | solution.py:486
  64.2 4.4 %collective-permute-start.20 = (f32[12,128]{1,0:T(8,128)S(1)}, f32[12,128]{1,0:T(8,128)S(1)}, u32[]{:S(2)}, u32[]{:S(2)}) collective-permute-start(f32[12,128]{1,0:T(8,128)S(1)} %get-tuple-element.99), channel_id=1, source_target_pairs={{0,1},{1,0},{2,3},{3,2},{4,8},{5,9},{6,10},{7,11},{8,4},{9,5},{10,... | collective-permute-start | bytes 18440 | tf_op jit(solution)/shard_map/ppermute | solution.py:480
  64.3 4.3 %collective-permute-start.21 = (f32[12,128]{1,0:T(8,128)S(1)}, f32[12,128]{1,0:T(8,128)S(1)}, u32[]{:S(2)}, u32[]{:S(2)}) collective-permute-start(f32[12,128]{1,0:T(8,128)S(1)} %get-tuple-element.100), channel_id=1, source_target_pairs={{0,3},{1,2},{2,1},{3,0},{4,7},{5,6},{6,5},{7,4},{8,11},{9,10},{10,... | collective-permute-start | bytes 18440 | tf_op jit(solution)/shard_map/ppermute | solution.py:480
  71.8 4.1 %collective-permute-start.26 = (f32[12,128]{1,0:T(8,128)S(1)}, f32[12,128]{1,0:T(8,128)S(1)}, u32[]{:S(2)}, u32[]{:S(2)}) collective-permute-start(f32[12,128]{1,0:T(8,128)S(1)} %get-tuple-element.107), channel_id=1, source_target_pairs={{0,4},{1,5},{2,6},{3,7},{4,0},{5,1},{6,2},{7,3},{8,12},{9,13},{10,... | collective-permute-start | bytes 18440 | tf_op jit(solution)/shard_map/ppermute | solution.py:480
  77.7 4.2 %collective-permute-start.28 = (f32[12,128]{1,0:T(8,128)S(1)}, f32[12,128]{1,0:T(8,128)S(1)}, u32[]{:S(2)}, u32[]{:S(2)}) collective-permute-start(f32[12,128]{1,0:T(8,128)S(1)} %get-tuple-element.110), channel_id=1, source_target_pairs={{0,1},{1,0},{2,3},{3,2},{4,8},{5,9},{6,10},{7,11},{8,4},{9,5},{10,... | collective-permute-start | bytes 18440 | tf_op jit(solution)/shard_map/ppermute | solution.py:480
  77.9 4.0 %collective-permute-start.29 = (f32[12,128]{1,0:T(8,128)S(1)}, f32[12,128]{1,0:T(8,128)S(1)}, u32[]{:S(2)}, u32[]{:S(2)}) collective-permute-start(f32[12,128]{1,0:T(8,128)S(1)} %get-tuple-element.111), channel_id=1, source_target_pairs={{0,3},{1,2},{2,1},{3,0},{4,7},{5,6},{6,5},{7,4},{8,11},{9,10},{10,... | collective-permute-start | bytes 18440 | tf_op jit(solution)/shard_map/ppermute | solution.py:480
  79.0 4.2 %collective-permute-start.30 = (f32[12,128]{1,0:T(8,128)S(1)}, f32[12,128]{1,0:T(8,128)S(1)}, u32[]{:S(2)}, u32[]{:S(2)}) collective-permute-start(f32[12,128]{1,0:T(8,128)S(1)} %get-tuple-element.112), channel_id=1, source_target_pairs={{0,4},{1,5},{2,6},{3,7},{4,0},{5,1},{6,2},{7,3},{8,12},{9,13},{10,... | collective-permute-start | bytes 18440 | tf_op jit(solution)/shard_map/ppermute | solution.py:480
  (28 other events, 137.5 us)

commit v7 on v6

--- a/solution.py
+++ b/solution.py
@@ -50,8 +50,9 @@
     return [top, values - top]
 
 
-def scatter_dot(hi_rows, lo_rows, value_rows, rows, total=None):
-    row_no = lax.broadcasted_iota(I32, (rows, LANES), 0)
+def scatter_dot(hi_rows, lo_rows, value_rows, rows, first=0):
+    row_no = first + lax.broadcasted_iota(I32, (rows, LANES), 0)
+    total = None
     lane_no = lax.broadcasted_iota(I32, (LANES, LANES), 0)
     group = 2
     for start in range(0, len(hi_rows), group):
@@ -78,28 +79,21 @@
     return total
 
 
-def scatter_some(index_row, value_row, numbers, rows, total=None):
+def scatter_add(index_row, value_row, count, rows, first=0):
     hi_rows, lo_rows = [], []
     value_rows = [[] for _ in range(6)]
-    for r in numbers:
+    for r in range(count):
         idx = index_row(r)
         hi_rows.append(idx >> 7)
         lo_rows.append(idx & (LANES - 1))
         for c in range(3):
             for part, vals in enumerate(halves(value_row(c, r))):
                 value_rows[2 * c + part].append(vals)
-    return scatter_dot(hi_rows, lo_rows, value_rows, rows, total)
-
-
-def add_halves(total, rows):
+    total = scatter_dot(hi_rows, lo_rows, value_rows, rows, first)
     return [
         total[2 * c * rows : (2 * c + 1) * rows] + total[(2 * c + 1) * rows : (2 * c + 2) * rows]
         for c in range(3)
     ]
-
-
-def scatter_add(index_row, value_row, count, rows):
-    return add_halves(scatter_some(index_row, value_row, range(count), rows), rows)
 
 
 def spread_rows(source, target, groups):
@@ -119,17 +113,11 @@
             sends[b][c * quarter : (c + 1) * quarter, :] = found[c][b * quarter : (b + 1) * quarter]
 
 
-def gather_slots(coords, disp, rows, inverse, outgoing):
+def gather_slots(position_row, rows, inverse, outgoing):
     slot_node = inverse[...]
-    used = slot_node >= 0
-    found = lookup(
-        lambda c, h: coords[c * rows + h : c * rows + h + 1, :]
-        + disp[c * rows + h : c * rows + h + 1, :],
-        range(rows),
-        jnp.maximum(slot_node, 0),
-    )
+    found = lookup(position_row, range(rows), jnp.maximum(slot_node, 0))
     for c in range(3):
-        outgoing[:, c, :] = jnp.where(used, found[c], FAR)
+        outgoing[:, c, :] = jnp.where(slot_node >= 0, found[c], FAR)
 
 
 def block_remap(index, own_count, width, px_no, py_no, px_count, py_count):
@@ -143,49 +131,18 @@
     return jnp.where(index < own_count, index, moved)
 
 
-def setup_kernel(devices, capacity, counts, *refs):
-    sources = refs[:11]
-    (coords, disp, vel, ext, nodes, lists, inverse, outgoing, splat, slow, select) = refs[11:22]
-    sends = refs[22:26]
-    buffers = refs[26:37]
-    sems = refs[37]
-    (coords_in, disp_in, vel_in, ext_in, nodes_in, lists_in, bucket, contact_nodes) = buffers[:8]
-    (stiff, classes, pairs) = buffers[8:]
+def slots_kernel(devices, capacity, *refs):
+    sources, (inverse, outgoing) = refs[:4], refs[4:6]
+    buffers, sems = refs[6:10], refs[10]
+    coords, disp, bucket, contact_nodes = buffers
     copies = [
         pltpu.make_async_copy(source, target, sems.at[n])
         for n, (source, target) in enumerate(zip(sources, buffers))
     ]
     for copy in copies:
         copy.start()
-    copies[1].wait()
-    copies[5].wait()
-    px_no = lax.axis_index("px")
-    py_no = lax.axis_index("py")
-    own_count = coords_in.shape[1]
-    rows = own_count // LANES
-    spread_rows(disp_in, disp, 3)
-    width = lists_in.shape[1]
-    quarter = width // LANES
-    for b in range(4):
-        place = px_no if b < 2 else py_no
-        count = counts[b // 2]
-        to_high = (place & 1) ^ (1 - b % 2)
-        row = (b // 2) * 2
-        missing = (place == to_high * (count - 1)).astype(I32)
-        for q in range(quarter):
-            span = slice(q * LANES, (q + 1) * LANES)
-            chosen = jnp.where(
-                jnp.full((1, LANES), to_high) == 1,
-                lists_in[row + 1 : row + 2, span],
-                lists_in[row : row + 1, span],
-            )
-            lists[b * quarter + q : b * quarter + q + 1, :] = jnp.where(
-                jnp.full((1, LANES), missing) == 1, -1, chosen
-            )
-    gather_halo(disp, rows, lists, sends)
-    for n in (0, 6, 7):
-        copies[n].wait()
-    spread_rows(coords_in, coords, 3)
+    for copy in copies[2:]:
+        copy.wait()
     count = bucket.shape[0]
     slot_rows = inverse.shape[0]
     dev_no = lax.broadcasted_iota(I32, (devices, LANES), 0)
@@ -208,18 +165,57 @@
         digits[1].append((value & 63).astype(F32))
     total = scatter_dot(hi_rows, lo_rows, digits, slot_rows)
     inverse[...] = (total[:slot_rows] * 64.0 + total[slot_rows:]).astype(I32) - 1
-    gather_slots(coords, disp, rows, inverse, outgoing)
-    for n in (2, 3, 4, 8, 9, 10):
-        copies[n].wait()
+    for copy in copies[:2]:
+        copy.wait()
+
+    def position_row(c, h):
+        span = slice(h * LANES, (h + 1) * LANES)
+        return coords[c : c + 1, span] + disp[c : c + 1, span]
+
+    gather_slots(position_row, coords.shape[1] // LANES, inverse, outgoing)
+
+
+def halo_kernel(
+    counts, disp_in, lists_in, nodes_in, stiff, after, disp, lists, nodes, splat, *sends
+):
+    px_no = lax.axis_index("px")
+    py_no = lax.axis_index("py")
+    own_count = disp_in.shape[1]
+    rows = own_count // LANES
+    spread_rows(disp_in, disp, 3)
+    width = lists_in.shape[1]
+    quarter = width // LANES
+    for b in range(4):
+        place = px_no if b < 2 else py_no
+        count = counts[b // 2]
+        to_high = (place & 1) ^ (1 - b % 2)
+        row = (b // 2) * 2
+        missing = (place == to_high * (count - 1)).astype(I32)
+        for q in range(quarter):
+            span = slice(q * LANES, (q + 1) * LANES)
+            chosen = jnp.where(
+                jnp.full((1, LANES), to_high) == 1,
+                lists_in[row + 1 : row + 2, span],
+                lists_in[row : row + 1, span],
+            )
+            lists[b * quarter + q : b * quarter + q + 1, :] = jnp.where(
+                jnp.full((1, LANES), missing) == 1, -1, chosen
+            )
+    gather_halo(disp, rows, lists, sends)
     spread_rows(nodes_in, nodes, 4)
     nodes[...] = block_remap(nodes[...], own_count, width, px_no, py_no, *counts)
-    spread_rows(vel_in, vel, 3)
-    spread_rows(ext_in, ext, 3)
     size = stiff.shape[0]
     for j in range(size):
         splat[j * size : (j + 1) * size, :] = jnp.broadcast_to(stiff[:, j : j + 1], (size, LANES))
-    for h in range(slow.shape[0]):
-        slow[h : h + 1, :] = jnp.full((1, LANES), classes[h])
+
+
+def rest_kernel(coords_in, vel_in, ext_in, classes, pairs, after, coords, vel, ext, slow, select):
+    spread_rows(coords_in, coords, 3)
+    spread_rows(vel_in, vel, 3)
+    spread_rows(ext_in, ext, 3)
+    blocks = classes.shape[1]
+    row = jnp.concatenate([classes[...], jnp.zeros((1, LANES - blocks), I32)], axis=1)
+    slow[...] = jnp.transpose(jnp.broadcast_to(row, (LANES, LANES)))[:blocks]
     ends = [pairs[0:1, :], pairs[1:2, :]]
     short = LANES - 2 * pairs.shape[1]
     if short:
@@ -267,17 +263,26 @@
     return forces
 
 
-def assemble(force_row, nodes, own, outs):
+def stored_row(forces, nodes):
+    count = nodes.shape[0]
+    return lambda c, r: forces[c * count + r : c * count + r + 1, :]
+
+
+def sum_own(force_row, nodes, own):
     rows = own.shape[0] // 3
+    sums = scatter_add(lambda r: nodes[r : r + 1, :], force_row, nodes.shape[0], rows)
+    for c in range(3):
+        own[c * rows : (c + 1) * rows, :] = sums[c]
+
+
+def sum_halo(force_row, nodes, rows, outs):
     quarter = outs[0].shape[0] // 3
     sums = scatter_add(
-        lambda r: nodes[r : r + 1, :], force_row, nodes.shape[0], rows + 4 * quarter
+        lambda r: nodes[r : r + 1, :], force_row, nodes.shape[0], 4 * quarter, rows
     )
     for c in range(3):
-        own[c * rows : (c + 1) * rows, :] = sums[c][:rows]
         for b in range(4):
-            start = rows + b * quarter
-            outs[b][c * quarter : (c + 1) * quarter, :] = sums[c][start : start + quarter]
+            outs[b][c * quarter : (c + 1) * quarter, :] = sums[c][b * quarter : (b + 1) * quarter]
 
 
 def force_kernel(rows, found, recv1, recv3, recv0, recv2, nodes, thick, splat, held):
@@ -287,11 +292,12 @@
         held[i * elem_rows : (i + 1) * elem_rows, :] = forces[i]
 
 
-def assemble_kernel(held, nodes, after, own, out0, out1, out2, out3):
-    count = nodes.shape[0]
-    assemble(
-        lambda c, r: held[c * count + r : c * count + r + 1, :], nodes, own, (out0, out1, out2, out3)
-    )
+def halo_sum_kernel(rows, held, nodes, after, *outs):
+    sum_halo(stored_row(held, nodes), nodes, rows, outs)
+
+
+def own_sum_kernel(held, nodes, after, own):
+    sum_own(stored_row(held, nodes), nodes, own)
 
 
 def later_kernel(
@@ -306,25 +312,44 @@
     splat,
     held,
     slow,
-    own,
-    out0,
-    out1,
-    out2,
-    out3,
+    mixed,
+    *outs,
 ):
     elem_rows = thick.shape[0]
     forces = corner_forces(found, rows, (recv0, recv1, recv2, recv3), nodes, thick, splat)
     kept = slow[...] == 1
-    forces = [
-        jnp.where(kept, held[i * elem_rows : (i + 1) * elem_rows, :], forces[i])
-        for i in range(12)
-    ]
+    for i in range(12):
+        span = slice(i * elem_rows, (i + 1) * elem_rows)
+        forces[i] = jnp.where(kept, held[span, :], forces[i])
+        mixed[span, :] = forces[i]
 
     def force_row(c, r):
         k, h = divmod(r, elem_rows)
         return forces[c * 4 + k][h : h + 1, :]
 
-    assemble(force_row, nodes, own, (out0, out1, out2, out3))
+    sum_halo(force_row, nodes, rows, outs)
+
+
+def returned_sums(backs, lists, rows):
+    quarter = backs[0].shape[0] // 3
+
+    def back_row(c, r):
+        b, q = divmod(r, quarter)
+        return backs[b][c * quarter + q : c * quarter + q + 1, :]
+
+    return scatter_add(lambda r: lists[r : r + 1, :], back_row, 4 * quarter, rows)
+
+
+def internal_kernel(own, back1, back3, back0, back2, lists, internal):
+    rows = own.shape[0] // 3
+    sums = returned_sums((back0, back1, back2, back3), lists, rows)
+    for c in range(3):
+        span = slice(c * rows, (c + 1) * rows)
+        internal[span, :] = own[span, :] + sums[c]
+
+
+def sends_kernel(disp, lists, after, *sends):
+    gather_halo(disp, disp.shape[0] // 3, lists, sends)
 
 
 def thirds(values):
@@ -379,58 +404,68 @@
         pushes[:, c, :] = total[:, c * LANES : (c + 1) * LANES]
 
 
-def update_kernel(first, last, final, *refs):
-    refs = list(refs)
-    own, back1, back3, back0, back2, lists, ext, inv_mass, vel, disp = refs[:10]
-    refs = refs[10:]
-    if first:
-        returned, inverse = refs[:2]
-        refs = refs[2:]
-    else:
-        contact_in = refs.pop(0)
-    if last and not final:
-        coords, inverse = refs[:2]
-        refs = refs[2:]
-    backs = (back0, back1, back2, back3)
-    rows = disp.shape[0] // 3
-    quarter = back0.shape[0] // 3
-    new_vel, new_disp = refs[:2]
-    refs = refs[2:]
-
-    def back_row(c, r):
-        b, q = divmod(r, quarter)
-        return backs[b][c * quarter + q : c * quarter + q + 1, :]
-
-    halo = scatter_add(lambda r: lists[r : r + 1, :], back_row, 4 * quarter, rows)
-    if first:
-        contact_out = refs.pop(0)
-        contact = scatter_add(
-            lambda r: inverse[r : r + 1, :],
-            lambda c, r: returned[r, c : c + 1, :],
-            inverse.shape[0],
-            rows,
-        )
-        for c in range(3):
-            contact_out[c * rows : (c + 1) * rows, :] = contact[c]
-    else:
-        contact = [contact_in[c * rows : (c + 1) * rows, :] for c in range(3)]
+def advance(internal, contact, ext, inv_mass, vel, disp, rows):
     for c in range(3):
         span = slice(c * rows, (c + 1) * rows)
-        internal = own[span, :] + halo[c]
-        accel = inv_mass[...] * (ext[span, :] - internal + contact[c])
+        accel = inv_mass[...] * (ext[span, :] - internal[c] + contact[c])
         vel_c = vel[span, :] + DT * accel
-        disp_c = disp[span, :] + DT * vel_c
-        if final:
+        yield c, vel_c, disp[span, :] + DT * vel_c
+
+
+def components(array):
+    rows = array.shape[0] // 3
+    return [array[c * rows : (c + 1) * rows, :] for c in range(3)]
+
+
+def first_update_kernel(
+    internal, returned, inverse, lists, ext, inv_mass, vel, disp, new_vel, new_disp, contact, *sends
+):
+    rows = disp.shape[0] // 3
+    sums = scatter_add(
+        lambda r: inverse[r : r + 1, :],
+        lambda c, r: returned[r, c : c + 1, :],
+        inverse.shape[0],
+        rows,
+    )
+    steps = advance(components(internal), sums, ext, inv_mass, vel, disp, rows)
+    for c, vel_c, disp_c in steps:
+        span = slice(c * rows, (c + 1) * rows)
+        contact[span, :] = sums[c]
+        new_vel[span, :] = vel_c
+        new_disp[span, :] = disp_c
+    gather_halo(new_disp, rows, lists, sends)
+
+
+def update_kernel(case, *refs):
+    refs = list(refs)
+    own, back1, back3, back0, back2, lists, ext, inv_mass, vel, disp, contact = refs[:11]
+    rows = disp.shape[0] // 3
+    sums = returned_sums((back0, back1, back2, back3), lists, rows)
+    internal = [mine + more for mine, more in zip(components(own), sums)]
+    steps = advance(internal, components(contact), ext, inv_mass, vel, disp, rows)
+    if case == "final":
+        new_vel, new_disp = refs[11:]
+        for c, vel_c, disp_c in steps:
             for h in range(rows):
                 new_vel[c : c + 1, h * LANES : (h + 1) * LANES] = vel_c[h : h + 1, :]
                 new_disp[c : c + 1, h * LANES : (h + 1) * LANES] = disp_c[h : h + 1, :]
-        else:
-            new_vel[span, :] = vel_c
-            new_disp[span, :] = disp_c
-    if not final:
-        gather_halo(new_disp, rows, lists, refs[:4])
-        if last:
-            gather_slots(coords, new_disp, rows, inverse, refs[4])
+        return
+    if case == "last":
+        coords, inverse, new_vel, new_disp, outgoing = refs[11:]
+    else:
+        new_vel, new_disp, *sends = refs[11:]
+    for c, vel_c, disp_c in steps:
+        new_vel[c * rows : (c + 1) * rows, :] = vel_c
+        new_disp[c * rows : (c + 1) * rows, :] = disp_c
+    if case == "last":
+
+        def position_row(c, h):
+            span = slice(c * rows + h, c * rows + h + 1)
+            return coords[span, :] + new_disp[span, :]
+
+        gather_slots(position_row, rows, inverse, outgoing)
+    else:
+        gather_halo(new_disp, rows, lists, sends)
 
 
 def vmem(count):
@@ -521,43 +556,45 @@
     sent = [shape(3 * quarter, LANES)] * 4
     slots = shape(slot_rows, 3, LANES)
 
+    counts = (lax.axis_size("px"), lax.axis_size("py"))
+    corner_values = shape(12 * elem_rows, LANES)
+
     sources = [
         coords,
         displacement,
-        velocity,
-        ext_force,
-        elem_nodes,
-        halo_lists,
         contact_bucket.reshape(-1, LANES),
         contact_nodes.reshape(-1, LANES),
-        stiffness,
-        block_class,
-        tile_pairs,
     ]
-    memories = [pltpu.SMEM if source is block_class else pltpu.VMEM for source in sources]
-    coords, disp, vel, ext, nodes, lists, inverse, outgoing, splat, slow, select, *sends = call(
-        functools.partial(
-            setup_kernel, devices, capacity, (lax.axis_size("px"), lax.axis_size("py"))
-        ),
+    inverse, outgoing = call(
+        functools.partial(slots_kernel, devices, capacity),
         sources,
-        [nodal] * 4
-        + [
+        [jax.ShapeDtypeStruct((slot_rows, LANES), I32), slots],
+        "slots",
+        far=range(4),
+        scratch=[pltpu.VMEM(source.shape, source.dtype) for source in sources]
+        + [pltpu.SemaphoreType.DMA((4,))],
+        vmem_bytes=WHOLE_VMEM,
+    )
+    disp, lists, nodes, splat, *sends = call(
+        functools.partial(halo_kernel, counts),
+        [displacement, halo_lists, elem_nodes, stiffness, inverse],
+        [
+            nodal,
+            jax.ShapeDtypeStruct((4 * quarter, LANES), I32),
             jax.ShapeDtypeStruct((4 * elem_rows, LANES), I32),
-            jax.ShapeDtypeStruct((4 * quarter, LANES), I32),
-            jax.ShapeDtypeStruct((slot_rows, LANES), I32),
-            slots,
             shape(144, LANES),
-            jax.ShapeDtypeStruct((elem_rows, LANES), I32),
-            shape(2, LANES, LANES),
         ]
         + sent,
-        "setup",
-        far=range(len(sources)),
-        scratch=[
-            memory(source.shape, source.dtype) for memory, source in zip(memories, sources)
-        ]
-        + [pltpu.SemaphoreType.DMA((len(sources),))],
-        vmem_bytes=WHOLE_VMEM,
+        "halo",
+        far=(4,),
+    )
+    coords, vel, ext, slow, select = call(
+        rest_kernel,
+        [coords, velocity, ext_force, block_class.reshape(1, -1), tile_pairs, lists],
+        [nodal] * 3
+        + [jax.ShapeDtypeStruct((elem_rows, LANES), I32), shape(2, LANES, LANES)],
+        "rest",
+        far=(5,),
     )
     for step_no in range(STEPS):
         for sub_no in range(SUBS):
@@ -566,15 +603,14 @@
             final = last and step_no == STEPS - 1
             if first:
                 arrived = swap(outgoing, devices, capacity)
+                if step_no:
+                    sends = call(sends_kernel, [disp, lists, outgoing], sent, "sends", far=(2,))
             recvs = exchange(sends)
-            (found,) = call(own_kernel, [disp, nodes], [shape(12 * elem_rows, LANES)], "own_corners")
+            (found,) = call(own_kernel, [disp, nodes], [corner_values], "own_corners")
             field = [found, *recvs, nodes, thickness, splat]
             if first:
                 (held,) = call(
-                    functools.partial(force_kernel, rows),
-                    field,
-                    [shape(12 * elem_rows, LANES)],
-                    "forces",
+                    functools.partial(force_kernel, rows), field, [corner_values], "forces"
                 )
                 (pushes,) = call(
                     functools.partial(contact_kernel, tile_pairs.shape[1]),
@@ -584,38 +620,57 @@
                     far=(2,),
                 )
                 returned = swap(pushes, devices, capacity)
-                own, *rest = call(
-                    assemble_kernel, [held, nodes, pushes], [nodal] + sent, "assemble", far=(2,)
-                )
+                outs = call(
+                    functools.partial(halo_sum_kernel, rows),
+                    [held, nodes, pushes],
+                    sent,
+                    "halo_sum",
+                    far=(2,),
+                )
+                forces = held
             else:
-                own, *rest = call(
+                forces, *outs = call(
                     functools.partial(later_kernel, rows),
                     field + [held, slow],
-                    [nodal] + sent,
-                    "forces_assemble",
-                )
-            backs = exchange(rest[:4])
-            inputs = [own, *backs]
-            inputs += [lists, ext, inv_mass, vel, disp]
-            inputs += [returned, inverse] if first else [contact]
-            outputs = [shape(3, rows * LANES)] * 2 if final else [nodal] * 2
+                    [corner_values] + sent,
+                    "forces_halo_sum",
+                )
+            backs = exchange(outs)
+            (own,) = call(own_sum_kernel, [forces, nodes, outs[0]], [nodal], "own_sum", far=(2,))
+            state = [lists, ext, inv_mass, vel, disp]
             if first:
-                outputs.append(nodal)
-            if last and not final:
-                inputs += [coords, inverse]
-            if not final:
-                outputs += sent
-                if last:
-                    outputs.append(slots)
-            vel, disp, *rest = call(
-                functools.partial(update_kernel, first, last, final), inputs, outputs, "update"
-            )
-            if first:
-                contact = rest.pop(0)
-            if not final:
-                sends = rest[:4]
-                if last:
-                    outgoing = rest[4]
+                (internal,) = call(
+                    internal_kernel, [own, *backs, lists], [nodal], "internal"
+                )
+                vel, disp, contact, *sends = call(
+                    first_update_kernel,
+                    [internal, returned, inverse] + state,
+                    [nodal] * 3 + sent,
+                    "first_update",
+                )
+                continue
+            inputs = [own, *backs] + state + [contact]
+            if final:
+                vel, disp = call(
+                    functools.partial(update_kernel, "final"),
+                    inputs,
+                    [shape(3, rows * LANES)] * 2,
+                    "final_update",
+                )
+            elif last:
+                vel, disp, outgoing = call(
+                    functools.partial(update_kernel, "last"),
+                    inputs + [coords, inverse],
+                    [nodal] * 2 + [slots],
+                    "last_update",
+                )
+            else:
+                vel, disp, *sends = call(
+                    functools.partial(update_kernel, "inner"),
+                    inputs,
+                    [nodal] * 2 + sent,
+                    "update",
+                )
     return (disp, vel)
 
 

time: 84.6 us -> 86.3 us (1.020)
  waiting for transfers between devices: 11.2 us -> 6.86 us
  starting transfers between devices: 52.3 us -> 54.8 us
  Pallas kernels: 19.6 us -> 21.3 us
  local copies, waits for them, and re-layouts: 0.07 us -> 1.58 us
    ppermute x32, waiting for transfers between devices: 8.42 us -> 6 us  [exchange(): lax.ppermute(blocks[n], ('px', 'py'), swaps[n])]
    all_to_all x4, waiting for transfers between devices: 2.74 us -> 0.86 us  [swap(): return lax.all_to_all(slots, axes, 0, 0, tiled=True)]
    pallas_call x17 -> x26, Pallas kernels: 19.6 us -> 21.3 us  [call(): pl.pallas_call(kernel, out_shape=tuple(outputs), in_specs=specs, out_spec...]
    unnamed x32 -> x24, local copies, waits for them, and re-layouts: 0.07 us -> 1.58 us
    ppermute x32, starting transfers between devices: 33.5 us -> 35 us  [exchange(): lax.ppermute(blocks[n], ('px', 'py'), swaps[n])]
    all_to_all x4, starting transfers between devices: 18.8 us -> 19.9 us  [swap(): return lax.all_to_all(slots, axes, 0, 0, tiled=True)]
  transfers between devices with their start and end apart: 36 -> 36, of which waited for: 12 -> 9; matrix products, arithmetic and copies ran while one was open for 0% -> 0% of each run, Pallas kernels for 6% -> 10%
where the time goes in v7:
time: 86.3 us; the launch traced here: 85.8 us
  starting transfers between devices  54.8 us (63%)
  Pallas kernels  21.3 us (25%)
  waiting for transfers between devices  6.86 us (8%)
  local copies, waits for them, and re-layouts  1.58 us (2%)
  between operations  1.16 us (1%)
    ppermute x32, starting transfers between devices, exchange(): lax.ppermute(blocks[n], ('px', 'py'), swaps[n])  35 us
    pallas_call x26, Pallas kernels, call(): pl.pallas_call(kernel, out_shape=tuple(outputs), in_specs=specs, out_spec...  21.3 us
    all_to_all x4, starting transfers between devices, swap(): return lax.all_to_all(slots, axes, 0, 0, tiled=True)  19.9 us
    ppermute x32, waiting for transfers between devices, exchange(): lax.ppermute(blocks[n], ('px', 'py'), swaps[n])  6 us
  transfers between devices with their start and end apart: 36, of which 9 were waited for; matrix products, arithmetic and copies ran while one was open for 0% of the time, Pallas kernels for 10%

profile of v7, /device:TPU:0, one launch (start us, length us, event | category | flops | bytes accessed | tf_op | source)
XLA Modules:
  0.0 85.8 jit_solution(8574202385391238192)
XLA Ops:
  0.6 2.2 %slots.1 = (s32[32,128]{1,0:T(8,128)}, f32[32,3,128]{2,1,0:T(4,128)}) custom-call(f32[3,2048]{1,0:T(4,128)} %coords_in.1, f32[3,2048]{1,0:T(4,128)} %disp_in.1, s32[16,128]{1,0:T(8,128)} %bitcast.14, s32[16,128]{1,0:T(8,128)} %bitcast.15), custom_call_target="tpu_custom_call" | custom-call | tf_op jit(solution)/shard_map/slots/pallas_call | solution.py:486
  2.9 7.3 %all-to-all-start = ((f32[32,3,128]{2,1,0:T(4,128)}), f32[32,3,128]{2,1,0:T(4,128)S(1)}, u32[]{:S(2)}, u32[]{:S(2)}) async-start(f32[32,3,128]{2,1,0:T(4,128)} %get-tuple-element.68), calls=%async_computation | async-start | bytes 131072 | tf_op jit(solution)/shard_map/all_to_all | solution.py:521
  10.8 1.6 %collective-permute-start.1 = (f32[12,128]{1,0:T(8,128)S(1)}, f32[12,128]{1,0:T(8,128)S(1)}, u32[]{:S(2)}, u32[]{:S(2)}) collective-permute-start(f32[12,128]{1,0:T(8,128)S(1)} %get-tuple-element.62), channel_id=1, source_target_pairs={{0,3},{1,2},{2,1},{3,0},{4,7},{5,6},{6,5},{7,4},{8,11},{9,10},{10,... | collective-permute-start | bytes 18440 | tf_op jit(solution)/shard_map/ppermute | solution.py:515
  12.5 2.3 %collective-permute-start.2 = (f32[12,128]{1,0:T(8,128)S(1)}, f32[12,128]{1,0:T(8,128)S(1)}, u32[]{:S(2)}, u32[]{:S(2)}) collective-permute-start(f32[12,128]{1,0:T(8,128)S(1)} %get-tuple-element.63), channel_id=1, source_target_pairs={{0,4},{1,5},{2,6},{3,7},{4,0},{5,1},{6,2},{7,3},{8,12},{9,13},{10,... | collective-permute-start | bytes 18440 | tf_op jit(solution)/shard_map/ppermute | solution.py:515
  17.6 2.1 %contact.2.after = f32[32,3,128]{2,1,0:T(4,128)} custom-call(f32[2,128,128]{2,1,0:T(8,128)S(1)} %get-tuple-element.67.select, f32[32,3,128]{2,1,0:T(4,128)S(1)} %all-to-all-done.arrived, f32[192,128]{1,0:T(8,128)S(1)} %forces.2.after.held), custom_call_target="tpu_custom_call" | custom-call | tf_op jit(solution)/shard_map/contact/pallas_call | solution.py:486
  19.8 3.7 %all-to-all-start.1 = ((f32[32,3,128]{2,1,0:T(4,128)}), f32[32,3,128]{2,1,0:T(4,128)S(1)}, u32[]{:S(2)}, u32[]{:S(2)}) async-start(f32[32,3,128]{2,1,0:T(4,128)} %contact.2.after), calls=%async_computation.1 | async-start | bytes 131072 | tf_op jit(solution)/shard_map/all_to_all | solution.py:521
  24.4 1.6 %collective-permute-start.5 = (f32[12,128]{1,0:T(8,128)S(1)}, f32[12,128]{1,0:T(8,128)S(1)}, u32[]{:S(2)}, u32[]{:S(2)}) collective-permute-start(f32[12,128]{1,0:T(8,128)S(1)} %get-tuple-element.71), channel_id=1, source_target_pairs={{0,3},{1,2},{2,1},{3,0},{4,7},{5,6},{6,5},{7,4},{8,11},{9,10},{10,... | collective-permute-start | bytes 18440 | tf_op jit(solution)/shard_map/ppermute | solution.py:515
  26.2 2.8 %collective-permute-start.6 = (f32[12,128]{1,0:T(8,128)S(1)}, f32[12,128]{1,0:T(8,128)S(1)}, u32[]{:S(2)}, u32[]{:S(2)}) collective-permute-start(f32[12,128]{1,0:T(8,128)S(1)} %get-tuple-element.69.after), channel_id=1, source_target_pairs={{0,4},{1,5},{2,6},{3,7},{4,0},{5,1},{6,2},{7,3},{8,12},{9,13},{10,... | collective-permute-start | bytes 18440 | tf_op jit(solution)/shard_map/ppermute | solution.py:515
  32.7 2.8 %collective-permute-start.10 = (f32[12,128]{1,0:T(8,128)S(1)}, f32[12,128]{1,0:T(8,128)S(1)}, u32[]{:S(2)}, u32[]{:S(2)}) collective-permute-start(f32[12,128]{1,0:T(8,128)S(1)} %get-tuple-element.78), channel_id=1, source_target_pairs={{0,4},{1,5},{2,6},{3,7},{4,0},{5,1},{6,2},{7,3},{8,12},{9,13},{10,... | collective-permute-start | bytes 18440 | tf_op jit(solution)/shard_map/ppermute | solution.py:515
  37.2 1.5 %forces_halo_sum.2 = (f32[192,128]{1,0:T(8,128)S(1)}, f32[12,128]{1,0:T(8,128)S(1)}, f32[12,128]{1,0:T(8,128)S(1)}, f32[12,128]{1,0:T(8,128)S(1)}, f32[12,128]{1,0:T(8,128)S(1)}) custom-call(f32[192,128]{1,0:T(8,128)S(1)} %own_corners.5.found, f32[12,128]{1,0:T(8,128)S(1)} %collective-permute-done.8.recv1, f32[12,128]{1,0:T(8,128)S(1)} %collective-permute-done.9.recv3, ...), custom_call_target="tpu_custom_call" | custom-call | tf_op jit(solution)/shard_map/forces_halo_sum/pallas_call | solution.py:486
  38.9 1.0 %collective-permute-start.13 = (f32[12,128]{1,0:T(8,128)S(1)}, f32[12,128]{1,0:T(8,128)S(1)}, u32[]{:S(2)}, u32[]{:S(2)}) collective-permute-start(f32[12,128]{1,0:T(8,128)S(1)} %get-tuple-element.84), channel_id=1, source_target_pairs={{0,3},{1,2},{2,1},{3,0},{4,7},{5,6},{6,5},{7,4},{8,11},{9,10},{10,... | collective-permute-start | bytes 18440 | tf_op jit(solution)/shard_map/ppermute | solution.py:515
  40.3 2.6 %collective-permute-start.14 = (f32[12,128]{1,0:T(8,128)S(1)}, f32[12,128]{1,0:T(8,128)S(1)}, u32[]{:S(2)}, u32[]{:S(2)}) collective-permute-start(f32[12,128]{1,0:T(8,128)S(1)} %get-tuple-element.82.after), channel_id=1, source_target_pairs={{0,4},{1,5},{2,6},{3,7},{4,0},{5,1},{6,2},{7,3},{8,12},{9,13},{10,... | collective-permute-start | bytes 18440 | tf_op jit(solution)/shard_map/ppermute | solution.py:515
  44.5 1.3 %last_update.1 = (f32[48,128]{1,0:T(8,128)S(1)}, f32[48,128]{1,0:T(8,128)S(1)}, f32[32,3,128]{2,1,0:T(4,128)}) custom-call(f32[48,128]{1,0:T(8,128)S(1)} %own_sum.5.refs_0_, f32[12,128]{1,0:T(8,128)S(1)} %collective-permute-done.12.refs_1_, f32[12,128]{1,0:T(8,128)S(1)} %collective-permute-done.13.refs_2_, f32[12,128]{1,0:T(8,128)S(1)} %collective-permute-done.14.refs_3_, ...), custom_call_target="tpu_custom_call" | custom-call | tf_op jit(solution)/shard_map/last_update/pallas_call | solution.py:486
  45.8 5.2 %all-to-all-start.2 = ((f32[32,3,128]{2,1,0:T(4,128)}), f32[32,3,128]{2,1,0:T(4,128)S(1)}, u32[]{:S(2)}, u32[]{:S(2)}) async-start(f32[32,3,128]{2,1,0:T(4,128)} %get-tuple-element.90.after), calls=%async_computation.2 | async-start | bytes 131072 | tf_op jit(solution)/shard_map/all_to_all | solution.py:521
  51.5 1.6 %collective-permute-start.17 = (f32[12,128]{1,0:T(8,128)S(1)}, f32[12,128]{1,0:T(8,128)S(1)}, u32[]{:S(2)}, u32[]{:S(2)}) collective-permute-start(f32[12,128]{1,0:T(8,128)S(1)} %get-tuple-element.92), channel_id=1, source_target_pairs={{0,3},{1,2},{2,1},{3,0},{4,7},{5,6},{6,5},{7,4},{8,11},{9,10},{10,... | collective-permute-start | bytes 18440 | tf_op jit(solution)/shard_map/ppermute | solution.py:515
  53.1 2.3 %collective-permute-start.18 = (f32[12,128]{1,0:T(8,128)S(1)}, f32[12,128]{1,0:T(8,128)S(1)}, u32[]{:S(2)}, u32[]{:S(2)}) collective-permute-start(f32[12,128]{1,0:T(8,128)S(1)} %get-tuple-element.93), channel_id=1, source_target_pairs={{0,4},{1,5},{2,6},{3,7},{4,0},{5,1},{6,2},{7,3},{8,12},{9,13},{10,... | collective-permute-start | bytes 18440 | tf_op jit(solution)/shard_map/ppermute | solution.py:515
  58.4 2.1 %contact.3.after = f32[32,3,128]{2,1,0:T(4,128)} custom-call(f32[2,128,128]{2,1,0:T(8,128)S(1)} %get-tuple-element.67.select, f32[32,3,128]{2,1,0:T(4,128)S(1)} %all-to-all-done.2.arrived, f32[192,128]{1,0:T(8,128)S(1)} %forces.3.after.held), custom_call_target="tpu_custom_call" | custom-call | tf_op jit(solution)/shard_map/contact/pallas_call | solution.py:486
  60.5 3.7 %all-to-all-start.3 = ((f32[32,3,128]{2,1,0:T(4,128)}), f32[32,3,128]{2,1,0:T(4,128)S(1)}, u32[]{:S(2)}, u32[]{:S(2)}) async-start(f32[32,3,128]{2,1,0:T(4,128)} %contact.3.after), calls=%async_computation.3 | async-start | bytes 131072 | tf_op jit(solution)/shard_map/all_to_all | solution.py:521
  65.1 1.6 %collective-permute-start.21 = (f32[12,128]{1,0:T(8,128)S(1)}, f32[12,128]{1,0:T(8,128)S(1)}, u32[]{:S(2)}, u32[]{:S(2)}) collective-permute-start(f32[12,128]{1,0:T(8,128)S(1)} %get-tuple-element.97), channel_id=1, source_target_pairs={{0,3},{1,2},{2,1},{3,0},{4,7},{5,6},{6,5},{7,4},{8,11},{9,10},{10,... | collective-permute-start | bytes 18440 | tf_op jit(solution)/shard_map/ppermute | solution.py:515
  66.9 2.8 %collective-permute-start.22 = (f32[12,128]{1,0:T(8,128)S(1)}, f32[12,128]{1,0:T(8,128)S(1)}, u32[]{:S(2)}, u32[]{:S(2)}) collective-permute-start(f32[12,128]{1,0:T(8,128)S(1)} %get-tuple-element.95.after), channel_id=1, source_target_pairs={{0,4},{1,5},{2,6},{3,7},{4,0},{5,1},{6,2},{7,3},{8,12},{9,13},{10,... | collective-permute-start | bytes 18440 | tf_op jit(solution)/shard_map/ppermute | solution.py:515
  73.0 2.8 %collective-permute-start.26 = (f32[12,128]{1,0:T(8,128)S(1)}, f32[12,128]{1,0:T(8,128)S(1)}, u32[]{:S(2)}, u32[]{:S(2)}) collective-permute-start(f32[12,128]{1,0:T(8,128)S(1)} %get-tuple-element.103), channel_id=1, source_target_pairs={{0,4},{1,5},{2,6},{3,7},{4,0},{5,1},{6,2},{7,3},{8,12},{9,13},{10,... | collective-permute-start | bytes 18440 | tf_op jit(solution)/shard_map/ppermute | solution.py:515
  77.5 1.5 %forces_halo_sum.3 = (f32[192,128]{1,0:T(8,128)S(1)}, f32[12,128]{1,0:T(8,128)S(1)}, f32[12,128]{1,0:T(8,128)S(1)}, f32[12,128]{1,0:T(8,128)S(1)}, f32[12,128]{1,0:T(8,128)S(1)}) custom-call(f32[192,128]{1,0:T(8,128)S(1)} %own_corners.7.found, f32[12,128]{1,0:T(8,128)S(1)} %collective-permute-done.24.recv1, f32[12,128]{1,0:T(8,128)S(1)} %collective-permute-done.25.recv3, ...), custom_call_target="tpu_custom_call" | custom-call | tf_op jit(solution)/shard_map/forces_halo_sum/pallas_call | solution.py:486
  79.2 1.0 %collective-permute-start.29 = (f32[12,128]{1,0:T(8,128)S(1)}, f32[12,128]{1,0:T(8,128)S(1)}, u32[]{:S(2)}, u32[]{:S(2)}) collective-permute-start(f32[12,128]{1,0:T(8,128)S(1)} %get-tuple-element.108), channel_id=1, source_target_pairs={{0,3},{1,2},{2,1},{3,0},{4,7},{5,6},{6,5},{7,4},{8,11},{9,10},{10,... | collective-permute-start | bytes 18440 | tf_op jit(solution)/shard_map/ppermute | solution.py:515
  80.5 2.6 %collective-permute-start.30 = (f32[12,128]{1,0:T(8,128)S(1)}, f32[12,128]{1,0:T(8,128)S(1)}, u32[]{:S(2)}, u32[]{:S(2)}) collective-permute-start(f32[12,128]{1,0:T(8,128)S(1)} %get-tuple-element.106.after), channel_id=1, source_target_pairs={{0,4},{1,5},{2,6},{3,7},{4,0},{5,1},{6,2},{7,3},{8,12},{9,13},{10,... | collective-permute-start | bytes 18440 | tf_op jit(solution)/shard_map/ppermute | solution.py:515
  (98 shorter events, 24.4 us)
Async XLA Ops:
  2.9 14.7 %all-to-all-start = ((f32[32,3,128]{2,1,0:T(4,128)}), f32[32,3,128]{2,1,0:T(4,128)S(1)}, u32[]{:S(2)}, u32[]{:S(2)}) async-start(f32[32,3,128]{2,1,0:T(4,128)} %get-tuple-element.68), calls=%async_computation | async-start | bytes 131072 | tf_op jit(solution)/shard_map/all_to_all | solution.py:521
  10.5 6.0 %collective-permute-start = (f32[12,128]{1,0:T(8,128)S(1)}, f32[12,128]{1,0:T(8,128)S(1)}, u32[]{:S(2)}, u32[]{:S(2)}) collective-permute-start(f32[12,128]{1,0:T(8,128)S(1)} %get-tuple-element.61), channel_id=1, source_target_pairs={{0,1},{1,0},{2,3},{3,2},{4,8},{5,9},{6,10},{7,11},{8,4},{9,5},{10,... | collective-permute-start | bytes 18440 | tf_op jit(solution)/shard_map/ppermute | solution.py:515
  10.8 5.7 %collective-permute-start.1 = (f32[12,128]{1,0:T(8,128)S(1)}, f32[12,128]{1,0:T(8,128)S(1)}, u32[]{:S(2)}, u32[]{:S(2)}) collective-permute-start(f32[12,128]{1,0:T(8,128)S(1)} %get-tuple-element.62), channel_id=1, source_target_pairs={{0,3},{1,2},{2,1},{3,0},{4,7},{5,6},{6,5},{7,4},{8,11},{9,10},{10,... | collective-permute-start | bytes 18440 | tf_op jit(solution)/shard_map/ppermute | solution.py:515
  19.8 11.2 %all-to-all-start.1 = ((f32[32,3,128]{2,1,0:T(4,128)}), f32[32,3,128]{2,1,0:T(4,128)S(1)}, u32[]{:S(2)}, u32[]{:S(2)}) async-start(f32[32,3,128]{2,1,0:T(4,128)} %contact.2.after), calls=%async_computation.1 | async-start | bytes 131072 | tf_op jit(solution)/shard_map/all_to_all | solution.py:521
  24.1 5.6 %collective-permute-start.4 = (f32[12,128]{1,0:T(8,128)S(1)}, f32[12,128]{1,0:T(8,128)S(1)}, u32[]{:S(2)}, u32[]{:S(2)}) collective-permute-start(f32[12,128]{1,0:T(8,128)S(1)} %get-tuple-element.70), channel_id=1, source_target_pairs={{0,1},{1,0},{2,3},{3,2},{4,8},{5,9},{6,10},{7,11},{8,4},{9,5},{10,... | collective-permute-start | bytes 18440 | tf_op jit(solution)/shard_map/ppermute | solution.py:515
  24.4 5.3 %collective-permute-start.5 = (f32[12,128]{1,0:T(8,128)S(1)}, f32[12,128]{1,0:T(8,128)S(1)}, u32[]{:S(2)}, u32[]{:S(2)}) collective-permute-start(f32[12,128]{1,0:T(8,128)S(1)} %get-tuple-element.71), channel_id=1, source_target_pairs={{0,3},{1,2},{2,1},{3,0},{4,7},{5,6},{6,5},{7,4},{8,11},{9,10},{10,... | collective-permute-start | bytes 18440 | tf_op jit(solution)/shard_map/ppermute | solution.py:515
  26.2 4.4 %collective-permute-start.6 = (f32[12,128]{1,0:T(8,128)S(1)}, f32[12,128]{1,0:T(8,128)S(1)}, u32[]{:S(2)}, u32[]{:S(2)}) collective-permute-start(f32[12,128]{1,0:T(8,128)S(1)} %get-tuple-element.69.after), channel_id=1, source_target_pairs={{0,4},{1,5},{2,6},{3,7},{4,0},{5,1},{6,2},{7,3},{8,12},{9,13},{10,... | collective-permute-start | bytes 18440 | tf_op jit(solution)/shard_map/ppermute | solution.py:515
  32.0 4.4 %collective-permute-start.8 = (f32[12,128]{1,0:T(8,128)S(1)}, f32[12,128]{1,0:T(8,128)S(1)}, u32[]{:S(2)}, u32[]{:S(2)}) collective-permute-start(f32[12,128]{1,0:T(8,128)S(1)} %get-tuple-element.76), channel_id=1, source_target_pairs={{0,1},{1,0},{2,3},{3,2},{4,8},{5,9},{6,10},{7,11},{8,4},{9,5},{10,... | collective-permute-start | bytes 18440 | tf_op jit(solution)/shard_map/ppermute | solution.py:515
  32.0 4.4 %collective-permute-start.9 = (f32[12,128]{1,0:T(8,128)S(1)}, f32[12,128]{1,0:T(8,128)S(1)}, u32[]{:S(2)}, u32[]{:S(2)}) collective-permute-start(f32[12,128]{1,0:T(8,128)S(1)} %get-tuple-element.77), channel_id=1, source_target_pairs={{0,3},{1,2},{2,1},{3,0},{4,7},{5,6},{6,5},{7,4},{8,11},{9,10},{10,... | collective-permute-start | bytes 18440 | tf_op jit(solution)/shard_map/ppermute | solution.py:515
  32.7 4.5 %collective-permute-start.10 = (f32[12,128]{1,0:T(8,128)S(1)}, f32[12,128]{1,0:T(8,128)S(1)}, u32[]{:S(2)}, u32[]{:S(2)}) collective-permute-start(f32[12,128]{1,0:T(8,128)S(1)} %get-tuple-element.78), channel_id=1, source_target_pairs={{0,4},{1,5},{2,6},{3,7},{4,0},{5,1},{6,2},{7,3},{8,12},{9,13},{10,... | collective-permute-start | bytes 18440 | tf_op jit(solution)/shard_map/ppermute | solution.py:515
  38.8 4.9 %collective-permute-start.12 = (f32[12,128]{1,0:T(8,128)S(1)}, f32[12,128]{1,0:T(8,128)S(1)}, u32[]{:S(2)}, u32[]{:S(2)}) collective-permute-start(f32[12,128]{1,0:T(8,128)S(1)} %get-tuple-element.83), channel_id=1, source_target_pairs={{0,1},{1,0},{2,3},{3,2},{4,8},{5,9},{6,10},{7,11},{8,4},{9,5},{10,... | collective-permute-start | bytes 18440 | tf_op jit(solution)/shard_map/ppermute | solution.py:515
  38.9 4.7 %collective-permute-start.13 = (f32[12,128]{1,0:T(8,128)S(1)}, f32[12,128]{1,0:T(8,128)S(1)}, u32[]{:S(2)}, u32[]{:S(2)}) collective-permute-start(f32[12,128]{1,0:T(8,128)S(1)} %get-tuple-element.84), channel_id=1, source_target_pairs={{0,3},{1,2},{2,1},{3,0},{4,7},{5,6},{6,5},{7,4},{8,11},{9,10},{10,... | collective-permute-start | bytes 18440 | tf_op jit(solution)/shard_map/ppermute | solution.py:515
  45.8 12.6 %all-to-all-start.2 = ((f32[32,3,128]{2,1,0:T(4,128)}), f32[32,3,128]{2,1,0:T(4,128)S(1)}, u32[]{:S(2)}, u32[]{:S(2)}) async-start(f32[32,3,128]{2,1,0:T(4,128)} %get-tuple-element.90.after), calls=%async_computation.2 | async-start | bytes 131072 | tf_op jit(solution)/shard_map/all_to_all | solution.py:521
  51.1 5.1 %collective-permute-start.16 = (f32[12,128]{1,0:T(8,128)S(1)}, f32[12,128]{1,0:T(8,128)S(1)}, u32[]{:S(2)}, u32[]{:S(2)}) collective-permute-start(f32[12,128]{1,0:T(8,128)S(1)} %get-tuple-element.91), channel_id=1, source_target_pairs={{0,1},{1,0},{2,3},{3,2},{4,8},{5,9},{6,10},{7,11},{8,4},{9,5},{10,... | collective-permute-start | bytes 18440 | tf_op jit(solution)/shard_map/ppermute | solution.py:515
  51.5 4.8 %collective-permute-start.17 = (f32[12,128]{1,0:T(8,128)S(1)}, f32[12,128]{1,0:T(8,128)S(1)}, u32[]{:S(2)}, u32[]{:S(2)}) collective-permute-start(f32[12,128]{1,0:T(8,128)S(1)} %get-tuple-element.92), channel_id=1, source_target_pairs={{0,3},{1,2},{2,1},{3,0},{4,7},{5,6},{6,5},{7,4},{8,11},{9,10},{10,... | collective-permute-start | bytes 18440 | tf_op jit(solution)/shard_map/ppermute | solution.py:515
  60.5 11.1 %all-to-all-start.3 = ((f32[32,3,128]{2,1,0:T(4,128)}), f32[32,3,128]{2,1,0:T(4,128)S(1)}, u32[]{:S(2)}, u32[]{:S(2)}) async-start(f32[32,3,128]{2,1,0:T(4,128)} %contact.3.after), calls=%async_computation.3 | async-start | bytes 131072 | tf_op jit(solution)/shard_map/all_to_all | solution.py:521
  64.9 5.4 %collective-permute-start.20 = (f32[12,128]{1,0:T(8,128)S(1)}, f32[12,128]{1,0:T(8,128)S(1)}, u32[]{:S(2)}, u32[]{:S(2)}) collective-permute-start(f32[12,128]{1,0:T(8,128)S(1)} %get-tuple-element.96), channel_id=1, source_target_pairs={{0,1},{1,0},{2,3},{3,2},{4,8},{5,9},{6,10},{7,11},{8,4},{9,5},{10,... | collective-permute-start | bytes 18440 | tf_op jit(solution)/shard_map/ppermute | solution.py:515
  65.1 5.3 %collective-permute-start.21 = (f32[12,128]{1,0:T(8,128)S(1)}, f32[12,128]{1,0:T(8,128)S(1)}, u32[]{:S(2)}, u32[]{:S(2)}) collective-permute-start(f32[12,128]{1,0:T(8,128)S(1)} %get-tuple-element.97), channel_id=1, source_target_pairs={{0,3},{1,2},{2,1},{3,0},{4,7},{5,6},{6,5},{7,4},{8,11},{9,10},{10,... | collective-permute-start | bytes 18440 | tf_op jit(solution)/shard_map/ppermute | solution.py:515
  66.9 4.4 %collective-permute-start.22 = (f32[12,128]{1,0:T(8,128)S(1)}, f32[12,128]{1,0:T(8,128)S(1)}, u32[]{:S(2)}, u32[]{:S(2)}) collective-permute-start(f32[12,128]{1,0:T(8,128)S(1)} %get-tuple-element.95.after), channel_id=1, source_target_pairs={{0,4},{1,5},{2,6},{3,7},{4,0},{5,1},{6,2},{7,3},{8,12},{9,13},{10,... | collective-permute-start | bytes 18440 | tf_op jit(solution)/shard_map/ppermute | solution.py:515
  72.2 4.4 %collective-permute-start.24 = (f32[12,128]{1,0:T(8,128)S(1)}, f32[12,128]{1,0:T(8,128)S(1)}, u32[]{:S(2)}, u32[]{:S(2)}) collective-permute-start(f32[12,128]{1,0:T(8,128)S(1)} %get-tuple-element.101), channel_id=1, source_target_pairs={{0,1},{1,0},{2,3},{3,2},{4,8},{5,9},{6,10},{7,11},{8,4},{9,5},{10,... | collective-permute-start | bytes 18440 | tf_op jit(solution)/shard_map/ppermute | solution.py:515
  72.3 4.4 %collective-permute-start.25 = (f32[12,128]{1,0:T(8,128)S(1)}, f32[12,128]{1,0:T(8,128)S(1)}, u32[]{:S(2)}, u32[]{:S(2)}) collective-permute-start(f32[12,128]{1,0:T(8,128)S(1)} %get-tuple-element.102), channel_id=1, source_target_pairs={{0,3},{1,2},{2,1},{3,0},{4,7},{5,6},{6,5},{7,4},{8,11},{9,10},{10,... | collective-permute-start | bytes 18440 | tf_op jit(solution)/shard_map/ppermute | solution.py:515
  73.0 4.5 %collective-permute-start.26 = (f32[12,128]{1,0:T(8,128)S(1)}, f32[12,128]{1,0:T(8,128)S(1)}, u32[]{:S(2)}, u32[]{:S(2)}) collective-permute-start(f32[12,128]{1,0:T(8,128)S(1)} %get-tuple-element.103), channel_id=1, source_target_pairs={{0,4},{1,5},{2,6},{3,7},{4,0},{5,1},{6,2},{7,3},{8,12},{9,13},{10,... | collective-permute-start | bytes 18440 | tf_op jit(solution)/shard_map/ppermute | solution.py:515
  79.0 4.9 %collective-permute-start.28 = (f32[12,128]{1,0:T(8,128)S(1)}, f32[12,128]{1,0:T(8,128)S(1)}, u32[]{:S(2)}, u32[]{:S(2)}) collective-permute-start(f32[12,128]{1,0:T(8,128)S(1)} %get-tuple-element.107), channel_id=1, source_target_pairs={{0,1},{1,0},{2,3},{3,2},{4,8},{5,9},{6,10},{7,11},{8,4},{9,5},{10,... | collective-permute-start | bytes 18440 | tf_op jit(solution)/shard_map/ppermute | solution.py:515
  79.2 4.7 %collective-permute-start.29 = (f32[12,128]{1,0:T(8,128)S(1)}, f32[12,128]{1,0:T(8,128)S(1)}, u32[]{:S(2)}, u32[]{:S(2)}) collective-permute-start(f32[12,128]{1,0:T(8,128)S(1)} %get-tuple-element.108), channel_id=1, source_target_pairs={{0,3},{1,2},{2,1},{3,0},{4,7},{5,6},{6,5},{7,4},{8,11},{9,10},{10,... | collective-permute-start | bytes 18440 | tf_op jit(solution)/shard_map/ppermute | solution.py:515
  (24 other events, 80.1 us)

commit v8 on v7

--- a/solution.py
+++ b/solution.py
@@ -636,7 +636,7 @@
                     "forces_halo_sum",
                 )
             backs = exchange(outs)
-            (own,) = call(own_sum_kernel, [forces, nodes, outs[0]], [nodal], "own_sum", far=(2,))
+            (own,) = call(own_sum_kernel, [forces, nodes, outs[2]], [nodal], "own_sum", far=(2,))
             state = [lists, ext, inv_mass, vel, disp]
             if first:
                 (internal,) = call(

time: 86.3 us -> 83.5 us (0.968)
  starting transfers between devices: 54.8 us -> 52.8 us
    ppermute x32, waiting for transfers between devices: 6 us -> 4.84 us  [exchange(): lax.ppermute(blocks[n], ('px', 'py'), swaps[n])]
    ppermute x32, starting transfers between devices: 35 us -> 33.9 us  [exchange(): lax.ppermute(blocks[n], ('px', 'py'), swaps[n])]
    all_to_all x4, starting transfers between devices: 19.9 us -> 18.9 us  [swap(): return lax.all_to_all(slots, axes, 0, 0, tiled=True)]
    all_to_all x4, waiting for transfers between devices: 0.86 us -> 1.74 us  [swap(): return lax.all_to_all(slots, axes, 0, 0, tiled=True)]
  transfers between devices with their start and end apart: 36 -> 36, of which waited for: 9 -> 11; matrix products, arithmetic and copies ran while one was open for 0% -> 0% of each run, Pallas kernels for 10% -> 10%
where the time goes in v8:
time: 83.5 us; the launch traced here: 83 us
  starting transfers between devices  52.8 us (63%)
  Pallas kernels  21.3 us (26%)
  waiting for transfers between devices  6.58 us (8%)
  local copies, waits for them, and re-layouts  1.21 us (1%)
  between operations  1.1 us (1%)
    ppermute x32, starting transfers between devices, exchange(): lax.ppermute(blocks[n], ('px', 'py'), swaps[n])  33.9 us
    pallas_call x26, Pallas kernels, call(): pl.pallas_call(kernel, out_shape=tuple(outputs), in_specs=specs, out_spec...  21.3 us
    all_to_all x4, starting transfers between devices, swap(): return lax.all_to_all(slots, axes, 0, 0, tiled=True)  18.9 us
    ppermute x32, waiting for transfers between devices, exchange(): lax.ppermute(blocks[n], ('px', 'py'), swaps[n])  4.84 us
    all_to_all x4, waiting for transfers between devices, swap(): return lax.all_to_all(slots, axes, 0, 0, tiled=True)  1.74 us
  transfers between devices with their start and end apart: 36, of which 11 were waited for; matrix products, arithmetic and copies ran while one was open for 0% of the time, Pallas kernels for 10%

profile of v8, /device:TPU:0, one launch (start us, length us, event | category | flops | bytes accessed | tf_op | source)
XLA Modules:
  0.0 83.0 jit_solution(2126995613717485411)
XLA Ops:
  0.6 2.2 %slots.1 = (s32[32,128]{1,0:T(8,128)}, f32[32,3,128]{2,1,0:T(4,128)}) custom-call(f32[3,2048]{1,0:T(4,128)} %coords_in.1, f32[3,2048]{1,0:T(4,128)} %disp_in.1, s32[16,128]{1,0:T(8,128)} %bitcast.14, s32[16,128]{1,0:T(8,128)} %bitcast.15), custom_call_target="tpu_custom_call" | custom-call | tf_op jit(solution)/shard_map/slots/pallas_call | solution.py:486
  2.9 7.3 %all-to-all-start = ((f32[32,3,128]{2,1,0:T(4,128)}), f32[32,3,128]{2,1,0:T(4,128)S(1)}, u32[]{:S(2)}, u32[]{:S(2)}) async-start(f32[32,3,128]{2,1,0:T(4,128)} %get-tuple-element.68), calls=%async_computation | async-start | bytes 131072 | tf_op jit(solution)/shard_map/all_to_all | solution.py:521
  10.8 1.6 %collective-permute-start.1 = (f32[12,128]{1,0:T(8,128)S(1)}, f32[12,128]{1,0:T(8,128)S(1)}, u32[]{:S(2)}, u32[]{:S(2)}) collective-permute-start(f32[12,128]{1,0:T(8,128)S(1)} %get-tuple-element.62), channel_id=1, source_target_pairs={{0,3},{1,2},{2,1},{3,0},{4,7},{5,6},{6,5},{7,4},{8,11},{9,10},{10,... | collective-permute-start | bytes 18440 | tf_op jit(solution)/shard_map/ppermute | solution.py:515
  12.5 2.3 %collective-permute-start.2 = (f32[12,128]{1,0:T(8,128)S(1)}, f32[12,128]{1,0:T(8,128)S(1)}, u32[]{:S(2)}, u32[]{:S(2)}) collective-permute-start(f32[12,128]{1,0:T(8,128)S(1)} %get-tuple-element.63), channel_id=1, source_target_pairs={{0,4},{1,5},{2,6},{3,7},{4,0},{5,1},{6,2},{7,3},{8,12},{9,13},{10,... | collective-permute-start | bytes 18440 | tf_op jit(solution)/shard_map/ppermute | solution.py:515
  17.6 2.1 %contact.2.after = f32[32,3,128]{2,1,0:T(4,128)} custom-call(f32[2,128,128]{2,1,0:T(8,128)S(1)} %get-tuple-element.67.select, f32[32,3,128]{2,1,0:T(4,128)S(1)} %all-to-all-done.arrived, f32[192,128]{1,0:T(8,128)S(1)} %forces.2.after.held), custom_call_target="tpu_custom_call" | custom-call | tf_op jit(solution)/shard_map/contact/pallas_call | solution.py:486
  19.8 3.7 %all-to-all-start.1 = ((f32[32,3,128]{2,1,0:T(4,128)}), f32[32,3,128]{2,1,0:T(4,128)S(1)}, u32[]{:S(2)}, u32[]{:S(2)}) async-start(f32[32,3,128]{2,1,0:T(4,128)} %contact.2.after), calls=%async_computation.1 | async-start | bytes 131072 | tf_op jit(solution)/shard_map/all_to_all | solution.py:521
  24.4 1.6 %collective-permute-start.5 = (f32[12,128]{1,0:T(8,128)S(1)}, f32[12,128]{1,0:T(8,128)S(1)}, u32[]{:S(2)}, u32[]{:S(2)}) collective-permute-start(f32[12,128]{1,0:T(8,128)S(1)} %get-tuple-element.71), channel_id=1, source_target_pairs={{0,3},{1,2},{2,1},{3,0},{4,7},{5,6},{6,5},{7,4},{8,11},{9,10},{10,... | collective-permute-start | bytes 18440 | tf_op jit(solution)/shard_map/ppermute | solution.py:515
  26.1 2.3 %collective-permute-start.6 = (f32[12,128]{1,0:T(8,128)S(1)}, f32[12,128]{1,0:T(8,128)S(1)}, u32[]{:S(2)}, u32[]{:S(2)}) collective-permute-start(f32[12,128]{1,0:T(8,128)S(1)} %get-tuple-element.72), channel_id=1, source_target_pairs={{0,4},{1,5},{2,6},{3,7},{4,0},{5,1},{6,2},{7,3},{8,12},{9,13},{10,... | collective-permute-start | bytes 18440 | tf_op jit(solution)/shard_map/ppermute | solution.py:515
  32.1 2.7 %collective-permute-start.10 = (f32[12,128]{1,0:T(8,128)S(1)}, f32[12,128]{1,0:T(8,128)S(1)}, u32[]{:S(2)}, u32[]{:S(2)}) collective-permute-start(f32[12,128]{1,0:T(8,128)S(1)} %get-tuple-element.78), channel_id=1, source_target_pairs={{0,4},{1,5},{2,6},{3,7},{4,0},{5,1},{6,2},{7,3},{8,12},{9,13},{10,... | collective-permute-start | bytes 18440 | tf_op jit(solution)/shard_map/ppermute | solution.py:515
  36.6 1.5 %forces_halo_sum.2 = (f32[192,128]{1,0:T(8,128)S(1)}, f32[12,128]{1,0:T(8,128)S(1)}, f32[12,128]{1,0:T(8,128)S(1)}, f32[12,128]{1,0:T(8,128)S(1)}, f32[12,128]{1,0:T(8,128)S(1)}) custom-call(f32[192,128]{1,0:T(8,128)S(1)} %own_corners.5.found, f32[12,128]{1,0:T(8,128)S(1)} %collective-permute-done.8.recv1, f32[12,128]{1,0:T(8,128)S(1)} %collective-permute-done.9.recv3, ...), custom_call_target="tpu_custom_call" | custom-call | tf_op jit(solution)/shard_map/forces_halo_sum/pallas_call | solution.py:486
  38.3 1.0 %collective-permute-start.13 = (f32[12,128]{1,0:T(8,128)S(1)}, f32[12,128]{1,0:T(8,128)S(1)}, u32[]{:S(2)}, u32[]{:S(2)}) collective-permute-start(f32[12,128]{1,0:T(8,128)S(1)} %get-tuple-element.84), channel_id=1, source_target_pairs={{0,3},{1,2},{2,1},{3,0},{4,7},{5,6},{6,5},{7,4},{8,11},{9,10},{10,... | collective-permute-start | bytes 18440 | tf_op jit(solution)/shard_map/ppermute | solution.py:515
  39.3 2.7 %collective-permute-start.14 = (f32[12,128]{1,0:T(8,128)S(1)}, f32[12,128]{1,0:T(8,128)S(1)}, u32[]{:S(2)}, u32[]{:S(2)}) collective-permute-start(f32[12,128]{1,0:T(8,128)S(1)} %get-tuple-element.85), channel_id=1, source_target_pairs={{0,4},{1,5},{2,6},{3,7},{4,0},{5,1},{6,2},{7,3},{8,12},{9,13},{10,... | collective-permute-start | bytes 18440 | tf_op jit(solution)/shard_map/ppermute | solution.py:515
  43.6 1.3 %last_update.1 = (f32[48,128]{1,0:T(8,128)S(1)}, f32[48,128]{1,0:T(8,128)S(1)}, f32[32,3,128]{2,1,0:T(4,128)}) custom-call(f32[48,128]{1,0:T(8,128)S(1)} %own_sum.5.refs_0_, f32[12,128]{1,0:T(8,128)S(1)} %collective-permute-done.12.refs_1_, f32[12,128]{1,0:T(8,128)S(1)} %collective-permute-done.13.refs_2_, f32[12,128]{1,0:T(8,128)S(1)} %collective-permute-done.14.refs_3_, ...), custom_call_target="tpu_custom_call" | custom-call | tf_op jit(solution)/shard_map/last_update/pallas_call | solution.py:486
  44.9 4.2 %all-to-all-start.2 = ((f32[32,3,128]{2,1,0:T(4,128)}), f32[32,3,128]{2,1,0:T(4,128)S(1)}, u32[]{:S(2)}, u32[]{:S(2)}) async-start(f32[32,3,128]{2,1,0:T(4,128)} %get-tuple-element.90.after), calls=%async_computation.2 | async-start | bytes 131072 | tf_op jit(solution)/shard_map/all_to_all | solution.py:521
  49.6 1.6 %collective-permute-start.17 = (f32[12,128]{1,0:T(8,128)S(1)}, f32[12,128]{1,0:T(8,128)S(1)}, u32[]{:S(2)}, u32[]{:S(2)}) collective-permute-start(f32[12,128]{1,0:T(8,128)S(1)} %get-tuple-element.92), channel_id=1, source_target_pairs={{0,3},{1,2},{2,1},{3,0},{4,7},{5,6},{6,5},{7,4},{8,11},{9,10},{10,... | collective-permute-start | bytes 18440 | tf_op jit(solution)/shard_map/ppermute | solution.py:515
  51.2 2.3 %collective-permute-start.18 = (f32[12,128]{1,0:T(8,128)S(1)}, f32[12,128]{1,0:T(8,128)S(1)}, u32[]{:S(2)}, u32[]{:S(2)}) collective-permute-start(f32[12,128]{1,0:T(8,128)S(1)} %get-tuple-element.93), channel_id=1, source_target_pairs={{0,4},{1,5},{2,6},{3,7},{4,0},{5,1},{6,2},{7,3},{8,12},{9,13},{10,... | collective-permute-start | bytes 18440 | tf_op jit(solution)/shard_map/ppermute | solution.py:515
  56.5 2.1 %contact.3.after = f32[32,3,128]{2,1,0:T(4,128)} custom-call(f32[2,128,128]{2,1,0:T(8,128)S(1)} %get-tuple-element.67.select, f32[32,3,128]{2,1,0:T(4,128)S(1)} %all-to-all-done.2.arrived, f32[192,128]{1,0:T(8,128)S(1)} %forces.3.after.held), custom_call_target="tpu_custom_call" | custom-call | tf_op jit(solution)/shard_map/contact/pallas_call | solution.py:486
  58.6 3.7 %all-to-all-start.3 = ((f32[32,3,128]{2,1,0:T(4,128)}), f32[32,3,128]{2,1,0:T(4,128)S(1)}, u32[]{:S(2)}, u32[]{:S(2)}) async-start(f32[32,3,128]{2,1,0:T(4,128)} %contact.3.after), calls=%async_computation.3 | async-start | bytes 131072 | tf_op jit(solution)/shard_map/all_to_all | solution.py:521
  63.2 1.6 %collective-permute-start.21 = (f32[12,128]{1,0:T(8,128)S(1)}, f32[12,128]{1,0:T(8,128)S(1)}, u32[]{:S(2)}, u32[]{:S(2)}) collective-permute-start(f32[12,128]{1,0:T(8,128)S(1)} %get-tuple-element.97), channel_id=1, source_target_pairs={{0,3},{1,2},{2,1},{3,0},{4,7},{5,6},{6,5},{7,4},{8,11},{9,10},{10,... | collective-permute-start | bytes 18440 | tf_op jit(solution)/shard_map/ppermute | solution.py:515
  64.8 2.3 %collective-permute-start.22 = (f32[12,128]{1,0:T(8,128)S(1)}, f32[12,128]{1,0:T(8,128)S(1)}, u32[]{:S(2)}, u32[]{:S(2)}) collective-permute-start(f32[12,128]{1,0:T(8,128)S(1)} %get-tuple-element.98), channel_id=1, source_target_pairs={{0,4},{1,5},{2,6},{3,7},{4,0},{5,1},{6,2},{7,3},{8,12},{9,13},{10,... | collective-permute-start | bytes 18440 | tf_op jit(solution)/shard_map/ppermute | solution.py:515
  70.8 2.4 %collective-permute-start.26 = (f32[12,128]{1,0:T(8,128)S(1)}, f32[12,128]{1,0:T(8,128)S(1)}, u32[]{:S(2)}, u32[]{:S(2)}) collective-permute-start(f32[12,128]{1,0:T(8,128)S(1)} %get-tuple-element.103), channel_id=1, source_target_pairs={{0,4},{1,5},{2,6},{3,7},{4,0},{5,1},{6,2},{7,3},{8,12},{9,13},{10,... | collective-permute-start | bytes 18440 | tf_op jit(solution)/shard_map/ppermute | solution.py:515
  75.0 1.5 %forces_halo_sum.3 = (f32[192,128]{1,0:T(8,128)S(1)}, f32[12,128]{1,0:T(8,128)S(1)}, f32[12,128]{1,0:T(8,128)S(1)}, f32[12,128]{1,0:T(8,128)S(1)}, f32[12,128]{1,0:T(8,128)S(1)}) custom-call(f32[192,128]{1,0:T(8,128)S(1)} %own_corners.7.found, f32[12,128]{1,0:T(8,128)S(1)} %collective-permute-done.24.recv1, f32[12,128]{1,0:T(8,128)S(1)} %collective-permute-done.25.recv3, ...), custom_call_target="tpu_custom_call" | custom-call | tf_op jit(solution)/shard_map/forces_halo_sum/pallas_call | solution.py:486
  76.7 1.1 %collective-permute-start.29 = (f32[12,128]{1,0:T(8,128)S(1)}, f32[12,128]{1,0:T(8,128)S(1)}, u32[]{:S(2)}, u32[]{:S(2)}) collective-permute-start(f32[12,128]{1,0:T(8,128)S(1)} %get-tuple-element.108), channel_id=1, source_target_pairs={{0,3},{1,2},{2,1},{3,0},{4,7},{5,6},{6,5},{7,4},{8,11},{9,10},{10,... | collective-permute-start | bytes 18440 | tf_op jit(solution)/shard_map/ppermute | solution.py:515
  77.8 2.5 %collective-permute-start.30 = (f32[12,128]{1,0:T(8,128)S(1)}, f32[12,128]{1,0:T(8,128)S(1)}, u32[]{:S(2)}, u32[]{:S(2)}) collective-permute-start(f32[12,128]{1,0:T(8,128)S(1)} %get-tuple-element.109), channel_id=1, source_target_pairs={{0,4},{1,5},{2,6},{3,7},{4,0},{5,1},{6,2},{7,3},{8,12},{9,13},{10,... | collective-permute-start | bytes 18440 | tf_op jit(solution)/shard_map/ppermute | solution.py:515
  (98 shorter events, 24.1 us)
Async XLA Ops:
  2.9 14.7 %all-to-all-start = ((f32[32,3,128]{2,1,0:T(4,128)}), f32[32,3,128]{2,1,0:T(4,128)S(1)}, u32[]{:S(2)}, u32[]{:S(2)}) async-start(f32[32,3,128]{2,1,0:T(4,128)} %get-tuple-element.68), calls=%async_computation | async-start | bytes 131072 | tf_op jit(solution)/shard_map/all_to_all | solution.py:521
  10.5 6.0 %collective-permute-start = (f32[12,128]{1,0:T(8,128)S(1)}, f32[12,128]{1,0:T(8,128)S(1)}, u32[]{:S(2)}, u32[]{:S(2)}) collective-permute-start(f32[12,128]{1,0:T(8,128)S(1)} %get-tuple-element.61), channel_id=1, source_target_pairs={{0,1},{1,0},{2,3},{3,2},{4,8},{5,9},{6,10},{7,11},{8,4},{9,5},{10,... | collective-permute-start | bytes 18440 | tf_op jit(solution)/shard_map/ppermute | solution.py:515
  10.8 5.7 %collective-permute-start.1 = (f32[12,128]{1,0:T(8,128)S(1)}, f32[12,128]{1,0:T(8,128)S(1)}, u32[]{:S(2)}, u32[]{:S(2)}) collective-permute-start(f32[12,128]{1,0:T(8,128)S(1)} %get-tuple-element.62), channel_id=1, source_target_pairs={{0,3},{1,2},{2,1},{3,0},{4,7},{5,6},{6,5},{7,4},{8,11},{9,10},{10,... | collective-permute-start | bytes 18440 | tf_op jit(solution)/shard_map/ppermute | solution.py:515
  12.5 4.0 %collective-permute-start.2 = (f32[12,128]{1,0:T(8,128)S(1)}, f32[12,128]{1,0:T(8,128)S(1)}, u32[]{:S(2)}, u32[]{:S(2)}) collective-permute-start(f32[12,128]{1,0:T(8,128)S(1)} %get-tuple-element.63), channel_id=1, source_target_pairs={{0,4},{1,5},{2,6},{3,7},{4,0},{5,1},{6,2},{7,3},{8,12},{9,13},{10,... | collective-permute-start | bytes 18440 | tf_op jit(solution)/shard_map/ppermute | solution.py:515
  19.8 11.1 %all-to-all-start.1 = ((f32[32,3,128]{2,1,0:T(4,128)}), f32[32,3,128]{2,1,0:T(4,128)S(1)}, u32[]{:S(2)}, u32[]{:S(2)}) async-start(f32[32,3,128]{2,1,0:T(4,128)} %contact.2.after), calls=%async_computation.1 | async-start | bytes 131072 | tf_op jit(solution)/shard_map/all_to_all | solution.py:521
  24.1 5.3 %collective-permute-start.4 = (f32[12,128]{1,0:T(8,128)S(1)}, f32[12,128]{1,0:T(8,128)S(1)}, u32[]{:S(2)}, u32[]{:S(2)}) collective-permute-start(f32[12,128]{1,0:T(8,128)S(1)} %get-tuple-element.70), channel_id=1, source_target_pairs={{0,1},{1,0},{2,3},{3,2},{4,8},{5,9},{6,10},{7,11},{8,4},{9,5},{10,... | collective-permute-start | bytes 18440 | tf_op jit(solution)/shard_map/ppermute | solution.py:515
  24.4 5.0 %collective-permute-start.5 = (f32[12,128]{1,0:T(8,128)S(1)}, f32[12,128]{1,0:T(8,128)S(1)}, u32[]{:S(2)}, u32[]{:S(2)}) collective-permute-start(f32[12,128]{1,0:T(8,128)S(1)} %get-tuple-element.71), channel_id=1, source_target_pairs={{0,3},{1,2},{2,1},{3,0},{4,7},{5,6},{6,5},{7,4},{8,11},{9,10},{10,... | collective-permute-start | bytes 18440 | tf_op jit(solution)/shard_map/ppermute | solution.py:515
  26.1 4.0 %collective-permute-start.6 = (f32[12,128]{1,0:T(8,128)S(1)}, f32[12,128]{1,0:T(8,128)S(1)}, u32[]{:S(2)}, u32[]{:S(2)}) collective-permute-start(f32[12,128]{1,0:T(8,128)S(1)} %get-tuple-element.72), channel_id=1, source_target_pairs={{0,4},{1,5},{2,6},{3,7},{4,0},{5,1},{6,2},{7,3},{8,12},{9,13},{10,... | collective-permute-start | bytes 18440 | tf_op jit(solution)/shard_map/ppermute | solution.py:515
  31.5 4.3 %collective-permute-start.8 = (f32[12,128]{1,0:T(8,128)S(1)}, f32[12,128]{1,0:T(8,128)S(1)}, u32[]{:S(2)}, u32[]{:S(2)}) collective-permute-start(f32[12,128]{1,0:T(8,128)S(1)} %get-tuple-element.76), channel_id=1, source_target_pairs={{0,1},{1,0},{2,3},{3,2},{4,8},{5,9},{6,10},{7,11},{8,4},{9,5},{10,... | collective-permute-start | bytes 18440 | tf_op jit(solution)/shard_map/ppermute | solution.py:515
  31.7 4.1 %collective-permute-start.9 = (f32[12,128]{1,0:T(8,128)S(1)}, f32[12,128]{1,0:T(8,128)S(1)}, u32[]{:S(2)}, u32[]{:S(2)}) collective-permute-start(f32[12,128]{1,0:T(8,128)S(1)} %get-tuple-element.77), channel_id=1, source_target_pairs={{0,3},{1,2},{2,1},{3,0},{4,7},{5,6},{6,5},{7,4},{8,11},{9,10},{10,... | collective-permute-start | bytes 18440 | tf_op jit(solution)/shard_map/ppermute | solution.py:515
  32.1 4.4 %collective-permute-start.10 = (f32[12,128]{1,0:T(8,128)S(1)}, f32[12,128]{1,0:T(8,128)S(1)}, u32[]{:S(2)}, u32[]{:S(2)}) collective-permute-start(f32[12,128]{1,0:T(8,128)S(1)} %get-tuple-element.78), channel_id=1, source_target_pairs={{0,4},{1,5},{2,6},{3,7},{4,0},{5,1},{6,2},{7,3},{8,12},{9,13},{10,... | collective-permute-start | bytes 18440 | tf_op jit(solution)/shard_map/ppermute | solution.py:515
  38.1 4.9 %collective-permute-start.12 = (f32[12,128]{1,0:T(8,128)S(1)}, f32[12,128]{1,0:T(8,128)S(1)}, u32[]{:S(2)}, u32[]{:S(2)}) collective-permute-start(f32[12,128]{1,0:T(8,128)S(1)} %get-tuple-element.83), channel_id=1, source_target_pairs={{0,1},{1,0},{2,3},{3,2},{4,8},{5,9},{6,10},{7,11},{8,4},{9,5},{10,... | collective-permute-start | bytes 18440 | tf_op jit(solution)/shard_map/ppermute | solution.py:515
  38.3 4.8 %collective-permute-start.13 = (f32[12,128]{1,0:T(8,128)S(1)}, f32[12,128]{1,0:T(8,128)S(1)}, u32[]{:S(2)}, u32[]{:S(2)}) collective-permute-start(f32[12,128]{1,0:T(8,128)S(1)} %get-tuple-element.84), channel_id=1, source_target_pairs={{0,3},{1,2},{2,1},{3,0},{4,7},{5,6},{6,5},{7,4},{8,11},{9,10},{10,... | collective-permute-start | bytes 18440 | tf_op jit(solution)/shard_map/ppermute | solution.py:515
  39.3 4.4 %collective-permute-start.14 = (f32[12,128]{1,0:T(8,128)S(1)}, f32[12,128]{1,0:T(8,128)S(1)}, u32[]{:S(2)}, u32[]{:S(2)}) collective-permute-start(f32[12,128]{1,0:T(8,128)S(1)} %get-tuple-element.85), channel_id=1, source_target_pairs={{0,4},{1,5},{2,6},{3,7},{4,0},{5,1},{6,2},{7,3},{8,12},{9,13},{10,... | collective-permute-start | bytes 18440 | tf_op jit(solution)/shard_map/ppermute | solution.py:515
  44.9 11.6 %all-to-all-start.2 = ((f32[32,3,128]{2,1,0:T(4,128)}), f32[32,3,128]{2,1,0:T(4,128)S(1)}, u32[]{:S(2)}, u32[]{:S(2)}) async-start(f32[32,3,128]{2,1,0:T(4,128)} %get-tuple-element.90.after), calls=%async_computation.2 | async-start | bytes 131072 | tf_op jit(solution)/shard_map/all_to_all | solution.py:521
  49.3 5.1 %collective-permute-start.16 = (f32[12,128]{1,0:T(8,128)S(1)}, f32[12,128]{1,0:T(8,128)S(1)}, u32[]{:S(2)}, u32[]{:S(2)}) collective-permute-start(f32[12,128]{1,0:T(8,128)S(1)} %get-tuple-element.91), channel_id=1, source_target_pairs={{0,1},{1,0},{2,3},{3,2},{4,8},{5,9},{6,10},{7,11},{8,4},{9,5},{10,... | collective-permute-start | bytes 18440 | tf_op jit(solution)/shard_map/ppermute | solution.py:515
  49.6 4.8 %collective-permute-start.17 = (f32[12,128]{1,0:T(8,128)S(1)}, f32[12,128]{1,0:T(8,128)S(1)}, u32[]{:S(2)}, u32[]{:S(2)}) collective-permute-start(f32[12,128]{1,0:T(8,128)S(1)} %get-tuple-element.92), channel_id=1, source_target_pairs={{0,3},{1,2},{2,1},{3,0},{4,7},{5,6},{6,5},{7,4},{8,11},{9,10},{10,... | collective-permute-start | bytes 18440 | tf_op jit(solution)/shard_map/ppermute | solution.py:515
  58.6 11.0 %all-to-all-start.3 = ((f32[32,3,128]{2,1,0:T(4,128)}), f32[32,3,128]{2,1,0:T(4,128)S(1)}, u32[]{:S(2)}, u32[]{:S(2)}) async-start(f32[32,3,128]{2,1,0:T(4,128)} %contact.3.after), calls=%async_computation.3 | async-start | bytes 131072 | tf_op jit(solution)/shard_map/all_to_all | solution.py:521
  63.1 5.1 %collective-permute-start.20 = (f32[12,128]{1,0:T(8,128)S(1)}, f32[12,128]{1,0:T(8,128)S(1)}, u32[]{:S(2)}, u32[]{:S(2)}) collective-permute-start(f32[12,128]{1,0:T(8,128)S(1)} %get-tuple-element.96), channel_id=1, source_target_pairs={{0,1},{1,0},{2,3},{3,2},{4,8},{5,9},{6,10},{7,11},{8,4},{9,5},{10,... | collective-permute-start | bytes 18440 | tf_op jit(solution)/shard_map/ppermute | solution.py:515
  63.2 5.0 %collective-permute-start.21 = (f32[12,128]{1,0:T(8,128)S(1)}, f32[12,128]{1,0:T(8,128)S(1)}, u32[]{:S(2)}, u32[]{:S(2)}) collective-permute-start(f32[12,128]{1,0:T(8,128)S(1)} %get-tuple-element.97), channel_id=1, source_target_pairs={{0,3},{1,2},{2,1},{3,0},{4,7},{5,6},{6,5},{7,4},{8,11},{9,10},{10,... | collective-permute-start | bytes 18440 | tf_op jit(solution)/shard_map/ppermute | solution.py:515
  70.8 4.1 %collective-permute-start.26 = (f32[12,128]{1,0:T(8,128)S(1)}, f32[12,128]{1,0:T(8,128)S(1)}, u32[]{:S(2)}, u32[]{:S(2)}) collective-permute-start(f32[12,128]{1,0:T(8,128)S(1)} %get-tuple-element.103), channel_id=1, source_target_pairs={{0,4},{1,5},{2,6},{3,7},{4,0},{5,1},{6,2},{7,3},{8,12},{9,13},{10,... | collective-permute-start | bytes 18440 | tf_op jit(solution)/shard_map/ppermute | solution.py:515
  76.5 4.9 %collective-permute-start.28 = (f32[12,128]{1,0:T(8,128)S(1)}, f32[12,128]{1,0:T(8,128)S(1)}, u32[]{:S(2)}, u32[]{:S(2)}) collective-permute-start(f32[12,128]{1,0:T(8,128)S(1)} %get-tuple-element.107), channel_id=1, source_target_pairs={{0,1},{1,0},{2,3},{3,2},{4,8},{5,9},{6,10},{7,11},{8,4},{9,5},{10,... | collective-permute-start | bytes 18440 | tf_op jit(solution)/shard_map/ppermute | solution.py:515
  76.7 4.8 %collective-permute-start.29 = (f32[12,128]{1,0:T(8,128)S(1)}, f32[12,128]{1,0:T(8,128)S(1)}, u32[]{:S(2)}, u32[]{:S(2)}) collective-permute-start(f32[12,128]{1,0:T(8,128)S(1)} %get-tuple-element.108), channel_id=1, source_target_pairs={{0,3},{1,2},{2,1},{3,0},{4,7},{5,6},{6,5},{7,4},{8,11},{9,10},{10,... | collective-permute-start | bytes 18440 | tf_op jit(solution)/shard_map/ppermute | solution.py:515
  77.8 4.2 %collective-permute-start.30 = (f32[12,128]{1,0:T(8,128)S(1)}, f32[12,128]{1,0:T(8,128)S(1)}, u32[]{:S(2)}, u32[]{:S(2)}) collective-permute-start(f32[12,128]{1,0:T(8,128)S(1)} %get-tuple-element.109), channel_id=1, source_target_pairs={{0,4},{1,5},{2,6},{3,7},{4,0},{5,1},{6,2},{7,3},{8,12},{9,13},{10,... | collective-permute-start | bytes 18440 | tf_op jit(solution)/shard_map/ppermute | solution.py:515
  (24 other events, 71.3 us)

commit v9 on v8

--- a/solution.py
+++ b/solution.py
@@ -175,9 +175,11 @@
     gather_slots(position_row, coords.shape[1] // LANES, inverse, outgoing)
 
 
-def halo_kernel(
-    counts, disp_in, lists_in, nodes_in, stiff, after, disp, lists, nodes, splat, *sends
-):
+def prepare_kernel(counts, *refs):
+    (disp_in, lists_in, nodes_in, stiff, coords_in, vel_in, ext_in) = refs[:7]
+    (classes, pairs, thick_in, mass_in, after) = refs[7:12]
+    (disp, lists, nodes, splat, coords, vel, ext, slow, select, thick, mass) = refs[12:23]
+    sends = refs[23:]
     px_no = lax.axis_index("px")
     py_no = lax.axis_index("py")
     own_count = disp_in.shape[1]
@@ -207,9 +209,6 @@
     size = stiff.shape[0]
     for j in range(size):
         splat[j * size : (j + 1) * size, :] = jnp.broadcast_to(stiff[:, j : j + 1], (size, LANES))
-
-
-def rest_kernel(coords_in, vel_in, ext_in, classes, pairs, after, coords, vel, ext, slow, select):
     spread_rows(coords_in, coords, 3)
     spread_rows(vel_in, vel, 3)
     spread_rows(ext_in, ext, 3)
@@ -224,6 +223,8 @@
     onehot = (tile_no == jnp.concatenate(ends, axis=1)).astype(F32)
     select[0] = onehot
     select[1] = jnp.transpose(onehot)
+    thick[...] = thick_in[...]
+    mass[...] = mass_in[...]
 
 
 def own_kernel(disp, nodes, found):
@@ -575,26 +576,51 @@
         + [pltpu.SemaphoreType.DMA((4,))],
         vmem_bytes=WHOLE_VMEM,
     )
-    disp, lists, nodes, splat, *sends = call(
-        functools.partial(halo_kernel, counts),
-        [displacement, halo_lists, elem_nodes, stiffness, inverse],
+    (
+        disp,
+        lists,
+        nodes,
+        splat,
+        coords,
+        vel,
+        ext,
+        slow,
+        select,
+        thickness,
+        inv_mass,
+        *sends,
+    ) = call(
+        functools.partial(prepare_kernel, counts),
+        [
+            displacement,
+            halo_lists,
+            elem_nodes,
+            stiffness,
+            coords,
+            velocity,
+            ext_force,
+            block_class.reshape(1, -1),
+            tile_pairs,
+            thickness,
+            inv_mass,
+            inverse,
+        ],
         [
             nodal,
             jax.ShapeDtypeStruct((4 * quarter, LANES), I32),
             jax.ShapeDtypeStruct((4 * elem_rows, LANES), I32),
             shape(144, LANES),
         ]
+        + [nodal] * 3
+        + [
+            jax.ShapeDtypeStruct((elem_rows, LANES), I32),
+            shape(2, LANES, LANES),
+            shape(elem_rows, LANES),
+            shape(rows, LANES),
+        ]
         + sent,
-        "halo",
-        far=(4,),
-    )
-    coords, vel, ext, slow, select = call(
-        rest_kernel,
-        [coords, velocity, ext_force, block_class.reshape(1, -1), tile_pairs, lists],
-        [nodal] * 3
-        + [jax.ShapeDtypeStruct((elem_rows, LANES), I32), shape(2, LANES, LANES)],
-        "rest",
-        far=(5,),
+        "prepare",
+        far=(11,),
     )
     for step_no in range(STEPS):
         for sub_no in range(SUBS):

time: 83.5 us -> 86.8 us (1.040)
  local copies, waits for them, and re-layouts: 1.21 us -> 3.51 us
    unnamed x24, local copies, waits for them, and re-layouts: 1.21 us -> 3.51 us
    pallas_call x26 -> x25, Pallas kernels: 21.3 us -> 21.3 us  [call(): pl.pallas_call(kernel, out_shape=tuple(outputs), in_specs=specs, out_spec...]
where the time goes in v9:
time: 86.8 us; the launch traced here: 86.2 us
  starting transfers between devices  53 us (61%)
  Pallas kernels  21.3 us (25%)
  waiting for transfers between devices  7.29 us (8%)
  local copies, waits for them, and re-layouts  3.51 us (4%)
  between operations  1.12 us (1%)
    ppermute x32, starting transfers between devices, exchange(): lax.ppermute(blocks[n], ('px', 'py'), swaps[n])  33.5 us
    pallas_call x25, Pallas kernels, call(): pl.pallas_call(kernel, out_shape=tuple(outputs), in_specs=specs, out_spec...  21.3 us
    all_to_all x4, starting transfers between devices, swap(): return lax.all_to_all(slots, axes, 0, 0, tiled=True)  19.5 us
    ppermute x32, waiting for transfers between devices, exchange(): lax.ppermute(blocks[n], ('px', 'py'), swaps[n])  5.62 us
    unnamed x24, local copies, waits for them, and re-layouts  3.51 us
  transfers between devices with their start and end apart: 36, of which 11 were waited for; matrix products, arithmetic and copies ran while one was open for 0% of the time, Pallas kernels for 10%

profile of v9, /device:TPU:0, one launch (start us, length us, event | category | flops | bytes accessed | tf_op | source)
XLA Modules:
  0.0 86.2 jit_solution(13392107039623661121)
XLA Ops:
  0.6 2.2 %slots.1 = (s32[32,128]{1,0:T(8,128)}, f32[32,3,128]{2,1,0:T(4,128)}) custom-call(f32[3,2048]{1,0:T(4,128)} %refs_4_.1, f32[3,2048]{1,0:T(4,128)} %refs_0_.3, s32[16,128]{1,0:T(8,128)} %bitcast.8, s32[16,128]{1,0:T(8,128)} %bitcast.9), custom_call_target="tpu_custom_call" | custom-call | tf_op jit(solution)/shard_map/slots/pallas_call | solution.py:487
  2.9 7.3 %all-to-all-start = ((f32[32,3,128]{2,1,0:T(4,128)}), f32[32,3,128]{2,1,0:T(4,128)S(1)}, u32[]{:S(2)}, u32[]{:S(2)}) async-start(f32[32,3,128]{2,1,0:T(4,128)} %get-tuple-element.70), calls=%async_computation | async-start | bytes 131072 | tf_op jit(solution)/shard_map/all_to_all | solution.py:522
  14.4 1.6 %collective-permute-start.1 = (f32[12,128]{1,0:T(8,128)S(1)}, f32[12,128]{1,0:T(8,128)S(1)}, u32[]{:S(2)}, u32[]{:S(2)}) collective-permute-start(f32[12,128]{1,0:T(8,128)S(1)} %get-tuple-element.64), channel_id=1, source_target_pairs={{0,3},{1,2},{2,1},{3,0},{4,7},{5,6},{6,5},{7,4},{8,11},{9,10},{10,... | collective-permute-start | bytes 18440 | tf_op jit(solution)/shard_map/ppermute | solution.py:516
  16.1 2.3 %collective-permute-start.2 = (f32[12,128]{1,0:T(8,128)S(1)}, f32[12,128]{1,0:T(8,128)S(1)}, u32[]{:S(2)}, u32[]{:S(2)}) collective-permute-start(f32[12,128]{1,0:T(8,128)S(1)} %get-tuple-element.65), channel_id=1, source_target_pairs={{0,4},{1,5},{2,6},{3,7},{4,0},{5,1},{6,2},{7,3},{8,12},{9,13},{10,... | collective-permute-start | bytes 18440 | tf_op jit(solution)/shard_map/ppermute | solution.py:516
  20.6 2.1 %contact.2.after = f32[32,3,128]{2,1,0:T(4,128)} custom-call(f32[2,128,128]{2,1,0:T(8,128)S(1)} %get-tuple-element.69.select, f32[32,3,128]{2,1,0:T(4,128)S(1)} %all-to-all-done.arrived, f32[192,128]{1,0:T(8,128)S(1)} %forces.2.after.held), custom_call_target="tpu_custom_call" | custom-call | tf_op jit(solution)/shard_map/contact/pallas_call | solution.py:487
  22.7 4.3 %all-to-all-start.1 = ((f32[32,3,128]{2,1,0:T(4,128)}), f32[32,3,128]{2,1,0:T(4,128)S(1)}, u32[]{:S(2)}, u32[]{:S(2)}) async-start(f32[32,3,128]{2,1,0:T(4,128)} %contact.2.after), calls=%async_computation.1 | async-start | bytes 131072 | tf_op jit(solution)/shard_map/all_to_all | solution.py:522
  28.1 1.6 %collective-permute-start.5 = (f32[12,128]{1,0:T(8,128)S(1)}, f32[12,128]{1,0:T(8,128)S(1)}, u32[]{:S(2)}, u32[]{:S(2)}) collective-permute-start(f32[12,128]{1,0:T(8,128)S(1)} %get-tuple-element.73), channel_id=1, source_target_pairs={{0,3},{1,2},{2,1},{3,0},{4,7},{5,6},{6,5},{7,4},{8,11},{9,10},{10,... | collective-permute-start | bytes 18440 | tf_op jit(solution)/shard_map/ppermute | solution.py:516
  29.7 2.3 %collective-permute-start.6 = (f32[12,128]{1,0:T(8,128)S(1)}, f32[12,128]{1,0:T(8,128)S(1)}, u32[]{:S(2)}, u32[]{:S(2)}) collective-permute-start(f32[12,128]{1,0:T(8,128)S(1)} %get-tuple-element.74), channel_id=1, source_target_pairs={{0,4},{1,5},{2,6},{3,7},{4,0},{5,1},{6,2},{7,3},{8,12},{9,13},{10,... | collective-permute-start | bytes 18440 | tf_op jit(solution)/shard_map/ppermute | solution.py:516
  35.7 2.4 %collective-permute-start.10 = (f32[12,128]{1,0:T(8,128)S(1)}, f32[12,128]{1,0:T(8,128)S(1)}, u32[]{:S(2)}, u32[]{:S(2)}) collective-permute-start(f32[12,128]{1,0:T(8,128)S(1)} %get-tuple-element.82), channel_id=1, source_target_pairs={{0,4},{1,5},{2,6},{3,7},{4,0},{5,1},{6,2},{7,3},{8,12},{9,13},{10,... | collective-permute-start | bytes 18440 | tf_op jit(solution)/shard_map/ppermute | solution.py:516
  39.8 1.5 %forces_halo_sum.2 = (f32[192,128]{1,0:T(8,128)S(1)}, f32[12,128]{1,0:T(8,128)S(1)}, f32[12,128]{1,0:T(8,128)S(1)}, f32[12,128]{1,0:T(8,128)S(1)}, f32[12,128]{1,0:T(8,128)S(1)}) custom-call(f32[192,128]{1,0:T(8,128)S(1)} %own_corners.5.found, f32[12,128]{1,0:T(8,128)S(1)} %collective-permute-done.8.recv1, f32[12,128]{1,0:T(8,128)S(1)} %collective-permute-done.9.recv3, ...), custom_call_target="tpu_custom_call" | custom-call | tf_op jit(solution)/shard_map/forces_halo_sum/pallas_call | solution.py:487
  41.5 1.2 %collective-permute-start.13 = (f32[12,128]{1,0:T(8,128)S(1)}, f32[12,128]{1,0:T(8,128)S(1)}, u32[]{:S(2)}, u32[]{:S(2)}) collective-permute-start(f32[12,128]{1,0:T(8,128)S(1)} %get-tuple-element.88), channel_id=1, source_target_pairs={{0,3},{1,2},{2,1},{3,0},{4,7},{5,6},{6,5},{7,4},{8,11},{9,10},{10,... | collective-permute-start | bytes 18440 | tf_op jit(solution)/shard_map/ppermute | solution.py:516
  42.7 2.5 %collective-permute-start.14 = (f32[12,128]{1,0:T(8,128)S(1)}, f32[12,128]{1,0:T(8,128)S(1)}, u32[]{:S(2)}, u32[]{:S(2)}) collective-permute-start(f32[12,128]{1,0:T(8,128)S(1)} %get-tuple-element.89), channel_id=1, source_target_pairs={{0,4},{1,5},{2,6},{3,7},{4,0},{5,1},{6,2},{7,3},{8,12},{9,13},{10,... | collective-permute-start | bytes 18440 | tf_op jit(solution)/shard_map/ppermute | solution.py:516
  46.9 1.3 %last_update.1 = (f32[48,128]{1,0:T(8,128)S(1)}, f32[48,128]{1,0:T(8,128)S(1)}, f32[32,3,128]{2,1,0:T(4,128)}) custom-call(f32[48,128]{1,0:T(8,128)S(1)} %own_sum.5.refs_0_, f32[12,128]{1,0:T(8,128)S(1)} %collective-permute-done.12.refs_1_, f32[12,128]{1,0:T(8,128)S(1)} %collective-permute-done.13.refs_2_, f32[12,128]{1,0:T(8,128)S(1)} %collective-permute-done.14.refs_3_, ...), custom_call_target="tpu_custom_call" | custom-call | tf_op jit(solution)/shard_map/last_update/pallas_call | solution.py:487
  48.1 4.2 %all-to-all-start.2 = ((f32[32,3,128]{2,1,0:T(4,128)}), f32[32,3,128]{2,1,0:T(4,128)S(1)}, u32[]{:S(2)}, u32[]{:S(2)}) async-start(f32[32,3,128]{2,1,0:T(4,128)} %get-tuple-element.94.after), calls=%async_computation.2 | async-start | bytes 131072 | tf_op jit(solution)/shard_map/all_to_all | solution.py:522
  52.8 1.6 %collective-permute-start.17 = (f32[12,128]{1,0:T(8,128)S(1)}, f32[12,128]{1,0:T(8,128)S(1)}, u32[]{:S(2)}, u32[]{:S(2)}) collective-permute-start(f32[12,128]{1,0:T(8,128)S(1)} %get-tuple-element.96), channel_id=1, source_target_pairs={{0,3},{1,2},{2,1},{3,0},{4,7},{5,6},{6,5},{7,4},{8,11},{9,10},{10,... | collective-permute-start | bytes 18440 | tf_op jit(solution)/shard_map/ppermute | solution.py:516
  54.5 2.3 %collective-permute-start.18 = (f32[12,128]{1,0:T(8,128)S(1)}, f32[12,128]{1,0:T(8,128)S(1)}, u32[]{:S(2)}, u32[]{:S(2)}) collective-permute-start(f32[12,128]{1,0:T(8,128)S(1)} %get-tuple-element.97), channel_id=1, source_target_pairs={{0,4},{1,5},{2,6},{3,7},{4,0},{5,1},{6,2},{7,3},{8,12},{9,13},{10,... | collective-permute-start | bytes 18440 | tf_op jit(solution)/shard_map/ppermute | solution.py:516
  59.7 2.1 %contact.3.after = f32[32,3,128]{2,1,0:T(4,128)} custom-call(f32[2,128,128]{2,1,0:T(8,128)S(1)} %get-tuple-element.69.select, f32[32,3,128]{2,1,0:T(4,128)S(1)} %all-to-all-done.2.arrived, f32[192,128]{1,0:T(8,128)S(1)} %forces.3.after.held), custom_call_target="tpu_custom_call" | custom-call | tf_op jit(solution)/shard_map/contact/pallas_call | solution.py:487
  61.9 3.7 %all-to-all-start.3 = ((f32[32,3,128]{2,1,0:T(4,128)}), f32[32,3,128]{2,1,0:T(4,128)S(1)}, u32[]{:S(2)}, u32[]{:S(2)}) async-start(f32[32,3,128]{2,1,0:T(4,128)} %contact.3.after), calls=%async_computation.3 | async-start | bytes 131072 | tf_op jit(solution)/shard_map/all_to_all | solution.py:522
  66.5 1.6 %collective-permute-start.21 = (f32[12,128]{1,0:T(8,128)S(1)}, f32[12,128]{1,0:T(8,128)S(1)}, u32[]{:S(2)}, u32[]{:S(2)}) collective-permute-start(f32[12,128]{1,0:T(8,128)S(1)} %get-tuple-element.101), channel_id=1, source_target_pairs={{0,3},{1,2},{2,1},{3,0},{4,7},{5,6},{6,5},{7,4},{8,11},{9,10},{10,... | collective-permute-start | bytes 18440 | tf_op jit(solution)/shard_map/ppermute | solution.py:516
  68.1 2.3 %collective-permute-start.22 = (f32[12,128]{1,0:T(8,128)S(1)}, f32[12,128]{1,0:T(8,128)S(1)}, u32[]{:S(2)}, u32[]{:S(2)}) collective-permute-start(f32[12,128]{1,0:T(8,128)S(1)} %get-tuple-element.102), channel_id=1, source_target_pairs={{0,4},{1,5},{2,6},{3,7},{4,0},{5,1},{6,2},{7,3},{8,12},{9,13},{10,... | collective-permute-start | bytes 18440 | tf_op jit(solution)/shard_map/ppermute | solution.py:516
  74.1 2.4 %collective-permute-start.26 = (f32[12,128]{1,0:T(8,128)S(1)}, f32[12,128]{1,0:T(8,128)S(1)}, u32[]{:S(2)}, u32[]{:S(2)}) collective-permute-start(f32[12,128]{1,0:T(8,128)S(1)} %get-tuple-element.107), channel_id=1, source_target_pairs={{0,4},{1,5},{2,6},{3,7},{4,0},{5,1},{6,2},{7,3},{8,12},{9,13},{10,... | collective-permute-start | bytes 18440 | tf_op jit(solution)/shard_map/ppermute | solution.py:516
  78.2 1.5 %forces_halo_sum.3 = (f32[192,128]{1,0:T(8,128)S(1)}, f32[12,128]{1,0:T(8,128)S(1)}, f32[12,128]{1,0:T(8,128)S(1)}, f32[12,128]{1,0:T(8,128)S(1)}, f32[12,128]{1,0:T(8,128)S(1)}) custom-call(f32[192,128]{1,0:T(8,128)S(1)} %own_corners.7.found, f32[12,128]{1,0:T(8,128)S(1)} %collective-permute-done.24.recv1, f32[12,128]{1,0:T(8,128)S(1)} %collective-permute-done.25.recv3, ...), custom_call_target="tpu_custom_call" | custom-call | tf_op jit(solution)/shard_map/forces_halo_sum/pallas_call | solution.py:487
  79.9 1.2 %collective-permute-start.29 = (f32[12,128]{1,0:T(8,128)S(1)}, f32[12,128]{1,0:T(8,128)S(1)}, u32[]{:S(2)}, u32[]{:S(2)}) collective-permute-start(f32[12,128]{1,0:T(8,128)S(1)} %get-tuple-element.112), channel_id=1, source_target_pairs={{0,3},{1,2},{2,1},{3,0},{4,7},{5,6},{6,5},{7,4},{8,11},{9,10},{10,... | collective-permute-start | bytes 18440 | tf_op jit(solution)/shard_map/ppermute | solution.py:516
  81.1 2.5 %collective-permute-start.30 = (f32[12,128]{1,0:T(8,128)S(1)}, f32[12,128]{1,0:T(8,128)S(1)}, u32[]{:S(2)}, u32[]{:S(2)}) collective-permute-start(f32[12,128]{1,0:T(8,128)S(1)} %get-tuple-element.113), channel_id=1, source_target_pairs={{0,4},{1,5},{2,6},{3,7},{4,0},{5,1},{6,2},{7,3},{8,12},{9,13},{10,... | collective-permute-start | bytes 18440 | tf_op jit(solution)/shard_map/ppermute | solution.py:516
  (97 shorter events, 27.0 us)
Async XLA Ops:
  2.9 17.6 %all-to-all-start = ((f32[32,3,128]{2,1,0:T(4,128)}), f32[32,3,128]{2,1,0:T(4,128)S(1)}, u32[]{:S(2)}, u32[]{:S(2)}) async-start(f32[32,3,128]{2,1,0:T(4,128)} %get-tuple-element.70), calls=%async_computation | async-start | bytes 131072 | tf_op jit(solution)/shard_map/all_to_all | solution.py:522
  14.1 5.1 %collective-permute-start = (f32[12,128]{1,0:T(8,128)S(1)}, f32[12,128]{1,0:T(8,128)S(1)}, u32[]{:S(2)}, u32[]{:S(2)}) collective-permute-start(f32[12,128]{1,0:T(8,128)S(1)} %get-tuple-element.63), channel_id=1, source_target_pairs={{0,1},{1,0},{2,3},{3,2},{4,8},{5,9},{6,10},{7,11},{8,4},{9,5},{10,... | collective-permute-start | bytes 18440 | tf_op jit(solution)/shard_map/ppermute | solution.py:516
  14.4 4.8 %collective-permute-start.1 = (f32[12,128]{1,0:T(8,128)S(1)}, f32[12,128]{1,0:T(8,128)S(1)}, u32[]{:S(2)}, u32[]{:S(2)}) collective-permute-start(f32[12,128]{1,0:T(8,128)S(1)} %get-tuple-element.64), channel_id=1, source_target_pairs={{0,3},{1,2},{2,1},{3,0},{4,7},{5,6},{6,5},{7,4},{8,11},{9,10},{10,... | collective-permute-start | bytes 18440 | tf_op jit(solution)/shard_map/ppermute | solution.py:516
  16.1 4.0 %collective-permute-start.2 = (f32[12,128]{1,0:T(8,128)S(1)}, f32[12,128]{1,0:T(8,128)S(1)}, u32[]{:S(2)}, u32[]{:S(2)}) collective-permute-start(f32[12,128]{1,0:T(8,128)S(1)} %get-tuple-element.65), channel_id=1, source_target_pairs={{0,4},{1,5},{2,6},{3,7},{4,0},{5,1},{6,2},{7,3},{8,12},{9,13},{10,... | collective-permute-start | bytes 18440 | tf_op jit(solution)/shard_map/ppermute | solution.py:516
  22.7 11.7 %all-to-all-start.1 = ((f32[32,3,128]{2,1,0:T(4,128)}), f32[32,3,128]{2,1,0:T(4,128)S(1)}, u32[]{:S(2)}, u32[]{:S(2)}) async-start(f32[32,3,128]{2,1,0:T(4,128)} %contact.2.after), calls=%async_computation.1 | async-start | bytes 131072 | tf_op jit(solution)/shard_map/all_to_all | solution.py:522
  27.7 5.3 %collective-permute-start.4 = (f32[12,128]{1,0:T(8,128)S(1)}, f32[12,128]{1,0:T(8,128)S(1)}, u32[]{:S(2)}, u32[]{:S(2)}) collective-permute-start(f32[12,128]{1,0:T(8,128)S(1)} %get-tuple-element.72), channel_id=1, source_target_pairs={{0,1},{1,0},{2,3},{3,2},{4,8},{5,9},{6,10},{7,11},{8,4},{9,5},{10,... | collective-permute-start | bytes 18440 | tf_op jit(solution)/shard_map/ppermute | solution.py:516
  28.1 5.0 %collective-permute-start.5 = (f32[12,128]{1,0:T(8,128)S(1)}, f32[12,128]{1,0:T(8,128)S(1)}, u32[]{:S(2)}, u32[]{:S(2)}) collective-permute-start(f32[12,128]{1,0:T(8,128)S(1)} %get-tuple-element.73), channel_id=1, source_target_pairs={{0,3},{1,2},{2,1},{3,0},{4,7},{5,6},{6,5},{7,4},{8,11},{9,10},{10,... | collective-permute-start | bytes 18440 | tf_op jit(solution)/shard_map/ppermute | solution.py:516
  29.7 4.0 %collective-permute-start.6 = (f32[12,128]{1,0:T(8,128)S(1)}, f32[12,128]{1,0:T(8,128)S(1)}, u32[]{:S(2)}, u32[]{:S(2)}) collective-permute-start(f32[12,128]{1,0:T(8,128)S(1)} %get-tuple-element.74), channel_id=1, source_target_pairs={{0,4},{1,5},{2,6},{3,7},{4,0},{5,1},{6,2},{7,3},{8,12},{9,13},{10,... | collective-permute-start | bytes 18440 | tf_op jit(solution)/shard_map/ppermute | solution.py:516
  35.7 4.1 %collective-permute-start.10 = (f32[12,128]{1,0:T(8,128)S(1)}, f32[12,128]{1,0:T(8,128)S(1)}, u32[]{:S(2)}, u32[]{:S(2)}) collective-permute-start(f32[12,128]{1,0:T(8,128)S(1)} %get-tuple-element.82), channel_id=1, source_target_pairs={{0,4},{1,5},{2,6},{3,7},{4,0},{5,1},{6,2},{7,3},{8,12},{9,13},{10,... | collective-permute-start | bytes 18440 | tf_op jit(solution)/shard_map/ppermute | solution.py:516
  41.4 4.9 %collective-permute-start.12 = (f32[12,128]{1,0:T(8,128)S(1)}, f32[12,128]{1,0:T(8,128)S(1)}, u32[]{:S(2)}, u32[]{:S(2)}) collective-permute-start(f32[12,128]{1,0:T(8,128)S(1)} %get-tuple-element.87), channel_id=1, source_target_pairs={{0,1},{1,0},{2,3},{3,2},{4,8},{5,9},{6,10},{7,11},{8,4},{9,5},{10,... | collective-permute-start | bytes 18440 | tf_op jit(solution)/shard_map/ppermute | solution.py:516
  41.5 4.8 %collective-permute-start.13 = (f32[12,128]{1,0:T(8,128)S(1)}, f32[12,128]{1,0:T(8,128)S(1)}, u32[]{:S(2)}, u32[]{:S(2)}) collective-permute-start(f32[12,128]{1,0:T(8,128)S(1)} %get-tuple-element.88), channel_id=1, source_target_pairs={{0,3},{1,2},{2,1},{3,0},{4,7},{5,6},{6,5},{7,4},{8,11},{9,10},{10,... | collective-permute-start | bytes 18440 | tf_op jit(solution)/shard_map/ppermute | solution.py:516
  42.7 4.2 %collective-permute-start.14 = (f32[12,128]{1,0:T(8,128)S(1)}, f32[12,128]{1,0:T(8,128)S(1)}, u32[]{:S(2)}, u32[]{:S(2)}) collective-permute-start(f32[12,128]{1,0:T(8,128)S(1)} %get-tuple-element.89), channel_id=1, source_target_pairs={{0,4},{1,5},{2,6},{3,7},{4,0},{5,1},{6,2},{7,3},{8,12},{9,13},{10,... | collective-permute-start | bytes 18440 | tf_op jit(solution)/shard_map/ppermute | solution.py:516
  48.1 11.6 %all-to-all-start.2 = ((f32[32,3,128]{2,1,0:T(4,128)}), f32[32,3,128]{2,1,0:T(4,128)S(1)}, u32[]{:S(2)}, u32[]{:S(2)}) async-start(f32[32,3,128]{2,1,0:T(4,128)} %get-tuple-element.94.after), calls=%async_computation.2 | async-start | bytes 131072 | tf_op jit(solution)/shard_map/all_to_all | solution.py:522
  52.5 5.1 %collective-permute-start.16 = (f32[12,128]{1,0:T(8,128)S(1)}, f32[12,128]{1,0:T(8,128)S(1)}, u32[]{:S(2)}, u32[]{:S(2)}) collective-permute-start(f32[12,128]{1,0:T(8,128)S(1)} %get-tuple-element.95), channel_id=1, source_target_pairs={{0,1},{1,0},{2,3},{3,2},{4,8},{5,9},{6,10},{7,11},{8,4},{9,5},{10,... | collective-permute-start | bytes 18440 | tf_op jit(solution)/shard_map/ppermute | solution.py:516
  52.8 4.8 %collective-permute-start.17 = (f32[12,128]{1,0:T(8,128)S(1)}, f32[12,128]{1,0:T(8,128)S(1)}, u32[]{:S(2)}, u32[]{:S(2)}) collective-permute-start(f32[12,128]{1,0:T(8,128)S(1)} %get-tuple-element.96), channel_id=1, source_target_pairs={{0,3},{1,2},{2,1},{3,0},{4,7},{5,6},{6,5},{7,4},{8,11},{9,10},{10,... | collective-permute-start | bytes 18440 | tf_op jit(solution)/shard_map/ppermute | solution.py:516
  54.5 4.0 %collective-permute-start.18 = (f32[12,128]{1,0:T(8,128)S(1)}, f32[12,128]{1,0:T(8,128)S(1)}, u32[]{:S(2)}, u32[]{:S(2)}) collective-permute-start(f32[12,128]{1,0:T(8,128)S(1)} %get-tuple-element.97), channel_id=1, source_target_pairs={{0,4},{1,5},{2,6},{3,7},{4,0},{5,1},{6,2},{7,3},{8,12},{9,13},{10,... | collective-permute-start | bytes 18440 | tf_op jit(solution)/shard_map/ppermute | solution.py:516
  61.9 11.0 %all-to-all-start.3 = ((f32[32,3,128]{2,1,0:T(4,128)}), f32[32,3,128]{2,1,0:T(4,128)S(1)}, u32[]{:S(2)}, u32[]{:S(2)}) async-start(f32[32,3,128]{2,1,0:T(4,128)} %contact.3.after), calls=%async_computation.3 | async-start | bytes 131072 | tf_op jit(solution)/shard_map/all_to_all | solution.py:522
  66.3 5.1 %collective-permute-start.20 = (f32[12,128]{1,0:T(8,128)S(1)}, f32[12,128]{1,0:T(8,128)S(1)}, u32[]{:S(2)}, u32[]{:S(2)}) collective-permute-start(f32[12,128]{1,0:T(8,128)S(1)} %get-tuple-element.100), channel_id=1, source_target_pairs={{0,1},{1,0},{2,3},{3,2},{4,8},{5,9},{6,10},{7,11},{8,4},{9,5},{10,... | collective-permute-start | bytes 18440 | tf_op jit(solution)/shard_map/ppermute | solution.py:516
  66.5 5.0 %collective-permute-start.21 = (f32[12,128]{1,0:T(8,128)S(1)}, f32[12,128]{1,0:T(8,128)S(1)}, u32[]{:S(2)}, u32[]{:S(2)}) collective-permute-start(f32[12,128]{1,0:T(8,128)S(1)} %get-tuple-element.101), channel_id=1, source_target_pairs={{0,3},{1,2},{2,1},{3,0},{4,7},{5,6},{6,5},{7,4},{8,11},{9,10},{10,... | collective-permute-start | bytes 18440 | tf_op jit(solution)/shard_map/ppermute | solution.py:516
  68.1 4.0 %collective-permute-start.22 = (f32[12,128]{1,0:T(8,128)S(1)}, f32[12,128]{1,0:T(8,128)S(1)}, u32[]{:S(2)}, u32[]{:S(2)}) collective-permute-start(f32[12,128]{1,0:T(8,128)S(1)} %get-tuple-element.102), channel_id=1, source_target_pairs={{0,4},{1,5},{2,6},{3,7},{4,0},{5,1},{6,2},{7,3},{8,12},{9,13},{10,... | collective-permute-start | bytes 18440 | tf_op jit(solution)/shard_map/ppermute | solution.py:516
  74.1 4.1 %collective-permute-start.26 = (f32[12,128]{1,0:T(8,128)S(1)}, f32[12,128]{1,0:T(8,128)S(1)}, u32[]{:S(2)}, u32[]{:S(2)}) collective-permute-start(f32[12,128]{1,0:T(8,128)S(1)} %get-tuple-element.107), channel_id=1, source_target_pairs={{0,4},{1,5},{2,6},{3,7},{4,0},{5,1},{6,2},{7,3},{8,12},{9,13},{10,... | collective-permute-start | bytes 18440 | tf_op jit(solution)/shard_map/ppermute | solution.py:516
  79.8 4.9 %collective-permute-start.28 = (f32[12,128]{1,0:T(8,128)S(1)}, f32[12,128]{1,0:T(8,128)S(1)}, u32[]{:S(2)}, u32[]{:S(2)}) collective-permute-start(f32[12,128]{1,0:T(8,128)S(1)} %get-tuple-element.111), channel_id=1, source_target_pairs={{0,1},{1,0},{2,3},{3,2},{4,8},{5,9},{6,10},{7,11},{8,4},{9,5},{10,... | collective-permute-start | bytes 18440 | tf_op jit(solution)/shard_map/ppermute | solution.py:516
  79.9 4.8 %collective-permute-start.29 = (f32[12,128]{1,0:T(8,128)S(1)}, f32[12,128]{1,0:T(8,128)S(1)}, u32[]{:S(2)}, u32[]{:S(2)}) collective-permute-start(f32[12,128]{1,0:T(8,128)S(1)} %get-tuple-element.112), channel_id=1, source_target_pairs={{0,3},{1,2},{2,1},{3,0},{4,7},{5,6},{6,5},{7,4},{8,11},{9,10},{10,... | collective-permute-start | bytes 18440 | tf_op jit(solution)/shard_map/ppermute | solution.py:516
  81.1 4.2 %collective-permute-start.30 = (f32[12,128]{1,0:T(8,128)S(1)}, f32[12,128]{1,0:T(8,128)S(1)}, u32[]{:S(2)}, u32[]{:S(2)}) collective-permute-start(f32[12,128]{1,0:T(8,128)S(1)} %get-tuple-element.113), channel_id=1, source_target_pairs={{0,4},{1,5},{2,6},{3,7},{4,0},{5,1},{6,2},{7,3},{8,12},{9,13},{10,... | collective-permute-start | bytes 18440 | tf_op jit(solution)/shard_map/ppermute | solution.py:516
  (24 other events, 84.3 us)

commit v10 on v8

--- a/solution.py
+++ b/solution.py
@@ -175,9 +175,10 @@
     gather_slots(position_row, coords.shape[1] // LANES, inverse, outgoing)
 
 
-def halo_kernel(
-    counts, disp_in, lists_in, nodes_in, stiff, after, disp, lists, nodes, splat, *sends
-):
+def prepare_kernel(counts, *refs):
+    (disp_in, lists_in, nodes_in, stiff, pairs, thick_in, after) = refs[:7]
+    (disp, lists, nodes, splat, select, thick) = refs[7:13]
+    sends = refs[13:]
     px_no = lax.axis_index("px")
     py_no = lax.axis_index("py")
     own_count = disp_in.shape[1]
@@ -207,15 +208,6 @@
     size = stiff.shape[0]
     for j in range(size):
         splat[j * size : (j + 1) * size, :] = jnp.broadcast_to(stiff[:, j : j + 1], (size, LANES))
-
-
-def rest_kernel(coords_in, vel_in, ext_in, classes, pairs, after, coords, vel, ext, slow, select):
-    spread_rows(coords_in, coords, 3)
-    spread_rows(vel_in, vel, 3)
-    spread_rows(ext_in, ext, 3)
-    blocks = classes.shape[1]
-    row = jnp.concatenate([classes[...], jnp.zeros((1, LANES - blocks), I32)], axis=1)
-    slow[...] = jnp.transpose(jnp.broadcast_to(row, (LANES, LANES)))[:blocks]
     ends = [pairs[0:1, :], pairs[1:2, :]]
     short = LANES - 2 * pairs.shape[1]
     if short:
@@ -224,6 +216,7 @@
     onehot = (tile_no == jnp.concatenate(ends, axis=1)).astype(F32)
     select[0] = onehot
     select[1] = jnp.transpose(onehot)
+    thick[...] = thick_in[...]
 
 
 def own_kernel(disp, nodes, found):
@@ -417,10 +410,20 @@
     return [array[c * rows : (c + 1) * rows, :] for c in range(3)]
 
 
-def first_update_kernel(
-    internal, returned, inverse, lists, ext, inv_mass, vel, disp, new_vel, new_disp, contact, *sends
-):
+def first_update_kernel(starting, *refs):
+    refs = list(refs)
+    internal, returned, inverse, lists, inv_mass, disp, vel, ext = refs[:8]
+    new_vel, new_disp, contact, *sends = refs[9 if starting else 8 :]
     rows = disp.shape[0] // 3
+    if starting:
+        classes = refs[8]
+        *sends, ext_rows, slow = sends
+        spread_rows(vel, new_vel, 3)
+        spread_rows(ext, ext_rows, 3)
+        vel, ext = new_vel, ext_rows
+        blocks = classes.shape[1]
+        row = jnp.concatenate([classes[...], jnp.zeros((1, LANES - blocks), I32)], axis=1)
+        slow[...] = jnp.transpose(jnp.broadcast_to(row, (LANES, LANES)))[:blocks]
     sums = scatter_add(
         lambda r: inverse[r : r + 1, :],
         lambda c, r: returned[r, c : c + 1, :],
@@ -460,8 +463,8 @@
     if case == "last":
 
         def position_row(c, h):
-            span = slice(c * rows + h, c * rows + h + 1)
-            return coords[span, :] + new_disp[span, :]
+            mine = coords[c : c + 1, h * LANES : (h + 1) * LANES]
+            return mine + new_disp[c * rows + h : c * rows + h + 1, :]
 
         gather_slots(position_row, rows, inverse, outgoing)
     else:
@@ -575,27 +578,22 @@
         + [pltpu.SemaphoreType.DMA((4,))],
         vmem_bytes=WHOLE_VMEM,
     )
-    disp, lists, nodes, splat, *sends = call(
-        functools.partial(halo_kernel, counts),
-        [displacement, halo_lists, elem_nodes, stiffness, inverse],
+    disp, lists, nodes, splat, select, thickness, *sends = call(
+        functools.partial(prepare_kernel, counts),
+        [displacement, halo_lists, elem_nodes, stiffness, tile_pairs, thickness, outgoing],
         [
             nodal,
             jax.ShapeDtypeStruct((4 * quarter, LANES), I32),
             jax.ShapeDtypeStruct((4 * elem_rows, LANES), I32),
             shape(144, LANES),
+            shape(2, LANES, LANES),
+            shape(elem_rows, LANES),
         ]
         + sent,
-        "halo",
-        far=(4,),
-    )
-    coords, vel, ext, slow, select = call(
-        rest_kernel,
-        [coords, velocity, ext_force, block_class.reshape(1, -1), tile_pairs, lists],
-        [nodal] * 3
-        + [jax.ShapeDtypeStruct((elem_rows, LANES), I32), shape(2, LANES, LANES)],
-        "rest",
-        far=(5,),
-    )
+        "prepare",
+        far=(6,),
+    )
+    vel = velocity
     for step_no in range(STEPS):
         for sub_no in range(SUBS):
             first = sub_no == 0
@@ -637,19 +635,27 @@
                 )
             backs = exchange(outs)
             (own,) = call(own_sum_kernel, [forces, nodes, outs[2]], [nodal], "own_sum", far=(2,))
-            state = [lists, ext, inv_mass, vel, disp]
             if first:
                 (internal,) = call(
                     internal_kernel, [own, *backs, lists], [nodal], "internal"
                 )
+                inputs = [internal, returned, inverse, lists, inv_mass, disp, vel]
+                outputs = [nodal] * 3 + sent
+                if step_no == 0:
+                    inputs += [ext_force, block_class.reshape(1, -1)]
+                    outputs += [nodal, jax.ShapeDtypeStruct((elem_rows, LANES), I32)]
+                else:
+                    inputs.append(ext)
                 vel, disp, contact, *sends = call(
-                    first_update_kernel,
-                    [internal, returned, inverse] + state,
-                    [nodal] * 3 + sent,
+                    functools.partial(first_update_kernel, step_no == 0),
+                    inputs,
+                    outputs,
                     "first_update",
                 )
+                if step_no == 0:
+                    *sends, ext, slow = sends
                 continue
-            inputs = [own, *backs] + state + [contact]
+            inputs = [own, *backs, lists, ext, inv_mass, vel, disp, contact]
             if final:
                 vel, disp = call(
                     functools.partial(update_kernel, "final"),

time: 83.5 us -> 86.7 us (1.038)
  local copies, waits for them, and re-layouts: 1.21 us -> 3.42 us
    unnamed x24 -> x26, local copies, waits for them, and re-layouts: 1.21 us -> 3.42 us
    pallas_call x26 -> x25, Pallas kernels: 21.3 us -> 21.3 us  [call(): pl.pallas_call(kernel, out_shape=tuple(outputs), in_specs=specs, out_spec...]
where the time goes in v10:
time: 86.7 us; the launch traced here: 86.1 us
  starting transfers between devices  53.1 us (61%)
  Pallas kernels  21.3 us (25%)
  waiting for transfers between devices  7.26 us (8%)
  local copies, waits for them, and re-layouts  3.42 us (4%)
  between operations  1.08 us (1%)
    ppermute x32, starting transfers between devices, exchange(): lax.ppermute(blocks[n], ('px', 'py'), swaps[n])  33.5 us
    pallas_call x25, Pallas kernels, call(): pl.pallas_call(kernel, out_shape=tuple(outputs), in_specs=specs, out_spec...  21.3 us
    all_to_all x4, starting transfers between devices, swap(): return lax.all_to_all(slots, axes, 0, 0, tiled=True)  19.5 us
    ppermute x32, waiting for transfers between devices, exchange(): lax.ppermute(blocks[n], ('px', 'py'), swaps[n])  5.62 us
    unnamed x26, local copies, waits for them, and re-layouts  3.42 us
  transfers between devices with their start and end apart: 36, of which 11 were waited for; matrix products, arithmetic and copies ran while one was open for 0% of the time, Pallas kernels for 10%

profile of v10, /device:TPU:0, one launch (start us, length us, event | category | flops | bytes accessed | tf_op | source)
XLA Modules:
  0.0 86.1 jit_solution(12387475407596859734)
XLA Ops:
  0.6 2.2 %slots.1 = (s32[32,128]{1,0:T(8,128)}, f32[32,3,128]{2,1,0:T(4,128)}) custom-call(f32[3,2048]{1,0:T(4,128)} %refs_11_.1, f32[3,2048]{1,0:T(4,128)} %refs_0_.3, s32[16,128]{1,0:T(8,128)} %bitcast.11, s32[16,128]{1,0:T(8,128)} %bitcast.12), custom_call_target="tpu_custom_call" | custom-call | tf_op jit(solution)/shard_map/slots/pallas_call | solution.py:489
  2.9 7.3 %all-to-all-start = ((f32[32,3,128]{2,1,0:T(4,128)}), f32[32,3,128]{2,1,0:T(4,128)S(1)}, u32[]{:S(2)}, u32[]{:S(2)}) async-start(f32[32,3,128]{2,1,0:T(4,128)} %get-tuple-element.57.refs_6_), calls=%async_computation | async-start | bytes 131072 | tf_op jit(solution)/shard_map/all_to_all | solution.py:524
  13.6 1.6 %collective-permute-start.1 = (f32[12,128]{1,0:T(8,128)S(1)}, f32[12,128]{1,0:T(8,128)S(1)}, u32[]{:S(2)}, u32[]{:S(2)}) collective-permute-start(f32[12,128]{1,0:T(8,128)S(1)} %get-tuple-element.61), channel_id=1, source_target_pairs={{0,3},{1,2},{2,1},{3,0},{4,7},{5,6},{6,5},{7,4},{8,11},{9,10},{10,... | collective-permute-start | bytes 18440 | tf_op jit(solution)/shard_map/ppermute | solution.py:518
  15.2 2.3 %collective-permute-start.2 = (f32[12,128]{1,0:T(8,128)S(1)}, f32[12,128]{1,0:T(8,128)S(1)}, u32[]{:S(2)}, u32[]{:S(2)}) collective-permute-start(f32[12,128]{1,0:T(8,128)S(1)} %get-tuple-element.62), channel_id=1, source_target_pairs={{0,4},{1,5},{2,6},{3,7},{4,0},{5,1},{6,2},{7,3},{8,12},{9,13},{10,... | collective-permute-start | bytes 18440 | tf_op jit(solution)/shard_map/ppermute | solution.py:518
  19.7 2.1 %contact.2.after = f32[32,3,128]{2,1,0:T(4,128)} custom-call(f32[2,128,128]{2,1,0:T(8,128)S(1)} %get-tuple-element.66.select, f32[32,3,128]{2,1,0:T(4,128)S(1)} %all-to-all-done.arrived, f32[192,128]{1,0:T(8,128)S(1)} %forces.2.after.held), custom_call_target="tpu_custom_call" | custom-call | tf_op jit(solution)/shard_map/contact/pallas_call | solution.py:489
  21.9 4.3 %all-to-all-start.1 = ((f32[32,3,128]{2,1,0:T(4,128)}), f32[32,3,128]{2,1,0:T(4,128)S(1)}, u32[]{:S(2)}, u32[]{:S(2)}) async-start(f32[32,3,128]{2,1,0:T(4,128)} %contact.2.after), calls=%async_computation.1 | async-start | bytes 131072 | tf_op jit(solution)/shard_map/all_to_all | solution.py:524
  27.2 1.6 %collective-permute-start.5 = (f32[12,128]{1,0:T(8,128)S(1)}, f32[12,128]{1,0:T(8,128)S(1)}, u32[]{:S(2)}, u32[]{:S(2)}) collective-permute-start(f32[12,128]{1,0:T(8,128)S(1)} %get-tuple-element.69), channel_id=1, source_target_pairs={{0,3},{1,2},{2,1},{3,0},{4,7},{5,6},{6,5},{7,4},{8,11},{9,10},{10,... | collective-permute-start | bytes 18440 | tf_op jit(solution)/shard_map/ppermute | solution.py:518
  28.8 2.3 %collective-permute-start.6 = (f32[12,128]{1,0:T(8,128)S(1)}, f32[12,128]{1,0:T(8,128)S(1)}, u32[]{:S(2)}, u32[]{:S(2)}) collective-permute-start(f32[12,128]{1,0:T(8,128)S(1)} %get-tuple-element.70), channel_id=1, source_target_pairs={{0,4},{1,5},{2,6},{3,7},{4,0},{5,1},{6,2},{7,3},{8,12},{9,13},{10,... | collective-permute-start | bytes 18440 | tf_op jit(solution)/shard_map/ppermute | solution.py:518
  35.6 2.4 %collective-permute-start.10 = (f32[12,128]{1,0:T(8,128)S(1)}, f32[12,128]{1,0:T(8,128)S(1)}, u32[]{:S(2)}, u32[]{:S(2)}) collective-permute-start(f32[12,128]{1,0:T(8,128)S(1)} %get-tuple-element.76), channel_id=1, source_target_pairs={{0,4},{1,5},{2,6},{3,7},{4,0},{5,1},{6,2},{7,3},{8,12},{9,13},{10,... | collective-permute-start | bytes 18440 | tf_op jit(solution)/shard_map/ppermute | solution.py:518
  39.7 1.5 %forces_halo_sum.2 = (f32[192,128]{1,0:T(8,128)S(1)}, f32[12,128]{1,0:T(8,128)S(1)}, f32[12,128]{1,0:T(8,128)S(1)}, f32[12,128]{1,0:T(8,128)S(1)}, f32[12,128]{1,0:T(8,128)S(1)}) custom-call(f32[192,128]{1,0:T(8,128)S(1)} %own_corners.5.found, f32[12,128]{1,0:T(8,128)S(1)} %collective-permute-done.8.recv1, f32[12,128]{1,0:T(8,128)S(1)} %collective-permute-done.9.recv3, ...), custom_call_target="tpu_custom_call" | custom-call | tf_op jit(solution)/shard_map/forces_halo_sum/pallas_call | solution.py:489
  41.4 1.1 %collective-permute-start.13 = (f32[12,128]{1,0:T(8,128)S(1)}, f32[12,128]{1,0:T(8,128)S(1)}, u32[]{:S(2)}, u32[]{:S(2)}) collective-permute-start(f32[12,128]{1,0:T(8,128)S(1)} %get-tuple-element.82), channel_id=1, source_target_pairs={{0,3},{1,2},{2,1},{3,0},{4,7},{5,6},{6,5},{7,4},{8,11},{9,10},{10,... | collective-permute-start | bytes 18440 | tf_op jit(solution)/shard_map/ppermute | solution.py:518
  42.5 2.5 %collective-permute-start.14 = (f32[12,128]{1,0:T(8,128)S(1)}, f32[12,128]{1,0:T(8,128)S(1)}, u32[]{:S(2)}, u32[]{:S(2)}) collective-permute-start(f32[12,128]{1,0:T(8,128)S(1)} %get-tuple-element.83), channel_id=1, source_target_pairs={{0,4},{1,5},{2,6},{3,7},{4,0},{5,1},{6,2},{7,3},{8,12},{9,13},{10,... | collective-permute-start | bytes 18440 | tf_op jit(solution)/shard_map/ppermute | solution.py:518
  46.7 1.3 %last_update.1 = (f32[48,128]{1,0:T(8,128)S(1)}, f32[48,128]{1,0:T(8,128)S(1)}, f32[32,3,128]{2,1,0:T(4,128)}) custom-call(f32[48,128]{1,0:T(8,128)S(1)} %own_sum.5.refs_0_, f32[12,128]{1,0:T(8,128)S(1)} %collective-permute-done.12.refs_1_, f32[12,128]{1,0:T(8,128)S(1)} %collective-permute-done.13.refs_2_, f32[12,128]{1,0:T(8,128)S(1)} %collective-permute-done.14.refs_3_, ...), custom_call_target="tpu_custom_call" | custom-call | tf_op jit(solution)/shard_map/last_update/pallas_call | solution.py:489
  48.0 4.2 %all-to-all-start.2 = ((f32[32,3,128]{2,1,0:T(4,128)}), f32[32,3,128]{2,1,0:T(4,128)S(1)}, u32[]{:S(2)}, u32[]{:S(2)}) async-start(f32[32,3,128]{2,1,0:T(4,128)} %get-tuple-element.88.after), calls=%async_computation.2 | async-start | bytes 131072 | tf_op jit(solution)/shard_map/all_to_all | solution.py:524
  52.7 1.6 %collective-permute-start.17 = (f32[12,128]{1,0:T(8,128)S(1)}, f32[12,128]{1,0:T(8,128)S(1)}, u32[]{:S(2)}, u32[]{:S(2)}) collective-permute-start(f32[12,128]{1,0:T(8,128)S(1)} %get-tuple-element.90), channel_id=1, source_target_pairs={{0,3},{1,2},{2,1},{3,0},{4,7},{5,6},{6,5},{7,4},{8,11},{9,10},{10,... | collective-permute-start | bytes 18440 | tf_op jit(solution)/shard_map/ppermute | solution.py:518
  54.3 2.3 %collective-permute-start.18 = (f32[12,128]{1,0:T(8,128)S(1)}, f32[12,128]{1,0:T(8,128)S(1)}, u32[]{:S(2)}, u32[]{:S(2)}) collective-permute-start(f32[12,128]{1,0:T(8,128)S(1)} %get-tuple-element.91), channel_id=1, source_target_pairs={{0,4},{1,5},{2,6},{3,7},{4,0},{5,1},{6,2},{7,3},{8,12},{9,13},{10,... | collective-permute-start | bytes 18440 | tf_op jit(solution)/shard_map/ppermute | solution.py:518
  59.6 2.1 %contact.3.after = f32[32,3,128]{2,1,0:T(4,128)} custom-call(f32[2,128,128]{2,1,0:T(8,128)S(1)} %get-tuple-element.66.select, f32[32,3,128]{2,1,0:T(4,128)S(1)} %all-to-all-done.2.arrived, f32[192,128]{1,0:T(8,128)S(1)} %forces.3.after.held), custom_call_target="tpu_custom_call" | custom-call | tf_op jit(solution)/shard_map/contact/pallas_call | solution.py:489
  61.7 3.7 %all-to-all-start.3 = ((f32[32,3,128]{2,1,0:T(4,128)}), f32[32,3,128]{2,1,0:T(4,128)S(1)}, u32[]{:S(2)}, u32[]{:S(2)}) async-start(f32[32,3,128]{2,1,0:T(4,128)} %contact.3.after), calls=%async_computation.3 | async-start | bytes 131072 | tf_op jit(solution)/shard_map/all_to_all | solution.py:524
  66.3 1.6 %collective-permute-start.21 = (f32[12,128]{1,0:T(8,128)S(1)}, f32[12,128]{1,0:T(8,128)S(1)}, u32[]{:S(2)}, u32[]{:S(2)}) collective-permute-start(f32[12,128]{1,0:T(8,128)S(1)} %get-tuple-element.95), channel_id=1, source_target_pairs={{0,3},{1,2},{2,1},{3,0},{4,7},{5,6},{6,5},{7,4},{8,11},{9,10},{10,... | collective-permute-start | bytes 18440 | tf_op jit(solution)/shard_map/ppermute | solution.py:518
  67.9 2.3 %collective-permute-start.22 = (f32[12,128]{1,0:T(8,128)S(1)}, f32[12,128]{1,0:T(8,128)S(1)}, u32[]{:S(2)}, u32[]{:S(2)}) collective-permute-start(f32[12,128]{1,0:T(8,128)S(1)} %get-tuple-element.96), channel_id=1, source_target_pairs={{0,4},{1,5},{2,6},{3,7},{4,0},{5,1},{6,2},{7,3},{8,12},{9,13},{10,... | collective-permute-start | bytes 18440 | tf_op jit(solution)/shard_map/ppermute | solution.py:518
  73.9 2.4 %collective-permute-start.26 = (f32[12,128]{1,0:T(8,128)S(1)}, f32[12,128]{1,0:T(8,128)S(1)}, u32[]{:S(2)}, u32[]{:S(2)}) collective-permute-start(f32[12,128]{1,0:T(8,128)S(1)} %get-tuple-element.101), channel_id=1, source_target_pairs={{0,4},{1,5},{2,6},{3,7},{4,0},{5,1},{6,2},{7,3},{8,12},{9,13},{10,... | collective-permute-start | bytes 18440 | tf_op jit(solution)/shard_map/ppermute | solution.py:518
  78.1 1.5 %forces_halo_sum.3 = (f32[192,128]{1,0:T(8,128)S(1)}, f32[12,128]{1,0:T(8,128)S(1)}, f32[12,128]{1,0:T(8,128)S(1)}, f32[12,128]{1,0:T(8,128)S(1)}, f32[12,128]{1,0:T(8,128)S(1)}) custom-call(f32[192,128]{1,0:T(8,128)S(1)} %own_corners.7.found, f32[12,128]{1,0:T(8,128)S(1)} %collective-permute-done.24.recv1, f32[12,128]{1,0:T(8,128)S(1)} %collective-permute-done.25.recv3, ...), custom_call_target="tpu_custom_call" | custom-call | tf_op jit(solution)/shard_map/forces_halo_sum/pallas_call | solution.py:489
  79.8 1.1 %collective-permute-start.29 = (f32[12,128]{1,0:T(8,128)S(1)}, f32[12,128]{1,0:T(8,128)S(1)}, u32[]{:S(2)}, u32[]{:S(2)}) collective-permute-start(f32[12,128]{1,0:T(8,128)S(1)} %get-tuple-element.106), channel_id=1, source_target_pairs={{0,3},{1,2},{2,1},{3,0},{4,7},{5,6},{6,5},{7,4},{8,11},{9,10},{10,... | collective-permute-start | bytes 18440 | tf_op jit(solution)/shard_map/ppermute | solution.py:518
  80.9 2.5 %collective-permute-start.30 = (f32[12,128]{1,0:T(8,128)S(1)}, f32[12,128]{1,0:T(8,128)S(1)}, u32[]{:S(2)}, u32[]{:S(2)}) collective-permute-start(f32[12,128]{1,0:T(8,128)S(1)} %get-tuple-element.107), channel_id=1, source_target_pairs={{0,4},{1,5},{2,6},{3,7},{4,0},{5,1},{6,2},{7,3},{8,12},{9,13},{10,... | collective-permute-start | bytes 18440 | tf_op jit(solution)/shard_map/ppermute | solution.py:518
  (99 shorter events, 26.9 us)
Async XLA Ops:
  2.9 16.8 %all-to-all-start = ((f32[32,3,128]{2,1,0:T(4,128)}), f32[32,3,128]{2,1,0:T(4,128)S(1)}, u32[]{:S(2)}, u32[]{:S(2)}) async-start(f32[32,3,128]{2,1,0:T(4,128)} %get-tuple-element.57.refs_6_), calls=%async_computation | async-start | bytes 131072 | tf_op jit(solution)/shard_map/all_to_all | solution.py:524
  13.3 5.1 %collective-permute-start = (f32[12,128]{1,0:T(8,128)S(1)}, f32[12,128]{1,0:T(8,128)S(1)}, u32[]{:S(2)}, u32[]{:S(2)}) collective-permute-start(f32[12,128]{1,0:T(8,128)S(1)} %get-tuple-element.60), channel_id=1, source_target_pairs={{0,1},{1,0},{2,3},{3,2},{4,8},{5,9},{6,10},{7,11},{8,4},{9,5},{10,... | collective-permute-start | bytes 18440 | tf_op jit(solution)/shard_map/ppermute | solution.py:518
  13.6 4.8 %collective-permute-start.1 = (f32[12,128]{1,0:T(8,128)S(1)}, f32[12,128]{1,0:T(8,128)S(1)}, u32[]{:S(2)}, u32[]{:S(2)}) collective-permute-start(f32[12,128]{1,0:T(8,128)S(1)} %get-tuple-element.61), channel_id=1, source_target_pairs={{0,3},{1,2},{2,1},{3,0},{4,7},{5,6},{6,5},{7,4},{8,11},{9,10},{10,... | collective-permute-start | bytes 18440 | tf_op jit(solution)/shard_map/ppermute | solution.py:518
  21.9 11.7 %all-to-all-start.1 = ((f32[32,3,128]{2,1,0:T(4,128)}), f32[32,3,128]{2,1,0:T(4,128)S(1)}, u32[]{:S(2)}, u32[]{:S(2)}) async-start(f32[32,3,128]{2,1,0:T(4,128)} %contact.2.after), calls=%async_computation.1 | async-start | bytes 131072 | tf_op jit(solution)/shard_map/all_to_all | solution.py:524
  26.9 5.3 %collective-permute-start.4 = (f32[12,128]{1,0:T(8,128)S(1)}, f32[12,128]{1,0:T(8,128)S(1)}, u32[]{:S(2)}, u32[]{:S(2)}) collective-permute-start(f32[12,128]{1,0:T(8,128)S(1)} %get-tuple-element.68), channel_id=1, source_target_pairs={{0,1},{1,0},{2,3},{3,2},{4,8},{5,9},{6,10},{7,11},{8,4},{9,5},{10,... | collective-permute-start | bytes 18440 | tf_op jit(solution)/shard_map/ppermute | solution.py:518
  27.2 5.0 %collective-permute-start.5 = (f32[12,128]{1,0:T(8,128)S(1)}, f32[12,128]{1,0:T(8,128)S(1)}, u32[]{:S(2)}, u32[]{:S(2)}) collective-permute-start(f32[12,128]{1,0:T(8,128)S(1)} %get-tuple-element.69), channel_id=1, source_target_pairs={{0,3},{1,2},{2,1},{3,0},{4,7},{5,6},{6,5},{7,4},{8,11},{9,10},{10,... | collective-permute-start | bytes 18440 | tf_op jit(solution)/shard_map/ppermute | solution.py:518
  28.8 4.0 %collective-permute-start.6 = (f32[12,128]{1,0:T(8,128)S(1)}, f32[12,128]{1,0:T(8,128)S(1)}, u32[]{:S(2)}, u32[]{:S(2)}) collective-permute-start(f32[12,128]{1,0:T(8,128)S(1)} %get-tuple-element.70), channel_id=1, source_target_pairs={{0,4},{1,5},{2,6},{3,7},{4,0},{5,1},{6,2},{7,3},{8,12},{9,13},{10,... | collective-permute-start | bytes 18440 | tf_op jit(solution)/shard_map/ppermute | solution.py:518
  34.9 4.0 %collective-permute-start.8 = (f32[12,128]{1,0:T(8,128)S(1)}, f32[12,128]{1,0:T(8,128)S(1)}, u32[]{:S(2)}, u32[]{:S(2)}) collective-permute-start(f32[12,128]{1,0:T(8,128)S(1)} %get-tuple-element.74), channel_id=1, source_target_pairs={{0,1},{1,0},{2,3},{3,2},{4,8},{5,9},{6,10},{7,11},{8,4},{9,5},{10,... | collective-permute-start | bytes 18440 | tf_op jit(solution)/shard_map/ppermute | solution.py:518
  35.6 4.1 %collective-permute-start.10 = (f32[12,128]{1,0:T(8,128)S(1)}, f32[12,128]{1,0:T(8,128)S(1)}, u32[]{:S(2)}, u32[]{:S(2)}) collective-permute-start(f32[12,128]{1,0:T(8,128)S(1)} %get-tuple-element.76), channel_id=1, source_target_pairs={{0,4},{1,5},{2,6},{3,7},{4,0},{5,1},{6,2},{7,3},{8,12},{9,13},{10,... | collective-permute-start | bytes 18440 | tf_op jit(solution)/shard_map/ppermute | solution.py:518
  41.2 4.9 %collective-permute-start.12 = (f32[12,128]{1,0:T(8,128)S(1)}, f32[12,128]{1,0:T(8,128)S(1)}, u32[]{:S(2)}, u32[]{:S(2)}) collective-permute-start(f32[12,128]{1,0:T(8,128)S(1)} %get-tuple-element.81), channel_id=1, source_target_pairs={{0,1},{1,0},{2,3},{3,2},{4,8},{5,9},{6,10},{7,11},{8,4},{9,5},{10,... | collective-permute-start | bytes 18440 | tf_op jit(solution)/shard_map/ppermute | solution.py:518
  41.4 4.8 %collective-permute-start.13 = (f32[12,128]{1,0:T(8,128)S(1)}, f32[12,128]{1,0:T(8,128)S(1)}, u32[]{:S(2)}, u32[]{:S(2)}) collective-permute-start(f32[12,128]{1,0:T(8,128)S(1)} %get-tuple-element.82), channel_id=1, source_target_pairs={{0,3},{1,2},{2,1},{3,0},{4,7},{5,6},{6,5},{7,4},{8,11},{9,10},{10,... | collective-permute-start | bytes 18440 | tf_op jit(solution)/shard_map/ppermute | solution.py:518
  42.5 4.2 %collective-permute-start.14 = (f32[12,128]{1,0:T(8,128)S(1)}, f32[12,128]{1,0:T(8,128)S(1)}, u32[]{:S(2)}, u32[]{:S(2)}) collective-permute-start(f32[12,128]{1,0:T(8,128)S(1)} %get-tuple-element.83), channel_id=1, source_target_pairs={{0,4},{1,5},{2,6},{3,7},{4,0},{5,1},{6,2},{7,3},{8,12},{9,13},{10,... | collective-permute-start | bytes 18440 | tf_op jit(solution)/shard_map/ppermute | solution.py:518
  48.0 11.6 %all-to-all-start.2 = ((f32[32,3,128]{2,1,0:T(4,128)}), f32[32,3,128]{2,1,0:T(4,128)S(1)}, u32[]{:S(2)}, u32[]{:S(2)}) async-start(f32[32,3,128]{2,1,0:T(4,128)} %get-tuple-element.88.after), calls=%async_computation.2 | async-start | bytes 131072 | tf_op jit(solution)/shard_map/all_to_all | solution.py:524
  52.4 5.1 %collective-permute-start.16 = (f32[12,128]{1,0:T(8,128)S(1)}, f32[12,128]{1,0:T(8,128)S(1)}, u32[]{:S(2)}, u32[]{:S(2)}) collective-permute-start(f32[12,128]{1,0:T(8,128)S(1)} %get-tuple-element.89), channel_id=1, source_target_pairs={{0,1},{1,0},{2,3},{3,2},{4,8},{5,9},{6,10},{7,11},{8,4},{9,5},{10,... | collective-permute-start | bytes 18440 | tf_op jit(solution)/shard_map/ppermute | solution.py:518
  52.7 4.8 %collective-permute-start.17 = (f32[12,128]{1,0:T(8,128)S(1)}, f32[12,128]{1,0:T(8,128)S(1)}, u32[]{:S(2)}, u32[]{:S(2)}) collective-permute-start(f32[12,128]{1,0:T(8,128)S(1)} %get-tuple-element.90), channel_id=1, source_target_pairs={{0,3},{1,2},{2,1},{3,0},{4,7},{5,6},{6,5},{7,4},{8,11},{9,10},{10,... | collective-permute-start | bytes 18440 | tf_op jit(solution)/shard_map/ppermute | solution.py:518
  54.3 4.0 %collective-permute-start.18 = (f32[12,128]{1,0:T(8,128)S(1)}, f32[12,128]{1,0:T(8,128)S(1)}, u32[]{:S(2)}, u32[]{:S(2)}) collective-permute-start(f32[12,128]{1,0:T(8,128)S(1)} %get-tuple-element.91), channel_id=1, source_target_pairs={{0,4},{1,5},{2,6},{3,7},{4,0},{5,1},{6,2},{7,3},{8,12},{9,13},{10,... | collective-permute-start | bytes 18440 | tf_op jit(solution)/shard_map/ppermute | solution.py:518
  61.7 11.0 %all-to-all-start.3 = ((f32[32,3,128]{2,1,0:T(4,128)}), f32[32,3,128]{2,1,0:T(4,128)S(1)}, u32[]{:S(2)}, u32[]{:S(2)}) async-start(f32[32,3,128]{2,1,0:T(4,128)} %contact.3.after), calls=%async_computation.3 | async-start | bytes 131072 | tf_op jit(solution)/shard_map/all_to_all | solution.py:524
  66.2 5.1 %collective-permute-start.20 = (f32[12,128]{1,0:T(8,128)S(1)}, f32[12,128]{1,0:T(8,128)S(1)}, u32[]{:S(2)}, u32[]{:S(2)}) collective-permute-start(f32[12,128]{1,0:T(8,128)S(1)} %get-tuple-element.94), channel_id=1, source_target_pairs={{0,1},{1,0},{2,3},{3,2},{4,8},{5,9},{6,10},{7,11},{8,4},{9,5},{10,... | collective-permute-start | bytes 18440 | tf_op jit(solution)/shard_map/ppermute | solution.py:518
  66.3 5.0 %collective-permute-start.21 = (f32[12,128]{1,0:T(8,128)S(1)}, f32[12,128]{1,0:T(8,128)S(1)}, u32[]{:S(2)}, u32[]{:S(2)}) collective-permute-start(f32[12,128]{1,0:T(8,128)S(1)} %get-tuple-element.95), channel_id=1, source_target_pairs={{0,3},{1,2},{2,1},{3,0},{4,7},{5,6},{6,5},{7,4},{8,11},{9,10},{10,... | collective-permute-start | bytes 18440 | tf_op jit(solution)/shard_map/ppermute | solution.py:518
  67.9 4.0 %collective-permute-start.22 = (f32[12,128]{1,0:T(8,128)S(1)}, f32[12,128]{1,0:T(8,128)S(1)}, u32[]{:S(2)}, u32[]{:S(2)}) collective-permute-start(f32[12,128]{1,0:T(8,128)S(1)} %get-tuple-element.96), channel_id=1, source_target_pairs={{0,4},{1,5},{2,6},{3,7},{4,0},{5,1},{6,2},{7,3},{8,12},{9,13},{10,... | collective-permute-start | bytes 18440 | tf_op jit(solution)/shard_map/ppermute | solution.py:518
  73.9 4.1 %collective-permute-start.26 = (f32[12,128]{1,0:T(8,128)S(1)}, f32[12,128]{1,0:T(8,128)S(1)}, u32[]{:S(2)}, u32[]{:S(2)}) collective-permute-start(f32[12,128]{1,0:T(8,128)S(1)} %get-tuple-element.101), channel_id=1, source_target_pairs={{0,4},{1,5},{2,6},{3,7},{4,0},{5,1},{6,2},{7,3},{8,12},{9,13},{10,... | collective-permute-start | bytes 18440 | tf_op jit(solution)/shard_map/ppermute | solution.py:518
  79.6 4.9 %collective-permute-start.28 = (f32[12,128]{1,0:T(8,128)S(1)}, f32[12,128]{1,0:T(8,128)S(1)}, u32[]{:S(2)}, u32[]{:S(2)}) collective-permute-start(f32[12,128]{1,0:T(8,128)S(1)} %get-tuple-element.105), channel_id=1, source_target_pairs={{0,1},{1,0},{2,3},{3,2},{4,8},{5,9},{6,10},{7,11},{8,4},{9,5},{10,... | collective-permute-start | bytes 18440 | tf_op jit(solution)/shard_map/ppermute | solution.py:518
  79.8 4.8 %collective-permute-start.29 = (f32[12,128]{1,0:T(8,128)S(1)}, f32[12,128]{1,0:T(8,128)S(1)}, u32[]{:S(2)}, u32[]{:S(2)}) collective-permute-start(f32[12,128]{1,0:T(8,128)S(1)} %get-tuple-element.106), channel_id=1, source_target_pairs={{0,3},{1,2},{2,1},{3,0},{4,7},{5,6},{6,5},{7,4},{8,11},{9,10},{10,... | collective-permute-start | bytes 18440 | tf_op jit(solution)/shard_map/ppermute | solution.py:518
  80.9 4.2 %collective-permute-start.30 = (f32[12,128]{1,0:T(8,128)S(1)}, f32[12,128]{1,0:T(8,128)S(1)}, u32[]{:S(2)}, u32[]{:S(2)}) collective-permute-start(f32[12,128]{1,0:T(8,128)S(1)} %get-tuple-element.107), channel_id=1, source_target_pairs={{0,4},{1,5},{2,6},{3,7},{4,0},{5,1},{6,2},{7,3},{8,12},{9,13},{10,... | collective-permute-start | bytes 18440 | tf_op jit(solution)/shard_map/ppermute | solution.py:518
  (25 other events, 59.0 us)

commit v11 on v10

--- a/solution.py
+++ b/solution.py
@@ -23,6 +23,10 @@
 
 VMEM_BYTES = 32 * 1024 * 1024
 WHOLE_VMEM = 64 * 1024 * 1024
+
+
+BESIDE = (1, 3, 0, 2)
+ALONE = (1, 3, 0, 2)
 
 
 def lookup(table_row, rows, index, start=None):
@@ -94,6 +98,10 @@
         total[2 * c * rows : (2 * c + 1) * rows] + total[(2 * c + 1) * rows : (2 * c + 2) * rows]
         for c in range(3)
     ]
+
+
+def in_place(refs, order):
+    return [refs[order.index(n)] for n in range(4)]
 
 
 def spread_rows(source, target, groups):
@@ -176,9 +184,9 @@
 
 
 def prepare_kernel(counts, *refs):
-    (disp_in, lists_in, nodes_in, stiff, pairs, thick_in, after) = refs[:7]
-    (disp, lists, nodes, splat, select, thick) = refs[7:13]
-    sends = refs[13:]
+    (disp_in, lists_in, nodes_in, stiff, after) = refs[:5]
+    (disp, lists, nodes, splat) = refs[5:9]
+    sends = refs[9:]
     px_no = lax.axis_index("px")
     py_no = lax.axis_index("py")
     own_count = disp_in.shape[1]
@@ -208,15 +216,25 @@
     size = stiff.shape[0]
     for j in range(size):
         splat[j * size : (j + 1) * size, :] = jnp.broadcast_to(stiff[:, j : j + 1], (size, LANES))
-    ends = [pairs[0:1, :], pairs[1:2, :]]
-    short = LANES - 2 * pairs.shape[1]
-    if short:
-        ends.append(jnp.full((1, short), -1))
-    tile_no = lax.broadcasted_iota(I32, (LANES, LANES), 0)
-    onehot = (tile_no == jnp.concatenate(ends, axis=1)).astype(F32)
+
+
+def masks_kernel(pairs, classes, after, select, spread, slow):
+    pair_count = pairs.shape[1]
+    row = pairs[0:1, :]
+    if pair_count < LANES:
+        row = jnp.concatenate([row, jnp.full((1, LANES - pair_count), -1)], axis=1)
+    onehot = (lax.broadcasted_iota(I32, (LANES, LANES), 0) == row).astype(F32)
     select[0] = onehot
     select[1] = jnp.transpose(onehot)
-    thick[...] = thick_in[...]
+    tiles = spread.shape[0] // 3
+    tile_no = lax.broadcasted_iota(I32, (tiles, LANES), 0)
+    tile_no = jnp.concatenate([tile_no] * 3, axis=0)
+    for p in range(pair_count):
+        other = jnp.broadcast_to(pairs[1:2, p : p + 1], tile_no.shape)
+        spread[:, p * LANES : (p + 1) * LANES] = (tile_no == other).astype(F32).astype(BF16)
+    blocks = classes.shape[1]
+    row = jnp.concatenate([classes[...], jnp.zeros((1, LANES - blocks), I32)], axis=1)
+    slow[...] = jnp.transpose(jnp.broadcast_to(row, (LANES, LANES)))[:blocks]
 
 
 def own_kernel(disp, nodes, found):
@@ -278,9 +296,11 @@
             outs[b][c * quarter : (c + 1) * quarter, :] = sums[c][b * quarter : (b + 1) * quarter]
 
 
-def force_kernel(rows, found, recv1, recv3, recv0, recv2, nodes, thick, splat, held):
+def force_kernel(rows, found, *refs):
+    recvs = in_place(refs[:4], BESIDE)
+    nodes, thick, splat, held = refs[4:]
     elem_rows = thick.shape[0]
-    forces = corner_forces(found, rows, (recv0, recv1, recv2, recv3), nodes, thick, splat)
+    forces = corner_forces(found, rows, recvs, nodes, thick, splat)
     for i in range(12):
         held[i * elem_rows : (i + 1) * elem_rows, :] = forces[i]
 
@@ -293,23 +313,12 @@
     sum_own(stored_row(held, nodes), nodes, own)
 
 
-def later_kernel(
-    rows,
-    found,
-    recv1,
-    recv3,
-    recv0,
-    recv2,
-    nodes,
-    thick,
-    splat,
-    held,
-    slow,
-    mixed,
-    *outs,
-):
+def later_kernel(rows, found, *refs):
+    recvs = in_place(refs[:4], ALONE)
+    nodes, thick, splat, held, slow, mixed = refs[4:10]
+    outs = refs[10:]
     elem_rows = thick.shape[0]
-    forces = corner_forces(found, rows, (recv0, recv1, recv2, recv3), nodes, thick, splat)
+    forces = corner_forces(found, rows, recvs, nodes, thick, splat)
     kept = slow[...] == 1
     for i in range(12):
         span = slice(i * elem_rows, (i + 1) * elem_rows)
@@ -331,14 +340,6 @@
         return backs[b][c * quarter + q : c * quarter + q + 1, :]
 
     return scatter_add(lambda r: lists[r : r + 1, :], back_row, 4 * quarter, rows)
-
-
-def internal_kernel(own, back1, back3, back0, back2, lists, internal):
-    rows = own.shape[0] // 3
-    sums = returned_sums((back0, back1, back2, back3), lists, rows)
-    for c in range(3):
-        span = slice(c * rows, (c + 1) * rows)
-        internal[span, :] = own[span, :] + sums[c]
 
 
 def sends_kernel(disp, lists, after, *sends):
@@ -351,47 +352,45 @@
         top = values.astype(BF16)
         parts.append(top)
         values = values - top.astype(F32)
-    return jnp.concatenate(parts, axis=1)
+    return parts
 
 
 def dot_thirds(onehot, values):
     width = values.shape[1]
-    sums = jnp.dot(onehot.astype(BF16), thirds(values), preferred_element_type=F32)
+    sums = jnp.dot(
+        onehot.astype(BF16),
+        jnp.concatenate(thirds(values), axis=1),
+        preferred_element_type=F32,
+    )
     return sums[:, :width] + sums[:, width : 2 * width] + sums[:, 2 * width :]
 
 
-def contact_kernel(pair_count, select, arrived, after, pushes):
+def contact_kernel(pair_count, select, spread, arrived, after, pushes):
     tiles = arrived.shape[0]
-    points = jnp.concatenate([arrived[:, c, :] for c in range(3)], axis=1)
-    picked = dot_thirds(select[1, : 2 * pair_count, :tiles], points)
-    first, second = picked[:pair_count], picked[pair_count:]
-    group = LANES // 4
+    points = [arrived[:, c, :] for c in range(3)]
+    first = dot_thirds(select[1, :pair_count, :tiles], jnp.concatenate(points, axis=1))
+    second = []
+    for c in range(3):
+        parts = [part.astype(F32) for part in thirds(points[c])]
+        rest = LANES - 3 * tiles
+        if rest:
+            parts.append(jnp.zeros((rest, LANES), F32))
+        turned = jnp.transpose(jnp.concatenate(parts, axis=0))[:, : 3 * tiles].astype(BF16)
+        second.append(jnp.dot(turned, spread[...], preferred_element_type=F32))
     pushed = []
-    for start in range(0, pair_count, group):
-        stop = min(start + group, pair_count)
-        block = jnp.concatenate(
-            [second[start:stop, c * LANES : (c + 1) * LANES] for c in range(3)]
-            + [jnp.zeros((LANES - 3 * (stop - start), LANES), F32)],
-            axis=0,
+    for p in range(pair_count):
+        gaps = [
+            jnp.broadcast_to(first[p : p + 1, c * LANES : (c + 1) * LANES], (LANES, LANES))
+            - second[c][:, p * LANES : (p + 1) * LANES]
+            for c in range(3)
+        ]
+        dist = gaps[0] * gaps[0] + gaps[1] * gaps[1] + gaps[2] * gaps[2]
+        weight = jnp.exp(dist * (-1.0 / REACH))
+        pushed.append(
+            jnp.concatenate(
+                [jnp.sum(weight * gaps[c], axis=0, keepdims=True) for c in range(3)], axis=1
+            )
         )
-        turned = jnp.transpose(block)
-        for p in range(start, stop):
-            gaps = []
-            for c in range(3):
-                column = c * (stop - start) + p - start
-                gaps.append(
-                    jnp.broadcast_to(
-                        first[p : p + 1, c * LANES : (c + 1) * LANES], (LANES, LANES)
-                    )
-                    - jnp.broadcast_to(turned[:, column : column + 1], (LANES, LANES))
-                )
-            dist = gaps[0] * gaps[0] + gaps[1] * gaps[1] + gaps[2] * gaps[2]
-            weight = jnp.exp(dist * (-1.0 / REACH))
-            pushed.append(
-                jnp.concatenate(
-                    [jnp.sum(weight * gaps[c], axis=0, keepdims=True) for c in range(3)], axis=1
-                )
-            )
     total = PENALTY * dot_thirds(select[0, :tiles, :pair_count], jnp.concatenate(pushed, axis=0))
     for c in range(3):
         pushes[:, c, :] = total[:, c * LANES : (c + 1) * LANES]
@@ -412,25 +411,24 @@
 
 def first_update_kernel(starting, *refs):
     refs = list(refs)
-    internal, returned, inverse, lists, inv_mass, disp, vel, ext = refs[:8]
-    new_vel, new_disp, contact, *sends = refs[9 if starting else 8 :]
+    own = refs[0]
+    returned, inverse, lists, inv_mass, disp, vel, ext = refs[5:12]
+    new_vel, new_disp, contact, *sends = refs[12:]
     rows = disp.shape[0] // 3
+    backs = returned_sums(in_place(refs[1:5], BESIDE), lists, rows)
+    internal = [mine + more for mine, more in zip(components(own), backs)]
     if starting:
-        classes = refs[8]
-        *sends, ext_rows, slow = sends
+        *sends, ext_rows = sends
         spread_rows(vel, new_vel, 3)
         spread_rows(ext, ext_rows, 3)
         vel, ext = new_vel, ext_rows
-        blocks = classes.shape[1]
-        row = jnp.concatenate([classes[...], jnp.zeros((1, LANES - blocks), I32)], axis=1)
-        slow[...] = jnp.transpose(jnp.broadcast_to(row, (LANES, LANES)))[:blocks]
     sums = scatter_add(
         lambda r: inverse[r : r + 1, :],
         lambda c, r: returned[r, c : c + 1, :],
         inverse.shape[0],
         rows,
     )
-    steps = advance(components(internal), sums, ext, inv_mass, vel, disp, rows)
+    steps = advance(internal, sums, ext, inv_mass, vel, disp, rows)
     for c, vel_c, disp_c in steps:
         span = slice(c * rows, (c + 1) * rows)
         contact[span, :] = sums[c]
@@ -440,10 +438,10 @@
 
 
 def update_kernel(case, *refs):
-    refs = list(refs)
-    own, back1, back3, back0, back2, lists, ext, inv_mass, vel, disp, contact = refs[:11]
+    own = refs[0]
+    lists, ext, inv_mass, vel, disp, contact = refs[5:11]
     rows = disp.shape[0] // 3
-    sums = returned_sums((back0, back1, back2, back3), lists, rows)
+    sums = returned_sums(in_place(refs[1:5], ALONE), lists, rows)
     internal = [mine + more for mine, more in zip(components(own), sums)]
     steps = advance(internal, components(contact), ext, inv_mass, vel, disp, rows)
     if case == "final":
@@ -513,9 +511,9 @@
     return swaps
 
 
-def exchange(blocks):
+def exchange(blocks, order):
     swaps = partners()
-    return [lax.ppermute(blocks[n], ("px", "py"), swaps[n]) for n in (1, 3, 0, 2)]
+    return [lax.ppermute(blocks[n], ("px", "py"), swaps[n]) for n in order]
 
 
 def swap(slots, devices, capacity):
@@ -578,20 +576,30 @@
         + [pltpu.SemaphoreType.DMA((4,))],
         vmem_bytes=WHOLE_VMEM,
     )
-    disp, lists, nodes, splat, select, thickness, *sends = call(
+    disp, lists, nodes, splat, *sends = call(
         functools.partial(prepare_kernel, counts),
-        [displacement, halo_lists, elem_nodes, stiffness, tile_pairs, thickness, outgoing],
+        [displacement, halo_lists, elem_nodes, stiffness, inverse],
         [
             nodal,
             jax.ShapeDtypeStruct((4 * quarter, LANES), I32),
             jax.ShapeDtypeStruct((4 * elem_rows, LANES), I32),
             shape(144, LANES),
-            shape(2, LANES, LANES),
-            shape(elem_rows, LANES),
         ]
         + sent,
         "prepare",
-        far=(6,),
+        far=(4,),
+    )
+    pair_count = tile_pairs.shape[1]
+    select, spread, slow = call(
+        masks_kernel,
+        [tile_pairs, block_class.reshape(1, -1), lists],
+        [
+            shape(2, LANES, LANES),
+            jax.ShapeDtypeStruct((3 * slot_rows, pair_count * LANES), BF16),
+            jax.ShapeDtypeStruct((elem_rows, LANES), I32),
+        ],
+        "masks",
+        far=(2,),
     )
     vel = velocity
     for step_no in range(STEPS):
@@ -603,7 +611,7 @@
                 arrived = swap(outgoing, devices, capacity)
                 if step_no:
                     sends = call(sends_kernel, [disp, lists, outgoing], sent, "sends", far=(2,))
-            recvs = exchange(sends)
+            recvs = exchange(sends, BESIDE if first else ALONE)
             (found,) = call(own_kernel, [disp, nodes], [corner_values], "own_corners")
             field = [found, *recvs, nodes, thickness, splat]
             if first:
@@ -611,11 +619,11 @@
                     functools.partial(force_kernel, rows), field, [corner_values], "forces"
                 )
                 (pushes,) = call(
-                    functools.partial(contact_kernel, tile_pairs.shape[1]),
-                    [select, arrived, held],
+                    functools.partial(contact_kernel, pair_count),
+                    [select, spread, arrived, held],
                     [slots],
                     "contact",
-                    far=(2,),
+                    far=(3,),
                 )
                 returned = swap(pushes, devices, capacity)
                 outs = call(
@@ -633,17 +641,14 @@
                     [corner_values] + sent,
                     "forces_halo_sum",
                 )
-            backs = exchange(outs)
+            backs = exchange(outs, BESIDE if first else ALONE)
             (own,) = call(own_sum_kernel, [forces, nodes, outs[2]], [nodal], "own_sum", far=(2,))
             if first:
-                (internal,) = call(
-                    internal_kernel, [own, *backs, lists], [nodal], "internal"
-                )
-                inputs = [internal, returned, inverse, lists, inv_mass, disp, vel]
+                inputs = [own, *backs, returned, inverse, lists, inv_mass, disp, vel]
                 outputs = [nodal] * 3 + sent
                 if step_no == 0:
-                    inputs += [ext_force, block_class.reshape(1, -1)]
-                    outputs += [nodal, jax.ShapeDtypeStruct((elem_rows, LANES), I32)]
+                    inputs.append(ext_force)
+                    outputs.append(nodal)
                 else:
                     inputs.append(ext)
                 vel, disp, contact, *sends = call(
@@ -653,7 +658,7 @@
                     "first_update",
                 )
                 if step_no == 0:
-                    *sends, ext, slow = sends
+                    *sends, ext = sends
                 continue
             inputs = [own, *backs, lists, ext, inv_mass, vel, disp, contact]
             if final:

time: 86.7 us -> 82.2 us (0.948)
  local copies, waits for them, and re-layouts: 3.42 us -> 0.22 us
  starting transfers between devices: 53.1 us -> 51.8 us
  waiting for transfers between devices: 7.26 us -> 8.2 us
    unnamed x26 -> x24, local copies, waits for them, and re-layouts: 3.42 us -> 0.22 us
    all_to_all x4, waiting for transfers between devices: 1.64 us -> 2.93 us  [swap(): return lax.all_to_all(slots, axes, 0, 0, tiled=True)]
    pallas_call x25 -> x24, Pallas kernels: 21.3 us -> 20.5 us  [call(): pl.pallas_call(kernel, out_shape=tuple(outputs), in_specs=specs, out_spec...]
  transfers between devices with their start and end apart: 36 -> 36, of which waited for: 11 -> 12; matrix products, arithmetic and copies ran while one was open for 0% -> 0% of each run, Pallas kernels for 10% -> 9%
where the time goes in v11:
time: 82.2 us; the launch traced here: 81.8 us
  starting transfers between devices  51.8 us (63%)
  Pallas kernels  20.5 us (25%)
  waiting for transfers between devices  8.2 us (10%)
  between operations  1.09 us (1%)
    ppermute x32, starting transfers between devices, exchange(): return [lax.ppermute(blocks[n], ('px', 'py'), swaps[n]) for n in order]  32.9 us
    pallas_call x24, Pallas kernels, call(): pl.pallas_call(kernel, out_shape=tuple(outputs), in_specs=specs, out_spec...  20.5 us
    all_to_all x4, starting transfers between devices, swap(): return lax.all_to_all(slots, axes, 0, 0, tiled=True)  18.9 us
    ppermute x32, waiting for transfers between devices, exchange(): return [lax.ppermute(blocks[n], ('px', 'py'), swaps[n]) for n in order]  5.27 us
    all_to_all x4, waiting for transfers between devices, swap(): return lax.all_to_all(slots, axes, 0, 0, tiled=True)  2.93 us
  transfers between devices with their start and end apart: 36, of which 12 were waited for; matrix products, arithmetic and copies ran while one was open for 0% of the time, Pallas kernels for 9%

profile of v11, /device:TPU:0, one launch (start us, length us, event | category | flops | bytes accessed | tf_op | source)
XLA Modules:
  0.0 81.8 jit_solution(9461276121554579052)
XLA Ops:
  0.6 2.2 %slots.1 = (s32[32,128]{1,0:T(8,128)}, f32[32,3,128]{2,1,0:T(4,128)}) custom-call(f32[3,2048]{1,0:T(4,128)} %refs_11_.3, f32[3,2048]{1,0:T(4,128)} %refs_0_.3, s32[16,128]{1,0:T(8,128)} %bitcast.14, s32[16,128]{1,0:T(8,128)} %bitcast.15), custom_call_target="tpu_custom_call" | custom-call | tf_op jit(solution)/shard_map/slots/pallas_call | solution.py:487
  2.9 7.3 %all-to-all-start = ((f32[32,3,128]{2,1,0:T(4,128)}), f32[32,3,128]{2,1,0:T(4,128)S(1)}, u32[]{:S(2)}, u32[]{:S(2)}) async-start(f32[32,3,128]{2,1,0:T(4,128)} %get-tuple-element.68), calls=%async_computation | async-start | bytes 131072 | tf_op jit(solution)/shard_map/all_to_all | solution.py:522
  10.8 1.6 %collective-permute-start.1 = (f32[12,128]{1,0:T(8,128)S(1)}, f32[12,128]{1,0:T(8,128)S(1)}, u32[]{:S(2)}, u32[]{:S(2)}) collective-permute-start(f32[12,128]{1,0:T(8,128)S(1)} %get-tuple-element.61), channel_id=1, source_target_pairs={{0,3},{1,2},{2,1},{3,0},{4,7},{5,6},{6,5},{7,4},{8,11},{9,10},{10,... | collective-permute-start | bytes 18440 | tf_op jit(solution)/shard_map/ppermute | solution.py:516
  12.5 2.3 %collective-permute-start.2 = (f32[12,128]{1,0:T(8,128)S(1)}, f32[12,128]{1,0:T(8,128)S(1)}, u32[]{:S(2)}, u32[]{:S(2)}) collective-permute-start(f32[12,128]{1,0:T(8,128)S(1)} %get-tuple-element.62), channel_id=1, source_target_pairs={{0,4},{1,5},{2,6},{3,7},{4,0},{5,1},{6,2},{7,3},{8,12},{9,13},{10,... | collective-permute-start | bytes 18440 | tf_op jit(solution)/shard_map/ppermute | solution.py:516
  17.6 1.9 %contact.2.after = f32[32,3,128]{2,1,0:T(4,128)} custom-call(f32[2,128,128]{2,1,0:T(8,128)S(1)} %get-tuple-element.66.select, bf16[96,2048]{1,0:T(8,128)(2,1)S(1)} %get-tuple-element.67.spread, f32[32,3,128]{2,1,0:T(4,128)S(1)} %all-to-all-done.arrived, f32[192,128]{1,0:T(8,128)S(1)} %forces.2.after.held.refs_7_), custom_call_target="tpu_custom_call" | custom-call | tf_op jit(solution)/shard_map/contact/pallas_call | solution.py:487
  19.5 3.7 %all-to-all-start.1 = ((f32[32,3,128]{2,1,0:T(4,128)}), f32[32,3,128]{2,1,0:T(4,128)S(1)}, u32[]{:S(2)}, u32[]{:S(2)}) async-start(f32[32,3,128]{2,1,0:T(4,128)} %contact.2.after), calls=%async_computation.1 | async-start | bytes 131072 | tf_op jit(solution)/shard_map/all_to_all | solution.py:522
  24.2 1.6 %collective-permute-start.5 = (f32[12,128]{1,0:T(8,128)S(1)}, f32[12,128]{1,0:T(8,128)S(1)}, u32[]{:S(2)}, u32[]{:S(2)}) collective-permute-start(f32[12,128]{1,0:T(8,128)S(1)} %get-tuple-element.71), channel_id=1, source_target_pairs={{0,3},{1,2},{2,1},{3,0},{4,7},{5,6},{6,5},{7,4},{8,11},{9,10},{10,... | collective-permute-start | bytes 18440 | tf_op jit(solution)/shard_map/ppermute | solution.py:516
  25.8 2.3 %collective-permute-start.6 = (f32[12,128]{1,0:T(8,128)S(1)}, f32[12,128]{1,0:T(8,128)S(1)}, u32[]{:S(2)}, u32[]{:S(2)}) collective-permute-start(f32[12,128]{1,0:T(8,128)S(1)} %get-tuple-element.72), channel_id=1, source_target_pairs={{0,4},{1,5},{2,6},{3,7},{4,0},{5,1},{6,2},{7,3},{8,12},{9,13},{10,... | collective-permute-start | bytes 18440 | tf_op jit(solution)/shard_map/ppermute | solution.py:516
  32.0 2.1 %collective-permute-start.10 = (f32[12,128]{1,0:T(8,128)S(1)}, f32[12,128]{1,0:T(8,128)S(1)}, u32[]{:S(2)}, u32[]{:S(2)}) collective-permute-start(f32[12,128]{1,0:T(8,128)S(1)} %get-tuple-element.76), channel_id=1, source_target_pairs={{0,4},{1,5},{2,6},{3,7},{4,0},{5,1},{6,2},{7,3},{8,12},{9,13},{10,... | collective-permute-start | bytes 18440 | tf_op jit(solution)/shard_map/ppermute | solution.py:516
  35.8 1.5 %forces_halo_sum.2 = (f32[192,128]{1,0:T(8,128)S(1)}, f32[12,128]{1,0:T(8,128)S(1)}, f32[12,128]{1,0:T(8,128)S(1)}, f32[12,128]{1,0:T(8,128)S(1)}, f32[12,128]{1,0:T(8,128)S(1)}) custom-call(f32[192,128]{1,0:T(8,128)S(1)} %own_corners.5.found, f32[12,128]{1,0:T(8,128)S(1)} %collective-permute-done.8.refs_0_, f32[12,128]{1,0:T(8,128)S(1)} %collective-permute-done.9.refs_1_, ...), custom_call_target="tpu_custom_call" | custom-call | tf_op jit(solution)/shard_map/forces_halo_sum/pallas_call | solution.py:487
  37.5 1.5 %collective-permute-start.13 = (f32[12,128]{1,0:T(8,128)S(1)}, f32[12,128]{1,0:T(8,128)S(1)}, u32[]{:S(2)}, u32[]{:S(2)}) collective-permute-start(f32[12,128]{1,0:T(8,128)S(1)} %get-tuple-element.82), channel_id=1, source_target_pairs={{0,3},{1,2},{2,1},{3,0},{4,7},{5,6},{6,5},{7,4},{8,11},{9,10},{10,... | collective-permute-start | bytes 18440 | tf_op jit(solution)/shard_map/ppermute | solution.py:516
  39.0 2.2 %collective-permute-start.14 = (f32[12,128]{1,0:T(8,128)S(1)}, f32[12,128]{1,0:T(8,128)S(1)}, u32[]{:S(2)}, u32[]{:S(2)}) collective-permute-start(f32[12,128]{1,0:T(8,128)S(1)} %get-tuple-element.83), channel_id=1, source_target_pairs={{0,4},{1,5},{2,6},{3,7},{4,0},{5,1},{6,2},{7,3},{8,12},{9,13},{10,... | collective-permute-start | bytes 18440 | tf_op jit(solution)/shard_map/ppermute | solution.py:516
  42.9 1.3 %last_update.1 = (f32[48,128]{1,0:T(8,128)S(1)}, f32[48,128]{1,0:T(8,128)S(1)}, f32[32,3,128]{2,1,0:T(4,128)}) custom-call(f32[48,128]{1,0:T(8,128)S(1)} %own_sum.5.refs_0_, f32[12,128]{1,0:T(8,128)S(1)} %collective-permute-done.12.refs_1_, f32[12,128]{1,0:T(8,128)S(1)} %collective-permute-done.13.refs_2_, f32[12,128]{1,0:T(8,128)S(1)} %collective-permute-done.14.refs_3_, ...), custom_call_target="tpu_custom_call" | custom-call | tf_op jit(solution)/shard_map/last_update/pallas_call | solution.py:487
  44.1 4.2 %all-to-all-start.2 = ((f32[32,3,128]{2,1,0:T(4,128)}), f32[32,3,128]{2,1,0:T(4,128)S(1)}, u32[]{:S(2)}, u32[]{:S(2)}) async-start(f32[32,3,128]{2,1,0:T(4,128)} %get-tuple-element.88.after), calls=%async_computation.2 | async-start | bytes 131072 | tf_op jit(solution)/shard_map/all_to_all | solution.py:522
  48.8 1.6 %collective-permute-start.17 = (f32[12,128]{1,0:T(8,128)S(1)}, f32[12,128]{1,0:T(8,128)S(1)}, u32[]{:S(2)}, u32[]{:S(2)}) collective-permute-start(f32[12,128]{1,0:T(8,128)S(1)} %get-tuple-element.90), channel_id=1, source_target_pairs={{0,3},{1,2},{2,1},{3,0},{4,7},{5,6},{6,5},{7,4},{8,11},{9,10},{10,... | collective-permute-start | bytes 18440 | tf_op jit(solution)/shard_map/ppermute | solution.py:516
  50.5 2.3 %collective-permute-start.18 = (f32[12,128]{1,0:T(8,128)S(1)}, f32[12,128]{1,0:T(8,128)S(1)}, u32[]{:S(2)}, u32[]{:S(2)}) collective-permute-start(f32[12,128]{1,0:T(8,128)S(1)} %get-tuple-element.91), channel_id=1, source_target_pairs={{0,4},{1,5},{2,6},{3,7},{4,0},{5,1},{6,2},{7,3},{8,12},{9,13},{10,... | collective-permute-start | bytes 18440 | tf_op jit(solution)/shard_map/ppermute | solution.py:516
  55.7 1.9 %contact.3.after = f32[32,3,128]{2,1,0:T(4,128)} custom-call(f32[2,128,128]{2,1,0:T(8,128)S(1)} %get-tuple-element.66.select, bf16[96,2048]{1,0:T(8,128)(2,1)S(1)} %get-tuple-element.67.spread, f32[32,3,128]{2,1,0:T(4,128)S(1)} %all-to-all-done.2.arrived, f32[192,128]{1,0:T(8,128)S(1)} %forces.3.after.held.refs_7_), custom_call_target="tpu_custom_call" | custom-call | tf_op jit(solution)/shard_map/contact/pallas_call | solution.py:487
  57.6 3.7 %all-to-all-start.3 = ((f32[32,3,128]{2,1,0:T(4,128)}), f32[32,3,128]{2,1,0:T(4,128)S(1)}, u32[]{:S(2)}, u32[]{:S(2)}) async-start(f32[32,3,128]{2,1,0:T(4,128)} %contact.3.after), calls=%async_computation.3 | async-start | bytes 131072 | tf_op jit(solution)/shard_map/all_to_all | solution.py:522
  62.2 1.6 %collective-permute-start.21 = (f32[12,128]{1,0:T(8,128)S(1)}, f32[12,128]{1,0:T(8,128)S(1)}, u32[]{:S(2)}, u32[]{:S(2)}) collective-permute-start(f32[12,128]{1,0:T(8,128)S(1)} %get-tuple-element.95), channel_id=1, source_target_pairs={{0,3},{1,2},{2,1},{3,0},{4,7},{5,6},{6,5},{7,4},{8,11},{9,10},{10,... | collective-permute-start | bytes 18440 | tf_op jit(solution)/shard_map/ppermute | solution.py:516
  63.8 2.3 %collective-permute-start.22 = (f32[12,128]{1,0:T(8,128)S(1)}, f32[12,128]{1,0:T(8,128)S(1)}, u32[]{:S(2)}, u32[]{:S(2)}) collective-permute-start(f32[12,128]{1,0:T(8,128)S(1)} %get-tuple-element.96), channel_id=1, source_target_pairs={{0,4},{1,5},{2,6},{3,7},{4,0},{5,1},{6,2},{7,3},{8,12},{9,13},{10,... | collective-permute-start | bytes 18440 | tf_op jit(solution)/shard_map/ppermute | solution.py:516
  70.0 2.1 %collective-permute-start.26 = (f32[12,128]{1,0:T(8,128)S(1)}, f32[12,128]{1,0:T(8,128)S(1)}, u32[]{:S(2)}, u32[]{:S(2)}) collective-permute-start(f32[12,128]{1,0:T(8,128)S(1)} %get-tuple-element.101), channel_id=1, source_target_pairs={{0,4},{1,5},{2,6},{3,7},{4,0},{5,1},{6,2},{7,3},{8,12},{9,13},{10,... | collective-permute-start | bytes 18440 | tf_op jit(solution)/shard_map/ppermute | solution.py:516
  73.8 1.5 %forces_halo_sum.3 = (f32[192,128]{1,0:T(8,128)S(1)}, f32[12,128]{1,0:T(8,128)S(1)}, f32[12,128]{1,0:T(8,128)S(1)}, f32[12,128]{1,0:T(8,128)S(1)}, f32[12,128]{1,0:T(8,128)S(1)}) custom-call(f32[192,128]{1,0:T(8,128)S(1)} %own_corners.7.found, f32[12,128]{1,0:T(8,128)S(1)} %collective-permute-done.24.refs_0_, f32[12,128]{1,0:T(8,128)S(1)} %collective-permute-done.25.refs_1_, ...), custom_call_target="tpu_custom_call" | custom-call | tf_op jit(solution)/shard_map/forces_halo_sum/pallas_call | solution.py:487
  75.5 1.5 %collective-permute-start.29 = (f32[12,128]{1,0:T(8,128)S(1)}, f32[12,128]{1,0:T(8,128)S(1)}, u32[]{:S(2)}, u32[]{:S(2)}) collective-permute-start(f32[12,128]{1,0:T(8,128)S(1)} %get-tuple-element.106), channel_id=1, source_target_pairs={{0,3},{1,2},{2,1},{3,0},{4,7},{5,6},{6,5},{7,4},{8,11},{9,10},{10,... | collective-permute-start | bytes 18440 | tf_op jit(solution)/shard_map/ppermute | solution.py:516
  77.0 2.1 %collective-permute-start.30 = (f32[12,128]{1,0:T(8,128)S(1)}, f32[12,128]{1,0:T(8,128)S(1)}, u32[]{:S(2)}, u32[]{:S(2)}) collective-permute-start(f32[12,128]{1,0:T(8,128)S(1)} %get-tuple-element.107), channel_id=1, source_target_pairs={{0,4},{1,5},{2,6},{3,7},{4,0},{5,1},{6,2},{7,3},{8,12},{9,13},{10,... | collective-permute-start | bytes 18440 | tf_op jit(solution)/shard_map/ppermute | solution.py:516
  (96 shorter events, 24.4 us)
Async XLA Ops:
  2.9 14.7 %all-to-all-start = ((f32[32,3,128]{2,1,0:T(4,128)}), f32[32,3,128]{2,1,0:T(4,128)S(1)}, u32[]{:S(2)}, u32[]{:S(2)}) async-start(f32[32,3,128]{2,1,0:T(4,128)} %get-tuple-element.68), calls=%async_computation | async-start | bytes 131072 | tf_op jit(solution)/shard_map/all_to_all | solution.py:522
  10.5 5.5 %collective-permute-start = (f32[12,128]{1,0:T(8,128)S(1)}, f32[12,128]{1,0:T(8,128)S(1)}, u32[]{:S(2)}, u32[]{:S(2)}) collective-permute-start(f32[12,128]{1,0:T(8,128)S(1)} %get-tuple-element.60), channel_id=1, source_target_pairs={{0,1},{1,0},{2,3},{3,2},{4,8},{5,9},{6,10},{7,11},{8,4},{9,5},{10,... | collective-permute-start | bytes 18440 | tf_op jit(solution)/shard_map/ppermute | solution.py:516
  10.8 5.2 %collective-permute-start.1 = (f32[12,128]{1,0:T(8,128)S(1)}, f32[12,128]{1,0:T(8,128)S(1)}, u32[]{:S(2)}, u32[]{:S(2)}) collective-permute-start(f32[12,128]{1,0:T(8,128)S(1)} %get-tuple-element.61), channel_id=1, source_target_pairs={{0,3},{1,2},{2,1},{3,0},{4,7},{5,6},{6,5},{7,4},{8,11},{9,10},{10,... | collective-permute-start | bytes 18440 | tf_op jit(solution)/shard_map/ppermute | solution.py:516
  12.5 4.0 %collective-permute-start.2 = (f32[12,128]{1,0:T(8,128)S(1)}, f32[12,128]{1,0:T(8,128)S(1)}, u32[]{:S(2)}, u32[]{:S(2)}) collective-permute-start(f32[12,128]{1,0:T(8,128)S(1)} %get-tuple-element.62), channel_id=1, source_target_pairs={{0,4},{1,5},{2,6},{3,7},{4,0},{5,1},{6,2},{7,3},{8,12},{9,13},{10,... | collective-permute-start | bytes 18440 | tf_op jit(solution)/shard_map/ppermute | solution.py:516
  19.5 11.1 %all-to-all-start.1 = ((f32[32,3,128]{2,1,0:T(4,128)}), f32[32,3,128]{2,1,0:T(4,128)S(1)}, u32[]{:S(2)}, u32[]{:S(2)}) async-start(f32[32,3,128]{2,1,0:T(4,128)} %contact.2.after), calls=%async_computation.1 | async-start | bytes 131072 | tf_op jit(solution)/shard_map/all_to_all | solution.py:522
  23.9 5.3 %collective-permute-start.4 = (f32[12,128]{1,0:T(8,128)S(1)}, f32[12,128]{1,0:T(8,128)S(1)}, u32[]{:S(2)}, u32[]{:S(2)}) collective-permute-start(f32[12,128]{1,0:T(8,128)S(1)} %get-tuple-element.70), channel_id=1, source_target_pairs={{0,1},{1,0},{2,3},{3,2},{4,8},{5,9},{6,10},{7,11},{8,4},{9,5},{10,... | collective-permute-start | bytes 18440 | tf_op jit(solution)/shard_map/ppermute | solution.py:516
  24.2 5.0 %collective-permute-start.5 = (f32[12,128]{1,0:T(8,128)S(1)}, f32[12,128]{1,0:T(8,128)S(1)}, u32[]{:S(2)}, u32[]{:S(2)}) collective-permute-start(f32[12,128]{1,0:T(8,128)S(1)} %get-tuple-element.71), channel_id=1, source_target_pairs={{0,3},{1,2},{2,1},{3,0},{4,7},{5,6},{6,5},{7,4},{8,11},{9,10},{10,... | collective-permute-start | bytes 18440 | tf_op jit(solution)/shard_map/ppermute | solution.py:516
  25.8 4.0 %collective-permute-start.6 = (f32[12,128]{1,0:T(8,128)S(1)}, f32[12,128]{1,0:T(8,128)S(1)}, u32[]{:S(2)}, u32[]{:S(2)}) collective-permute-start(f32[12,128]{1,0:T(8,128)S(1)} %get-tuple-element.72), channel_id=1, source_target_pairs={{0,4},{1,5},{2,6},{3,7},{4,0},{5,1},{6,2},{7,3},{8,12},{9,13},{10,... | collective-permute-start | bytes 18440 | tf_op jit(solution)/shard_map/ppermute | solution.py:516
  32.0 3.8 %collective-permute-start.10 = (f32[12,128]{1,0:T(8,128)S(1)}, f32[12,128]{1,0:T(8,128)S(1)}, u32[]{:S(2)}, u32[]{:S(2)}) collective-permute-start(f32[12,128]{1,0:T(8,128)S(1)} %get-tuple-element.76), channel_id=1, source_target_pairs={{0,4},{1,5},{2,6},{3,7},{4,0},{5,1},{6,2},{7,3},{8,12},{9,13},{10,... | collective-permute-start | bytes 18440 | tf_op jit(solution)/shard_map/ppermute | solution.py:516
  37.4 4.9 %collective-permute-start.12 = (f32[12,128]{1,0:T(8,128)S(1)}, f32[12,128]{1,0:T(8,128)S(1)}, u32[]{:S(2)}, u32[]{:S(2)}) collective-permute-start(f32[12,128]{1,0:T(8,128)S(1)} %get-tuple-element.81), channel_id=1, source_target_pairs={{0,1},{1,0},{2,3},{3,2},{4,8},{5,9},{6,10},{7,11},{8,4},{9,5},{10,... | collective-permute-start | bytes 18440 | tf_op jit(solution)/shard_map/ppermute | solution.py:516
  37.5 4.8 %collective-permute-start.13 = (f32[12,128]{1,0:T(8,128)S(1)}, f32[12,128]{1,0:T(8,128)S(1)}, u32[]{:S(2)}, u32[]{:S(2)}) collective-permute-start(f32[12,128]{1,0:T(8,128)S(1)} %get-tuple-element.82), channel_id=1, source_target_pairs={{0,3},{1,2},{2,1},{3,0},{4,7},{5,6},{6,5},{7,4},{8,11},{9,10},{10,... | collective-permute-start | bytes 18440 | tf_op jit(solution)/shard_map/ppermute | solution.py:516
  39.0 3.9 %collective-permute-start.14 = (f32[12,128]{1,0:T(8,128)S(1)}, f32[12,128]{1,0:T(8,128)S(1)}, u32[]{:S(2)}, u32[]{:S(2)}) collective-permute-start(f32[12,128]{1,0:T(8,128)S(1)} %get-tuple-element.83), channel_id=1, source_target_pairs={{0,4},{1,5},{2,6},{3,7},{4,0},{5,1},{6,2},{7,3},{8,12},{9,13},{10,... | collective-permute-start | bytes 18440 | tf_op jit(solution)/shard_map/ppermute | solution.py:516
  44.1 11.6 %all-to-all-start.2 = ((f32[32,3,128]{2,1,0:T(4,128)}), f32[32,3,128]{2,1,0:T(4,128)S(1)}, u32[]{:S(2)}, u32[]{:S(2)}) async-start(f32[32,3,128]{2,1,0:T(4,128)} %get-tuple-element.88.after), calls=%async_computation.2 | async-start | bytes 131072 | tf_op jit(solution)/shard_map/all_to_all | solution.py:522
  48.5 5.1 %collective-permute-start.16 = (f32[12,128]{1,0:T(8,128)S(1)}, f32[12,128]{1,0:T(8,128)S(1)}, u32[]{:S(2)}, u32[]{:S(2)}) collective-permute-start(f32[12,128]{1,0:T(8,128)S(1)} %get-tuple-element.89), channel_id=1, source_target_pairs={{0,1},{1,0},{2,3},{3,2},{4,8},{5,9},{6,10},{7,11},{8,4},{9,5},{10,... | collective-permute-start | bytes 18440 | tf_op jit(solution)/shard_map/ppermute | solution.py:516
  48.8 4.8 %collective-permute-start.17 = (f32[12,128]{1,0:T(8,128)S(1)}, f32[12,128]{1,0:T(8,128)S(1)}, u32[]{:S(2)}, u32[]{:S(2)}) collective-permute-start(f32[12,128]{1,0:T(8,128)S(1)} %get-tuple-element.90), channel_id=1, source_target_pairs={{0,3},{1,2},{2,1},{3,0},{4,7},{5,6},{6,5},{7,4},{8,11},{9,10},{10,... | collective-permute-start | bytes 18440 | tf_op jit(solution)/shard_map/ppermute | solution.py:516
  50.5 4.0 %collective-permute-start.18 = (f32[12,128]{1,0:T(8,128)S(1)}, f32[12,128]{1,0:T(8,128)S(1)}, u32[]{:S(2)}, u32[]{:S(2)}) collective-permute-start(f32[12,128]{1,0:T(8,128)S(1)} %get-tuple-element.91), channel_id=1, source_target_pairs={{0,4},{1,5},{2,6},{3,7},{4,0},{5,1},{6,2},{7,3},{8,12},{9,13},{10,... | collective-permute-start | bytes 18440 | tf_op jit(solution)/shard_map/ppermute | solution.py:516
  57.6 11.0 %all-to-all-start.3 = ((f32[32,3,128]{2,1,0:T(4,128)}), f32[32,3,128]{2,1,0:T(4,128)S(1)}, u32[]{:S(2)}, u32[]{:S(2)}) async-start(f32[32,3,128]{2,1,0:T(4,128)} %contact.3.after), calls=%async_computation.3 | async-start | bytes 131072 | tf_op jit(solution)/shard_map/all_to_all | solution.py:522
  62.1 5.1 %collective-permute-start.20 = (f32[12,128]{1,0:T(8,128)S(1)}, f32[12,128]{1,0:T(8,128)S(1)}, u32[]{:S(2)}, u32[]{:S(2)}) collective-permute-start(f32[12,128]{1,0:T(8,128)S(1)} %get-tuple-element.94), channel_id=1, source_target_pairs={{0,1},{1,0},{2,3},{3,2},{4,8},{5,9},{6,10},{7,11},{8,4},{9,5},{10,... | collective-permute-start | bytes 18440 | tf_op jit(solution)/shard_map/ppermute | solution.py:516
  62.2 5.0 %collective-permute-start.21 = (f32[12,128]{1,0:T(8,128)S(1)}, f32[12,128]{1,0:T(8,128)S(1)}, u32[]{:S(2)}, u32[]{:S(2)}) collective-permute-start(f32[12,128]{1,0:T(8,128)S(1)} %get-tuple-element.95), channel_id=1, source_target_pairs={{0,3},{1,2},{2,1},{3,0},{4,7},{5,6},{6,5},{7,4},{8,11},{9,10},{10,... | collective-permute-start | bytes 18440 | tf_op jit(solution)/shard_map/ppermute | solution.py:516
  63.8 4.0 %collective-permute-start.22 = (f32[12,128]{1,0:T(8,128)S(1)}, f32[12,128]{1,0:T(8,128)S(1)}, u32[]{:S(2)}, u32[]{:S(2)}) collective-permute-start(f32[12,128]{1,0:T(8,128)S(1)} %get-tuple-element.96), channel_id=1, source_target_pairs={{0,4},{1,5},{2,6},{3,7},{4,0},{5,1},{6,2},{7,3},{8,12},{9,13},{10,... | collective-permute-start | bytes 18440 | tf_op jit(solution)/shard_map/ppermute | solution.py:516
  70.0 3.8 %collective-permute-start.26 = (f32[12,128]{1,0:T(8,128)S(1)}, f32[12,128]{1,0:T(8,128)S(1)}, u32[]{:S(2)}, u32[]{:S(2)}) collective-permute-start(f32[12,128]{1,0:T(8,128)S(1)} %get-tuple-element.101), channel_id=1, source_target_pairs={{0,4},{1,5},{2,6},{3,7},{4,0},{5,1},{6,2},{7,3},{8,12},{9,13},{10,... | collective-permute-start | bytes 18440 | tf_op jit(solution)/shard_map/ppermute | solution.py:516
  75.3 4.9 %collective-permute-start.28 = (f32[12,128]{1,0:T(8,128)S(1)}, f32[12,128]{1,0:T(8,128)S(1)}, u32[]{:S(2)}, u32[]{:S(2)}) collective-permute-start(f32[12,128]{1,0:T(8,128)S(1)} %get-tuple-element.105), channel_id=1, source_target_pairs={{0,1},{1,0},{2,3},{3,2},{4,8},{5,9},{6,10},{7,11},{8,4},{9,5},{10,... | collective-permute-start | bytes 18440 | tf_op jit(solution)/shard_map/ppermute | solution.py:516
  75.5 4.8 %collective-permute-start.29 = (f32[12,128]{1,0:T(8,128)S(1)}, f32[12,128]{1,0:T(8,128)S(1)}, u32[]{:S(2)}, u32[]{:S(2)}) collective-permute-start(f32[12,128]{1,0:T(8,128)S(1)} %get-tuple-element.106), channel_id=1, source_target_pairs={{0,3},{1,2},{2,1},{3,0},{4,7},{5,6},{6,5},{7,4},{8,11},{9,10},{10,... | collective-permute-start | bytes 18440 | tf_op jit(solution)/shard_map/ppermute | solution.py:516
  77.0 3.9 %collective-permute-start.30 = (f32[12,128]{1,0:T(8,128)S(1)}, f32[12,128]{1,0:T(8,128)S(1)}, u32[]{:S(2)}, u32[]{:S(2)}) collective-permute-start(f32[12,128]{1,0:T(8,128)S(1)} %get-tuple-element.107), channel_id=1, source_target_pairs={{0,4},{1,5},{2,6},{3,7},{4,0},{5,1},{6,2},{7,3},{8,12},{9,13},{10,... | collective-permute-start | bytes 18440 | tf_op jit(solution)/shard_map/ppermute | solution.py:516
  (24 other events, 75.5 us)

commit v12 on v11

--- a/solution.py
+++ b/solution.py
@@ -305,31 +305,27 @@
         held[i * elem_rows : (i + 1) * elem_rows, :] = forces[i]
 
 
-def halo_sum_kernel(rows, held, nodes, after, *outs):
+def halo_sum_kernel(rows, held, nodes, *outs):
     sum_halo(stored_row(held, nodes), nodes, rows, outs)
+
+
+def after_kernel(kernel, place, *refs):
+    kernel(*refs[:place], *refs[place + 1 :])
 
 
 def own_sum_kernel(held, nodes, after, own):
     sum_own(stored_row(held, nodes), nodes, own)
 
 
-def later_kernel(rows, found, *refs):
+def later_force_kernel(rows, found, *refs):
     recvs = in_place(refs[:4], ALONE)
-    nodes, thick, splat, held, slow, mixed = refs[4:10]
-    outs = refs[10:]
+    nodes, thick, splat, held, slow, mixed = refs[4:]
     elem_rows = thick.shape[0]
     forces = corner_forces(found, rows, recvs, nodes, thick, splat)
     kept = slow[...] == 1
     for i in range(12):
         span = slice(i * elem_rows, (i + 1) * elem_rows)
-        forces[i] = jnp.where(kept, held[span, :], forces[i])
-        mixed[span, :] = forces[i]
-
-    def force_row(c, r):
-        k, h = divmod(r, elem_rows)
-        return forces[c * 4 + k][h : h + 1, :]
-
-    sum_halo(force_row, nodes, rows, outs)
+        mixed[span, :] = jnp.where(kept, held[span, :], forces[i])
 
 
 def returned_sums(backs, lists, rows):
@@ -627,7 +623,7 @@
                 )
                 returned = swap(pushes, devices, capacity)
                 outs = call(
-                    functools.partial(halo_sum_kernel, rows),
+                    functools.partial(after_kernel, functools.partial(halo_sum_kernel, rows), 2),
                     [held, nodes, pushes],
                     sent,
                     "halo_sum",
@@ -635,11 +631,14 @@
                 )
                 forces = held
             else:
-                forces, *outs = call(
-                    functools.partial(later_kernel, rows),
+                (forces,) = call(
+                    functools.partial(later_force_kernel, rows),
                     field + [held, slow],
-                    [corner_values] + sent,
-                    "forces_halo_sum",
+                    [corner_values],
+                    "forces_later",
+                )
+                outs = call(
+                    functools.partial(halo_sum_kernel, rows), [forces, nodes], sent, "halo_sum"
                 )
             backs = exchange(outs, BESIDE if first else ALONE)
             (own,) = call(own_sum_kernel, [forces, nodes, outs[2]], [nodal], "own_sum", far=(2,))

time: 82.2 us -> 81.6 us (level)
    pallas_call x24 -> x26, Pallas kernels: 20.5 us -> 19.9 us  [call(): pl.pallas_call(kernel, out_shape=tuple(outputs), in_specs=specs, out_spec...]
  transfers between devices with their start and end apart: 36 -> 36, of which waited for: 12 -> 12; matrix products, arithmetic and copies ran while one was open for 0% -> 0% of each run, Pallas kernels for 9% -> 10%
where the time goes in v12:
time: 81.6 us; the launch traced here: 81.2 us
  starting transfers between devices  51.8 us (63%)
  Pallas kernels  19.9 us (24%)
  waiting for transfers between devices  8.2 us (10%)
  between operations  1.09 us (1%)
    ppermute x32, starting transfers between devices, exchange(): return [lax.ppermute(blocks[n], ('px', 'py'), swaps[n]) for n in order]  32.9 us
    pallas_call x26, Pallas kernels, call(): pl.pallas_call(kernel, out_shape=tuple(outputs), in_specs=specs, out_spec...  19.9 us
    all_to_all x4, starting transfers between devices, swap(): return lax.all_to_all(slots, axes, 0, 0, tiled=True)  18.9 us
    ppermute x32, waiting for transfers between devices, exchange(): return [lax.ppermute(blocks[n], ('px', 'py'), swaps[n]) for n in order]  5.27 us
    all_to_all x4, waiting for transfers between devices, swap(): return lax.all_to_all(slots, axes, 0, 0, tiled=True)  2.93 us
  transfers between devices with their start and end apart: 36, of which 12 were waited for; matrix products, arithmetic and copies ran while one was open for 0% of the time, Pallas kernels for 10%

profile of v12, /device:TPU:0, one launch (start us, length us, event | category | flops | bytes accessed | tf_op | source)
XLA Modules:
  0.0 81.2 jit_solution(17455794827692358940)
XLA Ops:
  0.6 2.2 %slots.1 = (s32[32,128]{1,0:T(8,128)}, f32[32,3,128]{2,1,0:T(4,128)}) custom-call(f32[3,2048]{1,0:T(4,128)} %refs_11_.3, f32[3,2048]{1,0:T(4,128)} %refs_0_.3, s32[16,128]{1,0:T(8,128)} %bitcast.14, s32[16,128]{1,0:T(8,128)} %bitcast.15), custom_call_target="tpu_custom_call" | custom-call | tf_op jit(solution)/shard_map/slots/pallas_call | solution.py:483
  2.9 7.3 %all-to-all-start = ((f32[32,3,128]{2,1,0:T(4,128)}), f32[32,3,128]{2,1,0:T(4,128)S(1)}, u32[]{:S(2)}, u32[]{:S(2)}) async-start(f32[32,3,128]{2,1,0:T(4,128)} %get-tuple-element.66), calls=%async_computation | async-start | bytes 131072 | tf_op jit(solution)/shard_map/all_to_all | solution.py:518
  10.8 1.6 %collective-permute-start.1 = (f32[12,128]{1,0:T(8,128)S(1)}, f32[12,128]{1,0:T(8,128)S(1)}, u32[]{:S(2)}, u32[]{:S(2)}) collective-permute-start(f32[12,128]{1,0:T(8,128)S(1)} %get-tuple-element.59), channel_id=1, source_target_pairs={{0,3},{1,2},{2,1},{3,0},{4,7},{5,6},{6,5},{7,4},{8,11},{9,10},{10,... | collective-permute-start | bytes 18440 | tf_op jit(solution)/shard_map/ppermute | solution.py:512
  12.5 2.3 %collective-permute-start.2 = (f32[12,128]{1,0:T(8,128)S(1)}, f32[12,128]{1,0:T(8,128)S(1)}, u32[]{:S(2)}, u32[]{:S(2)}) collective-permute-start(f32[12,128]{1,0:T(8,128)S(1)} %get-tuple-element.60), channel_id=1, source_target_pairs={{0,4},{1,5},{2,6},{3,7},{4,0},{5,1},{6,2},{7,3},{8,12},{9,13},{10,... | collective-permute-start | bytes 18440 | tf_op jit(solution)/shard_map/ppermute | solution.py:512
  17.6 1.9 %contact.2.refs_2_ = f32[32,3,128]{2,1,0:T(4,128)} custom-call(f32[2,128,128]{2,1,0:T(8,128)S(1)} %get-tuple-element.64.select, bf16[96,2048]{1,0:T(8,128)(2,1)S(1)} %get-tuple-element.65.spread, f32[32,3,128]{2,1,0:T(4,128)S(1)} %all-to-all-done.arrived, f32[192,128]{1,0:T(8,128)S(1)} %forces.2.after.refs_0_.held.refs_7_), custom_call_target="tpu_custom_call" | custom-call | tf_op jit(solution)/shard_map/contact/pallas_call | solution.py:483
  19.5 3.7 %all-to-all-start.1 = ((f32[32,3,128]{2,1,0:T(4,128)}), f32[32,3,128]{2,1,0:T(4,128)S(1)}, u32[]{:S(2)}, u32[]{:S(2)}) async-start(f32[32,3,128]{2,1,0:T(4,128)} %contact.2.refs_2_), calls=%async_computation.1 | async-start | bytes 131072 | tf_op jit(solution)/shard_map/all_to_all | solution.py:518
  24.2 1.6 %collective-permute-start.5 = (f32[12,128]{1,0:T(8,128)S(1)}, f32[12,128]{1,0:T(8,128)S(1)}, u32[]{:S(2)}, u32[]{:S(2)}) collective-permute-start(f32[12,128]{1,0:T(8,128)S(1)} %get-tuple-element.69), channel_id=1, source_target_pairs={{0,3},{1,2},{2,1},{3,0},{4,7},{5,6},{6,5},{7,4},{8,11},{9,10},{10,... | collective-permute-start | bytes 18440 | tf_op jit(solution)/shard_map/ppermute | solution.py:512
  25.8 2.3 %collective-permute-start.6 = (f32[12,128]{1,0:T(8,128)S(1)}, f32[12,128]{1,0:T(8,128)S(1)}, u32[]{:S(2)}, u32[]{:S(2)}) collective-permute-start(f32[12,128]{1,0:T(8,128)S(1)} %get-tuple-element.70), channel_id=1, source_target_pairs={{0,4},{1,5},{2,6},{3,7},{4,0},{5,1},{6,2},{7,3},{8,12},{9,13},{10,... | collective-permute-start | bytes 18440 | tf_op jit(solution)/shard_map/ppermute | solution.py:512
  32.0 2.1 %collective-permute-start.10 = (f32[12,128]{1,0:T(8,128)S(1)}, f32[12,128]{1,0:T(8,128)S(1)}, u32[]{:S(2)}, u32[]{:S(2)}) collective-permute-start(f32[12,128]{1,0:T(8,128)S(1)} %get-tuple-element.74), channel_id=1, source_target_pairs={{0,4},{1,5},{2,6},{3,7},{4,0},{5,1},{6,2},{7,3},{8,12},{9,13},{10,... | collective-permute-start | bytes 18440 | tf_op jit(solution)/shard_map/ppermute | solution.py:512
  37.2 1.5 %collective-permute-start.13 = (f32[12,128]{1,0:T(8,128)S(1)}, f32[12,128]{1,0:T(8,128)S(1)}, u32[]{:S(2)}, u32[]{:S(2)}) collective-permute-start(f32[12,128]{1,0:T(8,128)S(1)} %get-tuple-element.79), channel_id=1, source_target_pairs={{0,3},{1,2},{2,1},{3,0},{4,7},{5,6},{6,5},{7,4},{8,11},{9,10},{10,... | collective-permute-start | bytes 18440 | tf_op jit(solution)/shard_map/ppermute | solution.py:512
  38.7 2.2 %collective-permute-start.14 = (f32[12,128]{1,0:T(8,128)S(1)}, f32[12,128]{1,0:T(8,128)S(1)}, u32[]{:S(2)}, u32[]{:S(2)}) collective-permute-start(f32[12,128]{1,0:T(8,128)S(1)} %get-tuple-element.80), channel_id=1, source_target_pairs={{0,4},{1,5},{2,6},{3,7},{4,0},{5,1},{6,2},{7,3},{8,12},{9,13},{10,... | collective-permute-start | bytes 18440 | tf_op jit(solution)/shard_map/ppermute | solution.py:512
  42.6 1.3 %last_update.1 = (f32[48,128]{1,0:T(8,128)S(1)}, f32[48,128]{1,0:T(8,128)S(1)}, f32[32,3,128]{2,1,0:T(4,128)}) custom-call(f32[48,128]{1,0:T(8,128)S(1)} %own_sum.5.refs_0_, f32[12,128]{1,0:T(8,128)S(1)} %collective-permute-done.12.refs_1_, f32[12,128]{1,0:T(8,128)S(1)} %collective-permute-done.13.refs_2_, f32[12,128]{1,0:T(8,128)S(1)} %collective-permute-done.14.refs_3_, ...), custom_call_target="tpu_custom_call" | custom-call | tf_op jit(solution)/shard_map/last_update/pallas_call | solution.py:483
  43.8 4.2 %all-to-all-start.2 = ((f32[32,3,128]{2,1,0:T(4,128)}), f32[32,3,128]{2,1,0:T(4,128)S(1)}, u32[]{:S(2)}, u32[]{:S(2)}) async-start(f32[32,3,128]{2,1,0:T(4,128)} %get-tuple-element.85.after), calls=%async_computation.2 | async-start | bytes 131072 | tf_op jit(solution)/shard_map/all_to_all | solution.py:518
  48.5 1.6 %collective-permute-start.17 = (f32[12,128]{1,0:T(8,128)S(1)}, f32[12,128]{1,0:T(8,128)S(1)}, u32[]{:S(2)}, u32[]{:S(2)}) collective-permute-start(f32[12,128]{1,0:T(8,128)S(1)} %get-tuple-element.87), channel_id=1, source_target_pairs={{0,3},{1,2},{2,1},{3,0},{4,7},{5,6},{6,5},{7,4},{8,11},{9,10},{10,... | collective-permute-start | bytes 18440 | tf_op jit(solution)/shard_map/ppermute | solution.py:512
  50.2 2.3 %collective-permute-start.18 = (f32[12,128]{1,0:T(8,128)S(1)}, f32[12,128]{1,0:T(8,128)S(1)}, u32[]{:S(2)}, u32[]{:S(2)}) collective-permute-start(f32[12,128]{1,0:T(8,128)S(1)} %get-tuple-element.88), channel_id=1, source_target_pairs={{0,4},{1,5},{2,6},{3,7},{4,0},{5,1},{6,2},{7,3},{8,12},{9,13},{10,... | collective-permute-start | bytes 18440 | tf_op jit(solution)/shard_map/ppermute | solution.py:512
  53.3 0.8 collective-permute-done.18.refs_2_
  55.4 1.9 %contact.3.refs_2_ = f32[32,3,128]{2,1,0:T(4,128)} custom-call(f32[2,128,128]{2,1,0:T(8,128)S(1)} %get-tuple-element.64.select, bf16[96,2048]{1,0:T(8,128)(2,1)S(1)} %get-tuple-element.65.spread, f32[32,3,128]{2,1,0:T(4,128)S(1)} %all-to-all-done.2.arrived, f32[192,128]{1,0:T(8,128)S(1)} %forces.3.after.refs_0_.held.refs_7_), custom_call_target="tpu_custom_call" | custom-call | tf_op jit(solution)/shard_map/contact/pallas_call | solution.py:483
  57.3 3.7 %all-to-all-start.3 = ((f32[32,3,128]{2,1,0:T(4,128)}), f32[32,3,128]{2,1,0:T(4,128)S(1)}, u32[]{:S(2)}, u32[]{:S(2)}) async-start(f32[32,3,128]{2,1,0:T(4,128)} %contact.3.refs_2_), calls=%async_computation.3 | async-start | bytes 131072 | tf_op jit(solution)/shard_map/all_to_all | solution.py:518
  61.9 1.6 %collective-permute-start.21 = (f32[12,128]{1,0:T(8,128)S(1)}, f32[12,128]{1,0:T(8,128)S(1)}, u32[]{:S(2)}, u32[]{:S(2)}) collective-permute-start(f32[12,128]{1,0:T(8,128)S(1)} %get-tuple-element.92), channel_id=1, source_target_pairs={{0,3},{1,2},{2,1},{3,0},{4,7},{5,6},{6,5},{7,4},{8,11},{9,10},{10,... | collective-permute-start | bytes 18440 | tf_op jit(solution)/shard_map/ppermute | solution.py:512
  63.5 2.3 %collective-permute-start.22 = (f32[12,128]{1,0:T(8,128)S(1)}, f32[12,128]{1,0:T(8,128)S(1)}, u32[]{:S(2)}, u32[]{:S(2)}) collective-permute-start(f32[12,128]{1,0:T(8,128)S(1)} %get-tuple-element.93), channel_id=1, source_target_pairs={{0,4},{1,5},{2,6},{3,7},{4,0},{5,1},{6,2},{7,3},{8,12},{9,13},{10,... | collective-permute-start | bytes 18440 | tf_op jit(solution)/shard_map/ppermute | solution.py:512
  69.7 2.1 %collective-permute-start.26 = (f32[12,128]{1,0:T(8,128)S(1)}, f32[12,128]{1,0:T(8,128)S(1)}, u32[]{:S(2)}, u32[]{:S(2)}) collective-permute-start(f32[12,128]{1,0:T(8,128)S(1)} %get-tuple-element.98), channel_id=1, source_target_pairs={{0,4},{1,5},{2,6},{3,7},{4,0},{5,1},{6,2},{7,3},{8,12},{9,13},{10,... | collective-permute-start | bytes 18440 | tf_op jit(solution)/shard_map/ppermute | solution.py:512
  74.9 1.5 %collective-permute-start.29 = (f32[12,128]{1,0:T(8,128)S(1)}, f32[12,128]{1,0:T(8,128)S(1)}, u32[]{:S(2)}, u32[]{:S(2)}) collective-permute-start(f32[12,128]{1,0:T(8,128)S(1)} %get-tuple-element.102), channel_id=1, source_target_pairs={{0,3},{1,2},{2,1},{3,0},{4,7},{5,6},{6,5},{7,4},{8,11},{9,10},{10,... | collective-permute-start | bytes 18440 | tf_op jit(solution)/shard_map/ppermute | solution.py:512
  76.4 2.2 %collective-permute-start.30 = (f32[12,128]{1,0:T(8,128)S(1)}, f32[12,128]{1,0:T(8,128)S(1)}, u32[]{:S(2)}, u32[]{:S(2)}) collective-permute-start(f32[12,128]{1,0:T(8,128)S(1)} %get-tuple-element.103), channel_id=1, source_target_pairs={{0,4},{1,5},{2,6},{3,7},{4,0},{5,1},{6,2},{7,3},{8,12},{9,13},{10,... | collective-permute-start | bytes 18440 | tf_op jit(solution)/shard_map/ppermute | solution.py:512
  80.2 1.0 %final_update.1 = (f32[3,2048]{1,0:T(4,128)}, f32[3,2048]{1,0:T(4,128)}) custom-call(f32[48,128]{1,0:T(8,128)S(1)} %own_sum.7.refs_0_, f32[12,128]{1,0:T(8,128)S(1)} %collective-permute-done.28.refs_1_, f32[12,128]{1,0:T(8,128)S(1)} %collective-permute-done.29.refs_2_, f32[12,128]{1,0:T(8,128)S(1)} %collective-permute-done.30.refs_3_, ...), custom_call_target="tpu_custom_call" | custom-call | tf_op jit(solution)/shard_map/final_update/pallas_call | solution.py:483
  (98 shorter events, 25.1 us)
Async XLA Ops:
  2.9 14.7 %all-to-all-start = ((f32[32,3,128]{2,1,0:T(4,128)}), f32[32,3,128]{2,1,0:T(4,128)S(1)}, u32[]{:S(2)}, u32[]{:S(2)}) async-start(f32[32,3,128]{2,1,0:T(4,128)} %get-tuple-element.66), calls=%async_computation | async-start | bytes 131072 | tf_op jit(solution)/shard_map/all_to_all | solution.py:518
  10.5 5.5 %collective-permute-start = (f32[12,128]{1,0:T(8,128)S(1)}, f32[12,128]{1,0:T(8,128)S(1)}, u32[]{:S(2)}, u32[]{:S(2)}) collective-permute-start(f32[12,128]{1,0:T(8,128)S(1)} %get-tuple-element.58), channel_id=1, source_target_pairs={{0,1},{1,0},{2,3},{3,2},{4,8},{5,9},{6,10},{7,11},{8,4},{9,5},{10,... | collective-permute-start | bytes 18440 | tf_op jit(solution)/shard_map/ppermute | solution.py:512
  10.8 5.2 %collective-permute-start.1 = (f32[12,128]{1,0:T(8,128)S(1)}, f32[12,128]{1,0:T(8,128)S(1)}, u32[]{:S(2)}, u32[]{:S(2)}) collective-permute-start(f32[12,128]{1,0:T(8,128)S(1)} %get-tuple-element.59), channel_id=1, source_target_pairs={{0,3},{1,2},{2,1},{3,0},{4,7},{5,6},{6,5},{7,4},{8,11},{9,10},{10,... | collective-permute-start | bytes 18440 | tf_op jit(solution)/shard_map/ppermute | solution.py:512
  12.5 4.0 %collective-permute-start.2 = (f32[12,128]{1,0:T(8,128)S(1)}, f32[12,128]{1,0:T(8,128)S(1)}, u32[]{:S(2)}, u32[]{:S(2)}) collective-permute-start(f32[12,128]{1,0:T(8,128)S(1)} %get-tuple-element.60), channel_id=1, source_target_pairs={{0,4},{1,5},{2,6},{3,7},{4,0},{5,1},{6,2},{7,3},{8,12},{9,13},{10,... | collective-permute-start | bytes 18440 | tf_op jit(solution)/shard_map/ppermute | solution.py:512
  19.5 11.1 %all-to-all-start.1 = ((f32[32,3,128]{2,1,0:T(4,128)}), f32[32,3,128]{2,1,0:T(4,128)S(1)}, u32[]{:S(2)}, u32[]{:S(2)}) async-start(f32[32,3,128]{2,1,0:T(4,128)} %contact.2.refs_2_), calls=%async_computation.1 | async-start | bytes 131072 | tf_op jit(solution)/shard_map/all_to_all | solution.py:518
  23.9 5.3 %collective-permute-start.4 = (f32[12,128]{1,0:T(8,128)S(1)}, f32[12,128]{1,0:T(8,128)S(1)}, u32[]{:S(2)}, u32[]{:S(2)}) collective-permute-start(f32[12,128]{1,0:T(8,128)S(1)} %get-tuple-element.68), channel_id=1, source_target_pairs={{0,1},{1,0},{2,3},{3,2},{4,8},{5,9},{6,10},{7,11},{8,4},{9,5},{10,... | collective-permute-start | bytes 18440 | tf_op jit(solution)/shard_map/ppermute | solution.py:512
  24.2 5.0 %collective-permute-start.5 = (f32[12,128]{1,0:T(8,128)S(1)}, f32[12,128]{1,0:T(8,128)S(1)}, u32[]{:S(2)}, u32[]{:S(2)}) collective-permute-start(f32[12,128]{1,0:T(8,128)S(1)} %get-tuple-element.69), channel_id=1, source_target_pairs={{0,3},{1,2},{2,1},{3,0},{4,7},{5,6},{6,5},{7,4},{8,11},{9,10},{10,... | collective-permute-start | bytes 18440 | tf_op jit(solution)/shard_map/ppermute | solution.py:512
  25.8 4.0 %collective-permute-start.6 = (f32[12,128]{1,0:T(8,128)S(1)}, f32[12,128]{1,0:T(8,128)S(1)}, u32[]{:S(2)}, u32[]{:S(2)}) collective-permute-start(f32[12,128]{1,0:T(8,128)S(1)} %get-tuple-element.70), channel_id=1, source_target_pairs={{0,4},{1,5},{2,6},{3,7},{4,0},{5,1},{6,2},{7,3},{8,12},{9,13},{10,... | collective-permute-start | bytes 18440 | tf_op jit(solution)/shard_map/ppermute | solution.py:512
  32.0 3.8 %collective-permute-start.10 = (f32[12,128]{1,0:T(8,128)S(1)}, f32[12,128]{1,0:T(8,128)S(1)}, u32[]{:S(2)}, u32[]{:S(2)}) collective-permute-start(f32[12,128]{1,0:T(8,128)S(1)} %get-tuple-element.74), channel_id=1, source_target_pairs={{0,4},{1,5},{2,6},{3,7},{4,0},{5,1},{6,2},{7,3},{8,12},{9,13},{10,... | collective-permute-start | bytes 18440 | tf_op jit(solution)/shard_map/ppermute | solution.py:512
  37.1 4.9 %collective-permute-start.12 = (f32[12,128]{1,0:T(8,128)S(1)}, f32[12,128]{1,0:T(8,128)S(1)}, u32[]{:S(2)}, u32[]{:S(2)}) collective-permute-start(f32[12,128]{1,0:T(8,128)S(1)} %get-tuple-element.78), channel_id=1, source_target_pairs={{0,1},{1,0},{2,3},{3,2},{4,8},{5,9},{6,10},{7,11},{8,4},{9,5},{10,... | collective-permute-start | bytes 18440 | tf_op jit(solution)/shard_map/ppermute | solution.py:512
  37.2 4.8 %collective-permute-start.13 = (f32[12,128]{1,0:T(8,128)S(1)}, f32[12,128]{1,0:T(8,128)S(1)}, u32[]{:S(2)}, u32[]{:S(2)}) collective-permute-start(f32[12,128]{1,0:T(8,128)S(1)} %get-tuple-element.79), channel_id=1, source_target_pairs={{0,3},{1,2},{2,1},{3,0},{4,7},{5,6},{6,5},{7,4},{8,11},{9,10},{10,... | collective-permute-start | bytes 18440 | tf_op jit(solution)/shard_map/ppermute | solution.py:512
  38.7 3.9 %collective-permute-start.14 = (f32[12,128]{1,0:T(8,128)S(1)}, f32[12,128]{1,0:T(8,128)S(1)}, u32[]{:S(2)}, u32[]{:S(2)}) collective-permute-start(f32[12,128]{1,0:T(8,128)S(1)} %get-tuple-element.80), channel_id=1, source_target_pairs={{0,4},{1,5},{2,6},{3,7},{4,0},{5,1},{6,2},{7,3},{8,12},{9,13},{10,... | collective-permute-start | bytes 18440 | tf_op jit(solution)/shard_map/ppermute | solution.py:512
  43.8 11.6 %all-to-all-start.2 = ((f32[32,3,128]{2,1,0:T(4,128)}), f32[32,3,128]{2,1,0:T(4,128)S(1)}, u32[]{:S(2)}, u32[]{:S(2)}) async-start(f32[32,3,128]{2,1,0:T(4,128)} %get-tuple-element.85.after), calls=%async_computation.2 | async-start | bytes 131072 | tf_op jit(solution)/shard_map/all_to_all | solution.py:518
  48.2 5.1 %collective-permute-start.16 = (f32[12,128]{1,0:T(8,128)S(1)}, f32[12,128]{1,0:T(8,128)S(1)}, u32[]{:S(2)}, u32[]{:S(2)}) collective-permute-start(f32[12,128]{1,0:T(8,128)S(1)} %get-tuple-element.86), channel_id=1, source_target_pairs={{0,1},{1,0},{2,3},{3,2},{4,8},{5,9},{6,10},{7,11},{8,4},{9,5},{10,... | collective-permute-start | bytes 18440 | tf_op jit(solution)/shard_map/ppermute | solution.py:512
  48.5 4.8 %collective-permute-start.17 = (f32[12,128]{1,0:T(8,128)S(1)}, f32[12,128]{1,0:T(8,128)S(1)}, u32[]{:S(2)}, u32[]{:S(2)}) collective-permute-start(f32[12,128]{1,0:T(8,128)S(1)} %get-tuple-element.87), channel_id=1, source_target_pairs={{0,3},{1,2},{2,1},{3,0},{4,7},{5,6},{6,5},{7,4},{8,11},{9,10},{10,... | collective-permute-start | bytes 18440 | tf_op jit(solution)/shard_map/ppermute | solution.py:512
  50.2 4.0 %collective-permute-start.18 = (f32[12,128]{1,0:T(8,128)S(1)}, f32[12,128]{1,0:T(8,128)S(1)}, u32[]{:S(2)}, u32[]{:S(2)}) collective-permute-start(f32[12,128]{1,0:T(8,128)S(1)} %get-tuple-element.88), channel_id=1, source_target_pairs={{0,4},{1,5},{2,6},{3,7},{4,0},{5,1},{6,2},{7,3},{8,12},{9,13},{10,... | collective-permute-start | bytes 18440 | tf_op jit(solution)/shard_map/ppermute | solution.py:512
  57.3 11.0 %all-to-all-start.3 = ((f32[32,3,128]{2,1,0:T(4,128)}), f32[32,3,128]{2,1,0:T(4,128)S(1)}, u32[]{:S(2)}, u32[]{:S(2)}) async-start(f32[32,3,128]{2,1,0:T(4,128)} %contact.3.refs_2_), calls=%async_computation.3 | async-start | bytes 131072 | tf_op jit(solution)/shard_map/all_to_all | solution.py:518
  61.8 5.1 %collective-permute-start.20 = (f32[12,128]{1,0:T(8,128)S(1)}, f32[12,128]{1,0:T(8,128)S(1)}, u32[]{:S(2)}, u32[]{:S(2)}) collective-permute-start(f32[12,128]{1,0:T(8,128)S(1)} %get-tuple-element.91), channel_id=1, source_target_pairs={{0,1},{1,0},{2,3},{3,2},{4,8},{5,9},{6,10},{7,11},{8,4},{9,5},{10,... | collective-permute-start | bytes 18440 | tf_op jit(solution)/shard_map/ppermute | solution.py:512
  61.9 5.0 %collective-permute-start.21 = (f32[12,128]{1,0:T(8,128)S(1)}, f32[12,128]{1,0:T(8,128)S(1)}, u32[]{:S(2)}, u32[]{:S(2)}) collective-permute-start(f32[12,128]{1,0:T(8,128)S(1)} %get-tuple-element.92), channel_id=1, source_target_pairs={{0,3},{1,2},{2,1},{3,0},{4,7},{5,6},{6,5},{7,4},{8,11},{9,10},{10,... | collective-permute-start | bytes 18440 | tf_op jit(solution)/shard_map/ppermute | solution.py:512
  63.5 4.0 %collective-permute-start.22 = (f32[12,128]{1,0:T(8,128)S(1)}, f32[12,128]{1,0:T(8,128)S(1)}, u32[]{:S(2)}, u32[]{:S(2)}) collective-permute-start(f32[12,128]{1,0:T(8,128)S(1)} %get-tuple-element.93), channel_id=1, source_target_pairs={{0,4},{1,5},{2,6},{3,7},{4,0},{5,1},{6,2},{7,3},{8,12},{9,13},{10,... | collective-permute-start | bytes 18440 | tf_op jit(solution)/shard_map/ppermute | solution.py:512
  69.7 3.8 %collective-permute-start.26 = (f32[12,128]{1,0:T(8,128)S(1)}, f32[12,128]{1,0:T(8,128)S(1)}, u32[]{:S(2)}, u32[]{:S(2)}) collective-permute-start(f32[12,128]{1,0:T(8,128)S(1)} %get-tuple-element.98), channel_id=1, source_target_pairs={{0,4},{1,5},{2,6},{3,7},{4,0},{5,1},{6,2},{7,3},{8,12},{9,13},{10,... | collective-permute-start | bytes 18440 | tf_op jit(solution)/shard_map/ppermute | solution.py:512
  74.7 4.9 %collective-permute-start.28 = (f32[12,128]{1,0:T(8,128)S(1)}, f32[12,128]{1,0:T(8,128)S(1)}, u32[]{:S(2)}, u32[]{:S(2)}) collective-permute-start(f32[12,128]{1,0:T(8,128)S(1)} %get-tuple-element.101), channel_id=1, source_target_pairs={{0,1},{1,0},{2,3},{3,2},{4,8},{5,9},{6,10},{7,11},{8,4},{9,5},{10,... | collective-permute-start | bytes 18440 | tf_op jit(solution)/shard_map/ppermute | solution.py:512
  74.9 4.8 %collective-permute-start.29 = (f32[12,128]{1,0:T(8,128)S(1)}, f32[12,128]{1,0:T(8,128)S(1)}, u32[]{:S(2)}, u32[]{:S(2)}) collective-permute-start(f32[12,128]{1,0:T(8,128)S(1)} %get-tuple-element.102), channel_id=1, source_target_pairs={{0,3},{1,2},{2,1},{3,0},{4,7},{5,6},{6,5},{7,4},{8,11},{9,10},{10,... | collective-permute-start | bytes 18440 | tf_op jit(solution)/shard_map/ppermute | solution.py:512
  76.4 3.9 %collective-permute-start.30 = (f32[12,128]{1,0:T(8,128)S(1)}, f32[12,128]{1,0:T(8,128)S(1)}, u32[]{:S(2)}, u32[]{:S(2)}) collective-permute-start(f32[12,128]{1,0:T(8,128)S(1)} %get-tuple-element.103), channel_id=1, source_target_pairs={{0,4},{1,5},{2,6},{3,7},{4,0},{5,1},{6,2},{7,3},{8,12},{9,13},{10,... | collective-permute-start | bytes 18440 | tf_op jit(solution)/shard_map/ppermute | solution.py:512
  (24 other events, 75.9 us)

commit v13 on v12

--- a/solution.py
+++ b/solution.py
@@ -338,6 +338,18 @@
     return scatter_add(lambda r: lists[r : r + 1, :], back_row, 4 * quarter, rows)
 
 
+def contact_sum_kernel(returned, inverse, contact):
+    rows = contact.shape[0] // 3
+    sums = scatter_add(
+        lambda r: inverse[r : r + 1, :],
+        lambda c, r: returned[r, c : c + 1, :],
+        inverse.shape[0],
+        rows,
+    )
+    for c in range(3):
+        contact[c * rows : (c + 1) * rows, :] = sums[c]
+
+
 def sends_kernel(disp, lists, after, *sends):
     gather_halo(disp, disp.shape[0] // 3, lists, sends)
 
@@ -408,8 +420,8 @@
 def first_update_kernel(starting, *refs):
     refs = list(refs)
     own = refs[0]
-    returned, inverse, lists, inv_mass, disp, vel, ext = refs[5:12]
-    new_vel, new_disp, contact, *sends = refs[12:]
+    contact, lists, inv_mass, disp, vel, ext = refs[5:11]
+    new_vel, new_disp, *sends = refs[11:]
     rows = disp.shape[0] // 3
     backs = returned_sums(in_place(refs[1:5], BESIDE), lists, rows)
     internal = [mine + more for mine, more in zip(components(own), backs)]
@@ -418,16 +430,10 @@
         spread_rows(vel, new_vel, 3)
         spread_rows(ext, ext_rows, 3)
         vel, ext = new_vel, ext_rows
-    sums = scatter_add(
-        lambda r: inverse[r : r + 1, :],
-        lambda c, r: returned[r, c : c + 1, :],
-        inverse.shape[0],
-        rows,
-    )
+    sums = components(contact)
     steps = advance(internal, sums, ext, inv_mass, vel, disp, rows)
     for c, vel_c, disp_c in steps:
         span = slice(c * rows, (c + 1) * rows)
-        contact[span, :] = sums[c]
         new_vel[span, :] = vel_c
         new_disp[span, :] = disp_c
     gather_halo(new_disp, rows, lists, sends)
@@ -643,14 +649,17 @@
             backs = exchange(outs, BESIDE if first else ALONE)
             (own,) = call(own_sum_kernel, [forces, nodes, outs[2]], [nodal], "own_sum", far=(2,))
             if first:
-                inputs = [own, *backs, returned, inverse, lists, inv_mass, disp, vel]
-                outputs = [nodal] * 3 + sent
+                (contact,) = call(
+                    contact_sum_kernel, [returned, inverse], [nodal], "contact_sum"
+                )
+                inputs = [own, *backs, contact, lists, inv_mass, disp, vel]
+                outputs = [nodal] * 2 + sent
                 if step_no == 0:
                     inputs.append(ext_force)
                     outputs.append(nodal)
                 else:
                     inputs.append(ext)
-                vel, disp, contact, *sends = call(
+                vel, disp, *sends = call(
                     functools.partial(first_update_kernel, step_no == 0),
                     inputs,
                     outputs,

time: 81.6 us -> 81.4 us (level)
  starting transfers between devices: 51.8 us -> 50.5 us
    all_to_all x4, waiting for transfers between devices: 2.93 us -> 4.2 us  [swap(): return lax.all_to_all(slots, axes, 0, 0, tiled=True)]
    ppermute x32, starting transfers between devices: 32.9 us -> 31.9 us  [exchange(): return [lax.ppermute(blocks[n], ('px', 'py'), swaps[n]) for n in order]]
    pallas_call x26 -> x28, Pallas kernels: 19.9 us -> 20.2 us  [call(): pl.pallas_call(kernel, out_shape=tuple(outputs), in_specs=specs, out_spec...]
  transfers between devices with their start and end apart: 36 -> 36, of which waited for: 12 -> 12; matrix products, arithmetic and copies ran while one was open for 0% -> 0% of each run, Pallas kernels for 10% -> 11%
where the time goes in v13:
time: 81.4 us; the launch traced here: 81 us
  starting transfers between devices  50.5 us (62%)
  Pallas kernels  20.2 us (25%)
  waiting for transfers between devices  8.85 us (11%)
  between operations  1.18 us (1%)
    ppermute x32, starting transfers between devices, exchange(): return [lax.ppermute(blocks[n], ('px', 'py'), swaps[n]) for n in order]  31.9 us
    pallas_call x28, Pallas kernels, call(): pl.pallas_call(kernel, out_shape=tuple(outputs), in_specs=specs, out_spec...  20.2 us
    all_to_all x4, starting transfers between devices, swap(): return lax.all_to_all(slots, axes, 0, 0, tiled=True)  18.5 us
    ppermute x32, waiting for transfers between devices, exchange(): return [lax.ppermute(blocks[n], ('px', 'py'), swaps[n]) for n in order]  4.65 us
    all_to_all x4, waiting for transfers between devices, swap(): return lax.all_to_all(slots, axes, 0, 0, tiled=True)  4.2 us
  transfers between devices with their start and end apart: 36, of which 12 were waited for; matrix products, arithmetic and copies ran while one was open for 0% of the time, Pallas kernels for 11%

profile of v13, /device:TPU:0, one launch (start us, length us, event | category | flops | bytes accessed | tf_op | source)
XLA Modules:
  0.0 81.0 jit_solution(1119090151470703550)
XLA Ops:
  0.6 2.2 %slots.1 = (s32[32,128]{1,0:T(8,128)}, f32[32,3,128]{2,1,0:T(4,128)}) custom-call(f32[3,2048]{1,0:T(4,128)} %refs_11_.1, f32[3,2048]{1,0:T(4,128)} %refs_0_.3, s32[16,128]{1,0:T(8,128)} %bitcast.14, s32[16,128]{1,0:T(8,128)} %bitcast.15), custom_call_target="tpu_custom_call" | custom-call | tf_op jit(solution)/shard_map/slots/pallas_call | solution.py:489
  2.9 7.3 %all-to-all-start = ((f32[32,3,128]{2,1,0:T(4,128)}), f32[32,3,128]{2,1,0:T(4,128)S(1)}, u32[]{:S(2)}, u32[]{:S(2)}) async-start(f32[32,3,128]{2,1,0:T(4,128)} %get-tuple-element.64), calls=%async_computation | async-start | bytes 131072 | tf_op jit(solution)/shard_map/all_to_all | solution.py:524
  10.8 1.6 %collective-permute-start.1 = (f32[12,128]{1,0:T(8,128)S(1)}, f32[12,128]{1,0:T(8,128)S(1)}, u32[]{:S(2)}, u32[]{:S(2)}) collective-permute-start(f32[12,128]{1,0:T(8,128)S(1)} %get-tuple-element.57), channel_id=1, source_target_pairs={{0,3},{1,2},{2,1},{3,0},{4,7},{5,6},{6,5},{7,4},{8,11},{9,10},{10,... | collective-permute-start | bytes 18440 | tf_op jit(solution)/shard_map/ppermute | solution.py:518
  12.5 2.3 %collective-permute-start.2 = (f32[12,128]{1,0:T(8,128)S(1)}, f32[12,128]{1,0:T(8,128)S(1)}, u32[]{:S(2)}, u32[]{:S(2)}) collective-permute-start(f32[12,128]{1,0:T(8,128)S(1)} %get-tuple-element.58), channel_id=1, source_target_pairs={{0,4},{1,5},{2,6},{3,7},{4,0},{5,1},{6,2},{7,3},{8,12},{9,13},{10,... | collective-permute-start | bytes 18440 | tf_op jit(solution)/shard_map/ppermute | solution.py:518
  17.6 1.9 %contact.2.refs_2_ = f32[32,3,128]{2,1,0:T(4,128)} custom-call(f32[2,128,128]{2,1,0:T(8,128)S(1)} %get-tuple-element.62.select, bf16[96,2048]{1,0:T(8,128)(2,1)S(1)} %get-tuple-element.63.spread, f32[32,3,128]{2,1,0:T(4,128)S(1)} %all-to-all-done.arrived, f32[192,128]{1,0:T(8,128)S(1)} %forces.2.after.refs_0_.held.refs_7_), custom_call_target="tpu_custom_call" | custom-call | tf_op jit(solution)/shard_map/contact/pallas_call | solution.py:489
  19.5 3.7 %all-to-all-start.1 = ((f32[32,3,128]{2,1,0:T(4,128)}), f32[32,3,128]{2,1,0:T(4,128)S(1)}, u32[]{:S(2)}, u32[]{:S(2)}) async-start(f32[32,3,128]{2,1,0:T(4,128)} %contact.2.refs_2_), calls=%async_computation.1 | async-start | bytes 131072 | tf_op jit(solution)/shard_map/all_to_all | solution.py:524
  24.2 1.6 %collective-permute-start.5 = (f32[12,128]{1,0:T(8,128)S(1)}, f32[12,128]{1,0:T(8,128)S(1)}, u32[]{:S(2)}, u32[]{:S(2)}) collective-permute-start(f32[12,128]{1,0:T(8,128)S(1)} %get-tuple-element.67), channel_id=1, source_target_pairs={{0,3},{1,2},{2,1},{3,0},{4,7},{5,6},{6,5},{7,4},{8,11},{9,10},{10,... | collective-permute-start | bytes 18440 | tf_op jit(solution)/shard_map/ppermute | solution.py:518
  25.8 2.3 %collective-permute-start.6 = (f32[12,128]{1,0:T(8,128)S(1)}, f32[12,128]{1,0:T(8,128)S(1)}, u32[]{:S(2)}, u32[]{:S(2)}) collective-permute-start(f32[12,128]{1,0:T(8,128)S(1)} %get-tuple-element.68), channel_id=1, source_target_pairs={{0,4},{1,5},{2,6},{3,7},{4,0},{5,1},{6,2},{7,3},{8,12},{9,13},{10,... | collective-permute-start | bytes 18440 | tf_op jit(solution)/shard_map/ppermute | solution.py:518
  29.2 1.4 %all-to-all-done.1.returned = f32[32,3,128]{2,1,0:T(4,128)S(1)} async-done(((f32[32,3,128]{2,1,0:T(4,128)}), f32[32,3,128]{2,1,0:T(4,128)S(1)}, u32[]{:S(2)}, u32[]{:S(2)}) %all-to-all-start.1) | async-done | bytes 49184 | tf_op jit(solution)/shard_map/all_to_all | solution.py:524
  32.3 1.6 %collective-permute-start.10 = (f32[12,128]{1,0:T(8,128)S(1)}, f32[12,128]{1,0:T(8,128)S(1)}, u32[]{:S(2)}, u32[]{:S(2)}) collective-permute-start(f32[12,128]{1,0:T(8,128)S(1)} %get-tuple-element.72), channel_id=1, source_target_pairs={{0,4},{1,5},{2,6},{3,7},{4,0},{5,1},{6,2},{7,3},{8,12},{9,13},{10,... | collective-permute-start | bytes 18440 | tf_op jit(solution)/shard_map/ppermute | solution.py:518
  37.2 1.7 %collective-permute-start.13 = (f32[12,128]{1,0:T(8,128)S(1)}, f32[12,128]{1,0:T(8,128)S(1)}, u32[]{:S(2)}, u32[]{:S(2)}) collective-permute-start(f32[12,128]{1,0:T(8,128)S(1)} %get-tuple-element.77), channel_id=1, source_target_pairs={{0,3},{1,2},{2,1},{3,0},{4,7},{5,6},{6,5},{7,4},{8,11},{9,10},{10,... | collective-permute-start | bytes 18440 | tf_op jit(solution)/shard_map/ppermute | solution.py:518
  38.9 1.6 %collective-permute-start.14 = (f32[12,128]{1,0:T(8,128)S(1)}, f32[12,128]{1,0:T(8,128)S(1)}, u32[]{:S(2)}, u32[]{:S(2)}) collective-permute-start(f32[12,128]{1,0:T(8,128)S(1)} %get-tuple-element.78), channel_id=1, source_target_pairs={{0,4},{1,5},{2,6},{3,7},{4,0},{5,1},{6,2},{7,3},{8,12},{9,13},{10,... | collective-permute-start | bytes 18440 | tf_op jit(solution)/shard_map/ppermute | solution.py:518
  42.7 1.3 %last_update.1 = (f32[48,128]{1,0:T(8,128)S(1)}, f32[48,128]{1,0:T(8,128)S(1)}, f32[32,3,128]{2,1,0:T(4,128)}) custom-call(f32[48,128]{1,0:T(8,128)S(1)} %own_sum.5.refs_0_, f32[12,128]{1,0:T(8,128)S(1)} %collective-permute-done.12.refs_1_, f32[12,128]{1,0:T(8,128)S(1)} %collective-permute-done.13.refs_2_, f32[12,128]{1,0:T(8,128)S(1)} %collective-permute-done.14.refs_3_, ...), custom_call_target="tpu_custom_call" | custom-call | tf_op jit(solution)/shard_map/last_update/pallas_call | solution.py:489
  43.9 3.8 %all-to-all-start.2 = ((f32[32,3,128]{2,1,0:T(4,128)}), f32[32,3,128]{2,1,0:T(4,128)S(1)}, u32[]{:S(2)}, u32[]{:S(2)}) async-start(f32[32,3,128]{2,1,0:T(4,128)} %get-tuple-element.82.after), calls=%async_computation.2 | async-start | bytes 131072 | tf_op jit(solution)/shard_map/all_to_all | solution.py:524
  48.3 1.6 %collective-permute-start.17 = (f32[12,128]{1,0:T(8,128)S(1)}, f32[12,128]{1,0:T(8,128)S(1)}, u32[]{:S(2)}, u32[]{:S(2)}) collective-permute-start(f32[12,128]{1,0:T(8,128)S(1)} %get-tuple-element.84), channel_id=1, source_target_pairs={{0,3},{1,2},{2,1},{3,0},{4,7},{5,6},{6,5},{7,4},{8,11},{9,10},{10,... | collective-permute-start | bytes 18440 | tf_op jit(solution)/shard_map/ppermute | solution.py:518
  49.9 2.3 %collective-permute-start.18 = (f32[12,128]{1,0:T(8,128)S(1)}, f32[12,128]{1,0:T(8,128)S(1)}, u32[]{:S(2)}, u32[]{:S(2)}) collective-permute-start(f32[12,128]{1,0:T(8,128)S(1)} %get-tuple-element.85), channel_id=1, source_target_pairs={{0,4},{1,5},{2,6},{3,7},{4,0},{5,1},{6,2},{7,3},{8,12},{9,13},{10,... | collective-permute-start | bytes 18440 | tf_op jit(solution)/shard_map/ppermute | solution.py:518
  55.2 1.9 %contact.3.refs_2_ = f32[32,3,128]{2,1,0:T(4,128)} custom-call(f32[2,128,128]{2,1,0:T(8,128)S(1)} %get-tuple-element.62.select, bf16[96,2048]{1,0:T(8,128)(2,1)S(1)} %get-tuple-element.63.spread, f32[32,3,128]{2,1,0:T(4,128)S(1)} %all-to-all-done.2.arrived, f32[192,128]{1,0:T(8,128)S(1)} %forces.3.after.refs_0_.held.refs_7_), custom_call_target="tpu_custom_call" | custom-call | tf_op jit(solution)/shard_map/contact/pallas_call | solution.py:489
  57.0 3.7 %all-to-all-start.3 = ((f32[32,3,128]{2,1,0:T(4,128)}), f32[32,3,128]{2,1,0:T(4,128)S(1)}, u32[]{:S(2)}, u32[]{:S(2)}) async-start(f32[32,3,128]{2,1,0:T(4,128)} %contact.3.refs_2_), calls=%async_computation.3 | async-start | bytes 131072 | tf_op jit(solution)/shard_map/all_to_all | solution.py:524
  61.6 1.6 %collective-permute-start.21 = (f32[12,128]{1,0:T(8,128)S(1)}, f32[12,128]{1,0:T(8,128)S(1)}, u32[]{:S(2)}, u32[]{:S(2)}) collective-permute-start(f32[12,128]{1,0:T(8,128)S(1)} %get-tuple-element.89), channel_id=1, source_target_pairs={{0,3},{1,2},{2,1},{3,0},{4,7},{5,6},{6,5},{7,4},{8,11},{9,10},{10,... | collective-permute-start | bytes 18440 | tf_op jit(solution)/shard_map/ppermute | solution.py:518
  63.3 2.3 %collective-permute-start.22 = (f32[12,128]{1,0:T(8,128)S(1)}, f32[12,128]{1,0:T(8,128)S(1)}, u32[]{:S(2)}, u32[]{:S(2)}) collective-permute-start(f32[12,128]{1,0:T(8,128)S(1)} %get-tuple-element.90), channel_id=1, source_target_pairs={{0,4},{1,5},{2,6},{3,7},{4,0},{5,1},{6,2},{7,3},{8,12},{9,13},{10,... | collective-permute-start | bytes 18440 | tf_op jit(solution)/shard_map/ppermute | solution.py:518
  66.6 1.4 %all-to-all-done.3.returned = f32[32,3,128]{2,1,0:T(4,128)S(1)} async-done(((f32[32,3,128]{2,1,0:T(4,128)}), f32[32,3,128]{2,1,0:T(4,128)S(1)}, u32[]{:S(2)}, u32[]{:S(2)}) %all-to-all-start.3) | async-done | bytes 49184 | tf_op jit(solution)/shard_map/all_to_all | solution.py:524
  69.6 1.6 %collective-permute-start.26 = (f32[12,128]{1,0:T(8,128)S(1)}, f32[12,128]{1,0:T(8,128)S(1)}, u32[]{:S(2)}, u32[]{:S(2)}) collective-permute-start(f32[12,128]{1,0:T(8,128)S(1)} %get-tuple-element.95), channel_id=1, source_target_pairs={{0,4},{1,5},{2,6},{3,7},{4,0},{5,1},{6,2},{7,3},{8,12},{9,13},{10,... | collective-permute-start | bytes 18440 | tf_op jit(solution)/shard_map/ppermute | solution.py:518
  74.6 1.7 %collective-permute-start.29 = (f32[12,128]{1,0:T(8,128)S(1)}, f32[12,128]{1,0:T(8,128)S(1)}, u32[]{:S(2)}, u32[]{:S(2)}) collective-permute-start(f32[12,128]{1,0:T(8,128)S(1)} %get-tuple-element.99), channel_id=1, source_target_pairs={{0,3},{1,2},{2,1},{3,0},{4,7},{5,6},{6,5},{7,4},{8,11},{9,10},{10,... | collective-permute-start | bytes 18440 | tf_op jit(solution)/shard_map/ppermute | solution.py:518
  76.3 1.7 %collective-permute-start.30 = (f32[12,128]{1,0:T(8,128)S(1)}, f32[12,128]{1,0:T(8,128)S(1)}, u32[]{:S(2)}, u32[]{:S(2)}) collective-permute-start(f32[12,128]{1,0:T(8,128)S(1)} %get-tuple-element.100), channel_id=1, source_target_pairs={{0,4},{1,5},{2,6},{3,7},{4,0},{5,1},{6,2},{7,3},{8,12},{9,13},{10,... | collective-permute-start | bytes 18440 | tf_op jit(solution)/shard_map/ppermute | solution.py:518
  (100 shorter events, 25.6 us)
Async XLA Ops:
  2.9 14.7 %all-to-all-start = ((f32[32,3,128]{2,1,0:T(4,128)}), f32[32,3,128]{2,1,0:T(4,128)S(1)}, u32[]{:S(2)}, u32[]{:S(2)}) async-start(f32[32,3,128]{2,1,0:T(4,128)} %get-tuple-element.64), calls=%async_computation | async-start | bytes 131072 | tf_op jit(solution)/shard_map/all_to_all | solution.py:524
  10.5 5.5 %collective-permute-start = (f32[12,128]{1,0:T(8,128)S(1)}, f32[12,128]{1,0:T(8,128)S(1)}, u32[]{:S(2)}, u32[]{:S(2)}) collective-permute-start(f32[12,128]{1,0:T(8,128)S(1)} %get-tuple-element.56), channel_id=1, source_target_pairs={{0,1},{1,0},{2,3},{3,2},{4,8},{5,9},{6,10},{7,11},{8,4},{9,5},{10,... | collective-permute-start | bytes 18440 | tf_op jit(solution)/shard_map/ppermute | solution.py:518
  10.8 5.2 %collective-permute-start.1 = (f32[12,128]{1,0:T(8,128)S(1)}, f32[12,128]{1,0:T(8,128)S(1)}, u32[]{:S(2)}, u32[]{:S(2)}) collective-permute-start(f32[12,128]{1,0:T(8,128)S(1)} %get-tuple-element.57), channel_id=1, source_target_pairs={{0,3},{1,2},{2,1},{3,0},{4,7},{5,6},{6,5},{7,4},{8,11},{9,10},{10,... | collective-permute-start | bytes 18440 | tf_op jit(solution)/shard_map/ppermute | solution.py:518
  12.5 4.0 %collective-permute-start.2 = (f32[12,128]{1,0:T(8,128)S(1)}, f32[12,128]{1,0:T(8,128)S(1)}, u32[]{:S(2)}, u32[]{:S(2)}) collective-permute-start(f32[12,128]{1,0:T(8,128)S(1)} %get-tuple-element.58), channel_id=1, source_target_pairs={{0,4},{1,5},{2,6},{3,7},{4,0},{5,1},{6,2},{7,3},{8,12},{9,13},{10,... | collective-permute-start | bytes 18440 | tf_op jit(solution)/shard_map/ppermute | solution.py:518
  19.5 11.1 %all-to-all-start.1 = ((f32[32,3,128]{2,1,0:T(4,128)}), f32[32,3,128]{2,1,0:T(4,128)S(1)}, u32[]{:S(2)}, u32[]{:S(2)}) async-start(f32[32,3,128]{2,1,0:T(4,128)} %contact.2.refs_2_), calls=%async_computation.1 | async-start | bytes 131072 | tf_op jit(solution)/shard_map/all_to_all | solution.py:524
  23.9 7.1 %collective-permute-start.4 = (f32[12,128]{1,0:T(8,128)S(1)}, f32[12,128]{1,0:T(8,128)S(1)}, u32[]{:S(2)}, u32[]{:S(2)}) collective-permute-start(f32[12,128]{1,0:T(8,128)S(1)} %get-tuple-element.66), channel_id=1, source_target_pairs={{0,1},{1,0},{2,3},{3,2},{4,8},{5,9},{6,10},{7,11},{8,4},{9,5},{10,... | collective-permute-start | bytes 18440 | tf_op jit(solution)/shard_map/ppermute | solution.py:518
  24.2 6.8 %collective-permute-start.5 = (f32[12,128]{1,0:T(8,128)S(1)}, f32[12,128]{1,0:T(8,128)S(1)}, u32[]{:S(2)}, u32[]{:S(2)}) collective-permute-start(f32[12,128]{1,0:T(8,128)S(1)} %get-tuple-element.67), channel_id=1, source_target_pairs={{0,3},{1,2},{2,1},{3,0},{4,7},{5,6},{6,5},{7,4},{8,11},{9,10},{10,... | collective-permute-start | bytes 18440 | tf_op jit(solution)/shard_map/ppermute | solution.py:518
  25.8 5.2 %collective-permute-start.6 = (f32[12,128]{1,0:T(8,128)S(1)}, f32[12,128]{1,0:T(8,128)S(1)}, u32[]{:S(2)}, u32[]{:S(2)}) collective-permute-start(f32[12,128]{1,0:T(8,128)S(1)} %get-tuple-element.68), channel_id=1, source_target_pairs={{0,4},{1,5},{2,6},{3,7},{4,0},{5,1},{6,2},{7,3},{8,12},{9,13},{10,... | collective-permute-start | bytes 18440 | tf_op jit(solution)/shard_map/ppermute | solution.py:518
  32.3 3.7 %collective-permute-start.10 = (f32[12,128]{1,0:T(8,128)S(1)}, f32[12,128]{1,0:T(8,128)S(1)}, u32[]{:S(2)}, u32[]{:S(2)}) collective-permute-start(f32[12,128]{1,0:T(8,128)S(1)} %get-tuple-element.72), channel_id=1, source_target_pairs={{0,4},{1,5},{2,6},{3,7},{4,0},{5,1},{6,2},{7,3},{8,12},{9,13},{10,... | collective-permute-start | bytes 18440 | tf_op jit(solution)/shard_map/ppermute | solution.py:518
  37.2 4.9 %collective-permute-start.12 = (f32[12,128]{1,0:T(8,128)S(1)}, f32[12,128]{1,0:T(8,128)S(1)}, u32[]{:S(2)}, u32[]{:S(2)}) collective-permute-start(f32[12,128]{1,0:T(8,128)S(1)} %get-tuple-element.76), channel_id=1, source_target_pairs={{0,1},{1,0},{2,3},{3,2},{4,8},{5,9},{6,10},{7,11},{8,4},{9,5},{10,... | collective-permute-start | bytes 18440 | tf_op jit(solution)/shard_map/ppermute | solution.py:518
  37.2 4.9 %collective-permute-start.13 = (f32[12,128]{1,0:T(8,128)S(1)}, f32[12,128]{1,0:T(8,128)S(1)}, u32[]{:S(2)}, u32[]{:S(2)}) collective-permute-start(f32[12,128]{1,0:T(8,128)S(1)} %get-tuple-element.77), channel_id=1, source_target_pairs={{0,3},{1,2},{2,1},{3,0},{4,7},{5,6},{6,5},{7,4},{8,11},{9,10},{10,... | collective-permute-start | bytes 18440 | tf_op jit(solution)/shard_map/ppermute | solution.py:518
  38.9 3.7 %collective-permute-start.14 = (f32[12,128]{1,0:T(8,128)S(1)}, f32[12,128]{1,0:T(8,128)S(1)}, u32[]{:S(2)}, u32[]{:S(2)}) collective-permute-start(f32[12,128]{1,0:T(8,128)S(1)} %get-tuple-element.78), channel_id=1, source_target_pairs={{0,4},{1,5},{2,6},{3,7},{4,0},{5,1},{6,2},{7,3},{8,12},{9,13},{10,... | collective-permute-start | bytes 18440 | tf_op jit(solution)/shard_map/ppermute | solution.py:518
  43.9 11.2 %all-to-all-start.2 = ((f32[32,3,128]{2,1,0:T(4,128)}), f32[32,3,128]{2,1,0:T(4,128)S(1)}, u32[]{:S(2)}, u32[]{:S(2)}) async-start(f32[32,3,128]{2,1,0:T(4,128)} %get-tuple-element.82.after), calls=%async_computation.2 | async-start | bytes 131072 | tf_op jit(solution)/shard_map/all_to_all | solution.py:524
  47.9 5.1 %collective-permute-start.16 = (f32[12,128]{1,0:T(8,128)S(1)}, f32[12,128]{1,0:T(8,128)S(1)}, u32[]{:S(2)}, u32[]{:S(2)}) collective-permute-start(f32[12,128]{1,0:T(8,128)S(1)} %get-tuple-element.83), channel_id=1, source_target_pairs={{0,1},{1,0},{2,3},{3,2},{4,8},{5,9},{6,10},{7,11},{8,4},{9,5},{10,... | collective-permute-start | bytes 18440 | tf_op jit(solution)/shard_map/ppermute | solution.py:518
  48.3 4.8 %collective-permute-start.17 = (f32[12,128]{1,0:T(8,128)S(1)}, f32[12,128]{1,0:T(8,128)S(1)}, u32[]{:S(2)}, u32[]{:S(2)}) collective-permute-start(f32[12,128]{1,0:T(8,128)S(1)} %get-tuple-element.84), channel_id=1, source_target_pairs={{0,3},{1,2},{2,1},{3,0},{4,7},{5,6},{6,5},{7,4},{8,11},{9,10},{10,... | collective-permute-start | bytes 18440 | tf_op jit(solution)/shard_map/ppermute | solution.py:518
  49.9 4.0 %collective-permute-start.18 = (f32[12,128]{1,0:T(8,128)S(1)}, f32[12,128]{1,0:T(8,128)S(1)}, u32[]{:S(2)}, u32[]{:S(2)}) collective-permute-start(f32[12,128]{1,0:T(8,128)S(1)} %get-tuple-element.85), channel_id=1, source_target_pairs={{0,4},{1,5},{2,6},{3,7},{4,0},{5,1},{6,2},{7,3},{8,12},{9,13},{10,... | collective-permute-start | bytes 18440 | tf_op jit(solution)/shard_map/ppermute | solution.py:518
  57.0 11.0 %all-to-all-start.3 = ((f32[32,3,128]{2,1,0:T(4,128)}), f32[32,3,128]{2,1,0:T(4,128)S(1)}, u32[]{:S(2)}, u32[]{:S(2)}) async-start(f32[32,3,128]{2,1,0:T(4,128)} %contact.3.refs_2_), calls=%async_computation.3 | async-start | bytes 131072 | tf_op jit(solution)/shard_map/all_to_all | solution.py:524
  61.5 7.0 %collective-permute-start.20 = (f32[12,128]{1,0:T(8,128)S(1)}, f32[12,128]{1,0:T(8,128)S(1)}, u32[]{:S(2)}, u32[]{:S(2)}) collective-permute-start(f32[12,128]{1,0:T(8,128)S(1)} %get-tuple-element.88), channel_id=1, source_target_pairs={{0,1},{1,0},{2,3},{3,2},{4,8},{5,9},{6,10},{7,11},{8,4},{9,5},{10,... | collective-permute-start | bytes 18440 | tf_op jit(solution)/shard_map/ppermute | solution.py:518
  61.6 6.8 %collective-permute-start.21 = (f32[12,128]{1,0:T(8,128)S(1)}, f32[12,128]{1,0:T(8,128)S(1)}, u32[]{:S(2)}, u32[]{:S(2)}) collective-permute-start(f32[12,128]{1,0:T(8,128)S(1)} %get-tuple-element.89), channel_id=1, source_target_pairs={{0,3},{1,2},{2,1},{3,0},{4,7},{5,6},{6,5},{7,4},{8,11},{9,10},{10,... | collective-permute-start | bytes 18440 | tf_op jit(solution)/shard_map/ppermute | solution.py:518
  63.3 5.2 %collective-permute-start.22 = (f32[12,128]{1,0:T(8,128)S(1)}, f32[12,128]{1,0:T(8,128)S(1)}, u32[]{:S(2)}, u32[]{:S(2)}) collective-permute-start(f32[12,128]{1,0:T(8,128)S(1)} %get-tuple-element.90), channel_id=1, source_target_pairs={{0,4},{1,5},{2,6},{3,7},{4,0},{5,1},{6,2},{7,3},{8,12},{9,13},{10,... | collective-permute-start | bytes 18440 | tf_op jit(solution)/shard_map/ppermute | solution.py:518
  69.6 3.7 %collective-permute-start.26 = (f32[12,128]{1,0:T(8,128)S(1)}, f32[12,128]{1,0:T(8,128)S(1)}, u32[]{:S(2)}, u32[]{:S(2)}) collective-permute-start(f32[12,128]{1,0:T(8,128)S(1)} %get-tuple-element.95), channel_id=1, source_target_pairs={{0,4},{1,5},{2,6},{3,7},{4,0},{5,1},{6,2},{7,3},{8,12},{9,13},{10,... | collective-permute-start | bytes 18440 | tf_op jit(solution)/shard_map/ppermute | solution.py:518
  74.5 5.0 %collective-permute-start.28 = (f32[12,128]{1,0:T(8,128)S(1)}, f32[12,128]{1,0:T(8,128)S(1)}, u32[]{:S(2)}, u32[]{:S(2)}) collective-permute-start(f32[12,128]{1,0:T(8,128)S(1)} %get-tuple-element.98), channel_id=1, source_target_pairs={{0,1},{1,0},{2,3},{3,2},{4,8},{5,9},{6,10},{7,11},{8,4},{9,5},{10,... | collective-permute-start | bytes 18440 | tf_op jit(solution)/shard_map/ppermute | solution.py:518
  74.6 4.9 %collective-permute-start.29 = (f32[12,128]{1,0:T(8,128)S(1)}, f32[12,128]{1,0:T(8,128)S(1)}, u32[]{:S(2)}, u32[]{:S(2)}) collective-permute-start(f32[12,128]{1,0:T(8,128)S(1)} %get-tuple-element.99), channel_id=1, source_target_pairs={{0,3},{1,2},{2,1},{3,0},{4,7},{5,6},{6,5},{7,4},{8,11},{9,10},{10,... | collective-permute-start | bytes 18440 | tf_op jit(solution)/shard_map/ppermute | solution.py:518
  76.3 3.7 %collective-permute-start.30 = (f32[12,128]{1,0:T(8,128)S(1)}, f32[12,128]{1,0:T(8,128)S(1)}, u32[]{:S(2)}, u32[]{:S(2)}) collective-permute-start(f32[12,128]{1,0:T(8,128)S(1)} %get-tuple-element.100), channel_id=1, source_target_pairs={{0,4},{1,5},{2,6},{3,7},{4,0},{5,1},{6,2},{7,3},{8,12},{9,13},{10,... | collective-permute-start | bytes 18440 | tf_op jit(solution)/shard_map/ppermute | solution.py:518
  (24 other events, 76.6 us)
